TPU v7x, 32 devices: a whole 2x2x4 slice. The times are simulated.
32 devices in a mesh: groups: 2 (over x), win: 4 (over y, core), rcv: 4 (over z).
Axes of the slice: x: 2, y: 2, z: 4, core: 2. Of those that a mesh axis runs over, the one named last changes fastest.
Arguments:
- traces: bfloat16 [32, 768, 4096], P('win', ('groups', 'rcv')), parts along dimension 1, may hold values from -6 to 6
- valid: int32 [64], P(('groups', 'win')), parts along dimension 0, may hold values 0 or 1
- src_station: int32 [64], P('groups'), parts along dimension 0, may hold values from 0 to 383, as said below
Outputs:
- stacks: float32 [32, 768, 2, 512], P(None, ('groups', 'rcv'), None, 'win'), parts along dimension 1
There are 2 independent parts, one for each index of `groups`. A program takes and returns all parts, laid end to end along the dimension named above; each array names one. Nothing has to cross between parts.
Inputs may be any that keep to these rules, and one draw needn't show every extreme that they name: `src_station`: distinct stations; station 0 and station 384 - 1 are always among them.
All inputs are finite; a program needn't handle non-finite values. No bound on the sum of `valid` on one device may be relied on, other than what follows from the above.
Results may differ from a plain program's by a relative error of at most 0.0049.
Values may be sent and summed in bfloat16 or wider, within the bound.
No kernel may reach another device: no remote copies, remote signals or barrier semaphores. Data moves between devices by JAX's collectives and lax.ppermute only.
A program may use at most 128 MiB of HBM per device.

v0:
```python
import functools
import math

import jax
import jax.numpy as jnp
import numpy as np
from jax import lax
from jax.experimental import pallas as pl
from jax.experimental.pallas import tpu as pltpu
from jax.sharding import PartitionSpec as P

F = 512
SMEM = pltpu.MemorySpace.SMEM
VMEM = pltpu.MemorySpace.VMEM


def angles(samples, freqs, count):
    phase = samples[:, None] * freqs[None, :] % count
    return phase.astype(np.float64) * (2.0 * math.pi / count)


def band_table(count, bins, first):
    angle = angles(np.arange(count), first + np.arange(bins), count)
    return np.concatenate([np.cos(angle), -np.sin(angle)], axis=1).astype(jnp.bfloat16)


FINE = 32


def angle_factors(count, bins, first, n_win):
    j = np.arange(bins // 4).reshape(n_win, 1, -1)
    turn = np.array([0.0, 0.5 * math.pi]).reshape(1, 2, 1)

    def factors(samples, shift):
        out = []
        for m in range(4):
            freqs = np.broadcast_to(first + 4 * j + m, (n_win, 2, bins // 4 // n_win))
            angle = angles(samples, freqs.reshape(-1), count)
            angle = angle + np.broadcast_to(shift, freqs.shape).reshape(1, -1)
            out.append(np.stack([np.cos(angle), np.sin(angle)]))
        return np.stack(out).astype(np.float32)

    return factors(np.arange(0, count // 4, FINE), 0.0 * turn), factors(np.arange(FINE), turn)


def make_tables(coarse_ref, fine_ref, table_ref):
    for m in range(table_ref.shape[0]):
        cos_b, sin_b = fine_ref[m, 0], fine_ref[m, 1]
        for a in range(coarse_ref.shape[2]):
            cos_a, sin_a = (coarse_ref[m, k, a:a + 1, :] for k in range(2))
            rows = slice(a * FINE, (a + 1) * FINE)
            table_ref[m, rows, :] = (cos_a * cos_b - sin_a * sin_b).astype(jnp.bfloat16)


def in_hbm(value):
    return pltpu.with_memory_space_constraint(value, pltpu.HBM)


def order_sources(src_ref, r_dev, n_own, order_ref, plan_ref, flag_ref):
    n_src = src_ref.shape[0]
    size = order_ref.shape
    down = lax.broadcasted_iota(jnp.int32, size, 0).astype(jnp.float32)
    along = lax.broadcasted_iota(jnp.int32, size, 1).astype(jnp.float32)
    none = jnp.full(size, float(2**20), jnp.float32)
    column, row = none, none
    for s in range(n_src):
        station = src_ref[s].astype(jnp.float32)
        column = jnp.where(down == s, station, column)
        row = jnp.where(along == s, station, row)
    rank_along = jnp.sum((column < row).astype(jnp.float32), axis=0, keepdims=True)
    rank_down = jnp.sum((row < column).astype(jnp.float32), axis=1, keepdims=True)
    sorted_down = jnp.sum(jnp.where(rank_along == down, row, 0.0), axis=1, keepdims=True)
    at_place = rank_down == along
    sorted_along = jnp.sum(jnp.where(at_place, column, 0.0), axis=0, keepdims=True)
    source_along = jnp.sum(jnp.where(at_place, down, 0.0), axis=0, keepdims=True)
    order_ref[...] = jnp.broadcast_to(sorted_down, size)
    place = along[:1]
    owner, share = jnp.zeros_like(place), jnp.zeros_like(place)
    for z in range(1, n_src // n_own):
        owner = owner + (sorted_along >= z * r_dev).astype(jnp.float32)
        share = share + (place >= z * n_own).astype(jnp.float32)
    far = jnp.where((place < n_src) & (jnp.abs(owner - share) > 1.5), 1.0, 0.0)
    plan_ref[...] = jnp.broadcast_to(source_along, plan_ref.shape).astype(jnp.int32)
    flag_ref[0] = jnp.max(far).astype(jnp.int32)


def spectra_kernel(
    n_win, n_rcv, r_dev, valid_hbm, src_hbm, x_hbm, coarse_hbm, fine_hbm, *refs
):
    r_refs = refs[:n_win]
    q_refs = refs[n_win:n_win + n_rcv]
    (plan_ref, flag_ref, x_ref, even_ref, odd_ref, white_ref, sel_ref, order_ref, table_ref,
     coarse_ref, fine_ref, valid_ref, src_ref, sems, x_sems) = refs[n_win + n_rcv:]
    chunks, rows, samples = x_ref.shape
    w_step = rows // r_dev
    n_own = src_ref.shape[0] // n_rcv
    quarter = samples // 4
    win = lax.axis_index("win")
    rcv = lax.axis_index("rcv")

    def small(k):
        source = (coarse_hbm, fine_hbm, src_hbm, valid_hbm)[k]
        target = (coarse_ref, fine_ref, src_ref, valid_ref)[k]
        return pltpu.make_async_copy(source, target, sems.at[k])

    def chunk(k):
        return pltpu.make_async_copy(x_hbm.at[pl.ds(k * rows, rows)], x_ref.at[k], x_sems.at[k])

    for k in range(4):
        small(k).start()
    for k in range(chunks):
        chunk(k).start()
    small(0).wait()
    small(1).wait()
    make_tables(coarse_ref, fine_ref, table_ref)
    small(2).wait()
    order_sources(src_ref, r_dev, n_own, order_ref, plan_ref, flag_ref)
    stations = []
    for d in range(n_rcv):
        share = pl.multiple_of((rcv ^ d) * n_own, n_own)
        stations += [order_ref[pl.ds(share, n_own), 0:1]] * w_step
    wanted = jnp.concatenate(stations, axis=0).astype(jnp.int32) - rcv * r_dev
    shape = (n_rcv * w_step * n_own, rows)
    out_row = lax.broadcasted_iota(jnp.int32, shape, 0)
    column = lax.broadcasted_iota(jnp.int32, shape, 1)
    inside = (wanted >= 0) & (wanted < r_dev)
    hit = inside & (column == wanted + (out_row // n_own) % w_step * r_dev)
    sel_ref[...] = hit.astype(jnp.float32).astype(jnp.bfloat16)
    small(3).wait()

    def product(lhs, table):
        return jnp.dot(lhs, table, preferred_element_type=jnp.float32)

    def add_quarters(k, first, last):
        part = slice(first, last)
        b0, b1, b2, b3 = (x_ref[k, part, q * quarter:(q + 1) * quarter] for q in range(4))
        x0, x1, x2, x3 = (b.astype(jnp.float32) for b in (b0, b1, b2, b3))
        even_ref[k, 0, part] = ((x0 + x2) + (x1 + x3)).astype(jnp.bfloat16)
        even_ref[k, 1, part] = ((x0 + x2) - (x1 + x3)).astype(jnp.bfloat16)
        odd_ref[k, part] = b0 - b2
        odd_ref[k, rows + first:rows + last] = b1 - b3

    lanes = table_ref.shape[2]
    lane = lax.broadcasted_iota(jnp.int32, (rows, lanes), 1)
    piece = lanes // n_win
    real = lane % piece < piece // 2

    def odd_spectra(k, m):
        both = product(odd_ref[k], table_ref[m])
        second = both[rows:]
        back, forth = pltpu.roll(second, lanes - piece // 2, 1), pltpu.roll(second, piece // 2, 1)
        turned = jnp.where(real, back, -forth)
        return both[:rows] + turned if m == 1 else both[:rows] - turned

    parts = 4
    size = rows // parts
    chunk(0).wait()
    add_quarters(0, 0, rows)
    row = lax.broadcasted_iota(jnp.int32, (rows, 1), 0)
    for k in range(chunks):
        more = k + 1 < chunks
        if more:
            chunk(k + 1).wait()
        spectra = []
        for m in range(4):
            if m % 2:
                spectra.append(odd_spectra(k, m))
            else:
                spectra.append(product(even_ref[k, m // 2], table_ref[m]))
            if more:
                add_quarters(k + 1, m * size, (m + 1) * size)
        squares = sum(jnp.sum(s * s, axis=1, keepdims=True) for s in spectra)
        gain = lax.rsqrt(squares / F + 1e-06)
        keep = jnp.zeros((rows, 1), jnp.float32)
        for t in range(w_step):
            own = (row >= t * r_dev) & (row < (t + 1) * r_dev)
            keep = jnp.where(own, valid_ref[k * w_step + t].astype(jnp.float32), keep)
        gain = gain * keep
        white = [s * gain for s in spectra]
        for d in range(n_win):
            columns = slice(d * piece, (d + 1) * piece)
            block = jnp.concatenate([part[:, columns] for part in white], axis=1)
            white_ref[k, d] = block.astype(jnp.bfloat16)
        count = w_step * n_own
        for j in range(n_win):
            block = white_ref[k, win ^ j]
            r_refs[j][k * rows:(k + 1) * rows, :] = block
            picked = product(sel_ref[...], block).astype(jnp.bfloat16)
            for d in range(n_rcv):
                q_refs[d][j, k * count:(k + 1) * count, :] = picked[d * count:(d + 1) * count]


def spectra_call(traces, valid, src_station, n_win, n_rcv):
    w_dev, r_dev, samples = traces.shape
    n_src = src_station.shape[0]
    n_own = n_src // n_rcv
    chunks = 4
    every = w_dev * r_dev
    rows = every // chunks
    lanes = 2 * F // n_win
    coarse, fine = (jnp.asarray(t) for t in angle_factors(samples, F, samples // 16, n_win))
    shapes = [jax.ShapeDtypeStruct((every, lanes), jnp.bfloat16)] * n_win
    shapes += [jax.ShapeDtypeStruct((n_win, w_dev * n_own, lanes), jnp.bfloat16)] * n_rcv
    shapes += [jax.ShapeDtypeStruct((8, 128), jnp.int32), jax.ShapeDtypeStruct((1,), jnp.int32)]
    vmem = pl.BlockSpec(memory_space=VMEM)
    out = pl.pallas_call(
        functools.partial(spectra_kernel, n_win, n_rcv, r_dev),
        in_specs=[pl.BlockSpec(memory_space=pltpu.HBM)] * 5,
        out_specs=[vmem] * (len(shapes) - 1) + [pl.BlockSpec(memory_space=SMEM)],
        out_shape=shapes,
        scratch_shapes=[
            pltpu.VMEM((chunks, rows, samples), jnp.bfloat16),
            pltpu.VMEM((chunks, 2, rows, samples // 4), jnp.bfloat16),
            pltpu.VMEM((chunks, 2 * rows, samples // 4), jnp.bfloat16),
            pltpu.VMEM((chunks, n_win, rows, lanes), jnp.bfloat16),
            pltpu.VMEM((n_src * (w_dev // chunks), rows), jnp.bfloat16),
            pltpu.VMEM((n_src, 128), jnp.float32),
            pltpu.VMEM((4, samples // 4, F // 2), jnp.bfloat16),
            pltpu.VMEM(coarse.shape, jnp.float32),
            pltpu.VMEM(fine.shape, jnp.float32),
            pltpu.SMEM(valid.shape, jnp.int32),
            pltpu.SMEM(src_station.shape, jnp.int32),
            pltpu.SemaphoreType.DMA((4,)),
            pltpu.SemaphoreType.DMA((chunks,)),
        ],
        compiler_params=pltpu.CompilerParams(vmem_limit_bytes=36 * 2**20),
        cost_estimate=pl.CostEstimate(
            flops=2 * every * (samples // 4) * 6 * (F // 2), bytes_accessed=every * samples * 2,
            transcendentals=0,
        ),
        name="spectra",
    )(*(in_hbm(x) for x in (valid, src_station, traces.reshape(every, samples), coarse, fine)))
    return out[:n_win], out[n_win:n_win + n_rcv], out[-2], out[-1]


def bin_order(lanes):
    quarter = lanes // 8
    lane = lax.broadcasted_iota(jnp.int32, (lanes, lanes), 1)
    row = lax.broadcasted_iota(jnp.int32, (lanes, lanes), 0)
    part = (lane // quarter) % 2
    bin_of = 4 * (lane % quarter) + lane // (2 * quarter)
    hit = row == part * (lanes // 2) + bin_of
    return hit.astype(jnp.float32).astype(jnp.bfloat16)


def turn_kernel(r_dev, *refs):
    x_refs, (out_ref, rows_ref) = refs[:-2], refs[-2:]
    lanes = x_refs[0].shape[1]
    bins = lanes // 2
    w_dev = out_ref.shape[1] // 2
    pad = out_ref.shape[2] // 2
    order = bin_order(lanes)
    windows = [(x, w) for x in x_refs for w in range(x.shape[0] // r_dev)]
    for k, (x_ref, w) in enumerate(windows):
        turned = lax.dot_general(
            order, x_ref[w * r_dev:(w + 1) * r_dev], (((1,), (1,)), ((), ())),
            preferred_element_type=jnp.float32,
        )
        rows_ref[pl.ds(k, lanes, stride=w_dev), :r_dev] = turned
    rr = rows_ref[:bins * w_dev].reshape(bins, w_dev, pad)
    ri = rows_ref[bins * w_dev:].reshape(bins, w_dev, pad)
    out_ref[:, :, :pad] = jnp.concatenate([rr, ri], axis=1).astype(jnp.bfloat16)
    out_ref[:, :, pad:] = jnp.concatenate([ri, -rr], axis=1).astype(jnp.bfloat16)


def turn_call(parts, w_dev, r_dev):
    lanes = parts[0].shape[1]
    pad = 128
    vmem = pl.BlockSpec(memory_space=VMEM)
    return pl.pallas_call(
        functools.partial(turn_kernel, r_dev),
        in_specs=[vmem] * len(parts),
        out_specs=vmem,
        out_shape=jax.ShapeDtypeStruct((lanes // 2, 2 * w_dev, 2 * pad), jnp.bfloat16),
        scratch_shapes=[pltpu.VMEM((lanes * w_dev, pad), jnp.float32)],
        compiler_params=pltpu.CompilerParams(vmem_limit_bytes=16 * 2**20),
        cost_estimate=pl.CostEstimate(
            flops=2 * w_dev * lanes * lanes * pad, bytes_accessed=2 * 2**20, transcendentals=0
        ),
        name="turn",
    )(*parts)


def merge_kernel(n_win, *refs):
    picked, outs = refs[:-n_win], refs[-n_win:]
    for j, out_ref in enumerate(outs):
        total = picked[0][j].astype(jnp.float32)
        for q_ref in picked[1:]:
            total = total + q_ref[j].astype(jnp.float32)
        out_ref[...] = total.astype(jnp.bfloat16)


def merge_call(*picked):
    n_win, rows, lanes = picked[0].shape
    vmem = pl.BlockSpec(memory_space=VMEM)
    return pl.pallas_call(
        functools.partial(merge_kernel, n_win),
        in_specs=[vmem] * len(picked),
        out_specs=[vmem] * n_win,
        out_shape=[jax.ShapeDtypeStruct((rows, lanes), jnp.bfloat16)] * n_win,
        compiler_params=pltpu.CompilerParams(vmem_limit_bytes=4 * 2**20),
        cost_estimate=pl.CostEstimate(flops=2**18, bytes_accessed=2**19, transcendentals=0),
        name="merge",
    )(*picked)


def join_kernel(n_win, *refs):
    out_ref = refs[-1]
    for j in range(n_win):
        out_ref[j] = refs[j][...]


def join_call(blocks, after, later):
    rows, lanes = blocks[0].shape
    n_win = len(blocks)
    vmem, anywhere = pl.BlockSpec(memory_space=VMEM), pl.BlockSpec(memory_space=pl.ANY)
    out = pl.pallas_call(
        functools.partial(join_kernel, n_win),
        in_specs=[vmem] * n_win + [anywhere] * (1 + len(later)),
        out_specs=[anywhere] * len(later) + [vmem],
        out_shape=[jax.ShapeDtypeStruct(x.shape, x.dtype) for x in later]
        + [jax.ShapeDtypeStruct((n_win, rows, lanes), jnp.bfloat16)],
        input_output_aliases={n_win + 1 + k: k for k in range(len(later))},
        compiler_params=pltpu.CompilerParams(vmem_limit_bytes=4 * 2**20),
        cost_estimate=pl.CostEstimate(flops=2**18, bytes_accessed=2**19, transcendentals=0),
        name="join",
    )(*blocks, after, *later)
    return out[-1], out[:-1]


def stacks_kernel(shares, n_win, w_dev, r_dev, n_own, bins, plan_hbm, *refs):
    t_refs = refs[:n_win]
    s_refs = refs[n_win:n_win + len(shares)]
    out_hbm, srow_ref, left_ref, prod_ref, out_ref, plan_ref, sems, plan_sem = refs[-8:]
    plan_copy = pltpu.make_async_copy(plan_hbm, plan_ref, plan_sem)
    plan_copy.start()
    lanes = 2 * bins
    windows = n_win * w_dev
    count = len(shares) * n_own
    pad = 128
    rcv = lax.axis_index("rcv")

    def product(lhs, rhs, dims=(((1,), (0,)), ((), ()))):
        return lax.dot_general(lhs, rhs, dims, preferred_element_type=jnp.float32)

    order = bin_order(lanes)
    both = order[:bins] + order[bins:]
    lane = lax.broadcasted_iota(jnp.int32, (w_dev, lanes), 1)
    real = (lane // (bins // 4)) % 2 == 0

    for k, s_ref in enumerate(s_refs):
        for j in range(n_win):
            block = s_ref[j].astype(jnp.float32)
            for h in range(lanes // pad):
                half = block[:, h * pad:(h + 1) * pad]
                srow_ref[h, pl.ds((k * n_win + j) * w_dev * n_own, w_dev * n_own), :] = half
    for s in range(count):
        first = s // n_own * windows * n_own + s % n_own
        values = jnp.concatenate(
            [srow_ref[h, pl.ds(first, windows, stride=n_own), :] for h in range(lanes // pad)],
            axis=1,
        )
        stacked = []
        for j in range(n_win):
            own = values[j * w_dev:(j + 1) * w_dev]
            stacked += [jnp.where(real, own, 0.0), jnp.where(real, 0.0, own)]
        stacked = jnp.concatenate(stacked, axis=0).astype(jnp.bfloat16)
        turned = product(both, stacked, (((1,), (1,)), ((), ())))
        left_ref[pl.ds(s, bins, stride=count), :2 * windows] = turned

    for f in range(bins):
        right = jnp.concatenate([t_ref[f] for t_ref in t_refs], axis=0)
        left = left_ref[pl.ds(f * count, count), :2 * windows].astype(jnp.bfloat16)
        result = product(left, right)
        for c in range(2):
            prod_ref[c, pl.ds(f, count, stride=bins), :] = result[:, c * pad:(c + 1) * pad]

    scale = 1.0 / math.sqrt(windows)
    plan_copy.wait()
    copies = []
    for s in range(count):
        for c in range(2):
            turned = prod_ref[c, s * bins:(s + 1) * bins, :].T
            out_ref[s, pl.ds(c, r_dev, stride=2), :] = turned[:r_dev] * scale
        row = plan_ref[0, (rcv ^ shares[s // n_own]) * n_own + s % n_own]
        copies.append(pltpu.make_async_copy(out_ref.at[s], out_hbm.at[row], sems.at[s]))
        copies[-1].start()
    for copy in copies:
        copy.wait()


def stacks_call(out, plan, turned, sources, shares, n_rcv, w_dev, r_dev, bins):
    n_win = len(turned)
    n_own = sources[0].shape[1] // w_dev
    windows = n_win * w_dev
    count = len(shares) * n_own
    whole = pl.BlockSpec(memory_space=VMEM)
    args = [plan] + list(turned) + [sources[i] for i in shares]
    specs = [pl.BlockSpec(memory_space=pl.ANY)] + [whole] * (len(args) - 1)
    aliases = {}
    if out is not None:
        aliases = {len(args): 0}
        args.append(out)
        specs.append(pl.BlockSpec(memory_space=pl.ANY))
    return pl.pallas_call(
        functools.partial(stacks_kernel, shares, n_win, w_dev, r_dev, n_own, bins),
        in_specs=specs,
        out_specs=pl.BlockSpec(memory_space=pltpu.HBM),
        out_shape=jax.ShapeDtypeStruct((n_rcv * n_own, 2 * r_dev, bins), jnp.float32),
        input_output_aliases=aliases,
        scratch_shapes=[
            pltpu.VMEM((2 * bins // 128, windows * count, 128), jnp.float32),
            pltpu.VMEM((bins * count, 128), jnp.float32),
            pltpu.VMEM((2, count * bins, 128), jnp.float32),
            pltpu.VMEM((count, 2 * r_dev, bins), jnp.float32),
            pltpu.SMEM(plan.shape, jnp.int32),
            pltpu.SemaphoreType.DMA((count,)),
            pltpu.SemaphoreType.DMA,
        ],
        compiler_params=pltpu.CompilerParams(vmem_limit_bytes=20 * 2**20),
        cost_estimate=pl.CostEstimate(
            flops=8 * windows * count * r_dev * bins, bytes_accessed=6 * 2**20, transcendentals=0
        ),
        name="stacks",
    )(*args)


def swap(value, axis, by):
    size = lax.axis_size(axis)
    return lax.ppermute(value, axis, [(i, i ^ by) for i in range(size)])


def near_and_far(n_rcv, by):
    pairs = [(z, z ^ by) for z in range(n_rcv)]
    return [p for p in pairs if abs(p[0] - p[1]) == 1], [p for p in pairs if abs(p[0] - p[1]) > 1]


def merge_near(picked, near):
    return merge_call(picked[0], *near)


def merge_all(picked, near):
    far = []
    for i in range(1, len(picked)):
        pairs = near_and_far(len(picked), i)[1]
        if pairs:
            far.append(lax.ppermute(picked[i], "rcv", pairs))
    return merge_call(picked[0], *near, *far)


def body(traces, valid, src_station):
    w_dev, r_dev, samples = traces.shape
    n_src = src_station.shape[0]
    n_win = lax.axis_size("win")
    n_rcv = lax.axis_size("rcv")
    bins = F // n_win
    early = n_win // 2

    blocks, picked, plan, flag = spectra_call(traces, valid, src_station, n_win, n_rcv)

    near = []
    for i in range(1, n_rcv):
        pairs = near_and_far(n_rcv, i)[0]
        if pairs:
            near.append(lax.ppermute(picked[i], "rcv", pairs))
    merged = lax.cond(flag.reshape(()) > 0, merge_all, merge_near, picked, near)

    merged = [merged[0]] + [swap(merged[j], "win", j) for j in range(1, n_win)]
    late = [j for j in range(1, n_win) if j != early]
    received = {0: blocks[0], early: swap(blocks[early], "win", early)}
    joined, later = join_call(merged, received[early], [blocks[j] for j in late])
    received.update({j: swap(block, "win", j) for j, block in zip(late, later)})
    sources = [joined] + [swap(joined, "rcv", i) for i in range(1, n_rcv)]

    turned = [turn_call([received[j]], w_dev, r_dev) for j in range(n_win)]
    half = n_rcv // 2
    sizes = (n_rcv, w_dev, r_dev, bins)
    stacks = stacks_call(None, plan, turned, sources, tuple(range(half)), *sizes)
    stacks = stacks_call(stacks, plan, turned, sources, tuple(range(half, n_rcv)), *sizes)
    return stacks.reshape(n_src, r_dev, 2, bins)


def correlate(received, sources):
    rr = received[:, :, 0]
    ri = received[:, :, 1]
    sr = sources[:, :, 0]
    si = sources[:, :, 1]
    real = jnp.einsum("wsf,wrf->srf", sr, rr, preferred_element_type=jnp.float32)
    real = real + jnp.einsum("wsf,wrf->srf", si, ri, preferred_element_type=jnp.float32)
    imag = jnp.einsum("wsf,wrf->srf", sr, ri, preferred_element_type=jnp.float32)
    imag = imag - jnp.einsum("wsf,wrf->srf", si, rr, preferred_element_type=jnp.float32)
    return jnp.stack([real, imag], axis=2)


def body_any(traces, valid, src_station):
    w_dev, r_dev, samples = traces.shape
    n_win = lax.axis_size("win")
    n_rcv = lax.axis_size("rcv")
    bins = F // n_win
    table = jnp.asarray(band_table(samples, F, samples // 16))
    spectra = jnp.dot(
        traces.reshape(w_dev * r_dev, samples), table, preferred_element_type=jnp.float32
    )
    spectra = spectra.reshape(w_dev, r_dev, 2, F)
    power = jnp.sum(spectra * spectra, axis=(2, 3), keepdims=True) / F
    keep = valid.astype(jnp.float32)[:, None, None, None]
    white = (spectra * lax.rsqrt(power + 1e-06) * keep).astype(jnp.bfloat16)
    blocks = white.reshape(w_dev, r_dev, 2, n_win, bins).transpose(3, 0, 1, 2, 4)
    me = lax.axis_index("win")
    offset = lax.axis_index("rcv") * r_dev
    station_ids = offset + jnp.arange(r_dev, dtype=jnp.int32)
    selector = (src_station[:, None] == station_ids[None, :]).astype(jnp.bfloat16)
    received = []
    for j in range(n_win):
        block = lax.dynamic_index_in_dim(blocks, me ^ j, 0, keepdims=False)
        received.append(swap(block, "win", j) if j else block)
    received = jnp.concatenate(received, axis=0)
    rows = jnp.einsum("sr,wrcf->wscf", selector, received, preferred_element_type=jnp.float32)
    rows = lax.all_to_all(rows.astype(jnp.bfloat16), "rcv", 0, 0, tiled=True)
    rows = rows.reshape((n_rcv, -1) + rows.shape[1:])
    merged = jnp.sum(rows.astype(jnp.float32), axis=0).astype(jnp.bfloat16)
    sources = lax.all_gather(merged, "rcv", axis=0, tiled=True)
    return correlate(received, sources) * (1.0 / math.sqrt(w_dev * n_win))


def solution(mesh):
    sizes = (mesh.shape["win"], mesh.shape["rcv"])
    return jax.shard_map(
        body if sizes == (4, 4) else body_any,
        mesh=mesh,
        in_specs=(P("win", ("groups", "rcv"), None), P(("groups", "win")), P("groups")),
        out_specs=P(None, ("groups", "rcv"), None, "win"),
        check_vma=False,
    )
```

profile of v0, /device:TPU:0, one launch (start us, length us, event | category | flops | bytes accessed | tf_op | source)
XLA Modules:
  0.0 46.6 jit_solution(18190596613957693456)
XLA Ops:
  0.0 9.9 %spectra.1 = (bf16[768,256]{1,0:T(8,128)(2,1)S(1)}, bf16[768,256]{1,0:T(8,128)(2,1)S(1)}, bf16[768,256]{1,0:T(8,128)(2,1)S(1)}, bf16[768,256]{1,0:T(8,128)(2,1)S...) custom-call(s32[8]{0:T(128)} %valid_hbm.1, ...), custom_call_target="tpu_custom_call" | custom-call | flops 2415919104 | bytes 6291456 | tf_op jit(solution)/shard_map/spectra/pallas_call | solution.py:206
  9.9 3.0 %collective-permute-start.7 = (bf16[768,256]{1,0:T(8,128)(2,1)S(1)}, bf16[768,256]{1,0:T(8,128)(2,1)S(1)}, u32[]{:S(2)}, u32[]{:S(2)}) collective-permute-start(bf16[768,256]{1,0:T(8,128)(2,1)S(1)} %get-tuple-element.57), channel_id=1, source_target_pairs={{0,8},{4,12},{8,0},{12,4},{1,9},{5,13},{9,1},{13,5},{2,10},{6,14},... | collective-permute-start | bytes 1179656 | tf_op jit(solution)/shard_map/ppermute | solution.py:430
  13.0 1.6 %collective-permute-start.2 = (bf16[4,64,256]{2,1,0:T(8,128)(2,1)S(1)}, bf16[4,64,256]{2,1,0:T(8,128)(2,1)S(1)}, u32[]{:S(2)}, u32[]{:S(2)}) collective-permute-start(bf16[4,64,256]{2,1,0:T(8,128)(2,1)S(1)} %get-tuple-element.50), channel_id=1, source_target_pairs={{0,1},{1,0},{2,3},{3,2},{4,5},{5,4},{6,7},{7,6},{8,9},{9,8},{10,11... | collective-permute-start | bytes 393224 | tf_op jit(solution)/shard_map/ppermute | solution.py:465
  14.5 0.7 %collective-permute-start.3 = (bf16[4,64,256]{2,1,0:T(8,128)(2,1)S(1)}, bf16[4,64,256]{2,1,0:T(8,128)(2,1)S(1)}, u32[]{:S(2)}, u32[]{:S(2)}) collective-permute-start(bf16[4,64,256]{2,1,0:T(8,128)(2,1)S(1)} %get-tuple-element.51), channel_id=1, source_target_pairs={{1,2},{2,1},{5,6},{6,5},{9,10},{10,9},{13,14},{14,13},{17,18},{18,... | collective-permute-start | bytes 393224 | tf_op jit(solution)/shard_map/ppermute | solution.py:465
  15.8 2.1 %collective-permute-done.2 = bf16[4,64,256]{2,1,0:T(8,128)(2,1)S(1)} collective-permute-done((bf16[4,64,256]{2,1,0:T(8,128)(2,1)S(1)}, bf16[4,64,256]{2,1,0:T(8,128)(2,1)S(1)}, u32[]{:S(2)}, u32[]{:S(2)}) %collective-permute-start.2) | collective-permute-done | bytes 131104 | tf_op jit(solution)/shard_map/ppermute | solution.py:465
  17.9 0.0 collective-permute-done.3
  17.9 0.2 conditional.1
  17.9 0.1 merge.2
  18.2 0.1 collective-permute-start.4
  18.3 0.4 collective-permute-start.5
  18.7 1.4 %collective-permute-start.6 = (bf16[64,256]{1,0:T(8,128)(2,1)S(1)}, bf16[64,256]{1,0:T(8,128)(2,1)S(1)}, u32[]{:S(2)}, u32[]{:S(2)}) collective-permute-start(bf16[64,256]{1,0:T(8,128)(2,1)S(1)} %get-tuple-element.56), channel_id=1, source_target_pairs={{0,12},{4,8},{8,4},{12,0},{1,13},{5,9},{9,5},{13,1},{2,14},{6,10},... | collective-permute-start | bytes 98312 | tf_op jit(solution)/shard_map/ppermute | solution.py:430
  20.1 3.0 %collective-permute-done.5.refs_2_ = bf16[64,256]{1,0:T(8,128)(2,1)S(1)} collective-permute-done((bf16[64,256]{1,0:T(8,128)(2,1)S(1)}, bf16[64,256]{1,0:T(8,128)(2,1)S(1)}, u32[]{:S(2)}, u32[]{:S(2)}) %collective-permute-start.5) | collective-permute-done | bytes 32800 | tf_op jit(solution)/shard_map/ppermute | solution.py:430
  23.2 1.6 %collective-permute-start.9 = (bf16[768,256]{1,0:T(8,128)(2,1)S(1)}, bf16[768,256]{1,0:T(8,128)(2,1)S(1)}, u32[]{:S(2)}, u32[]{:S(2)}) collective-permute-start(bf16[768,256]{1,0:T(8,128)(2,1)S(1)} %get-tuple-element.61), channel_id=1, source_target_pairs={{0,12},{4,8},{8,4},{12,0},{1,13},{5,9},{9,5},{13,1},{2,14},{6,10},... | collective-permute-start | bytes 1179656 | tf_op jit(solution)/shard_map/ppermute | solution.py:430
  24.7 0.3 collective-permute-start.8
  25.1 3.4 %collective-permute-start.12 = (bf16[4,64,256]{2,1,0:T(8,128)(2,1)S(1)}, bf16[4,64,256]{2,1,0:T(8,128)(2,1)S(1)}, u32[]{:S(2)}, u32[]{:S(2)}) collective-permute-start(bf16[4,64,256]{2,1,0:T(8,128)(2,1)S(1)} %get-tuple-element.62.refs_4_), channel_id=1, source_target_pairs={{0,1},{1,0},{2,3},{3,2},{4,5},{5,4},{6,7},{7,6},{8,9},{9,8},{10,11... | collective-permute-start | bytes 393224 | tf_op jit(solution)/shard_map/ppermute | solution.py:430
  28.5 2.9 %collective-permute-start.11 = (bf16[4,64,256]{2,1,0:T(8,128)(2,1)S(1)}, bf16[4,64,256]{2,1,0:T(8,128)(2,1)S(1)}, u32[]{:S(2)}, u32[]{:S(2)}) collective-permute-start(bf16[4,64,256]{2,1,0:T(8,128)(2,1)S(1)} %get-tuple-element.62.refs_4_), channel_id=1, source_target_pairs={{0,3},{1,2},{2,1},{3,0},{4,7},{5,6},{6,5},{7,4},{8,11},{9,10},{10,... | collective-permute-start | bytes 393224 | tf_op jit(solution)/shard_map/ppermute | solution.py:430
  31.4 0.5 %turn.4.refs_0_ = bf16[128,16,256]{2,1,0:T(8,128)(2,1)S(1)} custom-call(bf16[768,256]{1,0:T(8,128)(2,1)S(1)} %get-tuple-element.47.refs_0_), custom_call_target="tpu_custom_call" | custom-call | flops 134217728 | bytes 2097152 | tf_op jit(solution)/shard_map/turn/pallas_call | solution.py:270
  32.0 0.5 %turn.6.refs_2_ = bf16[128,16,256]{2,1,0:T(8,128)(2,1)S(1)} custom-call(bf16[768,256]{1,0:T(8,128)(2,1)S(1)} %collective-permute-done.7.refs_4_.refs_0_), custom_call_target="tpu_custom_call" | custom-call | flops 134217728 | bytes 2097152 | tf_op jit(solution)/shard_map/turn/pallas_call | solution.py:270
  32.5 1.9 %collective-permute-done.9.refs_0_ = bf16[768,256]{1,0:T(8,128)(2,1)S(1)} collective-permute-done((bf16[768,256]{1,0:T(8,128)(2,1)S(1)}, bf16[768,256]{1,0:T(8,128)(2,1)S(1)}, u32[]{:S(2)}, u32[]{:S(2)}) %collective-permute-start.9) | collective-permute-done | bytes 393248 | tf_op jit(solution)/shard_map/ppermute | solution.py:430
  34.4 0.5 %turn.7.refs_3_ = bf16[128,16,256]{2,1,0:T(8,128)(2,1)S(1)} custom-call(bf16[768,256]{1,0:T(8,128)(2,1)S(1)} %collective-permute-done.9.refs_0_), custom_call_target="tpu_custom_call" | custom-call | flops 134217728 | bytes 2097152 | tf_op jit(solution)/shard_map/turn/pallas_call | solution.py:270
  34.9 0.5 %turn.5.refs_1_ = bf16[128,16,256]{2,1,0:T(8,128)(2,1)S(1)} custom-call(bf16[768,256]{1,0:T(8,128)(2,1)S(1)} %collective-permute-done.8.refs_0_), custom_call_target="tpu_custom_call" | custom-call | flops 134217728 | bytes 2097152 | tf_op jit(solution)/shard_map/turn/pallas_call | solution.py:270
  35.5 3.7 %stacks.2.refs_6_ = f32[32,192,128]{2,1,0:T(8,128)} custom-call(s32[8,128]{1,0:T(8,128)S(1)} %get-tuple-element.46.plan_hbm, bf16[128,16,256]{2,1,0:T(8,128)(2,1)S(1)} %turn.4.refs_0_, bf16[128,16,256]{2,1,0:T(8,128)(2,1)S(1)} %turn.5.refs_1_, bf16[128,16,256]{2,1,0:T(8,128)(2,1)S(1)} %turn.6.refs_2_, bf16[128,16,256]{2,1,0:T(8,128)(2,1)S(1)} %turn.7.refs_3_, ...), custom_call_target="tpu_custom_call" | custom-call | flops 50331648 | bytes 6291456 | tf_op jit(solution)/shard_map/stacks/pallas_call | solution.py:405
  39.2 3.6 %collective-permute-done.10.refs_4_ = bf16[4,64,256]{2,1,0:T(8,128)(2,1)S(1)} collective-permute-done((bf16[4,64,256]{2,1,0:T(8,128)(2,1)S(1)}, bf16[4,64,256]{2,1,0:T(8,128)(2,1)S(1)}, u32[]{:S(2)}, u32[]{:S(2)}) %collective-permute-start.10) | collective-permute-done | bytes 131104 | tf_op jit(solution)/shard_map/ppermute | solution.py:430
  42.8 3.7 %stacks.3 = f32[32,192,128]{2,1,0:T(8,128)} custom-call(s32[8,128]{1,0:T(8,128)S(1)} %get-tuple-element.46.plan_hbm, bf16[128,16,256]{2,1,0:T(8,128)(2,1)S(1)} %turn.4.refs_0_, bf16[128,16,256]{2,1,0:T(8,128)(2,1)S(1)} %turn.5.refs_1_, bf16[128,16,256]{2,1,0:T(8,128)(2,1)S(1)} %turn.6.refs_2_, ...), custom_call_target="tpu_custom_call", output_to_operand_aliasing={{}: (7, {})} | custom-call | flops 50331648 | bytes 6291456 | tf_op jit(solution)/shard_map/stacks/pallas_call | solution.py:405
  (8 shorter events, 0.0 us)
Async XLA Ops:
  9.9 13.2 %collective-permute-start.7 = (bf16[768,256]{1,0:T(8,128)(2,1)S(1)}, bf16[768,256]{1,0:T(8,128)(2,1)S(1)}, u32[]{:S(2)}, u32[]{:S(2)}) collective-permute-start(bf16[768,256]{1,0:T(8,128)(2,1)S(1)} %get-tuple-element.57), channel_id=1, source_target_pairs={{0,8},{4,12},{8,0},{12,4},{1,9},{5,13},{9,1},{13,5},{2,10},{6,14},... | collective-permute-start | bytes 1179656 | tf_op jit(solution)/shard_map/ppermute | solution.py:430
  13.0 5.0 %collective-permute-start.2 = (bf16[4,64,256]{2,1,0:T(8,128)(2,1)S(1)}, bf16[4,64,256]{2,1,0:T(8,128)(2,1)S(1)}, u32[]{:S(2)}, u32[]{:S(2)}) collective-permute-start(bf16[4,64,256]{2,1,0:T(8,128)(2,1)S(1)} %get-tuple-element.50), channel_id=1, source_target_pairs={{0,1},{1,0},{2,3},{3,2},{4,5},{5,4},{6,7},{7,6},{8,9},{9,8},{10,11... | collective-permute-start | bytes 393224 | tf_op jit(solution)/shard_map/ppermute | solution.py:465
  14.5 3.4 %collective-permute-start.3 = (bf16[4,64,256]{2,1,0:T(8,128)(2,1)S(1)}, bf16[4,64,256]{2,1,0:T(8,128)(2,1)S(1)}, u32[]{:S(2)}, u32[]{:S(2)}) collective-permute-start(bf16[4,64,256]{2,1,0:T(8,128)(2,1)S(1)} %get-tuple-element.51), channel_id=1, source_target_pairs={{1,2},{2,1},{5,6},{6,5},{9,10},{10,9},{13,14},{14,13},{17,18},{18,... | collective-permute-start | bytes 393224 | tf_op jit(solution)/shard_map/ppermute | solution.py:465
  18.2 1.9 %collective-permute-start.4 = (bf16[64,256]{1,0:T(8,128)(2,1)S(1)}, bf16[64,256]{1,0:T(8,128)(2,1)S(1)}, u32[]{:S(2)}, u32[]{:S(2)}) collective-permute-start(bf16[64,256]{1,0:T(8,128)(2,1)S(1)} %get-tuple-element.54), channel_id=1, source_target_pairs={{0,4},{4,0},{8,12},{12,8},{1,5},{5,1},{9,13},{13,9},{2,6},{6,2},{1... | collective-permute-start | bytes 98312 | tf_op jit(solution)/shard_map/ppermute | solution.py:430
  18.3 4.9 %collective-permute-start.5 = (bf16[64,256]{1,0:T(8,128)(2,1)S(1)}, bf16[64,256]{1,0:T(8,128)(2,1)S(1)}, u32[]{:S(2)}, u32[]{:S(2)}) collective-permute-start(bf16[64,256]{1,0:T(8,128)(2,1)S(1)} %get-tuple-element.55), channel_id=1, source_target_pairs={{0,8},{4,12},{8,0},{12,4},{1,9},{5,13},{9,1},{13,5},{2,10},{6,14},... | collective-permute-start | bytes 98312 | tf_op jit(solution)/shard_map/ppermute | solution.py:430
  18.7 4.5 %collective-permute-start.6 = (bf16[64,256]{1,0:T(8,128)(2,1)S(1)}, bf16[64,256]{1,0:T(8,128)(2,1)S(1)}, u32[]{:S(2)}, u32[]{:S(2)}) collective-permute-start(bf16[64,256]{1,0:T(8,128)(2,1)S(1)} %get-tuple-element.56), channel_id=1, source_target_pairs={{0,12},{4,8},{8,4},{12,0},{1,13},{5,9},{9,5},{13,1},{2,14},{6,10},... | collective-permute-start | bytes 98312 | tf_op jit(solution)/shard_map/ppermute | solution.py:430
  23.2 11.2 %collective-permute-start.9 = (bf16[768,256]{1,0:T(8,128)(2,1)S(1)}, bf16[768,256]{1,0:T(8,128)(2,1)S(1)}, u32[]{:S(2)}, u32[]{:S(2)}) collective-permute-start(bf16[768,256]{1,0:T(8,128)(2,1)S(1)} %get-tuple-element.61), channel_id=1, source_target_pairs={{0,12},{4,8},{8,4},{12,0},{1,13},{5,9},{9,5},{13,1},{2,14},{6,10},... | collective-permute-start | bytes 1179656 | tf_op jit(solution)/shard_map/ppermute | solution.py:430
  24.7 10.2 %collective-permute-start.8 = (bf16[768,256]{1,0:T(8,128)(2,1)S(1)}, bf16[768,256]{1,0:T(8,128)(2,1)S(1)}, u32[]{:S(2)}, u32[]{:S(2)}) collective-permute-start(bf16[768,256]{1,0:T(8,128)(2,1)S(1)} %get-tuple-element.60), channel_id=1, source_target_pairs={{0,4},{4,0},{8,12},{12,8},{1,5},{5,1},{9,13},{13,9},{2,6},{6,2},{1... | collective-permute-start | bytes 1179656 | tf_op jit(solution)/shard_map/ppermute | solution.py:430
  25.1 10.4 %collective-permute-start.12 = (bf16[4,64,256]{2,1,0:T(8,128)(2,1)S(1)}, bf16[4,64,256]{2,1,0:T(8,128)(2,1)S(1)}, u32[]{:S(2)}, u32[]{:S(2)}) collective-permute-start(bf16[4,64,256]{2,1,0:T(8,128)(2,1)S(1)} %get-tuple-element.62.refs_4_), channel_id=1, source_target_pairs={{0,1},{1,0},{2,3},{3,2},{4,5},{5,4},{6,7},{7,6},{8,9},{9,8},{10,11... | collective-permute-start | bytes 393224 | tf_op jit(solution)/shard_map/ppermute | solution.py:430
  28.5 10.7 %collective-permute-start.11 = (bf16[4,64,256]{2,1,0:T(8,128)(2,1)S(1)}, bf16[4,64,256]{2,1,0:T(8,128)(2,1)S(1)}, u32[]{:S(2)}, u32[]{:S(2)}) collective-permute-start(bf16[4,64,256]{2,1,0:T(8,128)(2,1)S(1)} %get-tuple-element.62.refs_4_), channel_id=1, source_target_pairs={{0,3},{1,2},{2,1},{3,0},{4,7},{5,6},{6,5},{7,4},{8,11},{9,10},{10,... | collective-permute-start | bytes 393224 | tf_op jit(solution)/shard_map/ppermute | solution.py:430
  31.4 11.4 %collective-permute-start.10 = (bf16[4,64,256]{2,1,0:T(8,128)(2,1)S(1)}, bf16[4,64,256]{2,1,0:T(8,128)(2,1)S(1)}, u32[]{:S(2)}, u32[]{:S(2)}) collective-permute-start(bf16[4,64,256]{2,1,0:T(8,128)(2,1)S(1)} %get-tuple-element.62.refs_4_), channel_id=1, source_target_pairs={{0,2},{1,3},{2,0},{3,1},{4,6},{5,7},{6,4},{7,5},{8,10},{9,11},{10,... | collective-permute-start | bytes 393224 | tf_op jit(solution)/shard_map/ppermute | solution.py:430
where the time goes:
time: 46.7 us; the launch traced here: 46.6 us
  Pallas kernels  19.5 us (42%)
  starting transfers between devices  15.4 us (33%)
  waiting for transfers between devices  10.6 us (23%)
  between operations  0.92 us (2%)
    ppermute x9, starting transfers between devices, swap(): return lax.ppermute(value, axis, [(i, i ^ by) for i in range(size)])  13.2 us
    pallas_call x1, Pallas kernels, spectra_call(): pl.pallas_call(functools.partial(spectra_kernel, n_win, n_rcv, r_dev), in...  9.91 us
    ppermute x9, waiting for transfers between devices, swap(): return lax.ppermute(value, axis, [(i, i ^ by) for i in range(size)])  8.5 us
    pallas_call x2, Pallas kernels, stacks_call(): pl.pallas_call(functools.partial(stacks_kernel, shares, n_win, w_dev, r_d...  7.32 us
    ppermute x2, starting transfers between devices, body(): near.append(lax.ppermute(picked[i], 'rcv', pairs))  2.22 us
    pallas_call x4, Pallas kernels, turn_call(): pl.pallas_call(functools.partial(turn_kernel, r_dev), in_specs=[vmem] * l...  2.16 us
    ppermute x2, waiting for transfers between devices, body(): near.append(lax.ppermute(picked[i], 'rcv', pairs))  2.09 us
  transfers between devices with their start and end apart: 11, of which 4 were waited for; matrix products, arithmetic and copies ran while one was open for 0% of the time, Pallas kernels for 13%

commit v1 on v0

--- a/solution.py
+++ b/solution.py
@@ -24,32 +24,33 @@
     return np.concatenate([np.cos(angle), -np.sin(angle)], axis=1).astype(jnp.bfloat16)
 
 
-FINE = 32
-
-
-def angle_factors(count, bins, first, n_win):
-    j = np.arange(bins // 4).reshape(n_win, 1, -1)
+BLOCK = 32
+
+
+def table_seeds(count, bins, first, n_win):
+    j = np.arange(bins // 4)
     turn = np.array([0.0, 0.5 * math.pi]).reshape(1, 2, 1)
-
-    def factors(samples, shift):
-        out = []
-        for m in range(4):
-            freqs = np.broadcast_to(first + 4 * j + m, (n_win, 2, bins // 4 // n_win))
-            angle = angles(samples, freqs.reshape(-1), count)
-            angle = angle + np.broadcast_to(shift, freqs.shape).reshape(1, -1)
-            out.append(np.stack([np.cos(angle), np.sin(angle)]))
-        return np.stack(out).astype(np.float32)
-
-    return factors(np.arange(0, count // 4, FINE), 0.0 * turn), factors(np.arange(FINE), turn)
-
-
-def make_tables(coarse_ref, fine_ref, table_ref):
-    for m in range(table_ref.shape[0]):
-        cos_b, sin_b = fine_ref[m, 0], fine_ref[m, 1]
-        for a in range(coarse_ref.shape[2]):
-            cos_a, sin_a = (coarse_ref[m, k, a:a + 1, :] for k in range(2))
-            rows = slice(a * FINE, (a + 1) * FINE)
-            table_ref[m, rows, :] = (cos_a * cos_b - sin_a * sin_b).astype(jnp.bfloat16)
+    seeds, twice = [], []
+    for m in range(4):
+        freqs = np.broadcast_to((first + 4 * j + m).reshape(n_win, 1, -1), (n_win, 2, j.size // n_win))
+        angle = angles(np.arange(2 * BLOCK), freqs.reshape(-1), count)
+        angle = angle + np.broadcast_to(turn, freqs.shape).reshape(1, -1)
+        seeds.append(np.cos(angle).reshape(2, BLOCK, -1))
+        step = angles(np.full(8, BLOCK), freqs.reshape(-1), count)
+        twice.append(2.0 * np.cos(step))
+    return np.stack(seeds).astype(np.float32), np.stack(twice).astype(np.float32)
+
+
+def make_tables(seed_ref, twice_ref, table_ref):
+    for first in (0, 2):
+        state = {}
+        for m in (first, first + 1):
+            twice = jnp.concatenate([twice_ref[m]] * (BLOCK // 8), axis=0)
+            state[m] = (seed_ref[m, 0], seed_ref[m, 1], twice)
+        for a in range(table_ref.shape[1] // BLOCK):
+            for m, (here, after, twice) in state.items():
+                table_ref[m, a * BLOCK:(a + 1) * BLOCK, :] = here.astype(jnp.bfloat16)
+                state[m] = (after, twice * after - here, twice)
 
 
 def in_hbm(value):
@@ -85,12 +86,12 @@
 
 
 def spectra_kernel(
-    n_win, n_rcv, r_dev, valid_hbm, src_hbm, x_hbm, coarse_hbm, fine_hbm, *refs
+    n_win, n_rcv, r_dev, valid_hbm, src_hbm, x_hbm, seed_hbm, twice_hbm, *refs
 ):
     r_refs = refs[:n_win]
     q_refs = refs[n_win:n_win + n_rcv]
     (plan_ref, flag_ref, x_ref, even_ref, odd_ref, white_ref, sel_ref, order_ref, table_ref,
-     coarse_ref, fine_ref, valid_ref, src_ref, sems, x_sems) = refs[n_win + n_rcv:]
+     seed_ref, twice_ref, valid_ref, src_ref, sems, x_sems) = refs[n_win + n_rcv:]
     chunks, rows, samples = x_ref.shape
     w_step = rows // r_dev
     n_own = src_ref.shape[0] // n_rcv
@@ -99,8 +100,8 @@
     rcv = lax.axis_index("rcv")
 
     def small(k):
-        source = (coarse_hbm, fine_hbm, src_hbm, valid_hbm)[k]
-        target = (coarse_ref, fine_ref, src_ref, valid_ref)[k]
+        source = (seed_hbm, twice_hbm, src_hbm, valid_hbm)[k]
+        target = (seed_ref, twice_ref, src_ref, valid_ref)[k]
         return pltpu.make_async_copy(source, target, sems.at[k])
 
     def chunk(k):
@@ -112,7 +113,7 @@
         chunk(k).start()
     small(0).wait()
     small(1).wait()
-    make_tables(coarse_ref, fine_ref, table_ref)
+    make_tables(seed_ref, twice_ref, table_ref)
     small(2).wait()
     order_sources(src_ref, r_dev, n_own, order_ref, plan_ref, flag_ref)
     stations = []
@@ -198,7 +199,7 @@
     every = w_dev * r_dev
     rows = every // chunks
     lanes = 2 * F // n_win
-    coarse, fine = (jnp.asarray(t) for t in angle_factors(samples, F, samples // 16, n_win))
+    seed, twice = (jnp.asarray(t) for t in table_seeds(samples, F, samples // 16, n_win))
     shapes = [jax.ShapeDtypeStruct((every, lanes), jnp.bfloat16)] * n_win
     shapes += [jax.ShapeDtypeStruct((n_win, w_dev * n_own, lanes), jnp.bfloat16)] * n_rcv
     shapes += [jax.ShapeDtypeStruct((8, 128), jnp.int32), jax.ShapeDtypeStruct((1,), jnp.int32)]
@@ -216,8 +217,8 @@
             pltpu.VMEM((n_src * (w_dev // chunks), rows), jnp.bfloat16),
             pltpu.VMEM((n_src, 128), jnp.float32),
             pltpu.VMEM((4, samples // 4, F // 2), jnp.bfloat16),
-            pltpu.VMEM(coarse.shape, jnp.float32),
-            pltpu.VMEM(fine.shape, jnp.float32),
+            pltpu.VMEM(seed.shape, jnp.float32),
+            pltpu.VMEM(twice.shape, jnp.float32),
             pltpu.SMEM(valid.shape, jnp.int32),
             pltpu.SMEM(src_station.shape, jnp.int32),
             pltpu.SemaphoreType.DMA((4,)),
@@ -229,7 +230,7 @@
             transcendentals=0,
         ),
         name="spectra",
-    )(*(in_hbm(x) for x in (valid, src_station, traces.reshape(every, samples), coarse, fine)))
+    )(*(in_hbm(x) for x in (valid, src_station, traces.reshape(every, samples), seed, twice)))
     return out[:n_win], out[n_win:n_win + n_rcv], out[-2], out[-1]
 
 
@@ -304,33 +305,34 @@
     )(*picked)
 
 
-def join_kernel(n_win, *refs):
+def join_kernel(count, *refs):
     out_ref = refs[-1]
-    for j in range(n_win):
-        out_ref[j] = refs[j][...]
-
-
-def join_call(blocks, after, later):
+    for k in range(count):
+        out_ref[k] = refs[k][...]
+
+
+def join_call(blocks, after=(), later=()):
     rows, lanes = blocks[0].shape
-    n_win = len(blocks)
+    count = len(blocks)
+    first = count + len(after)
     vmem, anywhere = pl.BlockSpec(memory_space=VMEM), pl.BlockSpec(memory_space=pl.ANY)
     out = pl.pallas_call(
-        functools.partial(join_kernel, n_win),
-        in_specs=[vmem] * n_win + [anywhere] * (1 + len(later)),
+        functools.partial(join_kernel, count),
+        in_specs=[vmem] * count + [anywhere] * (len(after) + len(later)),
         out_specs=[anywhere] * len(later) + [vmem],
         out_shape=[jax.ShapeDtypeStruct(x.shape, x.dtype) for x in later]
-        + [jax.ShapeDtypeStruct((n_win, rows, lanes), jnp.bfloat16)],
-        input_output_aliases={n_win + 1 + k: k for k in range(len(later))},
+        + [jax.ShapeDtypeStruct((count, rows, lanes), jnp.bfloat16)],
+        input_output_aliases={first + k: k for k in range(len(later))},
         compiler_params=pltpu.CompilerParams(vmem_limit_bytes=4 * 2**20),
         cost_estimate=pl.CostEstimate(flops=2**18, bytes_accessed=2**19, transcendentals=0),
         name="join",
-    )(*blocks, after, *later)
+    )(*blocks, *after, *later)
     return out[-1], out[:-1]
 
 
-def stacks_kernel(shares, n_win, w_dev, r_dev, n_own, bins, plan_hbm, *refs):
+def stacks_kernel(shares, n_parts, n_win, w_dev, r_dev, n_own, bins, plan_hbm, *refs):
     t_refs = refs[:n_win]
-    s_refs = refs[n_win:n_win + len(shares)]
+    s_refs = refs[n_win:n_win + n_parts * len(shares)]
     out_hbm, srow_ref, left_ref, prod_ref, out_ref, plan_ref, sems, plan_sem = refs[-8:]
     plan_copy = pltpu.make_async_copy(plan_hbm, plan_ref, plan_sem)
     plan_copy.start()
@@ -348,9 +350,10 @@
     lane = lax.broadcasted_iota(jnp.int32, (w_dev, lanes), 1)
     real = (lane // (bins // 4)) % 2 == 0
 
-    for k, s_ref in enumerate(s_refs):
+    for k in range(len(shares)):
         for j in range(n_win):
-            block = s_ref[j].astype(jnp.float32)
+            part, place = divmod(j, n_win // n_parts)
+            block = s_refs[k * n_parts + part][place].astype(jnp.float32)
             for h in range(lanes // pad):
                 half = block[:, h * pad:(h + 1) * pad]
                 srow_ref[h, pl.ds((k * n_win + j) * w_dev * n_own, w_dev * n_own), :] = half
@@ -391,11 +394,12 @@
 
 def stacks_call(out, plan, turned, sources, shares, n_rcv, w_dev, r_dev, bins):
     n_win = len(turned)
-    n_own = sources[0].shape[1] // w_dev
+    n_parts = len(sources[0])
+    n_own = sources[0][0].shape[1] // w_dev
     windows = n_win * w_dev
     count = len(shares) * n_own
     whole = pl.BlockSpec(memory_space=VMEM)
-    args = [plan] + list(turned) + [sources[i] for i in shares]
+    args = [plan] + list(turned) + [part for i in shares for part in sources[i]]
     specs = [pl.BlockSpec(memory_space=pl.ANY)] + [whole] * (len(args) - 1)
     aliases = {}
     if out is not None:
@@ -403,7 +407,7 @@
         args.append(out)
         specs.append(pl.BlockSpec(memory_space=pl.ANY))
     return pl.pallas_call(
-        functools.partial(stacks_kernel, shares, n_win, w_dev, r_dev, n_own, bins),
+        functools.partial(stacks_kernel, shares, n_parts, n_win, w_dev, r_dev, n_own, bins),
         in_specs=specs,
         out_specs=pl.BlockSpec(memory_space=pltpu.HBM),
         out_shape=jax.ShapeDtypeStruct((n_rcv * n_own, 2 * r_dev, bins), jnp.float32),
@@ -468,9 +472,9 @@
     merged = [merged[0]] + [swap(merged[j], "win", j) for j in range(1, n_win)]
     late = [j for j in range(1, n_win) if j != early]
     received = {0: blocks[0], early: swap(blocks[early], "win", early)}
-    joined, later = join_call(merged, received[early], [blocks[j] for j in late])
+    joined, later = join_call(merged, [received[early]], [blocks[j] for j in late])
     received.update({j: swap(block, "win", j) for j, block in zip(late, later)})
-    sources = [joined] + [swap(joined, "rcv", i) for i in range(1, n_rcv)]
+    sources = [[joined]] + [[swap(joined, "rcv", i)] for i in range(1, n_rcv)]
 
     turned = [turn_call([received[j]], w_dev, r_dev) for j in range(n_win)]
     half = n_rcv // 2

time: 46.7 us -> 46.2 us (0.989)
  Pallas kernels: 19.5 us -> 18.9 us
    pallas_call x1, Pallas kernels: 9.91 us -> 9.38 us  [spectra_call(): pl.pallas_call(functools.partial(spectra_kernel, n_win, n_rcv, r_dev), in...]
where the time goes in v1:
time: 46.2 us; the launch traced here: 46.1 us
  Pallas kernels  18.9 us (41%)
  starting transfers between devices  15.5 us (34%)
  waiting for transfers between devices  10.6 us (23%)
  between operations  0.92 us (2%)
    ppermute x9, starting transfers between devices, swap(): return lax.ppermute(value, axis, [(i, i ^ by) for i in range(size)])  13.2 us
    pallas_call x1, Pallas kernels, spectra_call(): pl.pallas_call(functools.partial(spectra_kernel, n_win, n_rcv, r_dev), in...  9.38 us
    ppermute x9, waiting for transfers between devices, swap(): return lax.ppermute(value, axis, [(i, i ^ by) for i in range(size)])  8.49 us
    pallas_call x2, Pallas kernels, stacks_call(): pl.pallas_call(functools.partial(stacks_kernel, shares, n_parts, n_win, w...  7.33 us
    ppermute x2, starting transfers between devices, body(): near.append(lax.ppermute(picked[i], 'rcv', pairs))  2.23 us
    pallas_call x4, Pallas kernels, turn_call(): pl.pallas_call(functools.partial(turn_kernel, r_dev), in_specs=[vmem] * l...  2.16 us
    ppermute x2, waiting for transfers between devices, body(): near.append(lax.ppermute(picked[i], 'rcv', pairs))  2.08 us
  transfers between devices with their start and end apart: 11, of which 4 were waited for; matrix products, arithmetic and copies ran while one was open for 0% of the time, Pallas kernels for 13%

profile of v1, /device:TPU:0, one launch (start us, length us, event | category | flops | bytes accessed | tf_op | source)
XLA Modules:
  0.0 46.1 jit_solution(11497746055393891672)
XLA Ops:
  0.0 9.4 %spectra.1 = (bf16[768,256]{1,0:T(8,128)(2,1)S(1)}, bf16[768,256]{1,0:T(8,128)(2,1)S(1)}, bf16[768,256]{1,0:T(8,128)(2,1)S(1)}, bf16[768,256]{1,0:T(8,128)(2,1)S...) custom-call(s32[8]{0:T(128)} %valid_hbm.1, ...), custom_call_target="tpu_custom_call" | custom-call | flops 2415919104 | bytes 6291456 | tf_op jit(solution)/shard_map/spectra/pallas_call | solution.py:207
  9.4 3.0 %collective-permute-start.7 = (bf16[768,256]{1,0:T(8,128)(2,1)S(1)}, bf16[768,256]{1,0:T(8,128)(2,1)S(1)}, u32[]{:S(2)}, u32[]{:S(2)}) collective-permute-start(bf16[768,256]{1,0:T(8,128)(2,1)S(1)} %get-tuple-element.57), channel_id=1, source_target_pairs={{0,8},{4,12},{8,0},{12,4},{1,9},{5,13},{9,1},{13,5},{2,10},{6,14},... | collective-permute-start | bytes 1179656 | tf_op jit(solution)/shard_map/ppermute | solution.py:434
  12.4 1.6 %collective-permute-start.2 = (bf16[4,64,256]{2,1,0:T(8,128)(2,1)S(1)}, bf16[4,64,256]{2,1,0:T(8,128)(2,1)S(1)}, u32[]{:S(2)}, u32[]{:S(2)}) collective-permute-start(bf16[4,64,256]{2,1,0:T(8,128)(2,1)S(1)} %get-tuple-element.50), channel_id=1, source_target_pairs={{0,1},{1,0},{2,3},{3,2},{4,5},{5,4},{6,7},{7,6},{8,9},{9,8},{10,11... | collective-permute-start | bytes 393224 | tf_op jit(solution)/shard_map/ppermute | solution.py:469
  14.0 0.7 %collective-permute-start.3 = (bf16[4,64,256]{2,1,0:T(8,128)(2,1)S(1)}, bf16[4,64,256]{2,1,0:T(8,128)(2,1)S(1)}, u32[]{:S(2)}, u32[]{:S(2)}) collective-permute-start(bf16[4,64,256]{2,1,0:T(8,128)(2,1)S(1)} %get-tuple-element.51), channel_id=1, source_target_pairs={{1,2},{2,1},{5,6},{6,5},{9,10},{10,9},{13,14},{14,13},{17,18},{18,... | collective-permute-start | bytes 393224 | tf_op jit(solution)/shard_map/ppermute | solution.py:469
  15.3 2.1 %collective-permute-done.2 = bf16[4,64,256]{2,1,0:T(8,128)(2,1)S(1)} collective-permute-done((bf16[4,64,256]{2,1,0:T(8,128)(2,1)S(1)}, bf16[4,64,256]{2,1,0:T(8,128)(2,1)S(1)}, u32[]{:S(2)}, u32[]{:S(2)}) %collective-permute-start.2) | collective-permute-done | bytes 131104 | tf_op jit(solution)/shard_map/ppermute | solution.py:469
  17.4 0.0 collective-permute-done.3
  17.4 0.2 conditional.1
  17.4 0.1 merge.2
  17.7 0.1 collective-permute-start.4
  17.7 0.4 collective-permute-start.5
  18.2 1.4 %collective-permute-start.6 = (bf16[64,256]{1,0:T(8,128)(2,1)S(1)}, bf16[64,256]{1,0:T(8,128)(2,1)S(1)}, u32[]{:S(2)}, u32[]{:S(2)}) collective-permute-start(bf16[64,256]{1,0:T(8,128)(2,1)S(1)} %get-tuple-element.56), channel_id=1, source_target_pairs={{0,12},{4,8},{8,4},{12,0},{1,13},{5,9},{9,5},{13,1},{2,14},{6,10},... | collective-permute-start | bytes 98312 | tf_op jit(solution)/shard_map/ppermute | solution.py:434
  19.6 3.0 %collective-permute-done.5.refs_2_ = bf16[64,256]{1,0:T(8,128)(2,1)S(1)} collective-permute-done((bf16[64,256]{1,0:T(8,128)(2,1)S(1)}, bf16[64,256]{1,0:T(8,128)(2,1)S(1)}, u32[]{:S(2)}, u32[]{:S(2)}) %collective-permute-start.5) | collective-permute-done | bytes 32800 | tf_op jit(solution)/shard_map/ppermute | solution.py:434
  22.6 1.6 %collective-permute-start.9 = (bf16[768,256]{1,0:T(8,128)(2,1)S(1)}, bf16[768,256]{1,0:T(8,128)(2,1)S(1)}, u32[]{:S(2)}, u32[]{:S(2)}) collective-permute-start(bf16[768,256]{1,0:T(8,128)(2,1)S(1)} %get-tuple-element.61), channel_id=1, source_target_pairs={{0,12},{4,8},{8,4},{12,0},{1,13},{5,9},{9,5},{13,1},{2,14},{6,10},... | collective-permute-start | bytes 1179656 | tf_op jit(solution)/shard_map/ppermute | solution.py:434
  24.2 0.3 collective-permute-start.8
  24.6 3.4 %collective-permute-start.12 = (bf16[4,64,256]{2,1,0:T(8,128)(2,1)S(1)}, bf16[4,64,256]{2,1,0:T(8,128)(2,1)S(1)}, u32[]{:S(2)}, u32[]{:S(2)}) collective-permute-start(bf16[4,64,256]{2,1,0:T(8,128)(2,1)S(1)} %get-tuple-element.62.refs_4_), channel_id=1, source_target_pairs={{0,1},{1,0},{2,3},{3,2},{4,5},{5,4},{6,7},{7,6},{8,9},{9,8},{10,11... | collective-permute-start | bytes 393224 | tf_op jit(solution)/shard_map/ppermute | solution.py:434
  28.0 2.9 %collective-permute-start.11 = (bf16[4,64,256]{2,1,0:T(8,128)(2,1)S(1)}, bf16[4,64,256]{2,1,0:T(8,128)(2,1)S(1)}, u32[]{:S(2)}, u32[]{:S(2)}) collective-permute-start(bf16[4,64,256]{2,1,0:T(8,128)(2,1)S(1)} %get-tuple-element.62.refs_4_), channel_id=1, source_target_pairs={{0,3},{1,2},{2,1},{3,0},{4,7},{5,6},{6,5},{7,4},{8,11},{9,10},{10,... | collective-permute-start | bytes 393224 | tf_op jit(solution)/shard_map/ppermute | solution.py:434
  30.9 0.5 %turn.4.refs_0_ = bf16[128,16,256]{2,1,0:T(8,128)(2,1)S(1)} custom-call(bf16[768,256]{1,0:T(8,128)(2,1)S(1)} %get-tuple-element.47.refs_0_), custom_call_target="tpu_custom_call" | custom-call | flops 134217728 | bytes 2097152 | tf_op jit(solution)/shard_map/turn/pallas_call | solution.py:271
  31.4 0.5 %turn.6.refs_2_ = bf16[128,16,256]{2,1,0:T(8,128)(2,1)S(1)} custom-call(bf16[768,256]{1,0:T(8,128)(2,1)S(1)} %collective-permute-done.7.refs_4_.refs_0_), custom_call_target="tpu_custom_call" | custom-call | flops 134217728 | bytes 2097152 | tf_op jit(solution)/shard_map/turn/pallas_call | solution.py:271
  32.0 1.9 %collective-permute-done.9.refs_0_ = bf16[768,256]{1,0:T(8,128)(2,1)S(1)} collective-permute-done((bf16[768,256]{1,0:T(8,128)(2,1)S(1)}, bf16[768,256]{1,0:T(8,128)(2,1)S(1)}, u32[]{:S(2)}, u32[]{:S(2)}) %collective-permute-start.9) | collective-permute-done | bytes 393248 | tf_op jit(solution)/shard_map/ppermute | solution.py:434
  33.9 0.5 %turn.7.refs_3_ = bf16[128,16,256]{2,1,0:T(8,128)(2,1)S(1)} custom-call(bf16[768,256]{1,0:T(8,128)(2,1)S(1)} %collective-permute-done.9.refs_0_), custom_call_target="tpu_custom_call" | custom-call | flops 134217728 | bytes 2097152 | tf_op jit(solution)/shard_map/turn/pallas_call | solution.py:271
  34.4 0.5 %turn.5.refs_1_ = bf16[128,16,256]{2,1,0:T(8,128)(2,1)S(1)} custom-call(bf16[768,256]{1,0:T(8,128)(2,1)S(1)} %collective-permute-done.8.refs_0_), custom_call_target="tpu_custom_call" | custom-call | flops 134217728 | bytes 2097152 | tf_op jit(solution)/shard_map/turn/pallas_call | solution.py:271
  35.0 3.7 %stacks.2.refs_6_ = f32[32,192,128]{2,1,0:T(8,128)} custom-call(s32[8,128]{1,0:T(8,128)S(1)} %get-tuple-element.46.plan_hbm, bf16[128,16,256]{2,1,0:T(8,128)(2,1)S(1)} %turn.4.refs_0_, bf16[128,16,256]{2,1,0:T(8,128)(2,1)S(1)} %turn.5.refs_1_, bf16[128,16,256]{2,1,0:T(8,128)(2,1)S(1)} %turn.6.refs_2_, bf16[128,16,256]{2,1,0:T(8,128)(2,1)S(1)} %turn.7.refs_3_, ...), custom_call_target="tpu_custom_call" | custom-call | flops 50331648 | bytes 6291456 | tf_op jit(solution)/shard_map/stacks/pallas_call | solution.py:409
  38.7 3.6 %collective-permute-done.10.refs_4_ = bf16[4,64,256]{2,1,0:T(8,128)(2,1)S(1)} collective-permute-done((bf16[4,64,256]{2,1,0:T(8,128)(2,1)S(1)}, bf16[4,64,256]{2,1,0:T(8,128)(2,1)S(1)}, u32[]{:S(2)}, u32[]{:S(2)}) %collective-permute-start.10) | collective-permute-done | bytes 131104 | tf_op jit(solution)/shard_map/ppermute | solution.py:434
  42.2 3.7 %stacks.3 = f32[32,192,128]{2,1,0:T(8,128)} custom-call(s32[8,128]{1,0:T(8,128)S(1)} %get-tuple-element.46.plan_hbm, bf16[128,16,256]{2,1,0:T(8,128)(2,1)S(1)} %turn.4.refs_0_, bf16[128,16,256]{2,1,0:T(8,128)(2,1)S(1)} %turn.5.refs_1_, bf16[128,16,256]{2,1,0:T(8,128)(2,1)S(1)} %turn.6.refs_2_, ...), custom_call_target="tpu_custom_call", output_to_operand_aliasing={{}: (7, {})} | custom-call | flops 50331648 | bytes 6291456 | tf_op jit(solution)/shard_map/stacks/pallas_call | solution.py:409
  (8 shorter events, 0.0 us)
Async XLA Ops:
  9.4 13.2 %collective-permute-start.7 = (bf16[768,256]{1,0:T(8,128)(2,1)S(1)}, bf16[768,256]{1,0:T(8,128)(2,1)S(1)}, u32[]{:S(2)}, u32[]{:S(2)}) collective-permute-start(bf16[768,256]{1,0:T(8,128)(2,1)S(1)} %get-tuple-element.57), channel_id=1, source_target_pairs={{0,8},{4,12},{8,0},{12,4},{1,9},{5,13},{9,1},{13,5},{2,10},{6,14},... | collective-permute-start | bytes 1179656 | tf_op jit(solution)/shard_map/ppermute | solution.py:434
  12.4 5.0 %collective-permute-start.2 = (bf16[4,64,256]{2,1,0:T(8,128)(2,1)S(1)}, bf16[4,64,256]{2,1,0:T(8,128)(2,1)S(1)}, u32[]{:S(2)}, u32[]{:S(2)}) collective-permute-start(bf16[4,64,256]{2,1,0:T(8,128)(2,1)S(1)} %get-tuple-element.50), channel_id=1, source_target_pairs={{0,1},{1,0},{2,3},{3,2},{4,5},{5,4},{6,7},{7,6},{8,9},{9,8},{10,11... | collective-permute-start | bytes 393224 | tf_op jit(solution)/shard_map/ppermute | solution.py:469
  14.0 3.4 %collective-permute-start.3 = (bf16[4,64,256]{2,1,0:T(8,128)(2,1)S(1)}, bf16[4,64,256]{2,1,0:T(8,128)(2,1)S(1)}, u32[]{:S(2)}, u32[]{:S(2)}) collective-permute-start(bf16[4,64,256]{2,1,0:T(8,128)(2,1)S(1)} %get-tuple-element.51), channel_id=1, source_target_pairs={{1,2},{2,1},{5,6},{6,5},{9,10},{10,9},{13,14},{14,13},{17,18},{18,... | collective-permute-start | bytes 393224 | tf_op jit(solution)/shard_map/ppermute | solution.py:469
  17.7 1.9 %collective-permute-start.4 = (bf16[64,256]{1,0:T(8,128)(2,1)S(1)}, bf16[64,256]{1,0:T(8,128)(2,1)S(1)}, u32[]{:S(2)}, u32[]{:S(2)}) collective-permute-start(bf16[64,256]{1,0:T(8,128)(2,1)S(1)} %get-tuple-element.54), channel_id=1, source_target_pairs={{0,4},{4,0},{8,12},{12,8},{1,5},{5,1},{9,13},{13,9},{2,6},{6,2},{1... | collective-permute-start | bytes 98312 | tf_op jit(solution)/shard_map/ppermute | solution.py:434
  17.7 4.9 %collective-permute-start.5 = (bf16[64,256]{1,0:T(8,128)(2,1)S(1)}, bf16[64,256]{1,0:T(8,128)(2,1)S(1)}, u32[]{:S(2)}, u32[]{:S(2)}) collective-permute-start(bf16[64,256]{1,0:T(8,128)(2,1)S(1)} %get-tuple-element.55), channel_id=1, source_target_pairs={{0,8},{4,12},{8,0},{12,4},{1,9},{5,13},{9,1},{13,5},{2,10},{6,14},... | collective-permute-start | bytes 98312 | tf_op jit(solution)/shard_map/ppermute | solution.py:434
  18.2 4.5 %collective-permute-start.6 = (bf16[64,256]{1,0:T(8,128)(2,1)S(1)}, bf16[64,256]{1,0:T(8,128)(2,1)S(1)}, u32[]{:S(2)}, u32[]{:S(2)}) collective-permute-start(bf16[64,256]{1,0:T(8,128)(2,1)S(1)} %get-tuple-element.56), channel_id=1, source_target_pairs={{0,12},{4,8},{8,4},{12,0},{1,13},{5,9},{9,5},{13,1},{2,14},{6,10},... | collective-permute-start | bytes 98312 | tf_op jit(solution)/shard_map/ppermute | solution.py:434
  22.6 11.2 %collective-permute-start.9 = (bf16[768,256]{1,0:T(8,128)(2,1)S(1)}, bf16[768,256]{1,0:T(8,128)(2,1)S(1)}, u32[]{:S(2)}, u32[]{:S(2)}) collective-permute-start(bf16[768,256]{1,0:T(8,128)(2,1)S(1)} %get-tuple-element.61), channel_id=1, source_target_pairs={{0,12},{4,8},{8,4},{12,0},{1,13},{5,9},{9,5},{13,1},{2,14},{6,10},... | collective-permute-start | bytes 1179656 | tf_op jit(solution)/shard_map/ppermute | solution.py:434
  24.2 10.2 %collective-permute-start.8 = (bf16[768,256]{1,0:T(8,128)(2,1)S(1)}, bf16[768,256]{1,0:T(8,128)(2,1)S(1)}, u32[]{:S(2)}, u32[]{:S(2)}) collective-permute-start(bf16[768,256]{1,0:T(8,128)(2,1)S(1)} %get-tuple-element.60), channel_id=1, source_target_pairs={{0,4},{4,0},{8,12},{12,8},{1,5},{5,1},{9,13},{13,9},{2,6},{6,2},{1... | collective-permute-start | bytes 1179656 | tf_op jit(solution)/shard_map/ppermute | solution.py:434
  24.6 10.4 %collective-permute-start.12 = (bf16[4,64,256]{2,1,0:T(8,128)(2,1)S(1)}, bf16[4,64,256]{2,1,0:T(8,128)(2,1)S(1)}, u32[]{:S(2)}, u32[]{:S(2)}) collective-permute-start(bf16[4,64,256]{2,1,0:T(8,128)(2,1)S(1)} %get-tuple-element.62.refs_4_), channel_id=1, source_target_pairs={{0,1},{1,0},{2,3},{3,2},{4,5},{5,4},{6,7},{7,6},{8,9},{9,8},{10,11... | collective-permute-start | bytes 393224 | tf_op jit(solution)/shard_map/ppermute | solution.py:434
  28.0 10.7 %collective-permute-start.11 = (bf16[4,64,256]{2,1,0:T(8,128)(2,1)S(1)}, bf16[4,64,256]{2,1,0:T(8,128)(2,1)S(1)}, u32[]{:S(2)}, u32[]{:S(2)}) collective-permute-start(bf16[4,64,256]{2,1,0:T(8,128)(2,1)S(1)} %get-tuple-element.62.refs_4_), channel_id=1, source_target_pairs={{0,3},{1,2},{2,1},{3,0},{4,7},{5,6},{6,5},{7,4},{8,11},{9,10},{10,... | collective-permute-start | bytes 393224 | tf_op jit(solution)/shard_map/ppermute | solution.py:434
  30.9 11.4 %collective-permute-start.10 = (bf16[4,64,256]{2,1,0:T(8,128)(2,1)S(1)}, bf16[4,64,256]{2,1,0:T(8,128)(2,1)S(1)}, u32[]{:S(2)}, u32[]{:S(2)}) collective-permute-start(bf16[4,64,256]{2,1,0:T(8,128)(2,1)S(1)} %get-tuple-element.62.refs_4_), channel_id=1, source_target_pairs={{0,2},{1,3},{2,0},{3,1},{4,6},{5,7},{6,4},{7,5},{8,10},{9,11},{10,... | collective-permute-start | bytes 393224 | tf_op jit(solution)/shard_map/ppermute | solution.py:434

commit v2 on v1

--- a/solution.py
+++ b/solution.py
@@ -195,7 +195,7 @@
     w_dev, r_dev, samples = traces.shape
     n_src = src_station.shape[0]
     n_own = n_src // n_rcv
-    chunks = 4
+    chunks = 2
     every = w_dev * r_dev
     rows = every // chunks
     lanes = 2 * F // n_win
@@ -462,11 +462,13 @@
 
     blocks, picked, plan, flag = spectra_call(traces, valid, src_station, n_win, n_rcv)
 
-    near = []
+    near = {}
     for i in range(1, n_rcv):
         pairs = near_and_far(n_rcv, i)[0]
         if pairs:
-            near.append(lax.ppermute(picked[i], "rcv", pairs))
+            near[i] = lax.ppermute(picked[i], "rcv", pairs)
+    picked = [picked[0] + near.pop(n_rcv - 1)] + list(picked[1:])
+    near = list(near.values())
     merged = lax.cond(flag.reshape(()) > 0, merge_all, merge_near, picked, near)
 
     merged = [merged[0]] + [swap(merged[j], "win", j) for j in range(1, n_win)]

time: 46.2 us -> 45.1 us (0.976)
  Pallas kernels: 18.9 us -> 18.2 us
  starting transfers between devices: 15.5 us -> 14.9 us
    ppermute x9, starting transfers between devices: 13.2 us -> 9.81 us  [swap(): return lax.ppermute(value, axis, [(i, i ^ by) for i in range(size)])]
    ppermute x2, starting transfers between devices: 2.23 us -> 5.11 us  [body(): near[i] = lax.ppermute(picked[i], 'rcv', pairs)]
    pallas_call x1, Pallas kernels: 9.38 us -> 8.63 us  [spectra_call(): pl.pallas_call(functools.partial(spectra_kernel, n_win, n_rcv, r_dev), in...]
where the time goes in v2:
time: 45.1 us; the launch traced here: 45 us
  Pallas kernels  18.2 us (40%)
  starting transfers between devices  14.9 us (33%)
  waiting for transfers between devices  10.7 us (24%)
  between operations  0.94 us (2%)
    ppermute x9, starting transfers between devices, swap(): return lax.ppermute(value, axis, [(i, i ^ by) for i in range(size)])  9.81 us
    pallas_call x1, Pallas kernels, spectra_call(): pl.pallas_call(functools.partial(spectra_kernel, n_win, n_rcv, r_dev), in...  8.63 us
    ppermute x9, waiting for transfers between devices, swap(): return lax.ppermute(value, axis, [(i, i ^ by) for i in range(size)])  8.47 us
    pallas_call x2, Pallas kernels, stacks_call(): pl.pallas_call(functools.partial(stacks_kernel, shares, n_parts, n_win, w...  7.33 us
    ppermute x2, starting transfers between devices, body(): near[i] = lax.ppermute(picked[i], 'rcv', pairs)  5.11 us
    ppermute x2, waiting for transfers between devices, body(): near[i] = lax.ppermute(picked[i], 'rcv', pairs)  2.25 us
    pallas_call x4, Pallas kernels, turn_call(): pl.pallas_call(functools.partial(turn_kernel, r_dev), in_specs=[vmem] * l...  2.16 us
  transfers between devices with their start and end apart: 11, of which 4 were waited for; matrix products, arithmetic and copies ran while one was open for 0% of the time, Pallas kernels for 13%

profile of v2, /device:TPU:0, one launch (start us, length us, event | category | flops | bytes accessed | tf_op | source)
XLA Modules:
  0.0 45.0 jit_solution(13644458879548944144)
XLA Ops:
  0.0 8.6 %spectra.1 = (bf16[768,256]{1,0:T(8,128)(2,1)S(1)}, bf16[768,256]{1,0:T(8,128)(2,1)S(1)}, bf16[768,256]{1,0:T(8,128)(2,1)S(1)}, bf16[768,256]{1,0:T(8,128)(2,1)S...) custom-call(s32[8]{0:T(128)} %valid_hbm.1, ...), custom_call_target="tpu_custom_call" | custom-call | flops 2415919104 | bytes 6291456 | tf_op jit(solution)/shard_map/spectra/pallas_call | solution.py:207
  8.6 3.0 %collective-permute-start.7 = (bf16[768,256]{1,0:T(8,128)(2,1)S(1)}, bf16[768,256]{1,0:T(8,128)(2,1)S(1)}, u32[]{:S(2)}, u32[]{:S(2)}) collective-permute-start(bf16[768,256]{1,0:T(8,128)(2,1)S(1)} %get-tuple-element.51), channel_id=1, source_target_pairs={{0,8},{4,12},{8,0},{12,4},{1,9},{5,13},{9,1},{13,5},{2,10},{6,14},... | collective-permute-start | bytes 1179656 | tf_op jit(solution)/shard_map/ppermute | solution.py:434
  11.7 0.7 %collective-permute-start.2 = (bf16[4,64,256]{2,1,0:T(8,128)(2,1)S(1)}, bf16[4,64,256]{2,1,0:T(8,128)(2,1)S(1)}, u32[]{:S(2)}, u32[]{:S(2)}) collective-permute-start(bf16[4,64,256]{2,1,0:T(8,128)(2,1)S(1)} %get-tuple-element.44), channel_id=1, source_target_pairs={{1,2},{2,1},{5,6},{6,5},{9,10},{10,9},{13,14},{14,13},{17,18},{18,... | collective-permute-start | bytes 393224 | tf_op jit(solution)/shard_map/ppermute | solution.py:469
  12.3 4.5 %collective-permute-start.3 = (bf16[4,64,256]{2,1,0:T(8,128)(2,1)S(1)}, bf16[4,64,256]{2,1,0:T(8,128)(2,1)S(1)}, u32[]{:S(2)}, u32[]{:S(2)}) collective-permute-start(bf16[4,64,256]{2,1,0:T(8,128)(2,1)S(1)} %get-tuple-element.45), channel_id=1, source_target_pairs={{0,1},{1,0},{2,3},{3,2},{4,5},{5,4},{6,7},{7,6},{8,9},{9,8},{10,11... | collective-permute-start | bytes 393224 | tf_op jit(solution)/shard_map/ppermute | solution.py:469
  17.5 2.2 %collective-permute-done.3 = bf16[4,64,256]{2,1,0:T(8,128)(2,1)S(1)} collective-permute-done((bf16[4,64,256]{2,1,0:T(8,128)(2,1)S(1)}, bf16[4,64,256]{2,1,0:T(8,128)(2,1)S(1)}, u32[]{:S(2)}, u32[]{:S(2)}) %collective-permute-start.3) | collective-permute-done | bytes 131104 | tf_op jit(solution)/shard_map/ppermute | solution.py:469
  19.7 0.2 conditional.1
  20.0 0.1 collective-permute-start.4
  20.0 0.6 %collective-permute-start.5 = (bf16[64,256]{1,0:T(8,128)(2,1)S(1)}, bf16[64,256]{1,0:T(8,128)(2,1)S(1)}, u32[]{:S(2)}, u32[]{:S(2)}) collective-permute-start(bf16[64,256]{1,0:T(8,128)(2,1)S(1)} %get-tuple-element.49), channel_id=1, source_target_pairs={{0,8},{4,12},{8,0},{12,4},{1,9},{5,13},{9,1},{13,5},{2,10},{6,14},... | collective-permute-start | bytes 98312 | tf_op jit(solution)/shard_map/ppermute | solution.py:434
  20.6 1.3 %collective-permute-start.6 = (bf16[64,256]{1,0:T(8,128)(2,1)S(1)}, bf16[64,256]{1,0:T(8,128)(2,1)S(1)}, u32[]{:S(2)}, u32[]{:S(2)}) collective-permute-start(bf16[64,256]{1,0:T(8,128)(2,1)S(1)} %get-tuple-element.50), channel_id=1, source_target_pairs={{0,12},{4,8},{8,4},{12,0},{1,13},{5,9},{9,5},{13,1},{2,14},{6,10},... | collective-permute-start | bytes 98312 | tf_op jit(solution)/shard_map/ppermute | solution.py:434
  21.9 0.0 collective-permute-done.4.refs_1_
  21.9 2.4 %collective-permute-done.5.refs_2_ = bf16[64,256]{1,0:T(8,128)(2,1)S(1)} collective-permute-done((bf16[64,256]{1,0:T(8,128)(2,1)S(1)}, bf16[64,256]{1,0:T(8,128)(2,1)S(1)}, u32[]{:S(2)}, u32[]{:S(2)}) %collective-permute-start.5) | collective-permute-done | bytes 32800 | tf_op jit(solution)/shard_map/ppermute | solution.py:434
  24.3 1.0 %collective-permute-start.9 = (bf16[768,256]{1,0:T(8,128)(2,1)S(1)}, bf16[768,256]{1,0:T(8,128)(2,1)S(1)}, u32[]{:S(2)}, u32[]{:S(2)}) collective-permute-start(bf16[768,256]{1,0:T(8,128)(2,1)S(1)} %get-tuple-element.55), channel_id=1, source_target_pairs={{0,12},{4,8},{8,4},{12,0},{1,13},{5,9},{9,5},{13,1},{2,14},{6,10},... | collective-permute-start | bytes 1179656 | tf_op jit(solution)/shard_map/ppermute | solution.py:434
  25.3 0.3 collective-permute-start.8
  25.7 2.0 %collective-permute-start.12 = (bf16[4,64,256]{2,1,0:T(8,128)(2,1)S(1)}, bf16[4,64,256]{2,1,0:T(8,128)(2,1)S(1)}, u32[]{:S(2)}, u32[]{:S(2)}) collective-permute-start(bf16[4,64,256]{2,1,0:T(8,128)(2,1)S(1)} %get-tuple-element.56.refs_4_), channel_id=1, source_target_pairs={{0,1},{1,0},{2,3},{3,2},{4,5},{5,4},{6,7},{7,6},{8,9},{9,8},{10,11... | collective-permute-start | bytes 393224 | tf_op jit(solution)/shard_map/ppermute | solution.py:434
  27.7 1.3 %collective-permute-start.11 = (bf16[4,64,256]{2,1,0:T(8,128)(2,1)S(1)}, bf16[4,64,256]{2,1,0:T(8,128)(2,1)S(1)}, u32[]{:S(2)}, u32[]{:S(2)}) collective-permute-start(bf16[4,64,256]{2,1,0:T(8,128)(2,1)S(1)} %get-tuple-element.56.refs_4_), channel_id=1, source_target_pairs={{0,3},{1,2},{2,1},{3,0},{4,7},{5,6},{6,5},{7,4},{8,11},{9,10},{10,... | collective-permute-start | bytes 393224 | tf_op jit(solution)/shard_map/ppermute | solution.py:434
  29.0 0.1 collective-permute-start.10
  29.2 0.5 %turn.4.refs_0_ = bf16[128,16,256]{2,1,0:T(8,128)(2,1)S(1)} custom-call(bf16[768,256]{1,0:T(8,128)(2,1)S(1)} %get-tuple-element.41.refs_0_), custom_call_target="tpu_custom_call" | custom-call | flops 134217728 | bytes 2097152 | tf_op jit(solution)/shard_map/turn/pallas_call | solution.py:271
  29.7 0.5 %turn.6.refs_2_ = bf16[128,16,256]{2,1,0:T(8,128)(2,1)S(1)} custom-call(bf16[768,256]{1,0:T(8,128)(2,1)S(1)} %collective-permute-done.7.refs_4_.refs_0_), custom_call_target="tpu_custom_call" | custom-call | flops 134217728 | bytes 2097152 | tf_op jit(solution)/shard_map/turn/pallas_call | solution.py:271
  30.3 5.3 %collective-permute-done.9.refs_0_ = bf16[768,256]{1,0:T(8,128)(2,1)S(1)} collective-permute-done((bf16[768,256]{1,0:T(8,128)(2,1)S(1)}, bf16[768,256]{1,0:T(8,128)(2,1)S(1)}, u32[]{:S(2)}, u32[]{:S(2)}) %collective-permute-start.9) | collective-permute-done | bytes 393248 | tf_op jit(solution)/shard_map/ppermute | solution.py:434
  35.6 0.5 %turn.7.refs_3_ = bf16[128,16,256]{2,1,0:T(8,128)(2,1)S(1)} custom-call(bf16[768,256]{1,0:T(8,128)(2,1)S(1)} %collective-permute-done.9.refs_0_), custom_call_target="tpu_custom_call" | custom-call | flops 134217728 | bytes 2097152 | tf_op jit(solution)/shard_map/turn/pallas_call | solution.py:271
  36.1 0.5 %turn.5.refs_1_ = bf16[128,16,256]{2,1,0:T(8,128)(2,1)S(1)} custom-call(bf16[768,256]{1,0:T(8,128)(2,1)S(1)} %collective-permute-done.8.refs_0_), custom_call_target="tpu_custom_call" | custom-call | flops 134217728 | bytes 2097152 | tf_op jit(solution)/shard_map/turn/pallas_call | solution.py:271
  36.7 3.7 %stacks.2.refs_6_ = f32[32,192,128]{2,1,0:T(8,128)} custom-call(s32[8,128]{1,0:T(8,128)S(1)} %get-tuple-element.40.plan_hbm, bf16[128,16,256]{2,1,0:T(8,128)(2,1)S(1)} %turn.4.refs_0_, bf16[128,16,256]{2,1,0:T(8,128)(2,1)S(1)} %turn.5.refs_1_, bf16[128,16,256]{2,1,0:T(8,128)(2,1)S(1)} %turn.6.refs_2_, bf16[128,16,256]{2,1,0:T(8,128)(2,1)S(1)} %turn.7.refs_3_, ...), custom_call_target="tpu_custom_call" | custom-call | flops 50331648 | bytes 6291456 | tf_op jit(solution)/shard_map/stacks/pallas_call | solution.py:409
  40.4 0.8 %collective-permute-done.10.refs_4_ = bf16[4,64,256]{2,1,0:T(8,128)(2,1)S(1)} collective-permute-done((bf16[4,64,256]{2,1,0:T(8,128)(2,1)S(1)}, bf16[4,64,256]{2,1,0:T(8,128)(2,1)S(1)}, u32[]{:S(2)}, u32[]{:S(2)}) %collective-permute-start.10) | collective-permute-done | bytes 131104 | tf_op jit(solution)/shard_map/ppermute | solution.py:434
  41.1 3.7 %stacks.3 = f32[32,192,128]{2,1,0:T(8,128)} custom-call(s32[8,128]{1,0:T(8,128)S(1)} %get-tuple-element.40.plan_hbm, bf16[128,16,256]{2,1,0:T(8,128)(2,1)S(1)} %turn.4.refs_0_, bf16[128,16,256]{2,1,0:T(8,128)(2,1)S(1)} %turn.5.refs_1_, bf16[128,16,256]{2,1,0:T(8,128)(2,1)S(1)} %turn.6.refs_2_, ...), custom_call_target="tpu_custom_call", output_to_operand_aliasing={{}: (7, {})} | custom-call | flops 50331648 | bytes 6291456 | tf_op jit(solution)/shard_map/stacks/pallas_call | solution.py:409
  (9 shorter events, 0.1 us)
Async XLA Ops:
  8.6 15.7 %collective-permute-start.7 = (bf16[768,256]{1,0:T(8,128)(2,1)S(1)}, bf16[768,256]{1,0:T(8,128)(2,1)S(1)}, u32[]{:S(2)}, u32[]{:S(2)}) collective-permute-start(bf16[768,256]{1,0:T(8,128)(2,1)S(1)} %get-tuple-element.51), channel_id=1, source_target_pairs={{0,8},{4,12},{8,0},{12,4},{1,9},{5,13},{9,1},{13,5},{2,10},{6,14},... | collective-permute-start | bytes 1179656 | tf_op jit(solution)/shard_map/ppermute | solution.py:434
  11.7 5.8 %collective-permute-start.2 = (bf16[4,64,256]{2,1,0:T(8,128)(2,1)S(1)}, bf16[4,64,256]{2,1,0:T(8,128)(2,1)S(1)}, u32[]{:S(2)}, u32[]{:S(2)}) collective-permute-start(bf16[4,64,256]{2,1,0:T(8,128)(2,1)S(1)} %get-tuple-element.44), channel_id=1, source_target_pairs={{1,2},{2,1},{5,6},{6,5},{9,10},{10,9},{13,14},{14,13},{17,18},{18,... | collective-permute-start | bytes 393224 | tf_op jit(solution)/shard_map/ppermute | solution.py:469
  12.3 7.4 %collective-permute-start.3 = (bf16[4,64,256]{2,1,0:T(8,128)(2,1)S(1)}, bf16[4,64,256]{2,1,0:T(8,128)(2,1)S(1)}, u32[]{:S(2)}, u32[]{:S(2)}) collective-permute-start(bf16[4,64,256]{2,1,0:T(8,128)(2,1)S(1)} %get-tuple-element.45), channel_id=1, source_target_pairs={{0,1},{1,0},{2,3},{3,2},{4,5},{5,4},{6,7},{7,6},{8,9},{9,8},{10,11... | collective-permute-start | bytes 393224 | tf_op jit(solution)/shard_map/ppermute | solution.py:469
  20.0 1.9 %collective-permute-start.4 = (bf16[64,256]{1,0:T(8,128)(2,1)S(1)}, bf16[64,256]{1,0:T(8,128)(2,1)S(1)}, u32[]{:S(2)}, u32[]{:S(2)}) collective-permute-start(bf16[64,256]{1,0:T(8,128)(2,1)S(1)} %get-tuple-element.48), channel_id=1, source_target_pairs={{0,4},{4,0},{8,12},{12,8},{1,5},{5,1},{9,13},{13,9},{2,6},{6,2},{1... | collective-permute-start | bytes 98312 | tf_op jit(solution)/shard_map/ppermute | solution.py:434
  20.0 4.3 %collective-permute-start.5 = (bf16[64,256]{1,0:T(8,128)(2,1)S(1)}, bf16[64,256]{1,0:T(8,128)(2,1)S(1)}, u32[]{:S(2)}, u32[]{:S(2)}) collective-permute-start(bf16[64,256]{1,0:T(8,128)(2,1)S(1)} %get-tuple-element.49), channel_id=1, source_target_pairs={{0,8},{4,12},{8,0},{12,4},{1,9},{5,13},{9,1},{13,5},{2,10},{6,14},... | collective-permute-start | bytes 98312 | tf_op jit(solution)/shard_map/ppermute | solution.py:434
  20.6 3.7 %collective-permute-start.6 = (bf16[64,256]{1,0:T(8,128)(2,1)S(1)}, bf16[64,256]{1,0:T(8,128)(2,1)S(1)}, u32[]{:S(2)}, u32[]{:S(2)}) collective-permute-start(bf16[64,256]{1,0:T(8,128)(2,1)S(1)} %get-tuple-element.50), channel_id=1, source_target_pairs={{0,12},{4,8},{8,4},{12,0},{1,13},{5,9},{9,5},{13,1},{2,14},{6,10},... | collective-permute-start | bytes 98312 | tf_op jit(solution)/shard_map/ppermute | solution.py:434
  24.3 11.2 %collective-permute-start.9 = (bf16[768,256]{1,0:T(8,128)(2,1)S(1)}, bf16[768,256]{1,0:T(8,128)(2,1)S(1)}, u32[]{:S(2)}, u32[]{:S(2)}) collective-permute-start(bf16[768,256]{1,0:T(8,128)(2,1)S(1)} %get-tuple-element.55), channel_id=1, source_target_pairs={{0,12},{4,8},{8,4},{12,0},{1,13},{5,9},{9,5},{13,1},{2,14},{6,10},... | collective-permute-start | bytes 1179656 | tf_op jit(solution)/shard_map/ppermute | solution.py:434
  25.3 10.8 %collective-permute-start.8 = (bf16[768,256]{1,0:T(8,128)(2,1)S(1)}, bf16[768,256]{1,0:T(8,128)(2,1)S(1)}, u32[]{:S(2)}, u32[]{:S(2)}) collective-permute-start(bf16[768,256]{1,0:T(8,128)(2,1)S(1)} %get-tuple-element.54), channel_id=1, source_target_pairs={{0,4},{4,0},{8,12},{12,8},{1,5},{5,1},{9,13},{13,9},{2,6},{6,2},{1... | collective-permute-start | bytes 1179656 | tf_op jit(solution)/shard_map/ppermute | solution.py:434
  25.7 11.0 %collective-permute-start.12 = (bf16[4,64,256]{2,1,0:T(8,128)(2,1)S(1)}, bf16[4,64,256]{2,1,0:T(8,128)(2,1)S(1)}, u32[]{:S(2)}, u32[]{:S(2)}) collective-permute-start(bf16[4,64,256]{2,1,0:T(8,128)(2,1)S(1)} %get-tuple-element.56.refs_4_), channel_id=1, source_target_pairs={{0,1},{1,0},{2,3},{3,2},{4,5},{5,4},{6,7},{7,6},{8,9},{9,8},{10,11... | collective-permute-start | bytes 393224 | tf_op jit(solution)/shard_map/ppermute | solution.py:434
  27.7 12.6 %collective-permute-start.11 = (bf16[4,64,256]{2,1,0:T(8,128)(2,1)S(1)}, bf16[4,64,256]{2,1,0:T(8,128)(2,1)S(1)}, u32[]{:S(2)}, u32[]{:S(2)}) collective-permute-start(bf16[4,64,256]{2,1,0:T(8,128)(2,1)S(1)} %get-tuple-element.56.refs_4_), channel_id=1, source_target_pairs={{0,3},{1,2},{2,1},{3,0},{4,7},{5,6},{6,5},{7,4},{8,11},{9,10},{10,... | collective-permute-start | bytes 393224 | tf_op jit(solution)/shard_map/ppermute | solution.py:434
  29.0 12.1 %collective-permute-start.10 = (bf16[4,64,256]{2,1,0:T(8,128)(2,1)S(1)}, bf16[4,64,256]{2,1,0:T(8,128)(2,1)S(1)}, u32[]{:S(2)}, u32[]{:S(2)}) collective-permute-start(bf16[4,64,256]{2,1,0:T(8,128)(2,1)S(1)} %get-tuple-element.56.refs_4_), channel_id=1, source_target_pairs={{0,2},{1,3},{2,0},{3,1},{4,6},{5,7},{6,4},{7,5},{8,10},{9,11},{10,... | collective-permute-start | bytes 393224 | tf_op jit(solution)/shard_map/ppermute | solution.py:434

commit v3 on v2

--- a/solution.py
+++ b/solution.py
@@ -350,6 +350,11 @@
     lane = lax.broadcasted_iota(jnp.int32, (w_dev, lanes), 1)
     real = (lane // (bins // 4)) % 2 == 0
 
+    depth = 2 * windows
+    group = lanes // depth
+    lane = lax.broadcasted_iota(jnp.int32, (bins, lanes), 1)
+    row = lax.broadcasted_iota(jnp.int32, (bins, lanes), 0)
+    in_place = lane // depth == row % group
     for k in range(len(shares)):
         for j in range(n_win):
             part, place = divmod(j, n_win // n_parts)
@@ -368,15 +373,23 @@
             own = values[j * w_dev:(j + 1) * w_dev]
             stacked += [jnp.where(real, own, 0.0), jnp.where(real, 0.0, own)]
         stacked = jnp.concatenate(stacked, axis=0).astype(jnp.bfloat16)
+        stacked = jnp.concatenate([stacked] * group, axis=0)
         turned = product(both, stacked, (((1,), (1,)), ((), ())))
-        left_ref[pl.ds(s, bins, stride=count), :2 * windows] = turned
-
-    for f in range(bins):
-        right = jnp.concatenate([t_ref[f] for t_ref in t_refs], axis=0)
-        left = left_ref[pl.ds(f * count, count), :2 * windows].astype(jnp.bfloat16)
-        result = product(left, right)
-        for c in range(2):
-            prod_ref[c, pl.ds(f, count, stride=bins), :] = result[:, c * pad:(c + 1) * pad]
+        turned = jnp.where(in_place, turned, 0.0)
+        for h in range(lanes // pad):
+            half = turned[:, h * pad:(h + 1) * pad]
+            left_ref[h, pl.ds(s, bins, stride=count), :] = half
+
+    for first in range(0, bins, group):
+        members = range(first, first + group)
+        right = jnp.concatenate([t_ref[f] for f in members for t_ref in t_refs], axis=0)
+        rows = pl.ds(first * count, group * count)
+        left = jnp.concatenate([left_ref[h, rows, :] for h in range(lanes // pad)], axis=1)
+        result = product(left.astype(jnp.bfloat16), right)
+        for k, f in enumerate(members):
+            for c in range(2):
+                block = result[k * count:(k + 1) * count, c * pad:(c + 1) * pad]
+                prod_ref[c, pl.ds(f, count, stride=bins), :] = block
 
     scale = 1.0 / math.sqrt(windows)
     plan_copy.wait()
@@ -414,7 +427,7 @@
         input_output_aliases=aliases,
         scratch_shapes=[
             pltpu.VMEM((2 * bins // 128, windows * count, 128), jnp.float32),
-            pltpu.VMEM((bins * count, 128), jnp.float32),
+            pltpu.VMEM((2 * bins // 128, bins * count, 128), jnp.float32),
             pltpu.VMEM((2, count * bins, 128), jnp.float32),
             pltpu.VMEM((count, 2 * r_dev, bins), jnp.float32),
             pltpu.SMEM(plan.shape, jnp.int32),

time: 45.1 us -> 45.9 us (1.018)
  Pallas kernels: 18.2 us -> 19.7 us
  waiting for transfers between devices: 10.7 us -> 9.94 us
    pallas_call x2, Pallas kernels: 7.33 us -> 8.9 us  [stacks_call(): pl.pallas_call(functools.partial(stacks_kernel, shares, n_parts, n_win, w...]
    ppermute x9, waiting for transfers between devices: 8.47 us -> 7.69 us  [swap(): return lax.ppermute(value, axis, [(i, i ^ by) for i in range(size)])]
  transfers between devices with their start and end apart: 11 -> 11, of which waited for: 4 -> 3; matrix products, arithmetic and copies ran while one was open for 0% -> 0% of each run, Pallas kernels for 13% -> 14%
where the time goes in v3:
time: 45.9 us; the launch traced here: 45.8 us
  Pallas kernels  19.7 us (43%)
  starting transfers between devices  14.9 us (32%)
  waiting for transfers between devices  9.94 us (22%)
  between operations  0.94 us (2%)
    ppermute x9, starting transfers between devices, swap(): return lax.ppermute(value, axis, [(i, i ^ by) for i in range(size)])  9.81 us
    pallas_call x2, Pallas kernels, stacks_call(): pl.pallas_call(functools.partial(stacks_kernel, shares, n_parts, n_win, w...  8.9 us
    pallas_call x1, Pallas kernels, spectra_call(): pl.pallas_call(functools.partial(spectra_kernel, n_win, n_rcv, r_dev), in...  8.63 us
    ppermute x9, waiting for transfers between devices, swap(): return lax.ppermute(value, axis, [(i, i ^ by) for i in range(size)])  7.69 us
    ppermute x2, starting transfers between devices, body(): near[i] = lax.ppermute(picked[i], 'rcv', pairs)  5.11 us
    ppermute x2, waiting for transfers between devices, body(): near[i] = lax.ppermute(picked[i], 'rcv', pairs)  2.25 us
    pallas_call x4, Pallas kernels, turn_call(): pl.pallas_call(functools.partial(turn_kernel, r_dev), in_specs=[vmem] * l...  2.16 us
  transfers between devices with their start and end apart: 11, of which 3 were waited for; matrix products, arithmetic and copies ran while one was open for 0% of the time, Pallas kernels for 14%

profile of v3, /device:TPU:0, one launch (start us, length us, event | category | flops | bytes accessed | tf_op | source)
XLA Modules:
  0.0 45.8 jit_solution(14952193435123589098)
XLA Ops:
  0.0 8.6 %spectra.1 = (bf16[768,256]{1,0:T(8,128)(2,1)S(1)}, bf16[768,256]{1,0:T(8,128)(2,1)S(1)}, bf16[768,256]{1,0:T(8,128)(2,1)S(1)}, bf16[768,256]{1,0:T(8,128)(2,1)S...) custom-call(s32[8]{0:T(128)} %valid_hbm.1, ...), custom_call_target="tpu_custom_call" | custom-call | flops 2415919104 | bytes 6291456 | tf_op jit(solution)/shard_map/spectra/pallas_call | solution.py:207
  8.6 3.0 %collective-permute-start.7 = (bf16[768,256]{1,0:T(8,128)(2,1)S(1)}, bf16[768,256]{1,0:T(8,128)(2,1)S(1)}, u32[]{:S(2)}, u32[]{:S(2)}) collective-permute-start(bf16[768,256]{1,0:T(8,128)(2,1)S(1)} %get-tuple-element.51), channel_id=1, source_target_pairs={{0,8},{4,12},{8,0},{12,4},{1,9},{5,13},{9,1},{13,5},{2,10},{6,14},... | collective-permute-start | bytes 1179656 | tf_op jit(solution)/shard_map/ppermute | solution.py:447
  11.7 0.7 %collective-permute-start.2 = (bf16[4,64,256]{2,1,0:T(8,128)(2,1)S(1)}, bf16[4,64,256]{2,1,0:T(8,128)(2,1)S(1)}, u32[]{:S(2)}, u32[]{:S(2)}) collective-permute-start(bf16[4,64,256]{2,1,0:T(8,128)(2,1)S(1)} %get-tuple-element.44), channel_id=1, source_target_pairs={{1,2},{2,1},{5,6},{6,5},{9,10},{10,9},{13,14},{14,13},{17,18},{18,... | collective-permute-start | bytes 393224 | tf_op jit(solution)/shard_map/ppermute | solution.py:482
  12.3 4.5 %collective-permute-start.3 = (bf16[4,64,256]{2,1,0:T(8,128)(2,1)S(1)}, bf16[4,64,256]{2,1,0:T(8,128)(2,1)S(1)}, u32[]{:S(2)}, u32[]{:S(2)}) collective-permute-start(bf16[4,64,256]{2,1,0:T(8,128)(2,1)S(1)} %get-tuple-element.45), channel_id=1, source_target_pairs={{0,1},{1,0},{2,3},{3,2},{4,5},{5,4},{6,7},{7,6},{8,9},{9,8},{10,11... | collective-permute-start | bytes 393224 | tf_op jit(solution)/shard_map/ppermute | solution.py:482
  17.4 0.0 collective-permute-done.2
  17.5 2.2 %collective-permute-done.3 = bf16[4,64,256]{2,1,0:T(8,128)(2,1)S(1)} collective-permute-done((bf16[4,64,256]{2,1,0:T(8,128)(2,1)S(1)}, bf16[4,64,256]{2,1,0:T(8,128)(2,1)S(1)}, u32[]{:S(2)}, u32[]{:S(2)}) %collective-permute-start.3) | collective-permute-done | bytes 131104 | tf_op jit(solution)/shard_map/ppermute | solution.py:482
  19.7 0.2 conditional.1
  20.0 0.1 collective-permute-start.4
  20.0 0.6 %collective-permute-start.5 = (bf16[64,256]{1,0:T(8,128)(2,1)S(1)}, bf16[64,256]{1,0:T(8,128)(2,1)S(1)}, u32[]{:S(2)}, u32[]{:S(2)}) collective-permute-start(bf16[64,256]{1,0:T(8,128)(2,1)S(1)} %get-tuple-element.49), channel_id=1, source_target_pairs={{0,8},{4,12},{8,0},{12,4},{1,9},{5,13},{9,1},{13,5},{2,10},{6,14},... | collective-permute-start | bytes 98312 | tf_op jit(solution)/shard_map/ppermute | solution.py:447
  20.6 1.3 %collective-permute-start.6 = (bf16[64,256]{1,0:T(8,128)(2,1)S(1)}, bf16[64,256]{1,0:T(8,128)(2,1)S(1)}, u32[]{:S(2)}, u32[]{:S(2)}) collective-permute-start(bf16[64,256]{1,0:T(8,128)(2,1)S(1)} %get-tuple-element.50), channel_id=1, source_target_pairs={{0,12},{4,8},{8,4},{12,0},{1,13},{5,9},{9,5},{13,1},{2,14},{6,10},... | collective-permute-start | bytes 98312 | tf_op jit(solution)/shard_map/ppermute | solution.py:447
  21.9 2.4 %collective-permute-done.5.refs_2_ = bf16[64,256]{1,0:T(8,128)(2,1)S(1)} collective-permute-done((bf16[64,256]{1,0:T(8,128)(2,1)S(1)}, bf16[64,256]{1,0:T(8,128)(2,1)S(1)}, u32[]{:S(2)}, u32[]{:S(2)}) %collective-permute-start.5) | collective-permute-done | bytes 32800 | tf_op jit(solution)/shard_map/ppermute | solution.py:447
  24.3 1.0 %collective-permute-start.9 = (bf16[768,256]{1,0:T(8,128)(2,1)S(1)}, bf16[768,256]{1,0:T(8,128)(2,1)S(1)}, u32[]{:S(2)}, u32[]{:S(2)}) collective-permute-start(bf16[768,256]{1,0:T(8,128)(2,1)S(1)} %get-tuple-element.55), channel_id=1, source_target_pairs={{0,12},{4,8},{8,4},{12,0},{1,13},{5,9},{9,5},{13,1},{2,14},{6,10},... | collective-permute-start | bytes 1179656 | tf_op jit(solution)/shard_map/ppermute | solution.py:447
  25.3 0.3 collective-permute-start.8
  25.7 2.0 %collective-permute-start.12 = (bf16[4,64,256]{2,1,0:T(8,128)(2,1)S(1)}, bf16[4,64,256]{2,1,0:T(8,128)(2,1)S(1)}, u32[]{:S(2)}, u32[]{:S(2)}) collective-permute-start(bf16[4,64,256]{2,1,0:T(8,128)(2,1)S(1)} %get-tuple-element.56.refs_4_), channel_id=1, source_target_pairs={{0,1},{1,0},{2,3},{3,2},{4,5},{5,4},{6,7},{7,6},{8,9},{9,8},{10,11... | collective-permute-start | bytes 393224 | tf_op jit(solution)/shard_map/ppermute | solution.py:447
  27.7 1.3 %collective-permute-start.11 = (bf16[4,64,256]{2,1,0:T(8,128)(2,1)S(1)}, bf16[4,64,256]{2,1,0:T(8,128)(2,1)S(1)}, u32[]{:S(2)}, u32[]{:S(2)}) collective-permute-start(bf16[4,64,256]{2,1,0:T(8,128)(2,1)S(1)} %get-tuple-element.56.refs_4_), channel_id=1, source_target_pairs={{0,3},{1,2},{2,1},{3,0},{4,7},{5,6},{6,5},{7,4},{8,11},{9,10},{10,... | collective-permute-start | bytes 393224 | tf_op jit(solution)/shard_map/ppermute | solution.py:447
  29.0 0.1 collective-permute-start.10
  29.2 0.5 %turn.4.refs_0_ = bf16[128,16,256]{2,1,0:T(8,128)(2,1)S(1)} custom-call(bf16[768,256]{1,0:T(8,128)(2,1)S(1)} %get-tuple-element.41.refs_0_), custom_call_target="tpu_custom_call" | custom-call | flops 134217728 | bytes 2097152 | tf_op jit(solution)/shard_map/turn/pallas_call | solution.py:271
  29.7 0.5 %turn.6.refs_2_ = bf16[128,16,256]{2,1,0:T(8,128)(2,1)S(1)} custom-call(bf16[768,256]{1,0:T(8,128)(2,1)S(1)} %collective-permute-done.7.refs_4_.refs_0_), custom_call_target="tpu_custom_call" | custom-call | flops 134217728 | bytes 2097152 | tf_op jit(solution)/shard_map/turn/pallas_call | solution.py:271
  30.3 5.3 %collective-permute-done.9.refs_0_ = bf16[768,256]{1,0:T(8,128)(2,1)S(1)} collective-permute-done((bf16[768,256]{1,0:T(8,128)(2,1)S(1)}, bf16[768,256]{1,0:T(8,128)(2,1)S(1)}, u32[]{:S(2)}, u32[]{:S(2)}) %collective-permute-start.9) | collective-permute-done | bytes 393248 | tf_op jit(solution)/shard_map/ppermute | solution.py:447
  35.6 0.5 %turn.7.refs_3_ = bf16[128,16,256]{2,1,0:T(8,128)(2,1)S(1)} custom-call(bf16[768,256]{1,0:T(8,128)(2,1)S(1)} %collective-permute-done.9.refs_0_), custom_call_target="tpu_custom_call" | custom-call | flops 134217728 | bytes 2097152 | tf_op jit(solution)/shard_map/turn/pallas_call | solution.py:271
  36.1 0.5 %turn.5.refs_1_ = bf16[128,16,256]{2,1,0:T(8,128)(2,1)S(1)} custom-call(bf16[768,256]{1,0:T(8,128)(2,1)S(1)} %collective-permute-done.8.refs_0_), custom_call_target="tpu_custom_call" | custom-call | flops 134217728 | bytes 2097152 | tf_op jit(solution)/shard_map/turn/pallas_call | solution.py:271
  36.7 4.4 %stacks.2.refs_6_ = f32[32,192,128]{2,1,0:T(8,128)} custom-call(s32[8,128]{1,0:T(8,128)S(1)} %get-tuple-element.40.plan_hbm, bf16[128,16,256]{2,1,0:T(8,128)(2,1)S(1)} %turn.4.refs_0_, bf16[128,16,256]{2,1,0:T(8,128)(2,1)S(1)} %turn.5.refs_1_, bf16[128,16,256]{2,1,0:T(8,128)(2,1)S(1)} %turn.6.refs_2_, bf16[128,16,256]{2,1,0:T(8,128)(2,1)S(1)} %turn.7.refs_3_, ...), custom_call_target="tpu_custom_call" | custom-call | flops 50331648 | bytes 6291456 | tf_op jit(solution)/shard_map/stacks/pallas_call | solution.py:422
  41.1 0.0 collective-permute-done.10.refs_4_
  41.1 4.5 %stacks.3 = f32[32,192,128]{2,1,0:T(8,128)} custom-call(s32[8,128]{1,0:T(8,128)S(1)} %get-tuple-element.40.plan_hbm, bf16[128,16,256]{2,1,0:T(8,128)(2,1)S(1)} %turn.4.refs_0_, bf16[128,16,256]{2,1,0:T(8,128)(2,1)S(1)} %turn.5.refs_1_, bf16[128,16,256]{2,1,0:T(8,128)(2,1)S(1)} %turn.6.refs_2_, ...), custom_call_target="tpu_custom_call", output_to_operand_aliasing={{}: (7, {})} | custom-call | flops 50331648 | bytes 6291456 | tf_op jit(solution)/shard_map/stacks/pallas_call | solution.py:422
  (9 shorter events, 0.1 us)
Async XLA Ops:
  8.6 15.7 %collective-permute-start.7 = (bf16[768,256]{1,0:T(8,128)(2,1)S(1)}, bf16[768,256]{1,0:T(8,128)(2,1)S(1)}, u32[]{:S(2)}, u32[]{:S(2)}) collective-permute-start(bf16[768,256]{1,0:T(8,128)(2,1)S(1)} %get-tuple-element.51), channel_id=1, source_target_pairs={{0,8},{4,12},{8,0},{12,4},{1,9},{5,13},{9,1},{13,5},{2,10},{6,14},... | collective-permute-start | bytes 1179656 | tf_op jit(solution)/shard_map/ppermute | solution.py:447
  11.7 5.8 %collective-permute-start.2 = (bf16[4,64,256]{2,1,0:T(8,128)(2,1)S(1)}, bf16[4,64,256]{2,1,0:T(8,128)(2,1)S(1)}, u32[]{:S(2)}, u32[]{:S(2)}) collective-permute-start(bf16[4,64,256]{2,1,0:T(8,128)(2,1)S(1)} %get-tuple-element.44), channel_id=1, source_target_pairs={{1,2},{2,1},{5,6},{6,5},{9,10},{10,9},{13,14},{14,13},{17,18},{18,... | collective-permute-start | bytes 393224 | tf_op jit(solution)/shard_map/ppermute | solution.py:482
  12.3 7.4 %collective-permute-start.3 = (bf16[4,64,256]{2,1,0:T(8,128)(2,1)S(1)}, bf16[4,64,256]{2,1,0:T(8,128)(2,1)S(1)}, u32[]{:S(2)}, u32[]{:S(2)}) collective-permute-start(bf16[4,64,256]{2,1,0:T(8,128)(2,1)S(1)} %get-tuple-element.45), channel_id=1, source_target_pairs={{0,1},{1,0},{2,3},{3,2},{4,5},{5,4},{6,7},{7,6},{8,9},{9,8},{10,11... | collective-permute-start | bytes 393224 | tf_op jit(solution)/shard_map/ppermute | solution.py:482
  20.0 1.9 %collective-permute-start.4 = (bf16[64,256]{1,0:T(8,128)(2,1)S(1)}, bf16[64,256]{1,0:T(8,128)(2,1)S(1)}, u32[]{:S(2)}, u32[]{:S(2)}) collective-permute-start(bf16[64,256]{1,0:T(8,128)(2,1)S(1)} %get-tuple-element.48), channel_id=1, source_target_pairs={{0,4},{4,0},{8,12},{12,8},{1,5},{5,1},{9,13},{13,9},{2,6},{6,2},{1... | collective-permute-start | bytes 98312 | tf_op jit(solution)/shard_map/ppermute | solution.py:447
  20.0 4.3 %collective-permute-start.5 = (bf16[64,256]{1,0:T(8,128)(2,1)S(1)}, bf16[64,256]{1,0:T(8,128)(2,1)S(1)}, u32[]{:S(2)}, u32[]{:S(2)}) collective-permute-start(bf16[64,256]{1,0:T(8,128)(2,1)S(1)} %get-tuple-element.49), channel_id=1, source_target_pairs={{0,8},{4,12},{8,0},{12,4},{1,9},{5,13},{9,1},{13,5},{2,10},{6,14},... | collective-permute-start | bytes 98312 | tf_op jit(solution)/shard_map/ppermute | solution.py:447
  20.6 3.7 %collective-permute-start.6 = (bf16[64,256]{1,0:T(8,128)(2,1)S(1)}, bf16[64,256]{1,0:T(8,128)(2,1)S(1)}, u32[]{:S(2)}, u32[]{:S(2)}) collective-permute-start(bf16[64,256]{1,0:T(8,128)(2,1)S(1)} %get-tuple-element.50), channel_id=1, source_target_pairs={{0,12},{4,8},{8,4},{12,0},{1,13},{5,9},{9,5},{13,1},{2,14},{6,10},... | collective-permute-start | bytes 98312 | tf_op jit(solution)/shard_map/ppermute | solution.py:447
  24.3 11.2 %collective-permute-start.9 = (bf16[768,256]{1,0:T(8,128)(2,1)S(1)}, bf16[768,256]{1,0:T(8,128)(2,1)S(1)}, u32[]{:S(2)}, u32[]{:S(2)}) collective-permute-start(bf16[768,256]{1,0:T(8,128)(2,1)S(1)} %get-tuple-element.55), channel_id=1, source_target_pairs={{0,12},{4,8},{8,4},{12,0},{1,13},{5,9},{9,5},{13,1},{2,14},{6,10},... | collective-permute-start | bytes 1179656 | tf_op jit(solution)/shard_map/ppermute | solution.py:447
  25.3 10.8 %collective-permute-start.8 = (bf16[768,256]{1,0:T(8,128)(2,1)S(1)}, bf16[768,256]{1,0:T(8,128)(2,1)S(1)}, u32[]{:S(2)}, u32[]{:S(2)}) collective-permute-start(bf16[768,256]{1,0:T(8,128)(2,1)S(1)} %get-tuple-element.54), channel_id=1, source_target_pairs={{0,4},{4,0},{8,12},{12,8},{1,5},{5,1},{9,13},{13,9},{2,6},{6,2},{1... | collective-permute-start | bytes 1179656 | tf_op jit(solution)/shard_map/ppermute | solution.py:447
  25.7 11.0 %collective-permute-start.12 = (bf16[4,64,256]{2,1,0:T(8,128)(2,1)S(1)}, bf16[4,64,256]{2,1,0:T(8,128)(2,1)S(1)}, u32[]{:S(2)}, u32[]{:S(2)}) collective-permute-start(bf16[4,64,256]{2,1,0:T(8,128)(2,1)S(1)} %get-tuple-element.56.refs_4_), channel_id=1, source_target_pairs={{0,1},{1,0},{2,3},{3,2},{4,5},{5,4},{6,7},{7,6},{8,9},{9,8},{10,11... | collective-permute-start | bytes 393224 | tf_op jit(solution)/shard_map/ppermute | solution.py:447
  27.7 13.4 %collective-permute-start.11 = (bf16[4,64,256]{2,1,0:T(8,128)(2,1)S(1)}, bf16[4,64,256]{2,1,0:T(8,128)(2,1)S(1)}, u32[]{:S(2)}, u32[]{:S(2)}) collective-permute-start(bf16[4,64,256]{2,1,0:T(8,128)(2,1)S(1)} %get-tuple-element.56.refs_4_), channel_id=1, source_target_pairs={{0,3},{1,2},{2,1},{3,0},{4,7},{5,6},{6,5},{7,4},{8,11},{9,10},{10,... | collective-permute-start | bytes 393224 | tf_op jit(solution)/shard_map/ppermute | solution.py:447
  29.0 12.1 %collective-permute-start.10 = (bf16[4,64,256]{2,1,0:T(8,128)(2,1)S(1)}, bf16[4,64,256]{2,1,0:T(8,128)(2,1)S(1)}, u32[]{:S(2)}, u32[]{:S(2)}) collective-permute-start(bf16[4,64,256]{2,1,0:T(8,128)(2,1)S(1)} %get-tuple-element.56.refs_4_), channel_id=1, source_target_pairs={{0,2},{1,3},{2,0},{3,1},{4,6},{5,7},{6,4},{7,5},{8,10},{9,11},{10,... | collective-permute-start | bytes 393224 | tf_op jit(solution)/shard_map/ppermute | solution.py:447

commit v4 on v2

--- a/solution.py
+++ b/solution.py
@@ -305,78 +305,94 @@
     )(*picked)
 
 
-def join_kernel(count, *refs):
-    out_ref = refs[-1]
-    for k in range(count):
-        out_ref[k] = refs[k][...]
-
-
-def join_call(blocks, after=(), later=()):
-    rows, lanes = blocks[0].shape
-    count = len(blocks)
-    first = count + len(after)
-    vmem, anywhere = pl.BlockSpec(memory_space=VMEM), pl.BlockSpec(memory_space=pl.ANY)
-    out = pl.pallas_call(
-        functools.partial(join_kernel, count),
-        in_specs=[vmem] * count + [anywhere] * (len(after) + len(later)),
-        out_specs=[anywhere] * len(later) + [vmem],
-        out_shape=[jax.ShapeDtypeStruct(x.shape, x.dtype) for x in later]
-        + [jax.ShapeDtypeStruct((count, rows, lanes), jnp.bfloat16)],
-        input_output_aliases={first + k: k for k in range(len(later))},
-        compiler_params=pltpu.CompilerParams(vmem_limit_bytes=4 * 2**20),
-        cost_estimate=pl.CostEstimate(flops=2**18, bytes_accessed=2**19, transcendentals=0),
-        name="join",
-    )(*blocks, *after, *later)
-    return out[-1], out[:-1]
-
-
-def stacks_kernel(shares, n_parts, n_win, w_dev, r_dev, n_own, bins, plan_hbm, *refs):
-    t_refs = refs[:n_win]
-    s_refs = refs[n_win:n_win + n_parts * len(shares)]
-    out_hbm, srow_ref, left_ref, prod_ref, out_ref, plan_ref, sems, plan_sem = refs[-8:]
-    plan_copy = pltpu.make_async_copy(plan_hbm, plan_ref, plan_sem)
-    plan_copy.start()
-    lanes = 2 * bins
+def lefts_kernel(n_win, w_dev, n_own, *refs):
+    out_ref, srow_ref, rows_ref = refs[-3:]
+    rows, lanes = refs[0].shape
+    bins = lanes // 2
     windows = n_win * w_dev
-    count = len(shares) * n_own
-    pad = 128
-    rcv = lax.axis_index("rcv")
-
-    def product(lhs, rhs, dims=(((1,), (0,)), ((), ()))):
-        return lax.dot_general(lhs, rhs, dims, preferred_element_type=jnp.float32)
-
-    order = bin_order(lanes)
-    both = order[:bins] + order[bins:]
-    lane = lax.broadcasted_iota(jnp.int32, (w_dev, lanes), 1)
-    real = (lane // (bins // 4)) % 2 == 0
-
-    for k in range(len(shares)):
-        for j in range(n_win):
-            part, place = divmod(j, n_win // n_parts)
-            block = s_refs[k * n_parts + part][place].astype(jnp.float32)
-            for h in range(lanes // pad):
-                half = block[:, h * pad:(h + 1) * pad]
-                srow_ref[h, pl.ds((k * n_win + j) * w_dev * n_own, w_dev * n_own), :] = half
-    for s in range(count):
-        first = s // n_own * windows * n_own + s % n_own
+    pad = rows_ref.shape[1]
+    for j in range(n_win):
+        block = refs[j][...].astype(jnp.float32)
+        for h in range(lanes // pad):
+            srow_ref[h, j * rows:(j + 1) * rows, :] = block[:, h * pad:(h + 1) * pad]
+
+    lane = lax.broadcasted_iota(jnp.int32, (bins, lanes), 1)
+    row = lax.broadcasted_iota(jnp.int32, (bins, lanes), 0)
+    quarter = lanes // 8
+    bin_of = 4 * (lane % quarter) + lane // (2 * quarter)
+    pick = bin_of == 2 * (row % (bins // 2)) + row // (bins // 2)
+    pick = pick.astype(jnp.float32).astype(jnp.bfloat16)
+    real = (lane[:w_dev] // quarter) % 2 == 0
+    low = lax.broadcasted_iota(jnp.int32, (bins // 2, pad), 1) < pad // 2
+    for s in range(n_own):
         values = jnp.concatenate(
-            [srow_ref[h, pl.ds(first, windows, stride=n_own), :] for h in range(lanes // pad)],
-            axis=1,
+            [srow_ref[h, pl.ds(s, windows, stride=n_own), :] for h in range(lanes // pad)], axis=1
         )
         stacked = []
         for j in range(n_win):
             own = values[j * w_dev:(j + 1) * w_dev]
             stacked += [jnp.where(real, own, 0.0), jnp.where(real, 0.0, own)]
-        stacked = jnp.concatenate(stacked, axis=0).astype(jnp.bfloat16)
-        turned = product(both, stacked, (((1,), (1,)), ((), ())))
-        left_ref[pl.ds(s, bins, stride=count), :2 * windows] = turned
-
-    for f in range(bins):
-        right = jnp.concatenate([t_ref[f] for t_ref in t_refs], axis=0)
-        left = left_ref[pl.ds(f * count, count), :2 * windows].astype(jnp.bfloat16)
-        result = product(left, right)
-        for c in range(2):
-            prod_ref[c, pl.ds(f, count, stride=bins), :] = result[:, c * pad:(c + 1) * pad]
+        stacked = jnp.concatenate(stacked * 2, axis=0).astype(jnp.bfloat16)
+        turned = lax.dot_general(
+            pick, stacked, (((1,), (1,)), ((), ())), preferred_element_type=jnp.float32
+        )
+        pairs = jnp.where(low, turned[:bins // 2], turned[bins // 2:])
+        rows_ref[pl.ds(s, bins // 2, stride=n_own), :] = pairs
+    out_ref[...] = rows_ref[...].reshape(out_ref.shape).astype(jnp.bfloat16)
+
+
+def lefts_call(blocks, after, later, w_dev):
+    rows, lanes = blocks[0].shape
+    n_win = len(blocks)
+    n_own = rows // w_dev
+    pad = 128
+    first = n_win + len(after)
+    vmem, anywhere = pl.BlockSpec(memory_space=VMEM), pl.BlockSpec(memory_space=pl.ANY)
+    out = pl.pallas_call(
+        functools.partial(lefts_kernel, n_win, w_dev, n_own),
+        in_specs=[vmem] * n_win + [anywhere] * (len(after) + len(later)),
+        out_specs=[anywhere] * len(later) + [vmem],
+        out_shape=[jax.ShapeDtypeStruct(x.shape, x.dtype) for x in later]
+        + [jax.ShapeDtypeStruct((lanes // 8, 2 * n_own, pad), jnp.bfloat16)],
+        input_output_aliases={first + k: k for k in range(len(later))},
+        scratch_shapes=[
+            pltpu.VMEM((lanes // pad, n_win * rows, pad), jnp.float32),
+            pltpu.VMEM((lanes // 4 * n_own, pad), jnp.float32),
+        ],
+        compiler_params=pltpu.CompilerParams(vmem_limit_bytes=6 * 2**20),
+        cost_estimate=pl.CostEstimate(flops=2**26, bytes_accessed=2**19, transcendentals=0),
+        name="lefts",
+    )(*blocks, *after, *later)
+    return out[-1], out[:-1]
+
+
+def stacks_kernel(shares, n_win, w_dev, r_dev, n_own, bins, plan_hbm, *refs):
+    t_refs = refs[:n_win]
+    s_refs = refs[n_win:n_win + len(shares)]
+    out_hbm, prod_ref, out_ref, plan_ref, sems, plan_sem = refs[-6:]
+    plan_copy = pltpu.make_async_copy(plan_hbm, plan_ref, plan_sem)
+    plan_copy.start()
+    windows = n_win * w_dev
+    count = len(shares) * n_own
+    pad = 128
+    rcv = lax.axis_index("rcv")
+
+    low = lax.broadcasted_iota(jnp.int32, (count, pad), 1) < pad // 2
+    for group in range(bins // 4):
+        values = [s_ref[group].astype(jnp.float32) for s_ref in s_refs]
+        for p in range(2):
+            rows = jnp.concatenate([v[p * n_own:(p + 1) * n_own] for v in values], axis=0)
+            left = jnp.concatenate([jnp.where(low, rows, 0.0), jnp.where(low, 0.0, rows)], axis=0)
+            first = 4 * group + 2 * p
+            right = [t_ref[f] for f in (first, first + 1) for t_ref in t_refs]
+            result = jnp.dot(
+                left.astype(jnp.bfloat16), jnp.concatenate(right, axis=0),
+                preferred_element_type=jnp.float32,
+            )
+            for k in range(2):
+                for c in range(2):
+                    block = result[k * count:(k + 1) * count, c * pad:(c + 1) * pad]
+                    prod_ref[c, pl.ds(first + k, count, stride=bins), :] = block
 
     scale = 1.0 / math.sqrt(windows)
     plan_copy.wait()
@@ -394,12 +410,11 @@
 
 def stacks_call(out, plan, turned, sources, shares, n_rcv, w_dev, r_dev, bins):
     n_win = len(turned)
-    n_parts = len(sources[0])
-    n_own = sources[0][0].shape[1] // w_dev
+    n_own = sources[0].shape[1] // 2
     windows = n_win * w_dev
     count = len(shares) * n_own
     whole = pl.BlockSpec(memory_space=VMEM)
-    args = [plan] + list(turned) + [part for i in shares for part in sources[i]]
+    args = [plan] + list(turned) + [sources[i] for i in shares]
     specs = [pl.BlockSpec(memory_space=pl.ANY)] + [whole] * (len(args) - 1)
     aliases = {}
     if out is not None:
@@ -407,14 +422,12 @@
         args.append(out)
         specs.append(pl.BlockSpec(memory_space=pl.ANY))
     return pl.pallas_call(
-        functools.partial(stacks_kernel, shares, n_parts, n_win, w_dev, r_dev, n_own, bins),
+        functools.partial(stacks_kernel, shares, n_win, w_dev, r_dev, n_own, bins),
         in_specs=specs,
         out_specs=pl.BlockSpec(memory_space=pltpu.HBM),
         out_shape=jax.ShapeDtypeStruct((n_rcv * n_own, 2 * r_dev, bins), jnp.float32),
         input_output_aliases=aliases,
         scratch_shapes=[
-            pltpu.VMEM((2 * bins // 128, windows * count, 128), jnp.float32),
-            pltpu.VMEM((bins * count, 128), jnp.float32),
             pltpu.VMEM((2, count * bins, 128), jnp.float32),
             pltpu.VMEM((count, 2 * r_dev, bins), jnp.float32),
             pltpu.SMEM(plan.shape, jnp.int32),
@@ -474,9 +487,9 @@
     merged = [merged[0]] + [swap(merged[j], "win", j) for j in range(1, n_win)]
     late = [j for j in range(1, n_win) if j != early]
     received = {0: blocks[0], early: swap(blocks[early], "win", early)}
-    joined, later = join_call(merged, [received[early]], [blocks[j] for j in late])
+    lefts, later = lefts_call(merged, [received[early]], [blocks[j] for j in late], w_dev)
     received.update({j: swap(block, "win", j) for j, block in zip(late, later)})
-    sources = [[joined]] + [[swap(joined, "rcv", i)] for i in range(1, n_rcv)]
+    sources = [lefts] + [swap(lefts, "rcv", i) for i in range(1, n_rcv)]
 
     turned = [turn_call([received[j]], w_dev, r_dev) for j in range(n_win)]
     half = n_rcv // 2

time: 45.1 us -> 45.3 us (level)
  no operation moved by 1% of the time
where the time goes in v4:
time: 45.3 us; the launch traced here: 45.2 us
  Pallas kernels  18.3 us (40%)
  starting transfers between devices  14.9 us (33%)
  waiting for transfers between devices  10.8 us (24%)
  between operations  0.94 us (2%)
    ppermute x9, starting transfers between devices, swap(): return lax.ppermute(value, axis, [(i, i ^ by) for i in range(size)])  9.79 us
    pallas_call x1, Pallas kernels, spectra_call(): pl.pallas_call(functools.partial(spectra_kernel, n_win, n_rcv, r_dev), in...  8.63 us
    ppermute x9, waiting for transfers between devices, swap(): return lax.ppermute(value, axis, [(i, i ^ by) for i in range(size)])  8.57 us
    pallas_call x2, Pallas kernels, stacks_call(): pl.pallas_call(functools.partial(stacks_kernel, shares, n_win, w_dev, r_d...  7.13 us
    ppermute x2, starting transfers between devices, body(): near[i] = lax.ppermute(picked[i], 'rcv', pairs)  5.11 us
    ppermute x2, waiting for transfers between devices, body(): near[i] = lax.ppermute(picked[i], 'rcv', pairs)  2.25 us
    pallas_call x4, Pallas kernels, turn_call(): pl.pallas_call(functools.partial(turn_kernel, r_dev), in_specs=[vmem] * l...  2.16 us
  transfers between devices with their start and end apart: 11, of which 4 were waited for; matrix products, arithmetic and copies ran while one was open for 0% of the time, Pallas kernels for 13%

profile of v4, /device:TPU:0, one launch (start us, length us, event | category | flops | bytes accessed | tf_op | source)
XLA Modules:
  0.0 45.2 jit_solution(1441708957227575295)
XLA Ops:
  0.0 8.6 %spectra.1 = (bf16[768,256]{1,0:T(8,128)(2,1)S(1)}, bf16[768,256]{1,0:T(8,128)(2,1)S(1)}, bf16[768,256]{1,0:T(8,128)(2,1)S(1)}, bf16[768,256]{1,0:T(8,128)(2,1)S...) custom-call(s32[8]{0:T(128)} %valid_hbm.1, ...), custom_call_target="tpu_custom_call" | custom-call | flops 2415919104 | bytes 6291456 | tf_op jit(solution)/shard_map/spectra/pallas_call | solution.py:207
  8.6 3.0 %collective-permute-start.7 = (bf16[768,256]{1,0:T(8,128)(2,1)S(1)}, bf16[768,256]{1,0:T(8,128)(2,1)S(1)}, u32[]{:S(2)}, u32[]{:S(2)}) collective-permute-start(bf16[768,256]{1,0:T(8,128)(2,1)S(1)} %get-tuple-element.51), channel_id=1, source_target_pairs={{0,8},{4,12},{8,0},{12,4},{1,9},{5,13},{9,1},{13,5},{2,10},{6,14},... | collective-permute-start | bytes 1179656 | tf_op jit(solution)/shard_map/ppermute | solution.py:447
  11.7 0.7 %collective-permute-start.2 = (bf16[4,64,256]{2,1,0:T(8,128)(2,1)S(1)}, bf16[4,64,256]{2,1,0:T(8,128)(2,1)S(1)}, u32[]{:S(2)}, u32[]{:S(2)}) collective-permute-start(bf16[4,64,256]{2,1,0:T(8,128)(2,1)S(1)} %get-tuple-element.44), channel_id=1, source_target_pairs={{1,2},{2,1},{5,6},{6,5},{9,10},{10,9},{13,14},{14,13},{17,18},{18,... | collective-permute-start | bytes 393224 | tf_op jit(solution)/shard_map/ppermute | solution.py:482
  12.3 4.5 %collective-permute-start.3 = (bf16[4,64,256]{2,1,0:T(8,128)(2,1)S(1)}, bf16[4,64,256]{2,1,0:T(8,128)(2,1)S(1)}, u32[]{:S(2)}, u32[]{:S(2)}) collective-permute-start(bf16[4,64,256]{2,1,0:T(8,128)(2,1)S(1)} %get-tuple-element.45), channel_id=1, source_target_pairs={{0,1},{1,0},{2,3},{3,2},{4,5},{5,4},{6,7},{7,6},{8,9},{9,8},{10,11... | collective-permute-start | bytes 393224 | tf_op jit(solution)/shard_map/ppermute | solution.py:482
  17.5 2.2 %collective-permute-done.3 = bf16[4,64,256]{2,1,0:T(8,128)(2,1)S(1)} collective-permute-done((bf16[4,64,256]{2,1,0:T(8,128)(2,1)S(1)}, bf16[4,64,256]{2,1,0:T(8,128)(2,1)S(1)}, u32[]{:S(2)}, u32[]{:S(2)}) %collective-permute-start.3) | collective-permute-done | bytes 131104 | tf_op jit(solution)/shard_map/ppermute | solution.py:482
  19.7 0.2 conditional.1
  20.0 0.1 collective-permute-start.4
  20.0 0.6 %collective-permute-start.5 = (bf16[64,256]{1,0:T(8,128)(2,1)S(1)}, bf16[64,256]{1,0:T(8,128)(2,1)S(1)}, u32[]{:S(2)}, u32[]{:S(2)}) collective-permute-start(bf16[64,256]{1,0:T(8,128)(2,1)S(1)} %get-tuple-element.49), channel_id=1, source_target_pairs={{0,8},{4,12},{8,0},{12,4},{1,9},{5,13},{9,1},{13,5},{2,10},{6,14},... | collective-permute-start | bytes 98312 | tf_op jit(solution)/shard_map/ppermute | solution.py:447
  20.6 1.3 %collective-permute-start.6 = (bf16[64,256]{1,0:T(8,128)(2,1)S(1)}, bf16[64,256]{1,0:T(8,128)(2,1)S(1)}, u32[]{:S(2)}, u32[]{:S(2)}) collective-permute-start(bf16[64,256]{1,0:T(8,128)(2,1)S(1)} %get-tuple-element.50), channel_id=1, source_target_pairs={{0,12},{4,8},{8,4},{12,0},{1,13},{5,9},{9,5},{13,1},{2,14},{6,10},... | collective-permute-start | bytes 98312 | tf_op jit(solution)/shard_map/ppermute | solution.py:447
  21.9 2.4 %collective-permute-done.5.refs_2_ = bf16[64,256]{1,0:T(8,128)(2,1)S(1)} collective-permute-done((bf16[64,256]{1,0:T(8,128)(2,1)S(1)}, bf16[64,256]{1,0:T(8,128)(2,1)S(1)}, u32[]{:S(2)}, u32[]{:S(2)}) %collective-permute-start.5) | collective-permute-done | bytes 32800 | tf_op jit(solution)/shard_map/ppermute | solution.py:447
  24.3 0.3 lefts.1
  24.7 1.0 %collective-permute-start.9 = (bf16[768,256]{1,0:T(8,128)(2,1)S(1)}, bf16[768,256]{1,0:T(8,128)(2,1)S(1)}, u32[]{:S(2)}, u32[]{:S(2)}) collective-permute-start(bf16[768,256]{1,0:T(8,128)(2,1)S(1)} %get-tuple-element.55), channel_id=1, source_target_pairs={{0,12},{4,8},{8,4},{12,0},{1,13},{5,9},{9,5},{13,1},{2,14},{6,10},... | collective-permute-start | bytes 1179656 | tf_op jit(solution)/shard_map/ppermute | solution.py:447
  25.7 0.3 collective-permute-start.8
  26.0 2.0 %collective-permute-start.12 = (bf16[32,16,128]{2,1,0:T(8,128)(2,1)S(1)}, bf16[32,16,128]{2,1,0:T(8,128)(2,1)S(1)}, u32[]{:S(2)}, u32[]{:S(2)}) collective-permute-start(bf16[32,16,128]{2,1,0:T(8,128)(2,1)S(1)} %get-tuple-element.56.refs_4_), channel_id=1, source_target_pairs={{0,1},{1,0},{2,3},{3,2},{4,5},{5,4},{6,7},{7,6},{8,9},{9,8},{10,11... | collective-permute-start | bytes 393224 | tf_op jit(solution)/shard_map/ppermute | solution.py:447
  28.0 1.3 %collective-permute-start.11 = (bf16[32,16,128]{2,1,0:T(8,128)(2,1)S(1)}, bf16[32,16,128]{2,1,0:T(8,128)(2,1)S(1)}, u32[]{:S(2)}, u32[]{:S(2)}) collective-permute-start(bf16[32,16,128]{2,1,0:T(8,128)(2,1)S(1)} %get-tuple-element.56.refs_4_), channel_id=1, source_target_pairs={{0,3},{1,2},{2,1},{3,0},{4,7},{5,6},{6,5},{7,4},{8,11},{9,10},{10,... | collective-permute-start | bytes 393224 | tf_op jit(solution)/shard_map/ppermute | solution.py:447
  29.4 0.1 collective-permute-start.10
  29.5 0.5 %turn.4.refs_0_ = bf16[128,16,256]{2,1,0:T(8,128)(2,1)S(1)} custom-call(bf16[768,256]{1,0:T(8,128)(2,1)S(1)} %get-tuple-element.41.refs_0_), custom_call_target="tpu_custom_call" | custom-call | flops 134217728 | bytes 2097152 | tf_op jit(solution)/shard_map/turn/pallas_call | solution.py:271
  30.0 0.5 %turn.6.refs_2_ = bf16[128,16,256]{2,1,0:T(8,128)(2,1)S(1)} custom-call(bf16[768,256]{1,0:T(8,128)(2,1)S(1)} %collective-permute-done.7.refs_4_.refs_0_), custom_call_target="tpu_custom_call" | custom-call | flops 134217728 | bytes 2097152 | tf_op jit(solution)/shard_map/turn/pallas_call | solution.py:271
  30.6 5.2 %collective-permute-done.9.refs_0_ = bf16[768,256]{1,0:T(8,128)(2,1)S(1)} collective-permute-done((bf16[768,256]{1,0:T(8,128)(2,1)S(1)}, bf16[768,256]{1,0:T(8,128)(2,1)S(1)}, u32[]{:S(2)}, u32[]{:S(2)}) %collective-permute-start.9) | collective-permute-done | bytes 393248 | tf_op jit(solution)/shard_map/ppermute | solution.py:447
  35.8 0.5 %turn.7.refs_3_ = bf16[128,16,256]{2,1,0:T(8,128)(2,1)S(1)} custom-call(bf16[768,256]{1,0:T(8,128)(2,1)S(1)} %collective-permute-done.9.refs_0_), custom_call_target="tpu_custom_call" | custom-call | flops 134217728 | bytes 2097152 | tf_op jit(solution)/shard_map/turn/pallas_call | solution.py:271
  36.4 0.5 %turn.5.refs_1_ = bf16[128,16,256]{2,1,0:T(8,128)(2,1)S(1)} custom-call(bf16[768,256]{1,0:T(8,128)(2,1)S(1)} %collective-permute-done.8.refs_0_), custom_call_target="tpu_custom_call" | custom-call | flops 134217728 | bytes 2097152 | tf_op jit(solution)/shard_map/turn/pallas_call | solution.py:271
  36.9 3.6 %stacks.2.refs_6_ = f32[32,192,128]{2,1,0:T(8,128)} custom-call(s32[8,128]{1,0:T(8,128)S(1)} %get-tuple-element.40.plan_hbm, bf16[128,16,256]{2,1,0:T(8,128)(2,1)S(1)} %turn.4.refs_0_, bf16[128,16,256]{2,1,0:T(8,128)(2,1)S(1)} %turn.5.refs_1_, bf16[128,16,256]{2,1,0:T(8,128)(2,1)S(1)} %turn.6.refs_2_, bf16[128,16,256]{2,1,0:T(8,128)(2,1)S(1)} %turn.7.refs_3_, ...), custom_call_target="tpu_custom_call" | custom-call | flops 50331648 | bytes 6291456 | tf_op jit(solution)/shard_map/stacks/pallas_call | solution.py:424
  40.5 0.9 %collective-permute-done.10.refs_4_ = bf16[32,16,128]{2,1,0:T(8,128)(2,1)S(1)} collective-permute-done((bf16[32,16,128]{2,1,0:T(8,128)(2,1)S(1)}, bf16[32,16,128]{2,1,0:T(8,128)(2,1)S(1)}, u32[]{:S(2)}, u32[]{:S(2)}) %collective-permute-start.10) | collective-permute-done | bytes 131104 | tf_op jit(solution)/shard_map/ppermute | solution.py:447
  41.5 3.6 %stacks.3 = f32[32,192,128]{2,1,0:T(8,128)} custom-call(s32[8,128]{1,0:T(8,128)S(1)} %get-tuple-element.40.plan_hbm, bf16[128,16,256]{2,1,0:T(8,128)(2,1)S(1)} %turn.4.refs_0_, bf16[128,16,256]{2,1,0:T(8,128)(2,1)S(1)} %turn.5.refs_1_, bf16[128,16,256]{2,1,0:T(8,128)(2,1)S(1)} %turn.6.refs_2_, ...), custom_call_target="tpu_custom_call", output_to_operand_aliasing={{}: (7, {})} | custom-call | flops 50331648 | bytes 6291456 | tf_op jit(solution)/shard_map/stacks/pallas_call | solution.py:424
  (9 shorter events, 0.1 us)
Async XLA Ops:
  8.6 15.7 %collective-permute-start.7 = (bf16[768,256]{1,0:T(8,128)(2,1)S(1)}, bf16[768,256]{1,0:T(8,128)(2,1)S(1)}, u32[]{:S(2)}, u32[]{:S(2)}) collective-permute-start(bf16[768,256]{1,0:T(8,128)(2,1)S(1)} %get-tuple-element.51), channel_id=1, source_target_pairs={{0,8},{4,12},{8,0},{12,4},{1,9},{5,13},{9,1},{13,5},{2,10},{6,14},... | collective-permute-start | bytes 1179656 | tf_op jit(solution)/shard_map/ppermute | solution.py:447
  11.7 5.8 %collective-permute-start.2 = (bf16[4,64,256]{2,1,0:T(8,128)(2,1)S(1)}, bf16[4,64,256]{2,1,0:T(8,128)(2,1)S(1)}, u32[]{:S(2)}, u32[]{:S(2)}) collective-permute-start(bf16[4,64,256]{2,1,0:T(8,128)(2,1)S(1)} %get-tuple-element.44), channel_id=1, source_target_pairs={{1,2},{2,1},{5,6},{6,5},{9,10},{10,9},{13,14},{14,13},{17,18},{18,... | collective-permute-start | bytes 393224 | tf_op jit(solution)/shard_map/ppermute | solution.py:482
  12.3 7.4 %collective-permute-start.3 = (bf16[4,64,256]{2,1,0:T(8,128)(2,1)S(1)}, bf16[4,64,256]{2,1,0:T(8,128)(2,1)S(1)}, u32[]{:S(2)}, u32[]{:S(2)}) collective-permute-start(bf16[4,64,256]{2,1,0:T(8,128)(2,1)S(1)} %get-tuple-element.45), channel_id=1, source_target_pairs={{0,1},{1,0},{2,3},{3,2},{4,5},{5,4},{6,7},{7,6},{8,9},{9,8},{10,11... | collective-permute-start | bytes 393224 | tf_op jit(solution)/shard_map/ppermute | solution.py:482
  20.0 1.9 %collective-permute-start.4 = (bf16[64,256]{1,0:T(8,128)(2,1)S(1)}, bf16[64,256]{1,0:T(8,128)(2,1)S(1)}, u32[]{:S(2)}, u32[]{:S(2)}) collective-permute-start(bf16[64,256]{1,0:T(8,128)(2,1)S(1)} %get-tuple-element.48), channel_id=1, source_target_pairs={{0,4},{4,0},{8,12},{12,8},{1,5},{5,1},{9,13},{13,9},{2,6},{6,2},{1... | collective-permute-start | bytes 98312 | tf_op jit(solution)/shard_map/ppermute | solution.py:447
  20.0 4.3 %collective-permute-start.5 = (bf16[64,256]{1,0:T(8,128)(2,1)S(1)}, bf16[64,256]{1,0:T(8,128)(2,1)S(1)}, u32[]{:S(2)}, u32[]{:S(2)}) collective-permute-start(bf16[64,256]{1,0:T(8,128)(2,1)S(1)} %get-tuple-element.49), channel_id=1, source_target_pairs={{0,8},{4,12},{8,0},{12,4},{1,9},{5,13},{9,1},{13,5},{2,10},{6,14},... | collective-permute-start | bytes 98312 | tf_op jit(solution)/shard_map/ppermute | solution.py:447
  20.6 3.7 %collective-permute-start.6 = (bf16[64,256]{1,0:T(8,128)(2,1)S(1)}, bf16[64,256]{1,0:T(8,128)(2,1)S(1)}, u32[]{:S(2)}, u32[]{:S(2)}) collective-permute-start(bf16[64,256]{1,0:T(8,128)(2,1)S(1)} %get-tuple-element.50), channel_id=1, source_target_pairs={{0,12},{4,8},{8,4},{12,0},{1,13},{5,9},{9,5},{13,1},{2,14},{6,10},... | collective-permute-start | bytes 98312 | tf_op jit(solution)/shard_map/ppermute | solution.py:447
  24.7 11.1 %collective-permute-start.9 = (bf16[768,256]{1,0:T(8,128)(2,1)S(1)}, bf16[768,256]{1,0:T(8,128)(2,1)S(1)}, u32[]{:S(2)}, u32[]{:S(2)}) collective-permute-start(bf16[768,256]{1,0:T(8,128)(2,1)S(1)} %get-tuple-element.55), channel_id=1, source_target_pairs={{0,12},{4,8},{8,4},{12,0},{1,13},{5,9},{9,5},{13,1},{2,14},{6,10},... | collective-permute-start | bytes 1179656 | tf_op jit(solution)/shard_map/ppermute | solution.py:447
  25.7 10.7 %collective-permute-start.8 = (bf16[768,256]{1,0:T(8,128)(2,1)S(1)}, bf16[768,256]{1,0:T(8,128)(2,1)S(1)}, u32[]{:S(2)}, u32[]{:S(2)}) collective-permute-start(bf16[768,256]{1,0:T(8,128)(2,1)S(1)} %get-tuple-element.54), channel_id=1, source_target_pairs={{0,4},{4,0},{8,12},{12,8},{1,5},{5,1},{9,13},{13,9},{2,6},{6,2},{1... | collective-permute-start | bytes 1179656 | tf_op jit(solution)/shard_map/ppermute | solution.py:447
  26.0 10.9 %collective-permute-start.12 = (bf16[32,16,128]{2,1,0:T(8,128)(2,1)S(1)}, bf16[32,16,128]{2,1,0:T(8,128)(2,1)S(1)}, u32[]{:S(2)}, u32[]{:S(2)}) collective-permute-start(bf16[32,16,128]{2,1,0:T(8,128)(2,1)S(1)} %get-tuple-element.56.refs_4_), channel_id=1, source_target_pairs={{0,1},{1,0},{2,3},{3,2},{4,5},{5,4},{6,7},{7,6},{8,9},{9,8},{10,11... | collective-permute-start | bytes 393224 | tf_op jit(solution)/shard_map/ppermute | solution.py:447
  28.0 12.5 %collective-permute-start.11 = (bf16[32,16,128]{2,1,0:T(8,128)(2,1)S(1)}, bf16[32,16,128]{2,1,0:T(8,128)(2,1)S(1)}, u32[]{:S(2)}, u32[]{:S(2)}) collective-permute-start(bf16[32,16,128]{2,1,0:T(8,128)(2,1)S(1)} %get-tuple-element.56.refs_4_), channel_id=1, source_target_pairs={{0,3},{1,2},{2,1},{3,0},{4,7},{5,6},{6,5},{7,4},{8,11},{9,10},{10,... | collective-permute-start | bytes 393224 | tf_op jit(solution)/shard_map/ppermute | solution.py:447
  29.4 12.1 %collective-permute-start.10 = (bf16[32,16,128]{2,1,0:T(8,128)(2,1)S(1)}, bf16[32,16,128]{2,1,0:T(8,128)(2,1)S(1)}, u32[]{:S(2)}, u32[]{:S(2)}) collective-permute-start(bf16[32,16,128]{2,1,0:T(8,128)(2,1)S(1)} %get-tuple-element.56.refs_4_), channel_id=1, source_target_pairs={{0,2},{1,3},{2,0},{3,1},{4,6},{5,7},{6,4},{7,5},{8,10},{9,11},{10,... | collective-permute-start | bytes 393224 | tf_op jit(solution)/shard_map/ppermute | solution.py:447

commit v5 on v4

--- a/solution.py
+++ b/solution.py
@@ -252,12 +252,13 @@
     pad = out_ref.shape[2] // 2
     order = bin_order(lanes)
     windows = [(x, w) for x in x_refs for w in range(x.shape[0] // r_dev)]
+    none = jnp.zeros((pad - r_dev, lanes), jnp.bfloat16)
     for k, (x_ref, w) in enumerate(windows):
+        block = jnp.concatenate([x_ref[w * r_dev:(w + 1) * r_dev], none], axis=0)
         turned = lax.dot_general(
-            order, x_ref[w * r_dev:(w + 1) * r_dev], (((1,), (1,)), ((), ())),
-            preferred_element_type=jnp.float32,
+            order, block, (((1,), (1,)), ((), ())), preferred_element_type=jnp.float32
         )
-        rows_ref[pl.ds(k, lanes, stride=w_dev), :r_dev] = turned
+        rows_ref[pl.ds(k, lanes, stride=w_dev), :] = turned
     rr = rows_ref[:bins * w_dev].reshape(bins, w_dev, pad)
     ri = rows_ref[bins * w_dev:].reshape(bins, w_dev, pad)
     out_ref[:, :, :pad] = jnp.concatenate([rr, ri], axis=1).astype(jnp.bfloat16)
@@ -397,10 +398,20 @@
     scale = 1.0 / math.sqrt(windows)
     plan_copy.wait()
     copies = []
+    column = lax.broadcasted_iota(jnp.int32, (r_dev, 2 * pad), 1)
+    row = lax.broadcasted_iota(jnp.int32, (r_dev, 2 * pad), 0)
+    twice = (column % pad == row).astype(jnp.float32).astype(jnp.bfloat16)
     for s in range(count):
+        both = jnp.concatenate([prod_ref[c, s * bins:(s + 1) * bins, :] for c in range(2)], axis=0)
+        high = both.astype(jnp.bfloat16)
+        rest = (both - high.astype(jnp.float32)).astype(jnp.bfloat16)
+        turned = lax.dot_general(
+            twice, jnp.concatenate([high, rest], axis=1), (((1,), (1,)), ((), ())),
+            preferred_element_type=jnp.float32,
+        )
         for c in range(2):
-            turned = prod_ref[c, s * bins:(s + 1) * bins, :].T
-            out_ref[s, pl.ds(c, r_dev, stride=2), :] = turned[:r_dev] * scale
+            half = turned[:, c * bins:(c + 1) * bins] * scale
+            out_ref[s, pl.ds(c, r_dev, stride=2), :] = half
         row = plan_ref[0, (rcv ^ shares[s // n_own]) * n_own + s % n_own]
         copies.append(pltpu.make_async_copy(out_ref.at[s], out_hbm.at[row], sems.at[s]))
         copies[-1].start()

time: 45.3 us -> 45.5 us (level)
  no operation moved by 1% of the time
where the time goes in v5:
time: 45.5 us; the launch traced here: 45.4 us
  Pallas kernels  18.7 us (41%)
  starting transfers between devices  14.9 us (33%)
  waiting for transfers between devices  10.6 us (23%)
  between operations  0.94 us (2%)
    ppermute x9, starting transfers between devices, swap(): return lax.ppermute(value, axis, [(i, i ^ by) for i in range(size)])  9.79 us
    pallas_call x1, Pallas kernels, spectra_call(): pl.pallas_call(functools.partial(spectra_kernel, n_win, n_rcv, r_dev), in...  8.63 us
    ppermute x9, waiting for transfers between devices, swap(): return lax.ppermute(value, axis, [(i, i ^ by) for i in range(size)])  8.36 us
    pallas_call x2, Pallas kernels, stacks_call(): pl.pallas_call(functools.partial(stacks_kernel, shares, n_win, w_dev, r_d...  7.55 us
    ppermute x2, starting transfers between devices, body(): near[i] = lax.ppermute(picked[i], 'rcv', pairs)  5.11 us
    ppermute x2, waiting for transfers between devices, body(): near[i] = lax.ppermute(picked[i], 'rcv', pairs)  2.25 us
    pallas_call x4, Pallas kernels, turn_call(): pl.pallas_call(functools.partial(turn_kernel, r_dev), in_specs=[vmem] * l...  2.16 us
  transfers between devices with their start and end apart: 11, of which 4 were waited for; matrix products, arithmetic and copies ran while one was open for 0% of the time, Pallas kernels for 13%

profile of v5, /device:TPU:0, one launch (start us, length us, event | category | flops | bytes accessed | tf_op | source)
XLA Modules:
  0.0 45.4 jit_solution(1480794125260198146)
XLA Ops:
  0.0 8.6 %spectra.1 = (bf16[768,256]{1,0:T(8,128)(2,1)S(1)}, bf16[768,256]{1,0:T(8,128)(2,1)S(1)}, bf16[768,256]{1,0:T(8,128)(2,1)S(1)}, bf16[768,256]{1,0:T(8,128)(2,1)S...) custom-call(s32[8]{0:T(128)} %valid_hbm.1, ...), custom_call_target="tpu_custom_call" | custom-call | flops 2415919104 | bytes 6291456 | tf_op jit(solution)/shard_map/spectra/pallas_call | solution.py:207
  8.6 3.0 %collective-permute-start.7 = (bf16[768,256]{1,0:T(8,128)(2,1)S(1)}, bf16[768,256]{1,0:T(8,128)(2,1)S(1)}, u32[]{:S(2)}, u32[]{:S(2)}) collective-permute-start(bf16[768,256]{1,0:T(8,128)(2,1)S(1)} %get-tuple-element.51), channel_id=1, source_target_pairs={{0,8},{4,12},{8,0},{12,4},{1,9},{5,13},{9,1},{13,5},{2,10},{6,14},... | collective-permute-start | bytes 1179656 | tf_op jit(solution)/shard_map/ppermute | solution.py:458
  11.7 0.7 %collective-permute-start.2 = (bf16[4,64,256]{2,1,0:T(8,128)(2,1)S(1)}, bf16[4,64,256]{2,1,0:T(8,128)(2,1)S(1)}, u32[]{:S(2)}, u32[]{:S(2)}) collective-permute-start(bf16[4,64,256]{2,1,0:T(8,128)(2,1)S(1)} %get-tuple-element.44), channel_id=1, source_target_pairs={{1,2},{2,1},{5,6},{6,5},{9,10},{10,9},{13,14},{14,13},{17,18},{18,... | collective-permute-start | bytes 393224 | tf_op jit(solution)/shard_map/ppermute | solution.py:493
  12.3 4.5 %collective-permute-start.3 = (bf16[4,64,256]{2,1,0:T(8,128)(2,1)S(1)}, bf16[4,64,256]{2,1,0:T(8,128)(2,1)S(1)}, u32[]{:S(2)}, u32[]{:S(2)}) collective-permute-start(bf16[4,64,256]{2,1,0:T(8,128)(2,1)S(1)} %get-tuple-element.45), channel_id=1, source_target_pairs={{0,1},{1,0},{2,3},{3,2},{4,5},{5,4},{6,7},{7,6},{8,9},{9,8},{10,11... | collective-permute-start | bytes 393224 | tf_op jit(solution)/shard_map/ppermute | solution.py:493
  17.5 2.2 %collective-permute-done.3 = bf16[4,64,256]{2,1,0:T(8,128)(2,1)S(1)} collective-permute-done((bf16[4,64,256]{2,1,0:T(8,128)(2,1)S(1)}, bf16[4,64,256]{2,1,0:T(8,128)(2,1)S(1)}, u32[]{:S(2)}, u32[]{:S(2)}) %collective-permute-start.3) | collective-permute-done | bytes 131104 | tf_op jit(solution)/shard_map/ppermute | solution.py:493
  19.7 0.2 conditional.1
  20.0 0.1 collective-permute-start.4
  20.0 0.6 %collective-permute-start.5 = (bf16[64,256]{1,0:T(8,128)(2,1)S(1)}, bf16[64,256]{1,0:T(8,128)(2,1)S(1)}, u32[]{:S(2)}, u32[]{:S(2)}) collective-permute-start(bf16[64,256]{1,0:T(8,128)(2,1)S(1)} %get-tuple-element.49), channel_id=1, source_target_pairs={{0,8},{4,12},{8,0},{12,4},{1,9},{5,13},{9,1},{13,5},{2,10},{6,14},... | collective-permute-start | bytes 98312 | tf_op jit(solution)/shard_map/ppermute | solution.py:458
  20.6 1.3 %collective-permute-start.6 = (bf16[64,256]{1,0:T(8,128)(2,1)S(1)}, bf16[64,256]{1,0:T(8,128)(2,1)S(1)}, u32[]{:S(2)}, u32[]{:S(2)}) collective-permute-start(bf16[64,256]{1,0:T(8,128)(2,1)S(1)} %get-tuple-element.50), channel_id=1, source_target_pairs={{0,12},{4,8},{8,4},{12,0},{1,13},{5,9},{9,5},{13,1},{2,14},{6,10},... | collective-permute-start | bytes 98312 | tf_op jit(solution)/shard_map/ppermute | solution.py:458
  21.9 2.4 %collective-permute-done.5.refs_2_ = bf16[64,256]{1,0:T(8,128)(2,1)S(1)} collective-permute-done((bf16[64,256]{1,0:T(8,128)(2,1)S(1)}, bf16[64,256]{1,0:T(8,128)(2,1)S(1)}, u32[]{:S(2)}, u32[]{:S(2)}) %collective-permute-start.5) | collective-permute-done | bytes 32800 | tf_op jit(solution)/shard_map/ppermute | solution.py:458
  24.3 0.3 lefts.1
  24.7 1.0 %collective-permute-start.9 = (bf16[768,256]{1,0:T(8,128)(2,1)S(1)}, bf16[768,256]{1,0:T(8,128)(2,1)S(1)}, u32[]{:S(2)}, u32[]{:S(2)}) collective-permute-start(bf16[768,256]{1,0:T(8,128)(2,1)S(1)} %get-tuple-element.55), channel_id=1, source_target_pairs={{0,12},{4,8},{8,4},{12,0},{1,13},{5,9},{9,5},{13,1},{2,14},{6,10},... | collective-permute-start | bytes 1179656 | tf_op jit(solution)/shard_map/ppermute | solution.py:458
  25.7 0.3 collective-permute-start.8
  26.0 2.0 %collective-permute-start.12 = (bf16[32,16,128]{2,1,0:T(8,128)(2,1)S(1)}, bf16[32,16,128]{2,1,0:T(8,128)(2,1)S(1)}, u32[]{:S(2)}, u32[]{:S(2)}) collective-permute-start(bf16[32,16,128]{2,1,0:T(8,128)(2,1)S(1)} %get-tuple-element.56.refs_4_), channel_id=1, source_target_pairs={{0,1},{1,0},{2,3},{3,2},{4,5},{5,4},{6,7},{7,6},{8,9},{9,8},{10,11... | collective-permute-start | bytes 393224 | tf_op jit(solution)/shard_map/ppermute | solution.py:458
  28.0 1.3 %collective-permute-start.11 = (bf16[32,16,128]{2,1,0:T(8,128)(2,1)S(1)}, bf16[32,16,128]{2,1,0:T(8,128)(2,1)S(1)}, u32[]{:S(2)}, u32[]{:S(2)}) collective-permute-start(bf16[32,16,128]{2,1,0:T(8,128)(2,1)S(1)} %get-tuple-element.56.refs_4_), channel_id=1, source_target_pairs={{0,3},{1,2},{2,1},{3,0},{4,7},{5,6},{6,5},{7,4},{8,11},{9,10},{10,... | collective-permute-start | bytes 393224 | tf_op jit(solution)/shard_map/ppermute | solution.py:458
  29.4 0.1 collective-permute-start.10
  29.5 0.5 %turn.4.refs_0_ = bf16[128,16,256]{2,1,0:T(8,128)(2,1)S(1)} custom-call(bf16[768,256]{1,0:T(8,128)(2,1)S(1)} %get-tuple-element.41.refs_0_), custom_call_target="tpu_custom_call" | custom-call | flops 134217728 | bytes 2097152 | tf_op jit(solution)/shard_map/turn/pallas_call | solution.py:272
  30.0 0.5 %turn.6.refs_2_ = bf16[128,16,256]{2,1,0:T(8,128)(2,1)S(1)} custom-call(bf16[768,256]{1,0:T(8,128)(2,1)S(1)} %collective-permute-done.7.refs_4_.refs_0_), custom_call_target="tpu_custom_call" | custom-call | flops 134217728 | bytes 2097152 | tf_op jit(solution)/shard_map/turn/pallas_call | solution.py:272
  30.6 5.2 %collective-permute-done.9.refs_0_ = bf16[768,256]{1,0:T(8,128)(2,1)S(1)} collective-permute-done((bf16[768,256]{1,0:T(8,128)(2,1)S(1)}, bf16[768,256]{1,0:T(8,128)(2,1)S(1)}, u32[]{:S(2)}, u32[]{:S(2)}) %collective-permute-start.9) | collective-permute-done | bytes 393248 | tf_op jit(solution)/shard_map/ppermute | solution.py:458
  35.8 0.5 %turn.7.refs_3_ = bf16[128,16,256]{2,1,0:T(8,128)(2,1)S(1)} custom-call(bf16[768,256]{1,0:T(8,128)(2,1)S(1)} %collective-permute-done.9.refs_0_), custom_call_target="tpu_custom_call" | custom-call | flops 134217728 | bytes 2097152 | tf_op jit(solution)/shard_map/turn/pallas_call | solution.py:272
  36.4 0.5 %turn.5.refs_1_ = bf16[128,16,256]{2,1,0:T(8,128)(2,1)S(1)} custom-call(bf16[768,256]{1,0:T(8,128)(2,1)S(1)} %collective-permute-done.8.refs_0_), custom_call_target="tpu_custom_call" | custom-call | flops 134217728 | bytes 2097152 | tf_op jit(solution)/shard_map/turn/pallas_call | solution.py:272
  36.9 3.8 %stacks.2.refs_6_ = f32[32,192,128]{2,1,0:T(8,128)} custom-call(s32[8,128]{1,0:T(8,128)S(1)} %get-tuple-element.40.plan_hbm, bf16[128,16,256]{2,1,0:T(8,128)(2,1)S(1)} %turn.4.refs_0_, bf16[128,16,256]{2,1,0:T(8,128)(2,1)S(1)} %turn.5.refs_1_, bf16[128,16,256]{2,1,0:T(8,128)(2,1)S(1)} %turn.6.refs_2_, bf16[128,16,256]{2,1,0:T(8,128)(2,1)S(1)} %turn.7.refs_3_, ...), custom_call_target="tpu_custom_call" | custom-call | flops 50331648 | bytes 6291456 | tf_op jit(solution)/shard_map/stacks/pallas_call | solution.py:435
  40.7 0.7 %collective-permute-done.10.refs_4_ = bf16[32,16,128]{2,1,0:T(8,128)(2,1)S(1)} collective-permute-done((bf16[32,16,128]{2,1,0:T(8,128)(2,1)S(1)}, bf16[32,16,128]{2,1,0:T(8,128)(2,1)S(1)}, u32[]{:S(2)}, u32[]{:S(2)}) %collective-permute-start.10) | collective-permute-done | bytes 131104 | tf_op jit(solution)/shard_map/ppermute | solution.py:458
  41.5 3.8 %stacks.3 = f32[32,192,128]{2,1,0:T(8,128)} custom-call(s32[8,128]{1,0:T(8,128)S(1)} %get-tuple-element.40.plan_hbm, bf16[128,16,256]{2,1,0:T(8,128)(2,1)S(1)} %turn.4.refs_0_, bf16[128,16,256]{2,1,0:T(8,128)(2,1)S(1)} %turn.5.refs_1_, bf16[128,16,256]{2,1,0:T(8,128)(2,1)S(1)} %turn.6.refs_2_, ...), custom_call_target="tpu_custom_call", output_to_operand_aliasing={{}: (7, {})} | custom-call | flops 50331648 | bytes 6291456 | tf_op jit(solution)/shard_map/stacks/pallas_call | solution.py:435
  (9 shorter events, 0.1 us)
Async XLA Ops:
  8.6 15.7 %collective-permute-start.7 = (bf16[768,256]{1,0:T(8,128)(2,1)S(1)}, bf16[768,256]{1,0:T(8,128)(2,1)S(1)}, u32[]{:S(2)}, u32[]{:S(2)}) collective-permute-start(bf16[768,256]{1,0:T(8,128)(2,1)S(1)} %get-tuple-element.51), channel_id=1, source_target_pairs={{0,8},{4,12},{8,0},{12,4},{1,9},{5,13},{9,1},{13,5},{2,10},{6,14},... | collective-permute-start | bytes 1179656 | tf_op jit(solution)/shard_map/ppermute | solution.py:458
  11.7 5.8 %collective-permute-start.2 = (bf16[4,64,256]{2,1,0:T(8,128)(2,1)S(1)}, bf16[4,64,256]{2,1,0:T(8,128)(2,1)S(1)}, u32[]{:S(2)}, u32[]{:S(2)}) collective-permute-start(bf16[4,64,256]{2,1,0:T(8,128)(2,1)S(1)} %get-tuple-element.44), channel_id=1, source_target_pairs={{1,2},{2,1},{5,6},{6,5},{9,10},{10,9},{13,14},{14,13},{17,18},{18,... | collective-permute-start | bytes 393224 | tf_op jit(solution)/shard_map/ppermute | solution.py:493
  12.3 7.4 %collective-permute-start.3 = (bf16[4,64,256]{2,1,0:T(8,128)(2,1)S(1)}, bf16[4,64,256]{2,1,0:T(8,128)(2,1)S(1)}, u32[]{:S(2)}, u32[]{:S(2)}) collective-permute-start(bf16[4,64,256]{2,1,0:T(8,128)(2,1)S(1)} %get-tuple-element.45), channel_id=1, source_target_pairs={{0,1},{1,0},{2,3},{3,2},{4,5},{5,4},{6,7},{7,6},{8,9},{9,8},{10,11... | collective-permute-start | bytes 393224 | tf_op jit(solution)/shard_map/ppermute | solution.py:493
  20.0 1.9 %collective-permute-start.4 = (bf16[64,256]{1,0:T(8,128)(2,1)S(1)}, bf16[64,256]{1,0:T(8,128)(2,1)S(1)}, u32[]{:S(2)}, u32[]{:S(2)}) collective-permute-start(bf16[64,256]{1,0:T(8,128)(2,1)S(1)} %get-tuple-element.48), channel_id=1, source_target_pairs={{0,4},{4,0},{8,12},{12,8},{1,5},{5,1},{9,13},{13,9},{2,6},{6,2},{1... | collective-permute-start | bytes 98312 | tf_op jit(solution)/shard_map/ppermute | solution.py:458
  20.0 4.3 %collective-permute-start.5 = (bf16[64,256]{1,0:T(8,128)(2,1)S(1)}, bf16[64,256]{1,0:T(8,128)(2,1)S(1)}, u32[]{:S(2)}, u32[]{:S(2)}) collective-permute-start(bf16[64,256]{1,0:T(8,128)(2,1)S(1)} %get-tuple-element.49), channel_id=1, source_target_pairs={{0,8},{4,12},{8,0},{12,4},{1,9},{5,13},{9,1},{13,5},{2,10},{6,14},... | collective-permute-start | bytes 98312 | tf_op jit(solution)/shard_map/ppermute | solution.py:458
  20.6 3.7 %collective-permute-start.6 = (bf16[64,256]{1,0:T(8,128)(2,1)S(1)}, bf16[64,256]{1,0:T(8,128)(2,1)S(1)}, u32[]{:S(2)}, u32[]{:S(2)}) collective-permute-start(bf16[64,256]{1,0:T(8,128)(2,1)S(1)} %get-tuple-element.50), channel_id=1, source_target_pairs={{0,12},{4,8},{8,4},{12,0},{1,13},{5,9},{9,5},{13,1},{2,14},{6,10},... | collective-permute-start | bytes 98312 | tf_op jit(solution)/shard_map/ppermute | solution.py:458
  24.7 11.1 %collective-permute-start.9 = (bf16[768,256]{1,0:T(8,128)(2,1)S(1)}, bf16[768,256]{1,0:T(8,128)(2,1)S(1)}, u32[]{:S(2)}, u32[]{:S(2)}) collective-permute-start(bf16[768,256]{1,0:T(8,128)(2,1)S(1)} %get-tuple-element.55), channel_id=1, source_target_pairs={{0,12},{4,8},{8,4},{12,0},{1,13},{5,9},{9,5},{13,1},{2,14},{6,10},... | collective-permute-start | bytes 1179656 | tf_op jit(solution)/shard_map/ppermute | solution.py:458
  25.7 10.7 %collective-permute-start.8 = (bf16[768,256]{1,0:T(8,128)(2,1)S(1)}, bf16[768,256]{1,0:T(8,128)(2,1)S(1)}, u32[]{:S(2)}, u32[]{:S(2)}) collective-permute-start(bf16[768,256]{1,0:T(8,128)(2,1)S(1)} %get-tuple-element.54), channel_id=1, source_target_pairs={{0,4},{4,0},{8,12},{12,8},{1,5},{5,1},{9,13},{13,9},{2,6},{6,2},{1... | collective-permute-start | bytes 1179656 | tf_op jit(solution)/shard_map/ppermute | solution.py:458
  26.0 10.9 %collective-permute-start.12 = (bf16[32,16,128]{2,1,0:T(8,128)(2,1)S(1)}, bf16[32,16,128]{2,1,0:T(8,128)(2,1)S(1)}, u32[]{:S(2)}, u32[]{:S(2)}) collective-permute-start(bf16[32,16,128]{2,1,0:T(8,128)(2,1)S(1)} %get-tuple-element.56.refs_4_), channel_id=1, source_target_pairs={{0,1},{1,0},{2,3},{3,2},{4,5},{5,4},{6,7},{7,6},{8,9},{9,8},{10,11... | collective-permute-start | bytes 393224 | tf_op jit(solution)/shard_map/ppermute | solution.py:458
  28.0 12.7 %collective-permute-start.11 = (bf16[32,16,128]{2,1,0:T(8,128)(2,1)S(1)}, bf16[32,16,128]{2,1,0:T(8,128)(2,1)S(1)}, u32[]{:S(2)}, u32[]{:S(2)}) collective-permute-start(bf16[32,16,128]{2,1,0:T(8,128)(2,1)S(1)} %get-tuple-element.56.refs_4_), channel_id=1, source_target_pairs={{0,3},{1,2},{2,1},{3,0},{4,7},{5,6},{6,5},{7,4},{8,11},{9,10},{10,... | collective-permute-start | bytes 393224 | tf_op jit(solution)/shard_map/ppermute | solution.py:458
  29.4 12.1 %collective-permute-start.10 = (bf16[32,16,128]{2,1,0:T(8,128)(2,1)S(1)}, bf16[32,16,128]{2,1,0:T(8,128)(2,1)S(1)}, u32[]{:S(2)}, u32[]{:S(2)}) collective-permute-start(bf16[32,16,128]{2,1,0:T(8,128)(2,1)S(1)} %get-tuple-element.56.refs_4_), channel_id=1, source_target_pairs={{0,2},{1,3},{2,0},{3,1},{4,6},{5,7},{6,4},{7,5},{8,10},{9,11},{10,... | collective-permute-start | bytes 393224 | tf_op jit(solution)/shard_map/ppermute | solution.py:458

commit v6 on v4

--- a/solution.py
+++ b/solution.py
@@ -374,6 +374,7 @@
     plan_copy.start()
     windows = n_win * w_dev
     count = len(shares) * n_own
+    pitch = prod_ref.shape[1] // bins
     pad = 128
     rcv = lax.axis_index("rcv")
 
@@ -392,14 +393,14 @@
             for k in range(2):
                 for c in range(2):
                     block = result[k * count:(k + 1) * count, c * pad:(c + 1) * pad]
-                    prod_ref[c, pl.ds(first + k, count, stride=bins), :] = block
+                    prod_ref[c, pl.ds((first + k) * pitch, count), :] = block
 
     scale = 1.0 / math.sqrt(windows)
     plan_copy.wait()
     copies = []
     for s in range(count):
         for c in range(2):
-            turned = prod_ref[c, s * bins:(s + 1) * bins, :].T
+            turned = prod_ref[c, pl.ds(s, bins, stride=pitch), :].T
             out_ref[s, pl.ds(c, r_dev, stride=2), :] = turned[:r_dev] * scale
         row = plan_ref[0, (rcv ^ shares[s // n_own]) * n_own + s % n_own]
         copies.append(pltpu.make_async_copy(out_ref.at[s], out_hbm.at[row], sems.at[s]))
@@ -428,7 +429,7 @@
         out_shape=jax.ShapeDtypeStruct((n_rcv * n_own, 2 * r_dev, bins), jnp.float32),
         input_output_aliases=aliases,
         scratch_shapes=[
-            pltpu.VMEM((2, count * bins, 128), jnp.float32),
+            pltpu.VMEM((2, (count + 8) * bins, 128), jnp.float32),
             pltpu.VMEM((count, 2 * r_dev, bins), jnp.float32),
             pltpu.SMEM(plan.shape, jnp.int32),
             pltpu.SemaphoreType.DMA((count,)),

time: 45.3 us -> 44.3 us (0.978)
  Pallas kernels: 18.3 us -> 16.2 us
  waiting for transfers between devices: 10.8 us -> 11.8 us
    pallas_call x2, Pallas kernels: 7.13 us -> 5.07 us  [stacks_call(): pl.pallas_call(functools.partial(stacks_kernel, shares, n_win, w_dev, r_d...]
    ppermute x9, waiting for transfers between devices: 8.57 us -> 9.6 us  [swap(): return lax.ppermute(value, axis, [(i, i ^ by) for i in range(size)])]
  transfers between devices with their start and end apart: 11 -> 11, of which waited for: 4 -> 4; matrix products, arithmetic and copies ran while one was open for 0% -> 0% of each run, Pallas kernels for 13% -> 11%
where the time goes in v6:
time: 44.3 us; the launch traced here: 44.1 us
  Pallas kernels  16.2 us (37%)
  starting transfers between devices  14.9 us (34%)
  waiting for transfers between devices  11.8 us (27%)
  between operations  0.94 us (2%)
    ppermute x9, starting transfers between devices, swap(): return lax.ppermute(value, axis, [(i, i ^ by) for i in range(size)])  9.79 us
    ppermute x9, waiting for transfers between devices, swap(): return lax.ppermute(value, axis, [(i, i ^ by) for i in range(size)])  9.6 us
    pallas_call x1, Pallas kernels, spectra_call(): pl.pallas_call(functools.partial(spectra_kernel, n_win, n_rcv, r_dev), in...  8.63 us
    ppermute x2, starting transfers between devices, body(): near[i] = lax.ppermute(picked[i], 'rcv', pairs)  5.11 us
    pallas_call x2, Pallas kernels, stacks_call(): pl.pallas_call(functools.partial(stacks_kernel, shares, n_win, w_dev, r_d...  5.07 us
    ppermute x2, waiting for transfers between devices, body(): near[i] = lax.ppermute(picked[i], 'rcv', pairs)  2.25 us
    pallas_call x4, Pallas kernels, turn_call(): pl.pallas_call(functools.partial(turn_kernel, r_dev), in_specs=[vmem] * l...  2.16 us
  transfers between devices with their start and end apart: 11, of which 4 were waited for; matrix products, arithmetic and copies ran while one was open for 0% of the time, Pallas kernels for 11%

profile of v6, /device:TPU:0, one launch (start us, length us, event | category | flops | bytes accessed | tf_op | source)
XLA Modules:
  0.0 44.1 jit_solution(9449826210740149169)
XLA Ops:
  0.0 8.6 %spectra.1 = (bf16[768,256]{1,0:T(8,128)(2,1)S(1)}, bf16[768,256]{1,0:T(8,128)(2,1)S(1)}, bf16[768,256]{1,0:T(8,128)(2,1)S(1)}, bf16[768,256]{1,0:T(8,128)(2,1)S...) custom-call(s32[8]{0:T(128)} %valid_hbm.1, ...), custom_call_target="tpu_custom_call" | custom-call | flops 2415919104 | bytes 6291456 | tf_op jit(solution)/shard_map/spectra/pallas_call | solution.py:207
  8.6 3.0 %collective-permute-start.7 = (bf16[768,256]{1,0:T(8,128)(2,1)S(1)}, bf16[768,256]{1,0:T(8,128)(2,1)S(1)}, u32[]{:S(2)}, u32[]{:S(2)}) collective-permute-start(bf16[768,256]{1,0:T(8,128)(2,1)S(1)} %get-tuple-element.51), channel_id=1, source_target_pairs={{0,8},{4,12},{8,0},{12,4},{1,9},{5,13},{9,1},{13,5},{2,10},{6,14},... | collective-permute-start | bytes 1179656 | tf_op jit(solution)/shard_map/ppermute | solution.py:448
  11.7 0.7 %collective-permute-start.2 = (bf16[4,64,256]{2,1,0:T(8,128)(2,1)S(1)}, bf16[4,64,256]{2,1,0:T(8,128)(2,1)S(1)}, u32[]{:S(2)}, u32[]{:S(2)}) collective-permute-start(bf16[4,64,256]{2,1,0:T(8,128)(2,1)S(1)} %get-tuple-element.44), channel_id=1, source_target_pairs={{1,2},{2,1},{5,6},{6,5},{9,10},{10,9},{13,14},{14,13},{17,18},{18,... | collective-permute-start | bytes 393224 | tf_op jit(solution)/shard_map/ppermute | solution.py:483
  12.3 4.5 %collective-permute-start.3 = (bf16[4,64,256]{2,1,0:T(8,128)(2,1)S(1)}, bf16[4,64,256]{2,1,0:T(8,128)(2,1)S(1)}, u32[]{:S(2)}, u32[]{:S(2)}) collective-permute-start(bf16[4,64,256]{2,1,0:T(8,128)(2,1)S(1)} %get-tuple-element.45), channel_id=1, source_target_pairs={{0,1},{1,0},{2,3},{3,2},{4,5},{5,4},{6,7},{7,6},{8,9},{9,8},{10,11... | collective-permute-start | bytes 393224 | tf_op jit(solution)/shard_map/ppermute | solution.py:483
  17.5 2.2 %collective-permute-done.3 = bf16[4,64,256]{2,1,0:T(8,128)(2,1)S(1)} collective-permute-done((bf16[4,64,256]{2,1,0:T(8,128)(2,1)S(1)}, bf16[4,64,256]{2,1,0:T(8,128)(2,1)S(1)}, u32[]{:S(2)}, u32[]{:S(2)}) %collective-permute-start.3) | collective-permute-done | bytes 131104 | tf_op jit(solution)/shard_map/ppermute | solution.py:483
  19.7 0.2 conditional.1
  20.0 0.1 collective-permute-start.4
  20.0 0.6 %collective-permute-start.5 = (bf16[64,256]{1,0:T(8,128)(2,1)S(1)}, bf16[64,256]{1,0:T(8,128)(2,1)S(1)}, u32[]{:S(2)}, u32[]{:S(2)}) collective-permute-start(bf16[64,256]{1,0:T(8,128)(2,1)S(1)} %get-tuple-element.49), channel_id=1, source_target_pairs={{0,8},{4,12},{8,0},{12,4},{1,9},{5,13},{9,1},{13,5},{2,10},{6,14},... | collective-permute-start | bytes 98312 | tf_op jit(solution)/shard_map/ppermute | solution.py:448
  20.6 1.3 %collective-permute-start.6 = (bf16[64,256]{1,0:T(8,128)(2,1)S(1)}, bf16[64,256]{1,0:T(8,128)(2,1)S(1)}, u32[]{:S(2)}, u32[]{:S(2)}) collective-permute-start(bf16[64,256]{1,0:T(8,128)(2,1)S(1)} %get-tuple-element.50), channel_id=1, source_target_pairs={{0,12},{4,8},{8,4},{12,0},{1,13},{5,9},{9,5},{13,1},{2,14},{6,10},... | collective-permute-start | bytes 98312 | tf_op jit(solution)/shard_map/ppermute | solution.py:448
  21.9 2.4 %collective-permute-done.5.refs_2_ = bf16[64,256]{1,0:T(8,128)(2,1)S(1)} collective-permute-done((bf16[64,256]{1,0:T(8,128)(2,1)S(1)}, bf16[64,256]{1,0:T(8,128)(2,1)S(1)}, u32[]{:S(2)}, u32[]{:S(2)}) %collective-permute-start.5) | collective-permute-done | bytes 32800 | tf_op jit(solution)/shard_map/ppermute | solution.py:448
  24.3 0.3 lefts.1
  24.7 1.0 %collective-permute-start.9 = (bf16[768,256]{1,0:T(8,128)(2,1)S(1)}, bf16[768,256]{1,0:T(8,128)(2,1)S(1)}, u32[]{:S(2)}, u32[]{:S(2)}) collective-permute-start(bf16[768,256]{1,0:T(8,128)(2,1)S(1)} %get-tuple-element.55), channel_id=1, source_target_pairs={{0,12},{4,8},{8,4},{12,0},{1,13},{5,9},{9,5},{13,1},{2,14},{6,10},... | collective-permute-start | bytes 1179656 | tf_op jit(solution)/shard_map/ppermute | solution.py:448
  25.7 0.3 collective-permute-start.8
  26.0 2.0 %collective-permute-start.12 = (bf16[32,16,128]{2,1,0:T(8,128)(2,1)S(1)}, bf16[32,16,128]{2,1,0:T(8,128)(2,1)S(1)}, u32[]{:S(2)}, u32[]{:S(2)}) collective-permute-start(bf16[32,16,128]{2,1,0:T(8,128)(2,1)S(1)} %get-tuple-element.56.refs_4_), channel_id=1, source_target_pairs={{0,1},{1,0},{2,3},{3,2},{4,5},{5,4},{6,7},{7,6},{8,9},{9,8},{10,11... | collective-permute-start | bytes 393224 | tf_op jit(solution)/shard_map/ppermute | solution.py:448
  28.0 1.3 %collective-permute-start.11 = (bf16[32,16,128]{2,1,0:T(8,128)(2,1)S(1)}, bf16[32,16,128]{2,1,0:T(8,128)(2,1)S(1)}, u32[]{:S(2)}, u32[]{:S(2)}) collective-permute-start(bf16[32,16,128]{2,1,0:T(8,128)(2,1)S(1)} %get-tuple-element.56.refs_4_), channel_id=1, source_target_pairs={{0,3},{1,2},{2,1},{3,0},{4,7},{5,6},{6,5},{7,4},{8,11},{9,10},{10,... | collective-permute-start | bytes 393224 | tf_op jit(solution)/shard_map/ppermute | solution.py:448
  29.4 0.1 collective-permute-start.10
  29.5 0.5 %turn.4.refs_0_ = bf16[128,16,256]{2,1,0:T(8,128)(2,1)S(1)} custom-call(bf16[768,256]{1,0:T(8,128)(2,1)S(1)} %get-tuple-element.41.refs_0_), custom_call_target="tpu_custom_call" | custom-call | flops 134217728 | bytes 2097152 | tf_op jit(solution)/shard_map/turn/pallas_call | solution.py:271
  30.0 0.5 %turn.6.refs_2_ = bf16[128,16,256]{2,1,0:T(8,128)(2,1)S(1)} custom-call(bf16[768,256]{1,0:T(8,128)(2,1)S(1)} %collective-permute-done.7.refs_4_.refs_0_), custom_call_target="tpu_custom_call" | custom-call | flops 134217728 | bytes 2097152 | tf_op jit(solution)/shard_map/turn/pallas_call | solution.py:271
  30.6 5.2 %collective-permute-done.9.refs_0_ = bf16[768,256]{1,0:T(8,128)(2,1)S(1)} collective-permute-done((bf16[768,256]{1,0:T(8,128)(2,1)S(1)}, bf16[768,256]{1,0:T(8,128)(2,1)S(1)}, u32[]{:S(2)}, u32[]{:S(2)}) %collective-permute-start.9) | collective-permute-done | bytes 393248 | tf_op jit(solution)/shard_map/ppermute | solution.py:448
  35.8 0.5 %turn.7.refs_3_ = bf16[128,16,256]{2,1,0:T(8,128)(2,1)S(1)} custom-call(bf16[768,256]{1,0:T(8,128)(2,1)S(1)} %collective-permute-done.9.refs_0_), custom_call_target="tpu_custom_call" | custom-call | flops 134217728 | bytes 2097152 | tf_op jit(solution)/shard_map/turn/pallas_call | solution.py:271
  36.4 0.5 %turn.5.refs_1_ = bf16[128,16,256]{2,1,0:T(8,128)(2,1)S(1)} custom-call(bf16[768,256]{1,0:T(8,128)(2,1)S(1)} %collective-permute-done.8.refs_0_), custom_call_target="tpu_custom_call" | custom-call | flops 134217728 | bytes 2097152 | tf_op jit(solution)/shard_map/turn/pallas_call | solution.py:271
  36.9 2.5 %stacks.2.refs_6_ = f32[32,192,128]{2,1,0:T(8,128)} custom-call(s32[8,128]{1,0:T(8,128)S(1)} %get-tuple-element.40.plan_hbm, bf16[128,16,256]{2,1,0:T(8,128)(2,1)S(1)} %turn.4.refs_0_, bf16[128,16,256]{2,1,0:T(8,128)(2,1)S(1)} %turn.5.refs_1_, bf16[128,16,256]{2,1,0:T(8,128)(2,1)S(1)} %turn.6.refs_2_, bf16[128,16,256]{2,1,0:T(8,128)(2,1)S(1)} %turn.7.refs_3_, ...), custom_call_target="tpu_custom_call" | custom-call | flops 50331648 | bytes 6291456 | tf_op jit(solution)/shard_map/stacks/pallas_call | solution.py:425
  39.5 2.0 %collective-permute-done.10.refs_4_ = bf16[32,16,128]{2,1,0:T(8,128)(2,1)S(1)} collective-permute-done((bf16[32,16,128]{2,1,0:T(8,128)(2,1)S(1)}, bf16[32,16,128]{2,1,0:T(8,128)(2,1)S(1)}, u32[]{:S(2)}, u32[]{:S(2)}) %collective-permute-start.10) | collective-permute-done | bytes 131104 | tf_op jit(solution)/shard_map/ppermute | solution.py:448
  41.5 2.5 %stacks.3 = f32[32,192,128]{2,1,0:T(8,128)} custom-call(s32[8,128]{1,0:T(8,128)S(1)} %get-tuple-element.40.plan_hbm, bf16[128,16,256]{2,1,0:T(8,128)(2,1)S(1)} %turn.4.refs_0_, bf16[128,16,256]{2,1,0:T(8,128)(2,1)S(1)} %turn.5.refs_1_, bf16[128,16,256]{2,1,0:T(8,128)(2,1)S(1)} %turn.6.refs_2_, ...), custom_call_target="tpu_custom_call", output_to_operand_aliasing={{}: (7, {})} | custom-call | flops 50331648 | bytes 6291456 | tf_op jit(solution)/shard_map/stacks/pallas_call | solution.py:425
  (9 shorter events, 0.1 us)
Async XLA Ops:
  8.6 15.7 %collective-permute-start.7 = (bf16[768,256]{1,0:T(8,128)(2,1)S(1)}, bf16[768,256]{1,0:T(8,128)(2,1)S(1)}, u32[]{:S(2)}, u32[]{:S(2)}) collective-permute-start(bf16[768,256]{1,0:T(8,128)(2,1)S(1)} %get-tuple-element.51), channel_id=1, source_target_pairs={{0,8},{4,12},{8,0},{12,4},{1,9},{5,13},{9,1},{13,5},{2,10},{6,14},... | collective-permute-start | bytes 1179656 | tf_op jit(solution)/shard_map/ppermute | solution.py:448
  11.7 5.8 %collective-permute-start.2 = (bf16[4,64,256]{2,1,0:T(8,128)(2,1)S(1)}, bf16[4,64,256]{2,1,0:T(8,128)(2,1)S(1)}, u32[]{:S(2)}, u32[]{:S(2)}) collective-permute-start(bf16[4,64,256]{2,1,0:T(8,128)(2,1)S(1)} %get-tuple-element.44), channel_id=1, source_target_pairs={{1,2},{2,1},{5,6},{6,5},{9,10},{10,9},{13,14},{14,13},{17,18},{18,... | collective-permute-start | bytes 393224 | tf_op jit(solution)/shard_map/ppermute | solution.py:483
  12.3 7.4 %collective-permute-start.3 = (bf16[4,64,256]{2,1,0:T(8,128)(2,1)S(1)}, bf16[4,64,256]{2,1,0:T(8,128)(2,1)S(1)}, u32[]{:S(2)}, u32[]{:S(2)}) collective-permute-start(bf16[4,64,256]{2,1,0:T(8,128)(2,1)S(1)} %get-tuple-element.45), channel_id=1, source_target_pairs={{0,1},{1,0},{2,3},{3,2},{4,5},{5,4},{6,7},{7,6},{8,9},{9,8},{10,11... | collective-permute-start | bytes 393224 | tf_op jit(solution)/shard_map/ppermute | solution.py:483
  20.0 1.9 %collective-permute-start.4 = (bf16[64,256]{1,0:T(8,128)(2,1)S(1)}, bf16[64,256]{1,0:T(8,128)(2,1)S(1)}, u32[]{:S(2)}, u32[]{:S(2)}) collective-permute-start(bf16[64,256]{1,0:T(8,128)(2,1)S(1)} %get-tuple-element.48), channel_id=1, source_target_pairs={{0,4},{4,0},{8,12},{12,8},{1,5},{5,1},{9,13},{13,9},{2,6},{6,2},{1... | collective-permute-start | bytes 98312 | tf_op jit(solution)/shard_map/ppermute | solution.py:448
  20.0 4.3 %collective-permute-start.5 = (bf16[64,256]{1,0:T(8,128)(2,1)S(1)}, bf16[64,256]{1,0:T(8,128)(2,1)S(1)}, u32[]{:S(2)}, u32[]{:S(2)}) collective-permute-start(bf16[64,256]{1,0:T(8,128)(2,1)S(1)} %get-tuple-element.49), channel_id=1, source_target_pairs={{0,8},{4,12},{8,0},{12,4},{1,9},{5,13},{9,1},{13,5},{2,10},{6,14},... | collective-permute-start | bytes 98312 | tf_op jit(solution)/shard_map/ppermute | solution.py:448
  20.6 3.7 %collective-permute-start.6 = (bf16[64,256]{1,0:T(8,128)(2,1)S(1)}, bf16[64,256]{1,0:T(8,128)(2,1)S(1)}, u32[]{:S(2)}, u32[]{:S(2)}) collective-permute-start(bf16[64,256]{1,0:T(8,128)(2,1)S(1)} %get-tuple-element.50), channel_id=1, source_target_pairs={{0,12},{4,8},{8,4},{12,0},{1,13},{5,9},{9,5},{13,1},{2,14},{6,10},... | collective-permute-start | bytes 98312 | tf_op jit(solution)/shard_map/ppermute | solution.py:448
  24.7 11.1 %collective-permute-start.9 = (bf16[768,256]{1,0:T(8,128)(2,1)S(1)}, bf16[768,256]{1,0:T(8,128)(2,1)S(1)}, u32[]{:S(2)}, u32[]{:S(2)}) collective-permute-start(bf16[768,256]{1,0:T(8,128)(2,1)S(1)} %get-tuple-element.55), channel_id=1, source_target_pairs={{0,12},{4,8},{8,4},{12,0},{1,13},{5,9},{9,5},{13,1},{2,14},{6,10},... | collective-permute-start | bytes 1179656 | tf_op jit(solution)/shard_map/ppermute | solution.py:448
  25.7 10.7 %collective-permute-start.8 = (bf16[768,256]{1,0:T(8,128)(2,1)S(1)}, bf16[768,256]{1,0:T(8,128)(2,1)S(1)}, u32[]{:S(2)}, u32[]{:S(2)}) collective-permute-start(bf16[768,256]{1,0:T(8,128)(2,1)S(1)} %get-tuple-element.54), channel_id=1, source_target_pairs={{0,4},{4,0},{8,12},{12,8},{1,5},{5,1},{9,13},{13,9},{2,6},{6,2},{1... | collective-permute-start | bytes 1179656 | tf_op jit(solution)/shard_map/ppermute | solution.py:448
  26.0 10.9 %collective-permute-start.12 = (bf16[32,16,128]{2,1,0:T(8,128)(2,1)S(1)}, bf16[32,16,128]{2,1,0:T(8,128)(2,1)S(1)}, u32[]{:S(2)}, u32[]{:S(2)}) collective-permute-start(bf16[32,16,128]{2,1,0:T(8,128)(2,1)S(1)} %get-tuple-element.56.refs_4_), channel_id=1, source_target_pairs={{0,1},{1,0},{2,3},{3,2},{4,5},{5,4},{6,7},{7,6},{8,9},{9,8},{10,11... | collective-permute-start | bytes 393224 | tf_op jit(solution)/shard_map/ppermute | solution.py:448
  28.0 11.4 %collective-permute-start.11 = (bf16[32,16,128]{2,1,0:T(8,128)(2,1)S(1)}, bf16[32,16,128]{2,1,0:T(8,128)(2,1)S(1)}, u32[]{:S(2)}, u32[]{:S(2)}) collective-permute-start(bf16[32,16,128]{2,1,0:T(8,128)(2,1)S(1)} %get-tuple-element.56.refs_4_), channel_id=1, source_target_pairs={{0,3},{1,2},{2,1},{3,0},{4,7},{5,6},{6,5},{7,4},{8,11},{9,10},{10,... | collective-permute-start | bytes 393224 | tf_op jit(solution)/shard_map/ppermute | solution.py:448
  29.4 12.1 %collective-permute-start.10 = (bf16[32,16,128]{2,1,0:T(8,128)(2,1)S(1)}, bf16[32,16,128]{2,1,0:T(8,128)(2,1)S(1)}, u32[]{:S(2)}, u32[]{:S(2)}) collective-permute-start(bf16[32,16,128]{2,1,0:T(8,128)(2,1)S(1)} %get-tuple-element.56.refs_4_), channel_id=1, source_target_pairs={{0,2},{1,3},{2,0},{3,1},{4,6},{5,7},{6,4},{7,5},{8,10},{9,11},{10,... | collective-permute-start | bytes 393224 | tf_op jit(solution)/shard_map/ppermute | solution.py:448

commit v7 on v6

--- a/solution.py
+++ b/solution.py
@@ -490,7 +490,9 @@
     received = {0: blocks[0], early: swap(blocks[early], "win", early)}
     lefts, later = lefts_call(merged, [received[early]], [blocks[j] for j in late], w_dev)
     received.update({j: swap(block, "win", j) for j, block in zip(late, later)})
-    sources = [lefts] + [swap(lefts, "rcv", i) for i in range(1, n_rcv)]
+    sources = [lefts, swap(lefts, "rcv", 1), swap(lefts, "rcv", 2)]
+    sources.append(swap(sources[2], "rcv", 1))
+
 
     turned = [turn_call([received[j]], w_dev, r_dev) for j in range(n_win)]
     half = n_rcv // 2

time: 44.3 us -> 43.1 us (0.973)
  starting transfers between devices: 14.9 us -> 13.8 us
    ppermute x9, starting transfers between devices: 9.79 us -> 8.67 us  [swap(): return lax.ppermute(value, axis, [(i, i ^ by) for i in range(size)])]
where the time goes in v7:
time: 43.1 us; the launch traced here: 42.9 us
  Pallas kernels  16.2 us (38%)
  starting transfers between devices  13.8 us (32%)
  waiting for transfers between devices  11.8 us (27%)
  between operations  0.94 us (2%)
    ppermute x9, waiting for transfers between devices, swap(): return lax.ppermute(value, axis, [(i, i ^ by) for i in range(size)])  9.53 us
    ppermute x9, starting transfers between devices, swap(): return lax.ppermute(value, axis, [(i, i ^ by) for i in range(size)])  8.67 us
    pallas_call x1, Pallas kernels, spectra_call(): pl.pallas_call(functools.partial(spectra_kernel, n_win, n_rcv, r_dev), in...  8.63 us
    ppermute x2, starting transfers between devices, body(): near[i] = lax.ppermute(picked[i], 'rcv', pairs)  5.11 us
    pallas_call x2, Pallas kernels, stacks_call(): pl.pallas_call(functools.partial(stacks_kernel, shares, n_win, w_dev, r_d...  5.07 us
    ppermute x2, waiting for transfers between devices, body(): near[i] = lax.ppermute(picked[i], 'rcv', pairs)  2.25 us
    pallas_call x4, Pallas kernels, turn_call(): pl.pallas_call(functools.partial(turn_kernel, r_dev), in_specs=[vmem] * l...  2.16 us
  transfers between devices with their start and end apart: 11, of which 4 were waited for; matrix products, arithmetic and copies ran while one was open for 0% of the time, Pallas kernels for 11%

profile of v7, /device:TPU:0, one launch (start us, length us, event | category | flops | bytes accessed | tf_op | source)
XLA Modules:
  0.0 42.9 jit_solution(2086937092242777350)
XLA Ops:
  0.0 8.6 %spectra.1 = (bf16[768,256]{1,0:T(8,128)(2,1)S(1)}, bf16[768,256]{1,0:T(8,128)(2,1)S(1)}, bf16[768,256]{1,0:T(8,128)(2,1)S(1)}, bf16[768,256]{1,0:T(8,128)(2,1)S...) custom-call(s32[8]{0:T(128)} %valid_hbm.1, ...), custom_call_target="tpu_custom_call" | custom-call | flops 2415919104 | bytes 6291456 | tf_op jit(solution)/shard_map/spectra/pallas_call | solution.py:207
  8.6 3.0 %collective-permute-start.7 = (bf16[768,256]{1,0:T(8,128)(2,1)S(1)}, bf16[768,256]{1,0:T(8,128)(2,1)S(1)}, u32[]{:S(2)}, u32[]{:S(2)}) collective-permute-start(bf16[768,256]{1,0:T(8,128)(2,1)S(1)} %get-tuple-element.51), channel_id=1, source_target_pairs={{0,8},{4,12},{8,0},{12,4},{1,9},{5,13},{9,1},{13,5},{2,10},{6,14},... | collective-permute-start | bytes 1179656 | tf_op jit(solution)/shard_map/ppermute | solution.py:448
  11.7 0.7 %collective-permute-start.2 = (bf16[4,64,256]{2,1,0:T(8,128)(2,1)S(1)}, bf16[4,64,256]{2,1,0:T(8,128)(2,1)S(1)}, u32[]{:S(2)}, u32[]{:S(2)}) collective-permute-start(bf16[4,64,256]{2,1,0:T(8,128)(2,1)S(1)} %get-tuple-element.44), channel_id=1, source_target_pairs={{1,2},{2,1},{5,6},{6,5},{9,10},{10,9},{13,14},{14,13},{17,18},{18,... | collective-permute-start | bytes 393224 | tf_op jit(solution)/shard_map/ppermute | solution.py:483
  12.3 4.5 %collective-permute-start.3 = (bf16[4,64,256]{2,1,0:T(8,128)(2,1)S(1)}, bf16[4,64,256]{2,1,0:T(8,128)(2,1)S(1)}, u32[]{:S(2)}, u32[]{:S(2)}) collective-permute-start(bf16[4,64,256]{2,1,0:T(8,128)(2,1)S(1)} %get-tuple-element.45), channel_id=1, source_target_pairs={{0,1},{1,0},{2,3},{3,2},{4,5},{5,4},{6,7},{7,6},{8,9},{9,8},{10,11... | collective-permute-start | bytes 393224 | tf_op jit(solution)/shard_map/ppermute | solution.py:483
  17.5 2.2 %collective-permute-done.3 = bf16[4,64,256]{2,1,0:T(8,128)(2,1)S(1)} collective-permute-done((bf16[4,64,256]{2,1,0:T(8,128)(2,1)S(1)}, bf16[4,64,256]{2,1,0:T(8,128)(2,1)S(1)}, u32[]{:S(2)}, u32[]{:S(2)}) %collective-permute-start.3) | collective-permute-done | bytes 131104 | tf_op jit(solution)/shard_map/ppermute | solution.py:483
  19.7 0.2 conditional.1
  20.0 0.1 collective-permute-start.4
  20.0 0.6 %collective-permute-start.5 = (bf16[64,256]{1,0:T(8,128)(2,1)S(1)}, bf16[64,256]{1,0:T(8,128)(2,1)S(1)}, u32[]{:S(2)}, u32[]{:S(2)}) collective-permute-start(bf16[64,256]{1,0:T(8,128)(2,1)S(1)} %get-tuple-element.49), channel_id=1, source_target_pairs={{0,8},{4,12},{8,0},{12,4},{1,9},{5,13},{9,1},{13,5},{2,10},{6,14},... | collective-permute-start | bytes 98312 | tf_op jit(solution)/shard_map/ppermute | solution.py:448
  20.6 1.3 %collective-permute-start.6 = (bf16[64,256]{1,0:T(8,128)(2,1)S(1)}, bf16[64,256]{1,0:T(8,128)(2,1)S(1)}, u32[]{:S(2)}, u32[]{:S(2)}) collective-permute-start(bf16[64,256]{1,0:T(8,128)(2,1)S(1)} %get-tuple-element.50), channel_id=1, source_target_pairs={{0,12},{4,8},{8,4},{12,0},{1,13},{5,9},{9,5},{13,1},{2,14},{6,10},... | collective-permute-start | bytes 98312 | tf_op jit(solution)/shard_map/ppermute | solution.py:448
  21.9 2.4 %collective-permute-done.5.refs_2_ = bf16[64,256]{1,0:T(8,128)(2,1)S(1)} collective-permute-done((bf16[64,256]{1,0:T(8,128)(2,1)S(1)}, bf16[64,256]{1,0:T(8,128)(2,1)S(1)}, u32[]{:S(2)}, u32[]{:S(2)}) %collective-permute-start.5) | collective-permute-done | bytes 32800 | tf_op jit(solution)/shard_map/ppermute | solution.py:448
  24.3 0.3 lefts.1
  24.7 1.0 %collective-permute-start.9 = (bf16[768,256]{1,0:T(8,128)(2,1)S(1)}, bf16[768,256]{1,0:T(8,128)(2,1)S(1)}, u32[]{:S(2)}, u32[]{:S(2)}) collective-permute-start(bf16[768,256]{1,0:T(8,128)(2,1)S(1)} %get-tuple-element.55), channel_id=1, source_target_pairs={{0,12},{4,8},{8,4},{12,0},{1,13},{5,9},{9,5},{13,1},{2,14},{6,10},... | collective-permute-start | bytes 1179656 | tf_op jit(solution)/shard_map/ppermute | solution.py:448
  25.7 0.3 collective-permute-start.8
  26.0 1.9 %collective-permute-start.10 = (bf16[32,16,128]{2,1,0:T(8,128)(2,1)S(1)}, bf16[32,16,128]{2,1,0:T(8,128)(2,1)S(1)}, u32[]{:S(2)}, u32[]{:S(2)}) collective-permute-start(bf16[32,16,128]{2,1,0:T(8,128)(2,1)S(1)} %get-tuple-element.56.refs_4_), channel_id=1, source_target_pairs={{0,2},{1,3},{2,0},{3,1},{4,6},{5,7},{6,4},{7,5},{8,10},{9,11},{10,... | collective-permute-start | bytes 393224 | tf_op jit(solution)/shard_map/ppermute | solution.py:448
  27.9 0.4 %collective-permute-start.12 = (bf16[32,16,128]{2,1,0:T(8,128)(2,1)S(1)}, bf16[32,16,128]{2,1,0:T(8,128)(2,1)S(1)}, u32[]{:S(2)}, u32[]{:S(2)}) collective-permute-start(bf16[32,16,128]{2,1,0:T(8,128)(2,1)S(1)} %get-tuple-element.56.refs_4_), channel_id=1, source_target_pairs={{0,1},{1,0},{2,3},{3,2},{4,5},{5,4},{6,7},{7,6},{8,9},{9,8},{10,11... | collective-permute-start | bytes 393224 | tf_op jit(solution)/shard_map/ppermute | solution.py:448
  28.3 6.9 %collective-permute-done.10.refs_4_ = bf16[32,16,128]{2,1,0:T(8,128)(2,1)S(1)} collective-permute-done((bf16[32,16,128]{2,1,0:T(8,128)(2,1)S(1)}, bf16[32,16,128]{2,1,0:T(8,128)(2,1)S(1)}, u32[]{:S(2)}, u32[]{:S(2)}) %collective-permute-start.10) | collective-permute-done | bytes 131104 | tf_op jit(solution)/shard_map/ppermute | solution.py:448
  35.3 0.0 collective-permute-start.11
  35.3 0.5 %turn.4.refs_0_ = bf16[128,16,256]{2,1,0:T(8,128)(2,1)S(1)} custom-call(bf16[768,256]{1,0:T(8,128)(2,1)S(1)} %get-tuple-element.41.refs_0_), custom_call_target="tpu_custom_call" | custom-call | flops 134217728 | bytes 2097152 | tf_op jit(solution)/shard_map/turn/pallas_call | solution.py:271
  35.9 0.5 %turn.6.refs_2_ = bf16[128,16,256]{2,1,0:T(8,128)(2,1)S(1)} custom-call(bf16[768,256]{1,0:T(8,128)(2,1)S(1)} %collective-permute-done.7.refs_4_.refs_0_), custom_call_target="tpu_custom_call" | custom-call | flops 134217728 | bytes 2097152 | tf_op jit(solution)/shard_map/turn/pallas_call | solution.py:271
  36.4 0.5 %turn.7.refs_3_ = bf16[128,16,256]{2,1,0:T(8,128)(2,1)S(1)} custom-call(bf16[768,256]{1,0:T(8,128)(2,1)S(1)} %collective-permute-done.9.refs_0_), custom_call_target="tpu_custom_call" | custom-call | flops 134217728 | bytes 2097152 | tf_op jit(solution)/shard_map/turn/pallas_call | solution.py:271
  37.0 0.5 %turn.5.refs_1_ = bf16[128,16,256]{2,1,0:T(8,128)(2,1)S(1)} custom-call(bf16[768,256]{1,0:T(8,128)(2,1)S(1)} %collective-permute-done.8.refs_0_), custom_call_target="tpu_custom_call" | custom-call | flops 134217728 | bytes 2097152 | tf_op jit(solution)/shard_map/turn/pallas_call | solution.py:271
  37.5 2.5 %stacks.2.refs_6_ = f32[32,192,128]{2,1,0:T(8,128)} custom-call(s32[8,128]{1,0:T(8,128)S(1)} %get-tuple-element.40.plan_hbm, bf16[128,16,256]{2,1,0:T(8,128)(2,1)S(1)} %turn.4.refs_0_, bf16[128,16,256]{2,1,0:T(8,128)(2,1)S(1)} %turn.5.refs_1_, bf16[128,16,256]{2,1,0:T(8,128)(2,1)S(1)} %turn.6.refs_2_, bf16[128,16,256]{2,1,0:T(8,128)(2,1)S(1)} %turn.7.refs_3_, ...), custom_call_target="tpu_custom_call" | custom-call | flops 50331648 | bytes 6291456 | tf_op jit(solution)/shard_map/stacks/pallas_call | solution.py:425
  40.1 0.2 collective-permute-done.11.refs_5_
  40.3 2.5 %stacks.3 = f32[32,192,128]{2,1,0:T(8,128)} custom-call(s32[8,128]{1,0:T(8,128)S(1)} %get-tuple-element.40.plan_hbm, bf16[128,16,256]{2,1,0:T(8,128)(2,1)S(1)} %turn.4.refs_0_, bf16[128,16,256]{2,1,0:T(8,128)(2,1)S(1)} %turn.5.refs_1_, bf16[128,16,256]{2,1,0:T(8,128)(2,1)S(1)} %turn.6.refs_2_, ...), custom_call_target="tpu_custom_call", output_to_operand_aliasing={{}: (7, {})} | custom-call | flops 50331648 | bytes 6291456 | tf_op jit(solution)/shard_map/stacks/pallas_call | solution.py:425
  (9 shorter events, 0.1 us)
Async XLA Ops:
  8.6 15.7 %collective-permute-start.7 = (bf16[768,256]{1,0:T(8,128)(2,1)S(1)}, bf16[768,256]{1,0:T(8,128)(2,1)S(1)}, u32[]{:S(2)}, u32[]{:S(2)}) collective-permute-start(bf16[768,256]{1,0:T(8,128)(2,1)S(1)} %get-tuple-element.51), channel_id=1, source_target_pairs={{0,8},{4,12},{8,0},{12,4},{1,9},{5,13},{9,1},{13,5},{2,10},{6,14},... | collective-permute-start | bytes 1179656 | tf_op jit(solution)/shard_map/ppermute | solution.py:448
  11.7 5.8 %collective-permute-start.2 = (bf16[4,64,256]{2,1,0:T(8,128)(2,1)S(1)}, bf16[4,64,256]{2,1,0:T(8,128)(2,1)S(1)}, u32[]{:S(2)}, u32[]{:S(2)}) collective-permute-start(bf16[4,64,256]{2,1,0:T(8,128)(2,1)S(1)} %get-tuple-element.44), channel_id=1, source_target_pairs={{1,2},{2,1},{5,6},{6,5},{9,10},{10,9},{13,14},{14,13},{17,18},{18,... | collective-permute-start | bytes 393224 | tf_op jit(solution)/shard_map/ppermute | solution.py:483
  12.3 7.4 %collective-permute-start.3 = (bf16[4,64,256]{2,1,0:T(8,128)(2,1)S(1)}, bf16[4,64,256]{2,1,0:T(8,128)(2,1)S(1)}, u32[]{:S(2)}, u32[]{:S(2)}) collective-permute-start(bf16[4,64,256]{2,1,0:T(8,128)(2,1)S(1)} %get-tuple-element.45), channel_id=1, source_target_pairs={{0,1},{1,0},{2,3},{3,2},{4,5},{5,4},{6,7},{7,6},{8,9},{9,8},{10,11... | collective-permute-start | bytes 393224 | tf_op jit(solution)/shard_map/ppermute | solution.py:483
  20.0 1.9 %collective-permute-start.4 = (bf16[64,256]{1,0:T(8,128)(2,1)S(1)}, bf16[64,256]{1,0:T(8,128)(2,1)S(1)}, u32[]{:S(2)}, u32[]{:S(2)}) collective-permute-start(bf16[64,256]{1,0:T(8,128)(2,1)S(1)} %get-tuple-element.48), channel_id=1, source_target_pairs={{0,4},{4,0},{8,12},{12,8},{1,5},{5,1},{9,13},{13,9},{2,6},{6,2},{1... | collective-permute-start | bytes 98312 | tf_op jit(solution)/shard_map/ppermute | solution.py:448
  20.0 4.3 %collective-permute-start.5 = (bf16[64,256]{1,0:T(8,128)(2,1)S(1)}, bf16[64,256]{1,0:T(8,128)(2,1)S(1)}, u32[]{:S(2)}, u32[]{:S(2)}) collective-permute-start(bf16[64,256]{1,0:T(8,128)(2,1)S(1)} %get-tuple-element.49), channel_id=1, source_target_pairs={{0,8},{4,12},{8,0},{12,4},{1,9},{5,13},{9,1},{13,5},{2,10},{6,14},... | collective-permute-start | bytes 98312 | tf_op jit(solution)/shard_map/ppermute | solution.py:448
  20.6 3.7 %collective-permute-start.6 = (bf16[64,256]{1,0:T(8,128)(2,1)S(1)}, bf16[64,256]{1,0:T(8,128)(2,1)S(1)}, u32[]{:S(2)}, u32[]{:S(2)}) collective-permute-start(bf16[64,256]{1,0:T(8,128)(2,1)S(1)} %get-tuple-element.50), channel_id=1, source_target_pairs={{0,12},{4,8},{8,4},{12,0},{1,13},{5,9},{9,5},{13,1},{2,14},{6,10},... | collective-permute-start | bytes 98312 | tf_op jit(solution)/shard_map/ppermute | solution.py:448
  24.7 11.8 %collective-permute-start.9 = (bf16[768,256]{1,0:T(8,128)(2,1)S(1)}, bf16[768,256]{1,0:T(8,128)(2,1)S(1)}, u32[]{:S(2)}, u32[]{:S(2)}) collective-permute-start(bf16[768,256]{1,0:T(8,128)(2,1)S(1)} %get-tuple-element.55), channel_id=1, source_target_pairs={{0,12},{4,8},{8,4},{12,0},{1,13},{5,9},{9,5},{13,1},{2,14},{6,10},... | collective-permute-start | bytes 1179656 | tf_op jit(solution)/shard_map/ppermute | solution.py:448
  25.7 11.3 %collective-permute-start.8 = (bf16[768,256]{1,0:T(8,128)(2,1)S(1)}, bf16[768,256]{1,0:T(8,128)(2,1)S(1)}, u32[]{:S(2)}, u32[]{:S(2)}) collective-permute-start(bf16[768,256]{1,0:T(8,128)(2,1)S(1)} %get-tuple-element.54), channel_id=1, source_target_pairs={{0,4},{4,0},{8,12},{12,8},{1,5},{5,1},{9,13},{13,9},{2,6},{6,2},{1... | collective-permute-start | bytes 1179656 | tf_op jit(solution)/shard_map/ppermute | solution.py:448
  26.0 9.3 %collective-permute-start.10 = (bf16[32,16,128]{2,1,0:T(8,128)(2,1)S(1)}, bf16[32,16,128]{2,1,0:T(8,128)(2,1)S(1)}, u32[]{:S(2)}, u32[]{:S(2)}) collective-permute-start(bf16[32,16,128]{2,1,0:T(8,128)(2,1)S(1)} %get-tuple-element.56.refs_4_), channel_id=1, source_target_pairs={{0,2},{1,3},{2,0},{3,1},{4,6},{5,7},{6,4},{7,5},{8,10},{9,11},{10,... | collective-permute-start | bytes 393224 | tf_op jit(solution)/shard_map/ppermute | solution.py:448
  27.9 9.6 %collective-permute-start.12 = (bf16[32,16,128]{2,1,0:T(8,128)(2,1)S(1)}, bf16[32,16,128]{2,1,0:T(8,128)(2,1)S(1)}, u32[]{:S(2)}, u32[]{:S(2)}) collective-permute-start(bf16[32,16,128]{2,1,0:T(8,128)(2,1)S(1)} %get-tuple-element.56.refs_4_), channel_id=1, source_target_pairs={{0,1},{1,0},{2,3},{3,2},{4,5},{5,4},{6,7},{7,6},{8,9},{9,8},{10,11... | collective-permute-start | bytes 393224 | tf_op jit(solution)/shard_map/ppermute | solution.py:448
  35.3 5.0 %collective-permute-start.11 = (bf16[32,16,128]{2,1,0:T(8,128)(2,1)S(1)}, bf16[32,16,128]{2,1,0:T(8,128)(2,1)S(1)}, u32[]{:S(2)}, u32[]{:S(2)}) collective-permute-start(bf16[32,16,128]{2,1,0:T(8,128)(2,1)S(1)} %collective-permute-done.10.refs_4_), channel_id=1, source_target_pairs={{0,1},{1,0},{2,3},{3,2},{4,5},{5,4},{6,7},{7,6},{8,9},{9,8},{10,11... | collective-permute-start | bytes 393224 | tf_op jit(solution)/shard_map/ppermute | solution.py:448

commit v8 on v7

--- a/solution.py
+++ b/solution.py
@@ -366,6 +366,24 @@
     return out[-1], out[:-1]
 
 
+def gate_kernel(*refs):
+    pass
+
+
+def gate_call(after, arrays):
+    anywhere = pl.BlockSpec(memory_space=pl.ANY)
+    return pl.pallas_call(
+        gate_kernel,
+        in_specs=[anywhere] * (len(after) + len(arrays)),
+        out_specs=[anywhere] * len(arrays),
+        out_shape=[jax.ShapeDtypeStruct(x.shape, x.dtype) for x in arrays],
+        input_output_aliases={len(after) + k: k for k in range(len(arrays))},
+        compiler_params=pltpu.CompilerParams(vmem_limit_bytes=2**20),
+        cost_estimate=pl.CostEstimate(flops=1, bytes_accessed=1, transcendentals=0),
+        name="gate",
+    )(*after, *arrays)
+
+
 def stacks_kernel(shares, n_win, w_dev, r_dev, n_own, bins, plan_hbm, *refs):
     t_refs = refs[:n_win]
     s_refs = refs[n_win:n_win + len(shares)]
@@ -491,10 +509,10 @@
     lefts, later = lefts_call(merged, [received[early]], [blocks[j] for j in late], w_dev)
     received.update({j: swap(block, "win", j) for j, block in zip(late, later)})
     sources = [lefts, swap(lefts, "rcv", 1), swap(lefts, "rcv", 2)]
+    turned = [turn_call([received[j]], w_dev, r_dev) for j in range(n_win)]
+    sources[2] = gate_call(turned[:-1], [sources[2]])[0]
     sources.append(swap(sources[2], "rcv", 1))
 
-
-    turned = [turn_call([received[j]], w_dev, r_dev) for j in range(n_win)]
     half = n_rcv // 2
     sizes = (n_rcv, w_dev, r_dev, bins)
     stacks = stacks_call(None, plan, turned, sources, tuple(range(half)), *sizes)

time: 43.1 us -> 43.1 us (level)
  transfers between devices with their start and end apart: 11 -> 11, of which waited for: 4 -> 5; matrix products, arithmetic and copies ran while one was open for 0% -> 0% of each run, Pallas kernels for 11% -> 11%
where the time goes in v8:
time: 43.1 us; the launch traced here: 43 us
  Pallas kernels  16.2 us (38%)
  starting transfers between devices  13.8 us (32%)
  waiting for transfers between devices  11.7 us (27%)
  between operations  0.93 us (2%)
    ppermute x9, waiting for transfers between devices, swap(): return lax.ppermute(value, axis, [(i, i ^ by) for i in range(size)])  9.47 us
    ppermute x9, starting transfers between devices, swap(): return lax.ppermute(value, axis, [(i, i ^ by) for i in range(size)])  8.73 us
    pallas_call x1, Pallas kernels, spectra_call(): pl.pallas_call(functools.partial(spectra_kernel, n_win, n_rcv, r_dev), in...  8.63 us
    ppermute x2, starting transfers between devices, body(): near[i] = lax.ppermute(picked[i], 'rcv', pairs)  5.11 us
    pallas_call x2, Pallas kernels, stacks_call(): pl.pallas_call(functools.partial(stacks_kernel, shares, n_win, w_dev, r_d...  5.07 us
    ppermute x2, waiting for transfers between devices, body(): near[i] = lax.ppermute(picked[i], 'rcv', pairs)  2.25 us
    pallas_call x4, Pallas kernels, turn_call(): pl.pallas_call(functools.partial(turn_kernel, r_dev), in_specs=[vmem] * l...  2.15 us
  transfers between devices with their start and end apart: 11, of which 5 were waited for; matrix products, arithmetic and copies ran while one was open for 0% of the time, Pallas kernels for 11%

profile of v8, /device:TPU:0, one launch (start us, length us, event | category | flops | bytes accessed | tf_op | source)
XLA Modules:
  0.0 43.0 jit_solution(6183632628859663316)
XLA Ops:
  0.0 8.6 %spectra.1 = (bf16[768,256]{1,0:T(8,128)(2,1)S(1)}, bf16[768,256]{1,0:T(8,128)(2,1)S(1)}, bf16[768,256]{1,0:T(8,128)(2,1)S(1)}, bf16[768,256]{1,0:T(8,128)(2,1)S...) custom-call(s32[8]{0:T(128)} %valid_hbm.1, ...), custom_call_target="tpu_custom_call" | custom-call | flops 2415919104 | bytes 6291456 | tf_op jit(solution)/shard_map/spectra/pallas_call | solution.py:207
  8.6 3.0 %collective-permute-start.7 = (bf16[768,256]{1,0:T(8,128)(2,1)S(1)}, bf16[768,256]{1,0:T(8,128)(2,1)S(1)}, u32[]{:S(2)}, u32[]{:S(2)}) collective-permute-start(bf16[768,256]{1,0:T(8,128)(2,1)S(1)} %get-tuple-element.51), channel_id=1, source_target_pairs={{0,8},{4,12},{8,0},{12,4},{1,9},{5,13},{9,1},{13,5},{2,10},{6,14},... | collective-permute-start | bytes 1179656 | tf_op jit(solution)/shard_map/ppermute | solution.py:466
  11.7 0.7 %collective-permute-start.2 = (bf16[4,64,256]{2,1,0:T(8,128)(2,1)S(1)}, bf16[4,64,256]{2,1,0:T(8,128)(2,1)S(1)}, u32[]{:S(2)}, u32[]{:S(2)}) collective-permute-start(bf16[4,64,256]{2,1,0:T(8,128)(2,1)S(1)} %get-tuple-element.44), channel_id=1, source_target_pairs={{1,2},{2,1},{5,6},{6,5},{9,10},{10,9},{13,14},{14,13},{17,18},{18,... | collective-permute-start | bytes 393224 | tf_op jit(solution)/shard_map/ppermute | solution.py:501
  12.3 4.5 %collective-permute-start.3 = (bf16[4,64,256]{2,1,0:T(8,128)(2,1)S(1)}, bf16[4,64,256]{2,1,0:T(8,128)(2,1)S(1)}, u32[]{:S(2)}, u32[]{:S(2)}) collective-permute-start(bf16[4,64,256]{2,1,0:T(8,128)(2,1)S(1)} %get-tuple-element.45), channel_id=1, source_target_pairs={{0,1},{1,0},{2,3},{3,2},{4,5},{5,4},{6,7},{7,6},{8,9},{9,8},{10,11... | collective-permute-start | bytes 393224 | tf_op jit(solution)/shard_map/ppermute | solution.py:501
  17.5 2.2 %collective-permute-done.3 = bf16[4,64,256]{2,1,0:T(8,128)(2,1)S(1)} collective-permute-done((bf16[4,64,256]{2,1,0:T(8,128)(2,1)S(1)}, bf16[4,64,256]{2,1,0:T(8,128)(2,1)S(1)}, u32[]{:S(2)}, u32[]{:S(2)}) %collective-permute-start.3) | collective-permute-done | bytes 131104 | tf_op jit(solution)/shard_map/ppermute | solution.py:501
  19.7 0.2 conditional.1
  20.0 0.1 collective-permute-start.4
  20.0 0.6 %collective-permute-start.5 = (bf16[64,256]{1,0:T(8,128)(2,1)S(1)}, bf16[64,256]{1,0:T(8,128)(2,1)S(1)}, u32[]{:S(2)}, u32[]{:S(2)}) collective-permute-start(bf16[64,256]{1,0:T(8,128)(2,1)S(1)} %get-tuple-element.49), channel_id=1, source_target_pairs={{0,8},{4,12},{8,0},{12,4},{1,9},{5,13},{9,1},{13,5},{2,10},{6,14},... | collective-permute-start | bytes 98312 | tf_op jit(solution)/shard_map/ppermute | solution.py:466
  20.6 1.3 %collective-permute-start.6 = (bf16[64,256]{1,0:T(8,128)(2,1)S(1)}, bf16[64,256]{1,0:T(8,128)(2,1)S(1)}, u32[]{:S(2)}, u32[]{:S(2)}) collective-permute-start(bf16[64,256]{1,0:T(8,128)(2,1)S(1)} %get-tuple-element.50), channel_id=1, source_target_pairs={{0,12},{4,8},{8,4},{12,0},{1,13},{5,9},{9,5},{13,1},{2,14},{6,10},... | collective-permute-start | bytes 98312 | tf_op jit(solution)/shard_map/ppermute | solution.py:466
  21.9 2.4 %collective-permute-done.5.refs_2_ = bf16[64,256]{1,0:T(8,128)(2,1)S(1)} collective-permute-done((bf16[64,256]{1,0:T(8,128)(2,1)S(1)}, bf16[64,256]{1,0:T(8,128)(2,1)S(1)}, u32[]{:S(2)}, u32[]{:S(2)}) %collective-permute-start.5) | collective-permute-done | bytes 32800 | tf_op jit(solution)/shard_map/ppermute | solution.py:466
  24.3 0.3 lefts.1
  24.7 0.2 collective-permute-start.8
  24.9 1.1 %collective-permute-start.9 = (bf16[768,256]{1,0:T(8,128)(2,1)S(1)}, bf16[768,256]{1,0:T(8,128)(2,1)S(1)}, u32[]{:S(2)}, u32[]{:S(2)}) collective-permute-start(bf16[768,256]{1,0:T(8,128)(2,1)S(1)} %get-tuple-element.55), channel_id=1, source_target_pairs={{0,12},{4,8},{8,4},{12,0},{1,13},{5,9},{9,5},{13,1},{2,14},{6,10},... | collective-permute-start | bytes 1179656 | tf_op jit(solution)/shard_map/ppermute | solution.py:466
  26.0 1.9 %collective-permute-start.10 = (bf16[32,16,128]{2,1,0:T(8,128)(2,1)S(1)}, bf16[32,16,128]{2,1,0:T(8,128)(2,1)S(1)}, u32[]{:S(2)}, u32[]{:S(2)}) collective-permute-start(bf16[32,16,128]{2,1,0:T(8,128)(2,1)S(1)} %get-tuple-element.56.refs_4_), channel_id=1, source_target_pairs={{0,2},{1,3},{2,0},{3,1},{4,6},{5,7},{6,4},{7,5},{8,10},{9,11},{10,... | collective-permute-start | bytes 393224 | tf_op jit(solution)/shard_map/ppermute | solution.py:466
  27.9 0.5 %turn.4.refs_0_ = bf16[128,16,256]{2,1,0:T(8,128)(2,1)S(1)} custom-call(bf16[768,256]{1,0:T(8,128)(2,1)S(1)} %get-tuple-element.41.refs_0_), custom_call_target="tpu_custom_call" | custom-call | flops 134217728 | bytes 2097152 | tf_op jit(solution)/shard_map/turn/pallas_call | solution.py:271
  28.5 0.5 %collective-permute-start.12 = (bf16[32,16,128]{2,1,0:T(8,128)(2,1)S(1)}, bf16[32,16,128]{2,1,0:T(8,128)(2,1)S(1)}, u32[]{:S(2)}, u32[]{:S(2)}) collective-permute-start(bf16[32,16,128]{2,1,0:T(8,128)(2,1)S(1)} %get-tuple-element.56.refs_4_), channel_id=1, source_target_pairs={{0,1},{1,0},{2,3},{3,2},{4,5},{5,4},{6,7},{7,6},{8,9},{9,8},{10,11... | collective-permute-start | bytes 393224 | tf_op jit(solution)/shard_map/ppermute | solution.py:466
  29.0 0.5 %turn.6.refs_2_ = bf16[128,16,256]{2,1,0:T(8,128)(2,1)S(1)} custom-call(bf16[768,256]{1,0:T(8,128)(2,1)S(1)} %collective-permute-done.7.refs_4_.refs_0_), custom_call_target="tpu_custom_call" | custom-call | flops 134217728 | bytes 2097152 | tf_op jit(solution)/shard_map/turn/pallas_call | solution.py:271
  29.5 0.5 %turn.5.refs_1_ = bf16[128,16,256]{2,1,0:T(8,128)(2,1)S(1)} custom-call(bf16[768,256]{1,0:T(8,128)(2,1)S(1)} %collective-permute-done.8.refs_0_), custom_call_target="tpu_custom_call" | custom-call | flops 134217728 | bytes 2097152 | tf_op jit(solution)/shard_map/turn/pallas_call | solution.py:271
  30.1 5.2 %collective-permute-done.10.refs_3_ = bf16[32,16,128]{2,1,0:T(8,128)(2,1)S(1)} collective-permute-done((bf16[32,16,128]{2,1,0:T(8,128)(2,1)S(1)}, bf16[32,16,128]{2,1,0:T(8,128)(2,1)S(1)}, u32[]{:S(2)}, u32[]{:S(2)}) %collective-permute-start.10) | collective-permute-done | bytes 131104 | tf_op jit(solution)/shard_map/ppermute | solution.py:466
  35.3 0.5 %collective-permute-done.9.refs_0_ = bf16[768,256]{1,0:T(8,128)(2,1)S(1)} collective-permute-done((bf16[768,256]{1,0:T(8,128)(2,1)S(1)}, bf16[768,256]{1,0:T(8,128)(2,1)S(1)}, u32[]{:S(2)}, u32[]{:S(2)}) %collective-permute-start.9) | collective-permute-done | bytes 393248 | tf_op jit(solution)/shard_map/ppermute | solution.py:466
  35.9 0.5 %turn.7.refs_3_ = bf16[128,16,256]{2,1,0:T(8,128)(2,1)S(1)} custom-call(bf16[768,256]{1,0:T(8,128)(2,1)S(1)} %collective-permute-done.9.refs_0_), custom_call_target="tpu_custom_call" | custom-call | flops 134217728 | bytes 2097152 | tf_op jit(solution)/shard_map/turn/pallas_call | solution.py:271
  36.4 2.5 %stacks.2.refs_6_ = f32[32,192,128]{2,1,0:T(8,128)} custom-call(s32[8,128]{1,0:T(8,128)S(1)} %get-tuple-element.40.plan_hbm, bf16[128,16,256]{2,1,0:T(8,128)(2,1)S(1)} %turn.4.refs_0_, bf16[128,16,256]{2,1,0:T(8,128)(2,1)S(1)} %turn.5.refs_1_, bf16[128,16,256]{2,1,0:T(8,128)(2,1)S(1)} %turn.6.refs_2_, bf16[128,16,256]{2,1,0:T(8,128)(2,1)S(1)} %turn.7.refs_3_, ...), custom_call_target="tpu_custom_call" | custom-call | flops 50331648 | bytes 6291456 | tf_op jit(solution)/shard_map/stacks/pallas_call | solution.py:443
  39.0 1.3 %collective-permute-done.11.refs_5_ = bf16[32,16,128]{2,1,0:T(8,128)(2,1)S(1)} collective-permute-done((bf16[32,16,128]{2,1,0:T(8,128)(2,1)S(1)}, bf16[32,16,128]{2,1,0:T(8,128)(2,1)S(1)}, u32[]{:S(2)}, u32[]{:S(2)}) %collective-permute-start.11) | collective-permute-done | bytes 131104 | tf_op jit(solution)/shard_map/ppermute | solution.py:466
  40.3 2.5 %stacks.3 = f32[32,192,128]{2,1,0:T(8,128)} custom-call(s32[8,128]{1,0:T(8,128)S(1)} %get-tuple-element.40.plan_hbm, bf16[128,16,256]{2,1,0:T(8,128)(2,1)S(1)} %turn.4.refs_0_, bf16[128,16,256]{2,1,0:T(8,128)(2,1)S(1)} %turn.5.refs_1_, bf16[128,16,256]{2,1,0:T(8,128)(2,1)S(1)} %turn.6.refs_2_, ...), custom_call_target="tpu_custom_call", output_to_operand_aliasing={{}: (7, {})} | custom-call | flops 50331648 | bytes 6291456 | tf_op jit(solution)/shard_map/stacks/pallas_call | solution.py:443
  (10 shorter events, 0.1 us)
Async XLA Ops:
  8.6 15.7 %collective-permute-start.7 = (bf16[768,256]{1,0:T(8,128)(2,1)S(1)}, bf16[768,256]{1,0:T(8,128)(2,1)S(1)}, u32[]{:S(2)}, u32[]{:S(2)}) collective-permute-start(bf16[768,256]{1,0:T(8,128)(2,1)S(1)} %get-tuple-element.51), channel_id=1, source_target_pairs={{0,8},{4,12},{8,0},{12,4},{1,9},{5,13},{9,1},{13,5},{2,10},{6,14},... | collective-permute-start | bytes 1179656 | tf_op jit(solution)/shard_map/ppermute | solution.py:466
  11.7 5.8 %collective-permute-start.2 = (bf16[4,64,256]{2,1,0:T(8,128)(2,1)S(1)}, bf16[4,64,256]{2,1,0:T(8,128)(2,1)S(1)}, u32[]{:S(2)}, u32[]{:S(2)}) collective-permute-start(bf16[4,64,256]{2,1,0:T(8,128)(2,1)S(1)} %get-tuple-element.44), channel_id=1, source_target_pairs={{1,2},{2,1},{5,6},{6,5},{9,10},{10,9},{13,14},{14,13},{17,18},{18,... | collective-permute-start | bytes 393224 | tf_op jit(solution)/shard_map/ppermute | solution.py:501
  12.3 7.4 %collective-permute-start.3 = (bf16[4,64,256]{2,1,0:T(8,128)(2,1)S(1)}, bf16[4,64,256]{2,1,0:T(8,128)(2,1)S(1)}, u32[]{:S(2)}, u32[]{:S(2)}) collective-permute-start(bf16[4,64,256]{2,1,0:T(8,128)(2,1)S(1)} %get-tuple-element.45), channel_id=1, source_target_pairs={{0,1},{1,0},{2,3},{3,2},{4,5},{5,4},{6,7},{7,6},{8,9},{9,8},{10,11... | collective-permute-start | bytes 393224 | tf_op jit(solution)/shard_map/ppermute | solution.py:501
  20.0 1.9 %collective-permute-start.4 = (bf16[64,256]{1,0:T(8,128)(2,1)S(1)}, bf16[64,256]{1,0:T(8,128)(2,1)S(1)}, u32[]{:S(2)}, u32[]{:S(2)}) collective-permute-start(bf16[64,256]{1,0:T(8,128)(2,1)S(1)} %get-tuple-element.48), channel_id=1, source_target_pairs={{0,4},{4,0},{8,12},{12,8},{1,5},{5,1},{9,13},{13,9},{2,6},{6,2},{1... | collective-permute-start | bytes 98312 | tf_op jit(solution)/shard_map/ppermute | solution.py:466
  20.0 4.3 %collective-permute-start.5 = (bf16[64,256]{1,0:T(8,128)(2,1)S(1)}, bf16[64,256]{1,0:T(8,128)(2,1)S(1)}, u32[]{:S(2)}, u32[]{:S(2)}) collective-permute-start(bf16[64,256]{1,0:T(8,128)(2,1)S(1)} %get-tuple-element.49), channel_id=1, source_target_pairs={{0,8},{4,12},{8,0},{12,4},{1,9},{5,13},{9,1},{13,5},{2,10},{6,14},... | collective-permute-start | bytes 98312 | tf_op jit(solution)/shard_map/ppermute | solution.py:466
  20.6 3.7 %collective-permute-start.6 = (bf16[64,256]{1,0:T(8,128)(2,1)S(1)}, bf16[64,256]{1,0:T(8,128)(2,1)S(1)}, u32[]{:S(2)}, u32[]{:S(2)}) collective-permute-start(bf16[64,256]{1,0:T(8,128)(2,1)S(1)} %get-tuple-element.50), channel_id=1, source_target_pairs={{0,12},{4,8},{8,4},{12,0},{1,13},{5,9},{9,5},{13,1},{2,14},{6,10},... | collective-permute-start | bytes 98312 | tf_op jit(solution)/shard_map/ppermute | solution.py:466
  24.7 4.8 %collective-permute-start.8 = (bf16[768,256]{1,0:T(8,128)(2,1)S(1)}, bf16[768,256]{1,0:T(8,128)(2,1)S(1)}, u32[]{:S(2)}, u32[]{:S(2)}) collective-permute-start(bf16[768,256]{1,0:T(8,128)(2,1)S(1)} %get-tuple-element.54), channel_id=1, source_target_pairs={{0,4},{4,0},{8,12},{12,8},{1,5},{5,1},{9,13},{13,9},{2,6},{6,2},{1... | collective-permute-start | bytes 1179656 | tf_op jit(solution)/shard_map/ppermute | solution.py:466
  24.9 11.0 %collective-permute-start.9 = (bf16[768,256]{1,0:T(8,128)(2,1)S(1)}, bf16[768,256]{1,0:T(8,128)(2,1)S(1)}, u32[]{:S(2)}, u32[]{:S(2)}) collective-permute-start(bf16[768,256]{1,0:T(8,128)(2,1)S(1)} %get-tuple-element.55), channel_id=1, source_target_pairs={{0,12},{4,8},{8,4},{12,0},{1,13},{5,9},{9,5},{13,1},{2,14},{6,10},... | collective-permute-start | bytes 1179656 | tf_op jit(solution)/shard_map/ppermute | solution.py:466
  26.0 9.3 %collective-permute-start.10 = (bf16[32,16,128]{2,1,0:T(8,128)(2,1)S(1)}, bf16[32,16,128]{2,1,0:T(8,128)(2,1)S(1)}, u32[]{:S(2)}, u32[]{:S(2)}) collective-permute-start(bf16[32,16,128]{2,1,0:T(8,128)(2,1)S(1)} %get-tuple-element.56.refs_4_), channel_id=1, source_target_pairs={{0,2},{1,3},{2,0},{3,1},{4,6},{5,7},{6,4},{7,5},{8,10},{9,11},{10,... | collective-permute-start | bytes 393224 | tf_op jit(solution)/shard_map/ppermute | solution.py:466
  28.5 8.0 %collective-permute-start.12 = (bf16[32,16,128]{2,1,0:T(8,128)(2,1)S(1)}, bf16[32,16,128]{2,1,0:T(8,128)(2,1)S(1)}, u32[]{:S(2)}, u32[]{:S(2)}) collective-permute-start(bf16[32,16,128]{2,1,0:T(8,128)(2,1)S(1)} %get-tuple-element.56.refs_4_), channel_id=1, source_target_pairs={{0,1},{1,0},{2,3},{3,2},{4,5},{5,4},{6,7},{7,6},{8,9},{9,8},{10,11... | collective-permute-start | bytes 393224 | tf_op jit(solution)/shard_map/ppermute | solution.py:466
  35.3 5.0 %collective-permute-start.11 = (bf16[32,16,128]{2,1,0:T(8,128)(2,1)S(1)}, bf16[32,16,128]{2,1,0:T(8,128)(2,1)S(1)}, u32[]{:S(2)}, u32[]{:S(2)}) collective-permute-start(bf16[32,16,128]{2,1,0:T(8,128)(2,1)S(1)} %gate.1.refs_4_), channel_id=1, source_target_pairs={{0,1},{1,0},{2,3},{3,2},{4,5},{5,4},{6,7},{7,6},{8,9},{9,8},{10,11... | collective-permute-start | bytes 393224 | tf_op jit(solution)/shard_map/ppermute | solution.py:466

commit v9 on v8

--- a/solution.py
+++ b/solution.py
@@ -447,7 +447,7 @@
         out_shape=jax.ShapeDtypeStruct((n_rcv * n_own, 2 * r_dev, bins), jnp.float32),
         input_output_aliases=aliases,
         scratch_shapes=[
-            pltpu.VMEM((2, (count + 8) * bins, 128), jnp.float32),
+            pltpu.VMEM((2, (count // 8 | 1) * 8 * bins, 128), jnp.float32),
             pltpu.VMEM((count, 2 * r_dev, bins), jnp.float32),
             pltpu.SMEM(plan.shape, jnp.int32),
             pltpu.SemaphoreType.DMA((count,)),
@@ -513,10 +513,9 @@
     sources[2] = gate_call(turned[:-1], [sources[2]])[0]
     sources.append(swap(sources[2], "rcv", 1))
 
-    half = n_rcv // 2
     sizes = (n_rcv, w_dev, r_dev, bins)
-    stacks = stacks_call(None, plan, turned, sources, tuple(range(half)), *sizes)
-    stacks = stacks_call(stacks, plan, turned, sources, tuple(range(half, n_rcv)), *sizes)
+    stacks = stacks_call(None, plan, turned, sources, tuple(range(n_rcv - 1)), *sizes)
+    stacks = stacks_call(stacks, plan, turned, sources, (n_rcv - 1,), *sizes)
     return stacks.reshape(n_src, r_dev, 2, bins)
 
 

time: 43.1 us -> 42.3 us (0.981)
  Pallas kernels: 16.2 us -> 15.3 us
    pallas_call x2, Pallas kernels: 5.07 us -> 4.16 us  [stacks_call(): pl.pallas_call(functools.partial(stacks_kernel, shares, n_win, w_dev, r_d...]
where the time goes in v9:
time: 42.3 us; the launch traced here: 42.1 us
  Pallas kernels  15.3 us (36%)
  starting transfers between devices  13.8 us (33%)
  waiting for transfers between devices  11.8 us (28%)
  between operations  0.93 us (2%)
    ppermute x9, waiting for transfers between devices, swap(): return lax.ppermute(value, axis, [(i, i ^ by) for i in range(size)])  9.57 us
    ppermute x9, starting transfers between devices, swap(): return lax.ppermute(value, axis, [(i, i ^ by) for i in range(size)])  8.73 us
    pallas_call x1, Pallas kernels, spectra_call(): pl.pallas_call(functools.partial(spectra_kernel, n_win, n_rcv, r_dev), in...  8.63 us
    ppermute x2, starting transfers between devices, body(): near[i] = lax.ppermute(picked[i], 'rcv', pairs)  5.11 us
    pallas_call x2, Pallas kernels, stacks_call(): pl.pallas_call(functools.partial(stacks_kernel, shares, n_win, w_dev, r_d...  4.16 us
    ppermute x2, waiting for transfers between devices, body(): near[i] = lax.ppermute(picked[i], 'rcv', pairs)  2.25 us
    pallas_call x4, Pallas kernels, turn_call(): pl.pallas_call(functools.partial(turn_kernel, r_dev), in_specs=[vmem] * l...  2.15 us
  transfers between devices with their start and end apart: 11, of which 5 were waited for; matrix products, arithmetic and copies ran while one was open for 0% of the time, Pallas kernels for 11%

profile of v9, /device:TPU:0, one launch (start us, length us, event | category | flops | bytes accessed | tf_op | source)
XLA Modules:
  0.0 42.1 jit_solution(8145129897594386103)
XLA Ops:
  0.0 8.6 %spectra.1 = (bf16[768,256]{1,0:T(8,128)(2,1)S(1)}, bf16[768,256]{1,0:T(8,128)(2,1)S(1)}, bf16[768,256]{1,0:T(8,128)(2,1)S(1)}, bf16[768,256]{1,0:T(8,128)(2,1)S...) custom-call(s32[8]{0:T(128)} %valid_hbm.1, ...), custom_call_target="tpu_custom_call" | custom-call | flops 2415919104 | bytes 6291456 | tf_op jit(solution)/shard_map/spectra/pallas_call | solution.py:207
  8.6 3.0 %collective-permute-start.7 = (bf16[768,256]{1,0:T(8,128)(2,1)S(1)}, bf16[768,256]{1,0:T(8,128)(2,1)S(1)}, u32[]{:S(2)}, u32[]{:S(2)}) collective-permute-start(bf16[768,256]{1,0:T(8,128)(2,1)S(1)} %get-tuple-element.51), channel_id=1, source_target_pairs={{0,8},{4,12},{8,0},{12,4},{1,9},{5,13},{9,1},{13,5},{2,10},{6,14},... | collective-permute-start | bytes 1179656 | tf_op jit(solution)/shard_map/ppermute | solution.py:466
  11.7 0.7 %collective-permute-start.2 = (bf16[4,64,256]{2,1,0:T(8,128)(2,1)S(1)}, bf16[4,64,256]{2,1,0:T(8,128)(2,1)S(1)}, u32[]{:S(2)}, u32[]{:S(2)}) collective-permute-start(bf16[4,64,256]{2,1,0:T(8,128)(2,1)S(1)} %get-tuple-element.44), channel_id=1, source_target_pairs={{1,2},{2,1},{5,6},{6,5},{9,10},{10,9},{13,14},{14,13},{17,18},{18,... | collective-permute-start | bytes 393224 | tf_op jit(solution)/shard_map/ppermute | solution.py:501
  12.3 4.5 %collective-permute-start.3 = (bf16[4,64,256]{2,1,0:T(8,128)(2,1)S(1)}, bf16[4,64,256]{2,1,0:T(8,128)(2,1)S(1)}, u32[]{:S(2)}, u32[]{:S(2)}) collective-permute-start(bf16[4,64,256]{2,1,0:T(8,128)(2,1)S(1)} %get-tuple-element.45), channel_id=1, source_target_pairs={{0,1},{1,0},{2,3},{3,2},{4,5},{5,4},{6,7},{7,6},{8,9},{9,8},{10,11... | collective-permute-start | bytes 393224 | tf_op jit(solution)/shard_map/ppermute | solution.py:501
  17.5 2.2 %collective-permute-done.3 = bf16[4,64,256]{2,1,0:T(8,128)(2,1)S(1)} collective-permute-done((bf16[4,64,256]{2,1,0:T(8,128)(2,1)S(1)}, bf16[4,64,256]{2,1,0:T(8,128)(2,1)S(1)}, u32[]{:S(2)}, u32[]{:S(2)}) %collective-permute-start.3) | collective-permute-done | bytes 131104 | tf_op jit(solution)/shard_map/ppermute | solution.py:501
  19.7 0.2 conditional.1
  20.0 0.1 collective-permute-start.4
  20.0 0.6 %collective-permute-start.5 = (bf16[64,256]{1,0:T(8,128)(2,1)S(1)}, bf16[64,256]{1,0:T(8,128)(2,1)S(1)}, u32[]{:S(2)}, u32[]{:S(2)}) collective-permute-start(bf16[64,256]{1,0:T(8,128)(2,1)S(1)} %get-tuple-element.49), channel_id=1, source_target_pairs={{0,8},{4,12},{8,0},{12,4},{1,9},{5,13},{9,1},{13,5},{2,10},{6,14},... | collective-permute-start | bytes 98312 | tf_op jit(solution)/shard_map/ppermute | solution.py:466
  20.6 1.3 %collective-permute-start.6 = (bf16[64,256]{1,0:T(8,128)(2,1)S(1)}, bf16[64,256]{1,0:T(8,128)(2,1)S(1)}, u32[]{:S(2)}, u32[]{:S(2)}) collective-permute-start(bf16[64,256]{1,0:T(8,128)(2,1)S(1)} %get-tuple-element.50), channel_id=1, source_target_pairs={{0,12},{4,8},{8,4},{12,0},{1,13},{5,9},{9,5},{13,1},{2,14},{6,10},... | collective-permute-start | bytes 98312 | tf_op jit(solution)/shard_map/ppermute | solution.py:466
  21.9 2.4 %collective-permute-done.5.refs_2_ = bf16[64,256]{1,0:T(8,128)(2,1)S(1)} collective-permute-done((bf16[64,256]{1,0:T(8,128)(2,1)S(1)}, bf16[64,256]{1,0:T(8,128)(2,1)S(1)}, u32[]{:S(2)}, u32[]{:S(2)}) %collective-permute-start.5) | collective-permute-done | bytes 32800 | tf_op jit(solution)/shard_map/ppermute | solution.py:466
  24.3 0.3 lefts.1
  24.7 0.2 collective-permute-start.8
  24.9 1.1 %collective-permute-start.9 = (bf16[768,256]{1,0:T(8,128)(2,1)S(1)}, bf16[768,256]{1,0:T(8,128)(2,1)S(1)}, u32[]{:S(2)}, u32[]{:S(2)}) collective-permute-start(bf16[768,256]{1,0:T(8,128)(2,1)S(1)} %get-tuple-element.55), channel_id=1, source_target_pairs={{0,12},{4,8},{8,4},{12,0},{1,13},{5,9},{9,5},{13,1},{2,14},{6,10},... | collective-permute-start | bytes 1179656 | tf_op jit(solution)/shard_map/ppermute | solution.py:466
  26.0 1.9 %collective-permute-start.10 = (bf16[32,16,128]{2,1,0:T(8,128)(2,1)S(1)}, bf16[32,16,128]{2,1,0:T(8,128)(2,1)S(1)}, u32[]{:S(2)}, u32[]{:S(2)}) collective-permute-start(bf16[32,16,128]{2,1,0:T(8,128)(2,1)S(1)} %get-tuple-element.56.refs_4_), channel_id=1, source_target_pairs={{0,2},{1,3},{2,0},{3,1},{4,6},{5,7},{6,4},{7,5},{8,10},{9,11},{10,... | collective-permute-start | bytes 393224 | tf_op jit(solution)/shard_map/ppermute | solution.py:466
  27.9 0.5 %turn.4.refs_0_ = bf16[128,16,256]{2,1,0:T(8,128)(2,1)S(1)} custom-call(bf16[768,256]{1,0:T(8,128)(2,1)S(1)} %get-tuple-element.41.refs_0_), custom_call_target="tpu_custom_call" | custom-call | flops 134217728 | bytes 2097152 | tf_op jit(solution)/shard_map/turn/pallas_call | solution.py:271
  28.5 0.5 %collective-permute-start.12 = (bf16[32,16,128]{2,1,0:T(8,128)(2,1)S(1)}, bf16[32,16,128]{2,1,0:T(8,128)(2,1)S(1)}, u32[]{:S(2)}, u32[]{:S(2)}) collective-permute-start(bf16[32,16,128]{2,1,0:T(8,128)(2,1)S(1)} %get-tuple-element.56.refs_4_), channel_id=1, source_target_pairs={{0,1},{1,0},{2,3},{3,2},{4,5},{5,4},{6,7},{7,6},{8,9},{9,8},{10,11... | collective-permute-start | bytes 393224 | tf_op jit(solution)/shard_map/ppermute | solution.py:466
  29.0 0.5 %turn.6.refs_2_ = bf16[128,16,256]{2,1,0:T(8,128)(2,1)S(1)} custom-call(bf16[768,256]{1,0:T(8,128)(2,1)S(1)} %collective-permute-done.7.refs_4_.refs_0_), custom_call_target="tpu_custom_call" | custom-call | flops 134217728 | bytes 2097152 | tf_op jit(solution)/shard_map/turn/pallas_call | solution.py:271
  29.5 0.5 %turn.5.refs_1_ = bf16[128,16,256]{2,1,0:T(8,128)(2,1)S(1)} custom-call(bf16[768,256]{1,0:T(8,128)(2,1)S(1)} %collective-permute-done.8.refs_0_), custom_call_target="tpu_custom_call" | custom-call | flops 134217728 | bytes 2097152 | tf_op jit(solution)/shard_map/turn/pallas_call | solution.py:271
  30.1 5.2 %collective-permute-done.10.refs_3_ = bf16[32,16,128]{2,1,0:T(8,128)(2,1)S(1)} collective-permute-done((bf16[32,16,128]{2,1,0:T(8,128)(2,1)S(1)}, bf16[32,16,128]{2,1,0:T(8,128)(2,1)S(1)}, u32[]{:S(2)}, u32[]{:S(2)}) %collective-permute-start.10) | collective-permute-done | bytes 131104 | tf_op jit(solution)/shard_map/ppermute | solution.py:466
  35.3 0.5 %collective-permute-done.9.refs_0_ = bf16[768,256]{1,0:T(8,128)(2,1)S(1)} collective-permute-done((bf16[768,256]{1,0:T(8,128)(2,1)S(1)}, bf16[768,256]{1,0:T(8,128)(2,1)S(1)}, u32[]{:S(2)}, u32[]{:S(2)}) %collective-permute-start.9) | collective-permute-done | bytes 393248 | tf_op jit(solution)/shard_map/ppermute | solution.py:466
  35.9 0.5 %turn.7.refs_3_ = bf16[128,16,256]{2,1,0:T(8,128)(2,1)S(1)} custom-call(bf16[768,256]{1,0:T(8,128)(2,1)S(1)} %collective-permute-done.9.refs_0_), custom_call_target="tpu_custom_call" | custom-call | flops 134217728 | bytes 2097152 | tf_op jit(solution)/shard_map/turn/pallas_call | solution.py:271
  36.4 2.4 %stacks.2.refs_5_ = f32[32,192,128]{2,1,0:T(8,128)} custom-call(s32[8,128]{1,0:T(8,128)S(1)} %get-tuple-element.40.plan_hbm, bf16[128,16,256]{2,1,0:T(8,128)(2,1)S(1)} %turn.4.refs_0_, bf16[128,16,256]{2,1,0:T(8,128)(2,1)S(1)} %turn.5.refs_1_, bf16[128,16,256]{2,1,0:T(8,128)(2,1)S(1)} %turn.6.refs_2_, bf16[128,16,256]{2,1,0:T(8,128)(2,1)S(1)} %turn.7.refs_3_, ...), custom_call_target="tpu_custom_call" | custom-call | flops 75497472 | bytes 6291456 | tf_op jit(solution)/shard_map/stacks/pallas_call | solution.py:443
  38.9 1.4 %collective-permute-done.11.refs_4_ = bf16[32,16,128]{2,1,0:T(8,128)(2,1)S(1)} collective-permute-done((bf16[32,16,128]{2,1,0:T(8,128)(2,1)S(1)}, bf16[32,16,128]{2,1,0:T(8,128)(2,1)S(1)}, u32[]{:S(2)}, u32[]{:S(2)}) %collective-permute-start.11) | collective-permute-done | bytes 131104 | tf_op jit(solution)/shard_map/ppermute | solution.py:466
  40.3 1.7 %stacks.3 = f32[32,192,128]{2,1,0:T(8,128)} custom-call(s32[8,128]{1,0:T(8,128)S(1)} %get-tuple-element.40.plan_hbm, bf16[128,16,256]{2,1,0:T(8,128)(2,1)S(1)} %turn.4.refs_0_, bf16[128,16,256]{2,1,0:T(8,128)(2,1)S(1)} %turn.5.refs_1_, bf16[128,16,256]{2,1,0:T(8,128)(2,1)S(1)} %turn.6.refs_2_, ...), custom_call_target="tpu_custom_call", output_to_operand_aliasing={{}: (6, {})} | custom-call | flops 25165824 | bytes 6291456 | tf_op jit(solution)/shard_map/stacks/pallas_call | solution.py:443
  (10 shorter events, 0.1 us)
Async XLA Ops:
  8.6 15.7 %collective-permute-start.7 = (bf16[768,256]{1,0:T(8,128)(2,1)S(1)}, bf16[768,256]{1,0:T(8,128)(2,1)S(1)}, u32[]{:S(2)}, u32[]{:S(2)}) collective-permute-start(bf16[768,256]{1,0:T(8,128)(2,1)S(1)} %get-tuple-element.51), channel_id=1, source_target_pairs={{0,8},{4,12},{8,0},{12,4},{1,9},{5,13},{9,1},{13,5},{2,10},{6,14},... | collective-permute-start | bytes 1179656 | tf_op jit(solution)/shard_map/ppermute | solution.py:466
  11.7 5.8 %collective-permute-start.2 = (bf16[4,64,256]{2,1,0:T(8,128)(2,1)S(1)}, bf16[4,64,256]{2,1,0:T(8,128)(2,1)S(1)}, u32[]{:S(2)}, u32[]{:S(2)}) collective-permute-start(bf16[4,64,256]{2,1,0:T(8,128)(2,1)S(1)} %get-tuple-element.44), channel_id=1, source_target_pairs={{1,2},{2,1},{5,6},{6,5},{9,10},{10,9},{13,14},{14,13},{17,18},{18,... | collective-permute-start | bytes 393224 | tf_op jit(solution)/shard_map/ppermute | solution.py:501
  12.3 7.4 %collective-permute-start.3 = (bf16[4,64,256]{2,1,0:T(8,128)(2,1)S(1)}, bf16[4,64,256]{2,1,0:T(8,128)(2,1)S(1)}, u32[]{:S(2)}, u32[]{:S(2)}) collective-permute-start(bf16[4,64,256]{2,1,0:T(8,128)(2,1)S(1)} %get-tuple-element.45), channel_id=1, source_target_pairs={{0,1},{1,0},{2,3},{3,2},{4,5},{5,4},{6,7},{7,6},{8,9},{9,8},{10,11... | collective-permute-start | bytes 393224 | tf_op jit(solution)/shard_map/ppermute | solution.py:501
  20.0 1.9 %collective-permute-start.4 = (bf16[64,256]{1,0:T(8,128)(2,1)S(1)}, bf16[64,256]{1,0:T(8,128)(2,1)S(1)}, u32[]{:S(2)}, u32[]{:S(2)}) collective-permute-start(bf16[64,256]{1,0:T(8,128)(2,1)S(1)} %get-tuple-element.48), channel_id=1, source_target_pairs={{0,4},{4,0},{8,12},{12,8},{1,5},{5,1},{9,13},{13,9},{2,6},{6,2},{1... | collective-permute-start | bytes 98312 | tf_op jit(solution)/shard_map/ppermute | solution.py:466
  20.0 4.3 %collective-permute-start.5 = (bf16[64,256]{1,0:T(8,128)(2,1)S(1)}, bf16[64,256]{1,0:T(8,128)(2,1)S(1)}, u32[]{:S(2)}, u32[]{:S(2)}) collective-permute-start(bf16[64,256]{1,0:T(8,128)(2,1)S(1)} %get-tuple-element.49), channel_id=1, source_target_pairs={{0,8},{4,12},{8,0},{12,4},{1,9},{5,13},{9,1},{13,5},{2,10},{6,14},... | collective-permute-start | bytes 98312 | tf_op jit(solution)/shard_map/ppermute | solution.py:466
  20.6 3.7 %collective-permute-start.6 = (bf16[64,256]{1,0:T(8,128)(2,1)S(1)}, bf16[64,256]{1,0:T(8,128)(2,1)S(1)}, u32[]{:S(2)}, u32[]{:S(2)}) collective-permute-start(bf16[64,256]{1,0:T(8,128)(2,1)S(1)} %get-tuple-element.50), channel_id=1, source_target_pairs={{0,12},{4,8},{8,4},{12,0},{1,13},{5,9},{9,5},{13,1},{2,14},{6,10},... | collective-permute-start | bytes 98312 | tf_op jit(solution)/shard_map/ppermute | solution.py:466
  24.7 4.8 %collective-permute-start.8 = (bf16[768,256]{1,0:T(8,128)(2,1)S(1)}, bf16[768,256]{1,0:T(8,128)(2,1)S(1)}, u32[]{:S(2)}, u32[]{:S(2)}) collective-permute-start(bf16[768,256]{1,0:T(8,128)(2,1)S(1)} %get-tuple-element.54), channel_id=1, source_target_pairs={{0,4},{4,0},{8,12},{12,8},{1,5},{5,1},{9,13},{13,9},{2,6},{6,2},{1... | collective-permute-start | bytes 1179656 | tf_op jit(solution)/shard_map/ppermute | solution.py:466
  24.9 11.0 %collective-permute-start.9 = (bf16[768,256]{1,0:T(8,128)(2,1)S(1)}, bf16[768,256]{1,0:T(8,128)(2,1)S(1)}, u32[]{:S(2)}, u32[]{:S(2)}) collective-permute-start(bf16[768,256]{1,0:T(8,128)(2,1)S(1)} %get-tuple-element.55), channel_id=1, source_target_pairs={{0,12},{4,8},{8,4},{12,0},{1,13},{5,9},{9,5},{13,1},{2,14},{6,10},... | collective-permute-start | bytes 1179656 | tf_op jit(solution)/shard_map/ppermute | solution.py:466
  26.0 9.3 %collective-permute-start.10 = (bf16[32,16,128]{2,1,0:T(8,128)(2,1)S(1)}, bf16[32,16,128]{2,1,0:T(8,128)(2,1)S(1)}, u32[]{:S(2)}, u32[]{:S(2)}) collective-permute-start(bf16[32,16,128]{2,1,0:T(8,128)(2,1)S(1)} %get-tuple-element.56.refs_4_), channel_id=1, source_target_pairs={{0,2},{1,3},{2,0},{3,1},{4,6},{5,7},{6,4},{7,5},{8,10},{9,11},{10,... | collective-permute-start | bytes 393224 | tf_op jit(solution)/shard_map/ppermute | solution.py:466
  28.5 8.0 %collective-permute-start.12 = (bf16[32,16,128]{2,1,0:T(8,128)(2,1)S(1)}, bf16[32,16,128]{2,1,0:T(8,128)(2,1)S(1)}, u32[]{:S(2)}, u32[]{:S(2)}) collective-permute-start(bf16[32,16,128]{2,1,0:T(8,128)(2,1)S(1)} %get-tuple-element.56.refs_4_), channel_id=1, source_target_pairs={{0,1},{1,0},{2,3},{3,2},{4,5},{5,4},{6,7},{7,6},{8,9},{9,8},{10,11... | collective-permute-start | bytes 393224 | tf_op jit(solution)/shard_map/ppermute | solution.py:466
  35.3 5.0 %collective-permute-start.11 = (bf16[32,16,128]{2,1,0:T(8,128)(2,1)S(1)}, bf16[32,16,128]{2,1,0:T(8,128)(2,1)S(1)}, u32[]{:S(2)}, u32[]{:S(2)}) collective-permute-start(bf16[32,16,128]{2,1,0:T(8,128)(2,1)S(1)} %gate.1.refs_6_), channel_id=1, source_target_pairs={{0,1},{1,0},{2,3},{3,2},{4,5},{5,4},{6,7},{7,6},{8,9},{9,8},{10,11... | collective-permute-start | bytes 393224 | tf_op jit(solution)/shard_map/ppermute | solution.py:466

commit v10 on v9

--- a/solution.py
+++ b/solution.py
@@ -135,9 +135,9 @@
     def add_quarters(k, first, last):
         part = slice(first, last)
         b0, b1, b2, b3 = (x_ref[k, part, q * quarter:(q + 1) * quarter] for q in range(4))
-        x0, x1, x2, x3 = (b.astype(jnp.float32) for b in (b0, b1, b2, b3))
-        even_ref[k, 0, part] = ((x0 + x2) + (x1 + x3)).astype(jnp.bfloat16)
-        even_ref[k, 1, part] = ((x0 + x2) - (x1 + x3)).astype(jnp.bfloat16)
+        first_sum, second_sum = b0 + b2, b1 + b3
+        even_ref[k, 0, part] = first_sum + second_sum
+        even_ref[k, 1, part] = first_sum - second_sum
         odd_ref[k, part] = b0 - b2
         odd_ref[k, rows + first:rows + last] = b1 - b3
 

time: 42.3 us -> 41.9 us (level)
  no operation moved by 1% of the time
where the time goes in v10:
time: 41.9 us; the launch traced here: 41.7 us
  Pallas kernels  15.3 us (37%)
  starting transfers between devices  14 us (33%)
  waiting for transfers between devices  11.7 us (28%)
  between operations  0.77 us (2%)
    ppermute x9, waiting for transfers between devices, swap(): return lax.ppermute(value, axis, [(i, i ^ by) for i in range(size)])  9.43 us
    ppermute x9, starting transfers between devices, swap(): return lax.ppermute(value, axis, [(i, i ^ by) for i in range(size)])  8.87 us
    pallas_call x1, Pallas kernels, spectra_call(): pl.pallas_call(functools.partial(spectra_kernel, n_win, n_rcv, r_dev), in...  8.57 us
    ppermute x2, starting transfers between devices, body(): near[i] = lax.ppermute(picked[i], 'rcv', pairs)  5.11 us
    pallas_call x2, Pallas kernels, stacks_call(): pl.pallas_call(functools.partial(stacks_kernel, shares, n_win, w_dev, r_d...  4.16 us
    ppermute x2, waiting for transfers between devices, body(): near[i] = lax.ppermute(picked[i], 'rcv', pairs)  2.24 us
    pallas_call x4, Pallas kernels, turn_call(): pl.pallas_call(functools.partial(turn_kernel, r_dev), in_specs=[vmem] * l...  2.16 us
  transfers between devices with their start and end apart: 11, of which 5 were waited for; matrix products, arithmetic and copies ran while one was open for 0% of the time, Pallas kernels for 11%

profile of v10, /device:TPU:0, one launch (start us, length us, event | category | flops | bytes accessed | tf_op | source)
XLA Modules:
  0.0 41.7 jit_solution(6355653551343099291)
XLA Ops:
  0.0 8.6 %spectra.1 = (bf16[768,256]{1,0:T(8,128)(2,1)S(1)}, bf16[768,256]{1,0:T(8,128)(2,1)S(1)}, bf16[768,256]{1,0:T(8,128)(2,1)S(1)}, bf16[768,256]{1,0:T(8,128)(2,1)S...) custom-call(s32[8]{0:T(128)} %valid_hbm.1, ...), custom_call_target="tpu_custom_call" | custom-call | flops 2415919104 | bytes 6291456 | tf_op jit(solution)/shard_map/spectra/pallas_call | solution.py:207
  8.6 3.0 %collective-permute-start.7 = (bf16[768,256]{1,0:T(8,128)(2,1)S(1)}, bf16[768,256]{1,0:T(8,128)(2,1)S(1)}, u32[]{:S(2)}, u32[]{:S(2)}) collective-permute-start(bf16[768,256]{1,0:T(8,128)(2,1)S(1)} %get-tuple-element.51), channel_id=1, source_target_pairs={{0,8},{4,12},{8,0},{12,4},{1,9},{5,13},{9,1},{13,5},{2,10},{6,14},... | collective-permute-start | bytes 1179656 | tf_op jit(solution)/shard_map/ppermute | solution.py:466
  11.6 0.7 %collective-permute-start.2 = (bf16[4,64,256]{2,1,0:T(8,128)(2,1)S(1)}, bf16[4,64,256]{2,1,0:T(8,128)(2,1)S(1)}, u32[]{:S(2)}, u32[]{:S(2)}) collective-permute-start(bf16[4,64,256]{2,1,0:T(8,128)(2,1)S(1)} %get-tuple-element.44), channel_id=1, source_target_pairs={{1,2},{2,1},{5,6},{6,5},{9,10},{10,9},{13,14},{14,13},{17,18},{18,... | collective-permute-start | bytes 393224 | tf_op jit(solution)/shard_map/ppermute | solution.py:501
  12.3 4.5 %collective-permute-start.3 = (bf16[4,64,256]{2,1,0:T(8,128)(2,1)S(1)}, bf16[4,64,256]{2,1,0:T(8,128)(2,1)S(1)}, u32[]{:S(2)}, u32[]{:S(2)}) collective-permute-start(bf16[4,64,256]{2,1,0:T(8,128)(2,1)S(1)} %get-tuple-element.45), channel_id=1, source_target_pairs={{0,1},{1,0},{2,3},{3,2},{4,5},{5,4},{6,7},{7,6},{8,9},{9,8},{10,11... | collective-permute-start | bytes 393224 | tf_op jit(solution)/shard_map/ppermute | solution.py:501
  17.4 2.2 %collective-permute-done.3 = bf16[4,64,256]{2,1,0:T(8,128)(2,1)S(1)} collective-permute-done((bf16[4,64,256]{2,1,0:T(8,128)(2,1)S(1)}, bf16[4,64,256]{2,1,0:T(8,128)(2,1)S(1)}, u32[]{:S(2)}, u32[]{:S(2)}) %collective-permute-start.3) | collective-permute-done | bytes 131104 | tf_op jit(solution)/shard_map/ppermute | solution.py:501
  19.7 0.1 collective-permute-start.4
  19.8 0.6 %collective-permute-start.5 = (bf16[64,256]{1,0:T(8,128)(2,1)S(1)}, bf16[64,256]{1,0:T(8,128)(2,1)S(1)}, u32[]{:S(2)}, u32[]{:S(2)}) collective-permute-start(bf16[64,256]{1,0:T(8,128)(2,1)S(1)} %get-tuple-element.49), channel_id=1, source_target_pairs={{0,8},{4,12},{8,0},{12,4},{1,9},{5,13},{9,1},{13,5},{2,10},{6,14},... | collective-permute-start | bytes 98312 | tf_op jit(solution)/shard_map/ppermute | solution.py:466
  20.4 1.3 %collective-permute-start.6 = (bf16[64,256]{1,0:T(8,128)(2,1)S(1)}, bf16[64,256]{1,0:T(8,128)(2,1)S(1)}, u32[]{:S(2)}, u32[]{:S(2)}) collective-permute-start(bf16[64,256]{1,0:T(8,128)(2,1)S(1)} %get-tuple-element.50), channel_id=1, source_target_pairs={{0,12},{4,8},{8,4},{12,0},{1,13},{5,9},{9,5},{13,1},{2,14},{6,10},... | collective-permute-start | bytes 98312 | tf_op jit(solution)/shard_map/ppermute | solution.py:466
  21.7 2.4 %collective-permute-done.5.refs_2_ = bf16[64,256]{1,0:T(8,128)(2,1)S(1)} collective-permute-done((bf16[64,256]{1,0:T(8,128)(2,1)S(1)}, bf16[64,256]{1,0:T(8,128)(2,1)S(1)}, u32[]{:S(2)}, u32[]{:S(2)}) %collective-permute-start.5) | collective-permute-done | bytes 32800 | tf_op jit(solution)/shard_map/ppermute | solution.py:466
  24.1 0.3 lefts.1
  24.4 0.2 collective-permute-start.8
  24.7 1.1 %collective-permute-start.9 = (bf16[768,256]{1,0:T(8,128)(2,1)S(1)}, bf16[768,256]{1,0:T(8,128)(2,1)S(1)}, u32[]{:S(2)}, u32[]{:S(2)}) collective-permute-start(bf16[768,256]{1,0:T(8,128)(2,1)S(1)} %get-tuple-element.55), channel_id=1, source_target_pairs={{0,12},{4,8},{8,4},{12,0},{1,13},{5,9},{9,5},{13,1},{2,14},{6,10},... | collective-permute-start | bytes 1179656 | tf_op jit(solution)/shard_map/ppermute | solution.py:466
  25.8 1.9 %collective-permute-start.10 = (bf16[32,16,128]{2,1,0:T(8,128)(2,1)S(1)}, bf16[32,16,128]{2,1,0:T(8,128)(2,1)S(1)}, u32[]{:S(2)}, u32[]{:S(2)}) collective-permute-start(bf16[32,16,128]{2,1,0:T(8,128)(2,1)S(1)} %get-tuple-element.56.refs_4_), channel_id=1, source_target_pairs={{0,2},{1,3},{2,0},{3,1},{4,6},{5,7},{6,4},{7,5},{8,10},{9,11},{10,... | collective-permute-start | bytes 393224 | tf_op jit(solution)/shard_map/ppermute | solution.py:466
  27.7 0.5 %turn.4.refs_0_ = bf16[128,16,256]{2,1,0:T(8,128)(2,1)S(1)} custom-call(bf16[768,256]{1,0:T(8,128)(2,1)S(1)} %get-tuple-element.41.refs_0_), custom_call_target="tpu_custom_call" | custom-call | flops 134217728 | bytes 2097152 | tf_op jit(solution)/shard_map/turn/pallas_call | solution.py:271
  28.2 0.6 %collective-permute-start.12 = (bf16[32,16,128]{2,1,0:T(8,128)(2,1)S(1)}, bf16[32,16,128]{2,1,0:T(8,128)(2,1)S(1)}, u32[]{:S(2)}, u32[]{:S(2)}) collective-permute-start(bf16[32,16,128]{2,1,0:T(8,128)(2,1)S(1)} %get-tuple-element.56.refs_4_), channel_id=1, source_target_pairs={{0,1},{1,0},{2,3},{3,2},{4,5},{5,4},{6,7},{7,6},{8,9},{9,8},{10,11... | collective-permute-start | bytes 393224 | tf_op jit(solution)/shard_map/ppermute | solution.py:466
  28.8 0.5 %turn.6.refs_2_ = bf16[128,16,256]{2,1,0:T(8,128)(2,1)S(1)} custom-call(bf16[768,256]{1,0:T(8,128)(2,1)S(1)} %collective-permute-done.7.refs_4_.refs_0_), custom_call_target="tpu_custom_call" | custom-call | flops 134217728 | bytes 2097152 | tf_op jit(solution)/shard_map/turn/pallas_call | solution.py:271
  29.4 0.5 %turn.5.refs_1_ = bf16[128,16,256]{2,1,0:T(8,128)(2,1)S(1)} custom-call(bf16[768,256]{1,0:T(8,128)(2,1)S(1)} %collective-permute-done.8.refs_0_), custom_call_target="tpu_custom_call" | custom-call | flops 134217728 | bytes 2097152 | tf_op jit(solution)/shard_map/turn/pallas_call | solution.py:271
  29.9 5.1 %collective-permute-done.10.refs_3_ = bf16[32,16,128]{2,1,0:T(8,128)(2,1)S(1)} collective-permute-done((bf16[32,16,128]{2,1,0:T(8,128)(2,1)S(1)}, bf16[32,16,128]{2,1,0:T(8,128)(2,1)S(1)}, u32[]{:S(2)}, u32[]{:S(2)}) %collective-permute-start.10) | collective-permute-done | bytes 131104 | tf_op jit(solution)/shard_map/ppermute | solution.py:466
  35.0 0.0 collective-permute-start.11
  35.1 0.5 %collective-permute-done.9.refs_0_ = bf16[768,256]{1,0:T(8,128)(2,1)S(1)} collective-permute-done((bf16[768,256]{1,0:T(8,128)(2,1)S(1)}, bf16[768,256]{1,0:T(8,128)(2,1)S(1)}, u32[]{:S(2)}, u32[]{:S(2)}) %collective-permute-start.9) | collective-permute-done | bytes 393248 | tf_op jit(solution)/shard_map/ppermute | solution.py:466
  35.6 0.5 %turn.7.refs_3_ = bf16[128,16,256]{2,1,0:T(8,128)(2,1)S(1)} custom-call(bf16[768,256]{1,0:T(8,128)(2,1)S(1)} %collective-permute-done.9.refs_0_), custom_call_target="tpu_custom_call" | custom-call | flops 134217728 | bytes 2097152 | tf_op jit(solution)/shard_map/turn/pallas_call | solution.py:271
  36.2 2.4 %stacks.2.refs_5_ = f32[32,192,128]{2,1,0:T(8,128)} custom-call(s32[8,128]{1,0:T(8,128)S(1)} %get-tuple-element.40.plan_hbm, bf16[128,16,256]{2,1,0:T(8,128)(2,1)S(1)} %turn.4.refs_0_, bf16[128,16,256]{2,1,0:T(8,128)(2,1)S(1)} %turn.5.refs_1_, bf16[128,16,256]{2,1,0:T(8,128)(2,1)S(1)} %turn.6.refs_2_, bf16[128,16,256]{2,1,0:T(8,128)(2,1)S(1)} %turn.7.refs_3_, ...), custom_call_target="tpu_custom_call" | custom-call | flops 75497472 | bytes 6291456 | tf_op jit(solution)/shard_map/stacks/pallas_call | solution.py:443
  38.6 1.4 %collective-permute-done.11.refs_4_ = bf16[32,16,128]{2,1,0:T(8,128)(2,1)S(1)} collective-permute-done((bf16[32,16,128]{2,1,0:T(8,128)(2,1)S(1)}, bf16[32,16,128]{2,1,0:T(8,128)(2,1)S(1)}, u32[]{:S(2)}, u32[]{:S(2)}) %collective-permute-start.11) | collective-permute-done | bytes 131104 | tf_op jit(solution)/shard_map/ppermute | solution.py:466
  40.0 1.7 %stacks.3 = f32[32,192,128]{2,1,0:T(8,128)} custom-call(s32[8,128]{1,0:T(8,128)S(1)} %get-tuple-element.40.plan_hbm, bf16[128,16,256]{2,1,0:T(8,128)(2,1)S(1)} %turn.4.refs_0_, bf16[128,16,256]{2,1,0:T(8,128)(2,1)S(1)} %turn.5.refs_1_, bf16[128,16,256]{2,1,0:T(8,128)(2,1)S(1)} %turn.6.refs_2_, ...), custom_call_target="tpu_custom_call", output_to_operand_aliasing={{}: (6, {})} | custom-call | flops 25165824 | bytes 6291456 | tf_op jit(solution)/shard_map/stacks/pallas_call | solution.py:443
  (10 shorter events, 0.1 us)
Async XLA Ops:
  8.6 15.5 %collective-permute-start.7 = (bf16[768,256]{1,0:T(8,128)(2,1)S(1)}, bf16[768,256]{1,0:T(8,128)(2,1)S(1)}, u32[]{:S(2)}, u32[]{:S(2)}) collective-permute-start(bf16[768,256]{1,0:T(8,128)(2,1)S(1)} %get-tuple-element.51), channel_id=1, source_target_pairs={{0,8},{4,12},{8,0},{12,4},{1,9},{5,13},{9,1},{13,5},{2,10},{6,14},... | collective-permute-start | bytes 1179656 | tf_op jit(solution)/shard_map/ppermute | solution.py:466
  11.6 5.8 %collective-permute-start.2 = (bf16[4,64,256]{2,1,0:T(8,128)(2,1)S(1)}, bf16[4,64,256]{2,1,0:T(8,128)(2,1)S(1)}, u32[]{:S(2)}, u32[]{:S(2)}) collective-permute-start(bf16[4,64,256]{2,1,0:T(8,128)(2,1)S(1)} %get-tuple-element.44), channel_id=1, source_target_pairs={{1,2},{2,1},{5,6},{6,5},{9,10},{10,9},{13,14},{14,13},{17,18},{18,... | collective-permute-start | bytes 393224 | tf_op jit(solution)/shard_map/ppermute | solution.py:501
  12.3 7.4 %collective-permute-start.3 = (bf16[4,64,256]{2,1,0:T(8,128)(2,1)S(1)}, bf16[4,64,256]{2,1,0:T(8,128)(2,1)S(1)}, u32[]{:S(2)}, u32[]{:S(2)}) collective-permute-start(bf16[4,64,256]{2,1,0:T(8,128)(2,1)S(1)} %get-tuple-element.45), channel_id=1, source_target_pairs={{0,1},{1,0},{2,3},{3,2},{4,5},{5,4},{6,7},{7,6},{8,9},{9,8},{10,11... | collective-permute-start | bytes 393224 | tf_op jit(solution)/shard_map/ppermute | solution.py:501
  19.7 1.9 %collective-permute-start.4 = (bf16[64,256]{1,0:T(8,128)(2,1)S(1)}, bf16[64,256]{1,0:T(8,128)(2,1)S(1)}, u32[]{:S(2)}, u32[]{:S(2)}) collective-permute-start(bf16[64,256]{1,0:T(8,128)(2,1)S(1)} %get-tuple-element.48), channel_id=1, source_target_pairs={{0,4},{4,0},{8,12},{12,8},{1,5},{5,1},{9,13},{13,9},{2,6},{6,2},{1... | collective-permute-start | bytes 98312 | tf_op jit(solution)/shard_map/ppermute | solution.py:466
  19.8 4.3 %collective-permute-start.5 = (bf16[64,256]{1,0:T(8,128)(2,1)S(1)}, bf16[64,256]{1,0:T(8,128)(2,1)S(1)}, u32[]{:S(2)}, u32[]{:S(2)}) collective-permute-start(bf16[64,256]{1,0:T(8,128)(2,1)S(1)} %get-tuple-element.49), channel_id=1, source_target_pairs={{0,8},{4,12},{8,0},{12,4},{1,9},{5,13},{9,1},{13,5},{2,10},{6,14},... | collective-permute-start | bytes 98312 | tf_op jit(solution)/shard_map/ppermute | solution.py:466
  20.4 3.7 %collective-permute-start.6 = (bf16[64,256]{1,0:T(8,128)(2,1)S(1)}, bf16[64,256]{1,0:T(8,128)(2,1)S(1)}, u32[]{:S(2)}, u32[]{:S(2)}) collective-permute-start(bf16[64,256]{1,0:T(8,128)(2,1)S(1)} %get-tuple-element.50), channel_id=1, source_target_pairs={{0,12},{4,8},{8,4},{12,0},{1,13},{5,9},{9,5},{13,1},{2,14},{6,10},... | collective-permute-start | bytes 98312 | tf_op jit(solution)/shard_map/ppermute | solution.py:466
  24.4 5.0 %collective-permute-start.8 = (bf16[768,256]{1,0:T(8,128)(2,1)S(1)}, bf16[768,256]{1,0:T(8,128)(2,1)S(1)}, u32[]{:S(2)}, u32[]{:S(2)}) collective-permute-start(bf16[768,256]{1,0:T(8,128)(2,1)S(1)} %get-tuple-element.54), channel_id=1, source_target_pairs={{0,4},{4,0},{8,12},{12,8},{1,5},{5,1},{9,13},{13,9},{2,6},{6,2},{1... | collective-permute-start | bytes 1179656 | tf_op jit(solution)/shard_map/ppermute | solution.py:466
  24.7 10.9 %collective-permute-start.9 = (bf16[768,256]{1,0:T(8,128)(2,1)S(1)}, bf16[768,256]{1,0:T(8,128)(2,1)S(1)}, u32[]{:S(2)}, u32[]{:S(2)}) collective-permute-start(bf16[768,256]{1,0:T(8,128)(2,1)S(1)} %get-tuple-element.55), channel_id=1, source_target_pairs={{0,12},{4,8},{8,4},{12,0},{1,13},{5,9},{9,5},{13,1},{2,14},{6,10},... | collective-permute-start | bytes 1179656 | tf_op jit(solution)/shard_map/ppermute | solution.py:466
  25.8 9.3 %collective-permute-start.10 = (bf16[32,16,128]{2,1,0:T(8,128)(2,1)S(1)}, bf16[32,16,128]{2,1,0:T(8,128)(2,1)S(1)}, u32[]{:S(2)}, u32[]{:S(2)}) collective-permute-start(bf16[32,16,128]{2,1,0:T(8,128)(2,1)S(1)} %get-tuple-element.56.refs_4_), channel_id=1, source_target_pairs={{0,2},{1,3},{2,0},{3,1},{4,6},{5,7},{6,4},{7,5},{8,10},{9,11},{10,... | collective-permute-start | bytes 393224 | tf_op jit(solution)/shard_map/ppermute | solution.py:466
  28.2 7.9 %collective-permute-start.12 = (bf16[32,16,128]{2,1,0:T(8,128)(2,1)S(1)}, bf16[32,16,128]{2,1,0:T(8,128)(2,1)S(1)}, u32[]{:S(2)}, u32[]{:S(2)}) collective-permute-start(bf16[32,16,128]{2,1,0:T(8,128)(2,1)S(1)} %get-tuple-element.56.refs_4_), channel_id=1, source_target_pairs={{0,1},{1,0},{2,3},{3,2},{4,5},{5,4},{6,7},{7,6},{8,9},{9,8},{10,11... | collective-permute-start | bytes 393224 | tf_op jit(solution)/shard_map/ppermute | solution.py:466
  35.0 5.0 %collective-permute-start.11 = (bf16[32,16,128]{2,1,0:T(8,128)(2,1)S(1)}, bf16[32,16,128]{2,1,0:T(8,128)(2,1)S(1)}, u32[]{:S(2)}, u32[]{:S(2)}) collective-permute-start(bf16[32,16,128]{2,1,0:T(8,128)(2,1)S(1)} %gate.1.refs_6_), channel_id=1, source_target_pairs={{0,1},{1,0},{2,3},{3,2},{4,5},{5,4},{6,7},{7,6},{8,9},{9,8},{10,11... | collective-permute-start | bytes 393224 | tf_op jit(solution)/shard_map/ppermute | solution.py:466

commit v11 on v9

--- a/solution.py
+++ b/solution.py
@@ -104,13 +104,25 @@
         target = (seed_ref, twice_ref, src_ref, valid_ref)[k]
         return pltpu.make_async_copy(source, target, sems.at[k])
 
-    def chunk(k):
-        return pltpu.make_async_copy(x_hbm.at[pl.ds(k * rows, rows)], x_ref.at[k], x_sems.at[k])
+    pieces = x_sems.shape[1]
+    height = rows // pieces
+
+    def chunk(k, p):
+        return pltpu.make_async_copy(
+            x_hbm.at[pl.ds(k * rows + p * height, height)],
+            x_ref.at[k, pl.ds(p * height, height)],
+            x_sems.at[k, p],
+        )
+
+    def wait_for(k):
+        for p in range(pieces):
+            chunk(k, p).wait()
 
     for k in range(4):
         small(k).start()
     for k in range(chunks):
-        chunk(k).start()
+        for p in range(pieces):
+            chunk(k, p).start()
     small(0).wait()
     small(1).wait()
     make_tables(seed_ref, twice_ref, table_ref)
@@ -155,13 +167,13 @@
 
     parts = 4
     size = rows // parts
-    chunk(0).wait()
+    wait_for(0)
     add_quarters(0, 0, rows)
     row = lax.broadcasted_iota(jnp.int32, (rows, 1), 0)
     for k in range(chunks):
         more = k + 1 < chunks
         if more:
-            chunk(k + 1).wait()
+            wait_for(k + 1)
         spectra = []
         for m in range(4):
             if m % 2:
@@ -222,7 +234,7 @@
             pltpu.SMEM(valid.shape, jnp.int32),
             pltpu.SMEM(src_station.shape, jnp.int32),
             pltpu.SemaphoreType.DMA((4,)),
-            pltpu.SemaphoreType.DMA((chunks,)),
+            pltpu.SemaphoreType.DMA((chunks, 4)),
         ],
         compiler_params=pltpu.CompilerParams(vmem_limit_bytes=36 * 2**20),
         cost_estimate=pl.CostEstimate(

time: 42.3 us -> 43 us (1.017)
  Pallas kernels: 15.3 us -> 16 us
    pallas_call x1, Pallas kernels: 8.63 us -> 9.36 us  [spectra_call(): pl.pallas_call(functools.partial(spectra_kernel, n_win, n_rcv, r_dev), in...]
where the time goes in v11:
time: 43 us; the launch traced here: 42.9 us
  Pallas kernels  16 us (37%)
  starting transfers between devices  13.9 us (32%)
  waiting for transfers between devices  11.8 us (27%)
  between operations  0.93 us (2%)
    ppermute x9, waiting for transfers between devices, swap(): return lax.ppermute(value, axis, [(i, i ^ by) for i in range(size)])  9.56 us
    pallas_call x1, Pallas kernels, spectra_call(): pl.pallas_call(functools.partial(spectra_kernel, n_win, n_rcv, r_dev), in...  9.36 us
    ppermute x9, starting transfers between devices, swap(): return lax.ppermute(value, axis, [(i, i ^ by) for i in range(size)])  8.74 us
    ppermute x2, starting transfers between devices, body(): near[i] = lax.ppermute(picked[i], 'rcv', pairs)  5.11 us
    pallas_call x2, Pallas kernels, stacks_call(): pl.pallas_call(functools.partial(stacks_kernel, shares, n_win, w_dev, r_d...  4.16 us
    ppermute x2, waiting for transfers between devices, body(): near[i] = lax.ppermute(picked[i], 'rcv', pairs)  2.25 us
    pallas_call x4, Pallas kernels, turn_call(): pl.pallas_call(functools.partial(turn_kernel, r_dev), in_specs=[vmem] * l...  2.15 us
  transfers between devices with their start and end apart: 11, of which 5 were waited for; matrix products, arithmetic and copies ran while one was open for 0% of the time, Pallas kernels for 11%

profile of v11, /device:TPU:0, one launch (start us, length us, event | category | flops | bytes accessed | tf_op | source)
XLA Modules:
  0.0 42.9 jit_solution(15318121642716851241)
XLA Ops:
  0.0 9.4 %spectra.1 = (bf16[768,256]{1,0:T(8,128)(2,1)S(1)}, bf16[768,256]{1,0:T(8,128)(2,1)S(1)}, bf16[768,256]{1,0:T(8,128)(2,1)S(1)}, bf16[768,256]{1,0:T(8,128)(2,1)S...) custom-call(s32[8]{0:T(128)} %valid_hbm.1, ...), custom_call_target="tpu_custom_call" | custom-call | flops 2415919104 | bytes 6291456 | tf_op jit(solution)/shard_map/spectra/pallas_call | solution.py:219
  9.4 3.0 %collective-permute-start.7 = (bf16[768,256]{1,0:T(8,128)(2,1)S(1)}, bf16[768,256]{1,0:T(8,128)(2,1)S(1)}, u32[]{:S(2)}, u32[]{:S(2)}) collective-permute-start(bf16[768,256]{1,0:T(8,128)(2,1)S(1)} %get-tuple-element.51), channel_id=1, source_target_pairs={{0,8},{4,12},{8,0},{12,4},{1,9},{5,13},{9,1},{13,5},{2,10},{6,14},... | collective-permute-start | bytes 1179656 | tf_op jit(solution)/shard_map/ppermute | solution.py:478
  12.4 0.7 %collective-permute-start.2 = (bf16[4,64,256]{2,1,0:T(8,128)(2,1)S(1)}, bf16[4,64,256]{2,1,0:T(8,128)(2,1)S(1)}, u32[]{:S(2)}, u32[]{:S(2)}) collective-permute-start(bf16[4,64,256]{2,1,0:T(8,128)(2,1)S(1)} %get-tuple-element.44), channel_id=1, source_target_pairs={{1,2},{2,1},{5,6},{6,5},{9,10},{10,9},{13,14},{14,13},{17,18},{18,... | collective-permute-start | bytes 393224 | tf_op jit(solution)/shard_map/ppermute | solution.py:513
  13.1 4.5 %collective-permute-start.3 = (bf16[4,64,256]{2,1,0:T(8,128)(2,1)S(1)}, bf16[4,64,256]{2,1,0:T(8,128)(2,1)S(1)}, u32[]{:S(2)}, u32[]{:S(2)}) collective-permute-start(bf16[4,64,256]{2,1,0:T(8,128)(2,1)S(1)} %get-tuple-element.45), channel_id=1, source_target_pairs={{0,1},{1,0},{2,3},{3,2},{4,5},{5,4},{6,7},{7,6},{8,9},{9,8},{10,11... | collective-permute-start | bytes 393224 | tf_op jit(solution)/shard_map/ppermute | solution.py:513
  18.2 2.2 %collective-permute-done.3 = bf16[4,64,256]{2,1,0:T(8,128)(2,1)S(1)} collective-permute-done((bf16[4,64,256]{2,1,0:T(8,128)(2,1)S(1)}, bf16[4,64,256]{2,1,0:T(8,128)(2,1)S(1)}, u32[]{:S(2)}, u32[]{:S(2)}) %collective-permute-start.3) | collective-permute-done | bytes 131104 | tf_op jit(solution)/shard_map/ppermute | solution.py:513
  20.5 0.2 conditional.1
  20.7 0.1 collective-permute-start.4
  20.8 0.6 %collective-permute-start.5 = (bf16[64,256]{1,0:T(8,128)(2,1)S(1)}, bf16[64,256]{1,0:T(8,128)(2,1)S(1)}, u32[]{:S(2)}, u32[]{:S(2)}) collective-permute-start(bf16[64,256]{1,0:T(8,128)(2,1)S(1)} %get-tuple-element.49), channel_id=1, source_target_pairs={{0,8},{4,12},{8,0},{12,4},{1,9},{5,13},{9,1},{13,5},{2,10},{6,14},... | collective-permute-start | bytes 98312 | tf_op jit(solution)/shard_map/ppermute | solution.py:478
  21.3 1.3 %collective-permute-start.6 = (bf16[64,256]{1,0:T(8,128)(2,1)S(1)}, bf16[64,256]{1,0:T(8,128)(2,1)S(1)}, u32[]{:S(2)}, u32[]{:S(2)}) collective-permute-start(bf16[64,256]{1,0:T(8,128)(2,1)S(1)} %get-tuple-element.50), channel_id=1, source_target_pairs={{0,12},{4,8},{8,4},{12,0},{1,13},{5,9},{9,5},{13,1},{2,14},{6,10},... | collective-permute-start | bytes 98312 | tf_op jit(solution)/shard_map/ppermute | solution.py:478
  22.6 2.4 %collective-permute-done.5.refs_2_ = bf16[64,256]{1,0:T(8,128)(2,1)S(1)} collective-permute-done((bf16[64,256]{1,0:T(8,128)(2,1)S(1)}, bf16[64,256]{1,0:T(8,128)(2,1)S(1)}, u32[]{:S(2)}, u32[]{:S(2)}) %collective-permute-start.5) | collective-permute-done | bytes 32800 | tf_op jit(solution)/shard_map/ppermute | solution.py:478
  25.0 0.3 lefts.1
  25.4 0.2 collective-permute-start.8
  25.6 1.1 %collective-permute-start.9 = (bf16[768,256]{1,0:T(8,128)(2,1)S(1)}, bf16[768,256]{1,0:T(8,128)(2,1)S(1)}, u32[]{:S(2)}, u32[]{:S(2)}) collective-permute-start(bf16[768,256]{1,0:T(8,128)(2,1)S(1)} %get-tuple-element.55), channel_id=1, source_target_pairs={{0,12},{4,8},{8,4},{12,0},{1,13},{5,9},{9,5},{13,1},{2,14},{6,10},... | collective-permute-start | bytes 1179656 | tf_op jit(solution)/shard_map/ppermute | solution.py:478
  26.7 1.9 %collective-permute-start.10 = (bf16[32,16,128]{2,1,0:T(8,128)(2,1)S(1)}, bf16[32,16,128]{2,1,0:T(8,128)(2,1)S(1)}, u32[]{:S(2)}, u32[]{:S(2)}) collective-permute-start(bf16[32,16,128]{2,1,0:T(8,128)(2,1)S(1)} %get-tuple-element.56.refs_4_), channel_id=1, source_target_pairs={{0,2},{1,3},{2,0},{3,1},{4,6},{5,7},{6,4},{7,5},{8,10},{9,11},{10,... | collective-permute-start | bytes 393224 | tf_op jit(solution)/shard_map/ppermute | solution.py:478
  28.6 0.5 %turn.4.refs_0_ = bf16[128,16,256]{2,1,0:T(8,128)(2,1)S(1)} custom-call(bf16[768,256]{1,0:T(8,128)(2,1)S(1)} %get-tuple-element.41.refs_0_), custom_call_target="tpu_custom_call" | custom-call | flops 134217728 | bytes 2097152 | tf_op jit(solution)/shard_map/turn/pallas_call | solution.py:283
  29.2 0.5 %collective-permute-start.12 = (bf16[32,16,128]{2,1,0:T(8,128)(2,1)S(1)}, bf16[32,16,128]{2,1,0:T(8,128)(2,1)S(1)}, u32[]{:S(2)}, u32[]{:S(2)}) collective-permute-start(bf16[32,16,128]{2,1,0:T(8,128)(2,1)S(1)} %get-tuple-element.56.refs_4_), channel_id=1, source_target_pairs={{0,1},{1,0},{2,3},{3,2},{4,5},{5,4},{6,7},{7,6},{8,9},{9,8},{10,11... | collective-permute-start | bytes 393224 | tf_op jit(solution)/shard_map/ppermute | solution.py:478
  29.7 0.5 %turn.6.refs_2_ = bf16[128,16,256]{2,1,0:T(8,128)(2,1)S(1)} custom-call(bf16[768,256]{1,0:T(8,128)(2,1)S(1)} %collective-permute-done.7.refs_4_.refs_0_), custom_call_target="tpu_custom_call" | custom-call | flops 134217728 | bytes 2097152 | tf_op jit(solution)/shard_map/turn/pallas_call | solution.py:283
  30.2 0.5 %turn.5.refs_1_ = bf16[128,16,256]{2,1,0:T(8,128)(2,1)S(1)} custom-call(bf16[768,256]{1,0:T(8,128)(2,1)S(1)} %collective-permute-done.8.refs_0_), custom_call_target="tpu_custom_call" | custom-call | flops 134217728 | bytes 2097152 | tf_op jit(solution)/shard_map/turn/pallas_call | solution.py:283
  30.8 5.2 %collective-permute-done.10.refs_3_ = bf16[32,16,128]{2,1,0:T(8,128)(2,1)S(1)} collective-permute-done((bf16[32,16,128]{2,1,0:T(8,128)(2,1)S(1)}, bf16[32,16,128]{2,1,0:T(8,128)(2,1)S(1)}, u32[]{:S(2)}, u32[]{:S(2)}) %collective-permute-start.10) | collective-permute-done | bytes 131104 | tf_op jit(solution)/shard_map/ppermute | solution.py:478
  36.0 0.5 %collective-permute-done.9.refs_0_ = bf16[768,256]{1,0:T(8,128)(2,1)S(1)} collective-permute-done((bf16[768,256]{1,0:T(8,128)(2,1)S(1)}, bf16[768,256]{1,0:T(8,128)(2,1)S(1)}, u32[]{:S(2)}, u32[]{:S(2)}) %collective-permute-start.9) | collective-permute-done | bytes 393248 | tf_op jit(solution)/shard_map/ppermute | solution.py:478
  36.6 0.5 %turn.7.refs_3_ = bf16[128,16,256]{2,1,0:T(8,128)(2,1)S(1)} custom-call(bf16[768,256]{1,0:T(8,128)(2,1)S(1)} %collective-permute-done.9.refs_0_), custom_call_target="tpu_custom_call" | custom-call | flops 134217728 | bytes 2097152 | tf_op jit(solution)/shard_map/turn/pallas_call | solution.py:283
  37.1 2.4 %stacks.2.refs_5_ = f32[32,192,128]{2,1,0:T(8,128)} custom-call(s32[8,128]{1,0:T(8,128)S(1)} %get-tuple-element.40.plan_hbm, bf16[128,16,256]{2,1,0:T(8,128)(2,1)S(1)} %turn.4.refs_0_, bf16[128,16,256]{2,1,0:T(8,128)(2,1)S(1)} %turn.5.refs_1_, bf16[128,16,256]{2,1,0:T(8,128)(2,1)S(1)} %turn.6.refs_2_, bf16[128,16,256]{2,1,0:T(8,128)(2,1)S(1)} %turn.7.refs_3_, ...), custom_call_target="tpu_custom_call" | custom-call | flops 75497472 | bytes 6291456 | tf_op jit(solution)/shard_map/stacks/pallas_call | solution.py:455
  39.6 1.4 %collective-permute-done.11.refs_4_ = bf16[32,16,128]{2,1,0:T(8,128)(2,1)S(1)} collective-permute-done((bf16[32,16,128]{2,1,0:T(8,128)(2,1)S(1)}, bf16[32,16,128]{2,1,0:T(8,128)(2,1)S(1)}, u32[]{:S(2)}, u32[]{:S(2)}) %collective-permute-start.11) | collective-permute-done | bytes 131104 | tf_op jit(solution)/shard_map/ppermute | solution.py:478
  41.0 1.7 %stacks.3 = f32[32,192,128]{2,1,0:T(8,128)} custom-call(s32[8,128]{1,0:T(8,128)S(1)} %get-tuple-element.40.plan_hbm, bf16[128,16,256]{2,1,0:T(8,128)(2,1)S(1)} %turn.4.refs_0_, bf16[128,16,256]{2,1,0:T(8,128)(2,1)S(1)} %turn.5.refs_1_, bf16[128,16,256]{2,1,0:T(8,128)(2,1)S(1)} %turn.6.refs_2_, ...), custom_call_target="tpu_custom_call", output_to_operand_aliasing={{}: (6, {})} | custom-call | flops 25165824 | bytes 6291456 | tf_op jit(solution)/shard_map/stacks/pallas_call | solution.py:455
  (10 shorter events, 0.1 us)
Async XLA Ops:
  9.4 15.7 %collective-permute-start.7 = (bf16[768,256]{1,0:T(8,128)(2,1)S(1)}, bf16[768,256]{1,0:T(8,128)(2,1)S(1)}, u32[]{:S(2)}, u32[]{:S(2)}) collective-permute-start(bf16[768,256]{1,0:T(8,128)(2,1)S(1)} %get-tuple-element.51), channel_id=1, source_target_pairs={{0,8},{4,12},{8,0},{12,4},{1,9},{5,13},{9,1},{13,5},{2,10},{6,14},... | collective-permute-start | bytes 1179656 | tf_op jit(solution)/shard_map/ppermute | solution.py:478
  12.4 5.8 %collective-permute-start.2 = (bf16[4,64,256]{2,1,0:T(8,128)(2,1)S(1)}, bf16[4,64,256]{2,1,0:T(8,128)(2,1)S(1)}, u32[]{:S(2)}, u32[]{:S(2)}) collective-permute-start(bf16[4,64,256]{2,1,0:T(8,128)(2,1)S(1)} %get-tuple-element.44), channel_id=1, source_target_pairs={{1,2},{2,1},{5,6},{6,5},{9,10},{10,9},{13,14},{14,13},{17,18},{18,... | collective-permute-start | bytes 393224 | tf_op jit(solution)/shard_map/ppermute | solution.py:513
  13.1 7.4 %collective-permute-start.3 = (bf16[4,64,256]{2,1,0:T(8,128)(2,1)S(1)}, bf16[4,64,256]{2,1,0:T(8,128)(2,1)S(1)}, u32[]{:S(2)}, u32[]{:S(2)}) collective-permute-start(bf16[4,64,256]{2,1,0:T(8,128)(2,1)S(1)} %get-tuple-element.45), channel_id=1, source_target_pairs={{0,1},{1,0},{2,3},{3,2},{4,5},{5,4},{6,7},{7,6},{8,9},{9,8},{10,11... | collective-permute-start | bytes 393224 | tf_op jit(solution)/shard_map/ppermute | solution.py:513
  20.7 1.9 %collective-permute-start.4 = (bf16[64,256]{1,0:T(8,128)(2,1)S(1)}, bf16[64,256]{1,0:T(8,128)(2,1)S(1)}, u32[]{:S(2)}, u32[]{:S(2)}) collective-permute-start(bf16[64,256]{1,0:T(8,128)(2,1)S(1)} %get-tuple-element.48), channel_id=1, source_target_pairs={{0,4},{4,0},{8,12},{12,8},{1,5},{5,1},{9,13},{13,9},{2,6},{6,2},{1... | collective-permute-start | bytes 98312 | tf_op jit(solution)/shard_map/ppermute | solution.py:478
  20.8 4.3 %collective-permute-start.5 = (bf16[64,256]{1,0:T(8,128)(2,1)S(1)}, bf16[64,256]{1,0:T(8,128)(2,1)S(1)}, u32[]{:S(2)}, u32[]{:S(2)}) collective-permute-start(bf16[64,256]{1,0:T(8,128)(2,1)S(1)} %get-tuple-element.49), channel_id=1, source_target_pairs={{0,8},{4,12},{8,0},{12,4},{1,9},{5,13},{9,1},{13,5},{2,10},{6,14},... | collective-permute-start | bytes 98312 | tf_op jit(solution)/shard_map/ppermute | solution.py:478
  21.3 3.7 %collective-permute-start.6 = (bf16[64,256]{1,0:T(8,128)(2,1)S(1)}, bf16[64,256]{1,0:T(8,128)(2,1)S(1)}, u32[]{:S(2)}, u32[]{:S(2)}) collective-permute-start(bf16[64,256]{1,0:T(8,128)(2,1)S(1)} %get-tuple-element.50), channel_id=1, source_target_pairs={{0,12},{4,8},{8,4},{12,0},{1,13},{5,9},{9,5},{13,1},{2,14},{6,10},... | collective-permute-start | bytes 98312 | tf_op jit(solution)/shard_map/ppermute | solution.py:478
  25.4 4.8 %collective-permute-start.8 = (bf16[768,256]{1,0:T(8,128)(2,1)S(1)}, bf16[768,256]{1,0:T(8,128)(2,1)S(1)}, u32[]{:S(2)}, u32[]{:S(2)}) collective-permute-start(bf16[768,256]{1,0:T(8,128)(2,1)S(1)} %get-tuple-element.54), channel_id=1, source_target_pairs={{0,4},{4,0},{8,12},{12,8},{1,5},{5,1},{9,13},{13,9},{2,6},{6,2},{1... | collective-permute-start | bytes 1179656 | tf_op jit(solution)/shard_map/ppermute | solution.py:478
  25.6 10.9 %collective-permute-start.9 = (bf16[768,256]{1,0:T(8,128)(2,1)S(1)}, bf16[768,256]{1,0:T(8,128)(2,1)S(1)}, u32[]{:S(2)}, u32[]{:S(2)}) collective-permute-start(bf16[768,256]{1,0:T(8,128)(2,1)S(1)} %get-tuple-element.55), channel_id=1, source_target_pairs={{0,12},{4,8},{8,4},{12,0},{1,13},{5,9},{9,5},{13,1},{2,14},{6,10},... | collective-permute-start | bytes 1179656 | tf_op jit(solution)/shard_map/ppermute | solution.py:478
  26.7 9.3 %collective-permute-start.10 = (bf16[32,16,128]{2,1,0:T(8,128)(2,1)S(1)}, bf16[32,16,128]{2,1,0:T(8,128)(2,1)S(1)}, u32[]{:S(2)}, u32[]{:S(2)}) collective-permute-start(bf16[32,16,128]{2,1,0:T(8,128)(2,1)S(1)} %get-tuple-element.56.refs_4_), channel_id=1, source_target_pairs={{0,2},{1,3},{2,0},{3,1},{4,6},{5,7},{6,4},{7,5},{8,10},{9,11},{10,... | collective-permute-start | bytes 393224 | tf_op jit(solution)/shard_map/ppermute | solution.py:478
  29.2 7.9 %collective-permute-start.12 = (bf16[32,16,128]{2,1,0:T(8,128)(2,1)S(1)}, bf16[32,16,128]{2,1,0:T(8,128)(2,1)S(1)}, u32[]{:S(2)}, u32[]{:S(2)}) collective-permute-start(bf16[32,16,128]{2,1,0:T(8,128)(2,1)S(1)} %get-tuple-element.56.refs_4_), channel_id=1, source_target_pairs={{0,1},{1,0},{2,3},{3,2},{4,5},{5,4},{6,7},{7,6},{8,9},{9,8},{10,11... | collective-permute-start | bytes 393224 | tf_op jit(solution)/shard_map/ppermute | solution.py:478
  36.0 5.0 %collective-permute-start.11 = (bf16[32,16,128]{2,1,0:T(8,128)(2,1)S(1)}, bf16[32,16,128]{2,1,0:T(8,128)(2,1)S(1)}, u32[]{:S(2)}, u32[]{:S(2)}) collective-permute-start(bf16[32,16,128]{2,1,0:T(8,128)(2,1)S(1)} %gate.1.refs_6_), channel_id=1, source_target_pairs={{0,1},{1,0},{2,3},{3,2},{4,5},{5,4},{6,7},{7,6},{8,9},{9,8},{10,11... | collective-permute-start | bytes 393224 | tf_op jit(solution)/shard_map/ppermute | solution.py:478

commit v12 on v9

--- a/solution.py
+++ b/solution.py
@@ -305,8 +305,8 @@
     )(*picked)
 
 
-def lefts_kernel(n_win, w_dev, n_own, *refs):
-    out_ref, srow_ref, rows_ref = refs[-3:]
+def lefts_kernel(n_parts, n_win, w_dev, n_own, *refs):
+    *part_refs, out_ref, srow_ref, rows_ref = refs[-3 - n_parts:]
     rows, lanes = refs[0].shape
     bins = lanes // 2
     windows = n_win * w_dev
@@ -338,10 +338,14 @@
         )
         pairs = jnp.where(low, turned[:bins // 2], turned[bins // 2:])
         rows_ref[pl.ds(s, bins // 2, stride=n_own), :] = pairs
-    out_ref[...] = rows_ref[...].reshape(out_ref.shape).astype(jnp.bfloat16)
-
-
-def lefts_call(blocks, after, later, w_dev):
+    whole = rows_ref[...].reshape(out_ref.shape).astype(jnp.bfloat16)
+    out_ref[...] = whole
+    size = whole.shape[0] // n_parts
+    for k, part_ref in enumerate(part_refs):
+        part_ref[...] = whole[k * size:(k + 1) * size]
+
+
+def lefts_call(blocks, after, later, w_dev, n_parts):
     rows, lanes = blocks[0].shape
     n_win = len(blocks)
     n_own = rows // w_dev
@@ -349,10 +353,11 @@
     first = n_win + len(after)
     vmem, anywhere = pl.BlockSpec(memory_space=VMEM), pl.BlockSpec(memory_space=pl.ANY)
     out = pl.pallas_call(
-        functools.partial(lefts_kernel, n_win, w_dev, n_own),
+        functools.partial(lefts_kernel, n_parts, n_win, w_dev, n_own),
         in_specs=[vmem] * n_win + [anywhere] * (len(after) + len(later)),
-        out_specs=[anywhere] * len(later) + [vmem],
+        out_specs=[anywhere] * len(later) + [vmem] * (n_parts + 1),
         out_shape=[jax.ShapeDtypeStruct(x.shape, x.dtype) for x in later]
+        + [jax.ShapeDtypeStruct((lanes // 8 // n_parts, 2 * n_own, pad), jnp.bfloat16)] * n_parts
         + [jax.ShapeDtypeStruct((lanes // 8, 2 * n_own, pad), jnp.bfloat16)],
         input_output_aliases={first + k: k for k in range(len(later))},
         scratch_shapes=[
@@ -363,7 +368,7 @@
         cost_estimate=pl.CostEstimate(flops=2**26, bytes_accessed=2**19, transcendentals=0),
         name="lefts",
     )(*blocks, *after, *later)
-    return out[-1], out[:-1]
+    return out[-1], out[len(later):-1], out[:len(later)]
 
 
 def gate_kernel(*refs):
@@ -384,9 +389,12 @@
     )(*after, *arrays)
 
 
-def stacks_kernel(shares, n_win, w_dev, r_dev, n_own, bins, plan_hbm, *refs):
+def stacks_kernel(shares, parts, n_win, w_dev, r_dev, n_own, bins, plan_hbm, *refs):
     t_refs = refs[:n_win]
-    s_refs = refs[n_win:n_win + len(shares)]
+    s_refs, taken = [], n_win
+    for n_parts in parts:
+        s_refs.append(refs[taken:taken + n_parts])
+        taken += n_parts
     out_hbm, prod_ref, out_ref, plan_ref, sems, plan_sem = refs[-6:]
     plan_copy = pltpu.make_async_copy(plan_hbm, plan_ref, plan_sem)
     plan_copy.start()
@@ -398,7 +406,10 @@
 
     low = lax.broadcasted_iota(jnp.int32, (count, pad), 1) < pad // 2
     for group in range(bins // 4):
-        values = [s_ref[group].astype(jnp.float32) for s_ref in s_refs]
+        values = []
+        for part_refs in s_refs:
+            k, place = divmod(group, bins // 4 // len(part_refs))
+            values.append(part_refs[k][place].astype(jnp.float32))
         for p in range(2):
             rows = jnp.concatenate([v[p * n_own:(p + 1) * n_own] for v in values], axis=0)
             left = jnp.concatenate([jnp.where(low, rows, 0.0), jnp.where(low, 0.0, rows)], axis=0)
@@ -429,11 +440,12 @@
 
 def stacks_call(out, plan, turned, sources, shares, n_rcv, w_dev, r_dev, bins):
     n_win = len(turned)
-    n_own = sources[0].shape[1] // 2
+    n_own = sources[0][0].shape[1] // 2
+    parts = [len(sources[i]) for i in shares]
     windows = n_win * w_dev
     count = len(shares) * n_own
     whole = pl.BlockSpec(memory_space=VMEM)
-    args = [plan] + list(turned) + [sources[i] for i in shares]
+    args = [plan] + list(turned) + [part for i in shares for part in sources[i]]
     specs = [pl.BlockSpec(memory_space=pl.ANY)] + [whole] * (len(args) - 1)
     aliases = {}
     if out is not None:
@@ -441,7 +453,7 @@
         args.append(out)
         specs.append(pl.BlockSpec(memory_space=pl.ANY))
     return pl.pallas_call(
-        functools.partial(stacks_kernel, shares, n_win, w_dev, r_dev, n_own, bins),
+        functools.partial(stacks_kernel, shares, parts, n_win, w_dev, r_dev, n_own, bins),
         in_specs=specs,
         out_specs=pl.BlockSpec(memory_space=pltpu.HBM),
         out_shape=jax.ShapeDtypeStruct((n_rcv * n_own, 2 * r_dev, bins), jnp.float32),
@@ -506,12 +518,13 @@
     merged = [merged[0]] + [swap(merged[j], "win", j) for j in range(1, n_win)]
     late = [j for j in range(1, n_win) if j != early]
     received = {0: blocks[0], early: swap(blocks[early], "win", early)}
-    lefts, later = lefts_call(merged, [received[early]], [blocks[j] for j in late], w_dev)
+    lefts, halves, later = lefts_call(merged, [received[early]], [blocks[j] for j in late], w_dev, 2)
     received.update({j: swap(block, "win", j) for j, block in zip(late, later)})
-    sources = [lefts, swap(lefts, "rcv", 1), swap(lefts, "rcv", 2)]
     turned = [turn_call([received[j]], w_dev, r_dev) for j in range(n_win)]
-    sources[2] = gate_call(turned[:-1], [sources[2]])[0]
-    sources.append(swap(sources[2], "rcv", 1))
+    near = swap(lefts, "rcv", 1)
+    middle = [swap(half, "rcv", 2) for half in halves]
+    middle[:1] = gate_call(turned[:-1], middle[:1])
+    sources = [[lefts], [near], middle, [swap(half, "rcv", 1) for half in middle]]
 
     sizes = (n_rcv, w_dev, r_dev, bins)
     stacks = stacks_call(None, plan, turned, sources, tuple(range(n_rcv - 1)), *sizes)

time: 42.3 us -> 43.1 us (1.019)
  starting transfers between devices: 13.8 us -> 21.7 us
  waiting for transfers between devices: 11.8 us -> 4.77 us
    ppermute x9 -> x11, starting transfers between devices: 8.73 us -> 16.5 us  [swap(): return lax.ppermute(value, axis, [(i, i ^ by) for i in range(size)])]
    ppermute x9 -> x11, waiting for transfers between devices: 9.57 us -> 2.52 us  [swap(): return lax.ppermute(value, axis, [(i, i ^ by) for i in range(size)])]
  transfers between devices with their start and end apart: 11 -> 13, of which waited for: 5 -> 3; matrix products, arithmetic and copies ran while one was open for 0% -> 0% of each run, Pallas kernels for 11% -> 11%
where the time goes in v12:
time: 43.1 us; the launch traced here: 42.9 us
  starting transfers between devices  21.7 us (50%)
  Pallas kernels  15.3 us (35%)
  waiting for transfers between devices  4.77 us (11%)
  between operations  0.95 us (2%)
    ppermute x11, starting transfers between devices, swap(): return lax.ppermute(value, axis, [(i, i ^ by) for i in range(size)])  16.5 us
    pallas_call x1, Pallas kernels, spectra_call(): pl.pallas_call(functools.partial(spectra_kernel, n_win, n_rcv, r_dev), in...  8.63 us
    ppermute x2, starting transfers between devices, body(): near[i] = lax.ppermute(picked[i], 'rcv', pairs)  5.11 us
    pallas_call x2, Pallas kernels, stacks_call(): pl.pallas_call(functools.partial(stacks_kernel, shares, parts, n_win, w_d...  4.16 us
    ppermute x11, waiting for transfers between devices, swap(): return lax.ppermute(value, axis, [(i, i ^ by) for i in range(size)])  2.52 us
    ppermute x2, waiting for transfers between devices, body(): near[i] = lax.ppermute(picked[i], 'rcv', pairs)  2.25 us
    pallas_call x4, Pallas kernels, turn_call(): pl.pallas_call(functools.partial(turn_kernel, r_dev), in_specs=[vmem] * l...  2.16 us
  transfers between devices with their start and end apart: 13, of which 3 were waited for; matrix products, arithmetic and copies ran while one was open for 0% of the time, Pallas kernels for 11%

profile of v12, /device:TPU:0, one launch (start us, length us, event | category | flops | bytes accessed | tf_op | source)
XLA Modules:
  0.0 42.9 jit_solution(1854535027783613668)
XLA Ops:
  0.0 8.6 %spectra.1 = (bf16[768,256]{1,0:T(8,128)(2,1)S(1)}, bf16[768,256]{1,0:T(8,128)(2,1)S(1)}, bf16[768,256]{1,0:T(8,128)(2,1)S(1)}, bf16[768,256]{1,0:T(8,128)(2,1)S...) custom-call(s32[8]{0:T(128)} %valid_hbm.1, ...), custom_call_target="tpu_custom_call" | custom-call | flops 2415919104 | bytes 6291456 | tf_op jit(solution)/shard_map/spectra/pallas_call | solution.py:207
  8.6 3.0 %collective-permute-start.7 = (bf16[768,256]{1,0:T(8,128)(2,1)S(1)}, bf16[768,256]{1,0:T(8,128)(2,1)S(1)}, u32[]{:S(2)}, u32[]{:S(2)}) collective-permute-start(bf16[768,256]{1,0:T(8,128)(2,1)S(1)} %get-tuple-element.53), channel_id=1, source_target_pairs={{0,8},{4,12},{8,0},{12,4},{1,9},{5,13},{9,1},{13,5},{2,10},{6,14},... | collective-permute-start | bytes 1179656 | tf_op jit(solution)/shard_map/ppermute | solution.py:478
  11.7 0.7 %collective-permute-start.2 = (bf16[4,64,256]{2,1,0:T(8,128)(2,1)S(1)}, bf16[4,64,256]{2,1,0:T(8,128)(2,1)S(1)}, u32[]{:S(2)}, u32[]{:S(2)}) collective-permute-start(bf16[4,64,256]{2,1,0:T(8,128)(2,1)S(1)} %get-tuple-element.46), channel_id=1, source_target_pairs={{1,2},{2,1},{5,6},{6,5},{9,10},{10,9},{13,14},{14,13},{17,18},{18,... | collective-permute-start | bytes 393224 | tf_op jit(solution)/shard_map/ppermute | solution.py:513
  12.3 4.5 %collective-permute-start.3 = (bf16[4,64,256]{2,1,0:T(8,128)(2,1)S(1)}, bf16[4,64,256]{2,1,0:T(8,128)(2,1)S(1)}, u32[]{:S(2)}, u32[]{:S(2)}) collective-permute-start(bf16[4,64,256]{2,1,0:T(8,128)(2,1)S(1)} %get-tuple-element.47), channel_id=1, source_target_pairs={{0,1},{1,0},{2,3},{3,2},{4,5},{5,4},{6,7},{7,6},{8,9},{9,8},{10,11... | collective-permute-start | bytes 393224 | tf_op jit(solution)/shard_map/ppermute | solution.py:513
  17.5 2.2 %collective-permute-done.3 = bf16[4,64,256]{2,1,0:T(8,128)(2,1)S(1)} collective-permute-done((bf16[4,64,256]{2,1,0:T(8,128)(2,1)S(1)}, bf16[4,64,256]{2,1,0:T(8,128)(2,1)S(1)}, u32[]{:S(2)}, u32[]{:S(2)}) %collective-permute-start.3) | collective-permute-done | bytes 131104 | tf_op jit(solution)/shard_map/ppermute | solution.py:513
  19.7 0.2 conditional.1
  20.0 0.6 %collective-permute-start.5 = (bf16[64,256]{1,0:T(8,128)(2,1)S(1)}, bf16[64,256]{1,0:T(8,128)(2,1)S(1)}, u32[]{:S(2)}, u32[]{:S(2)}) collective-permute-start(bf16[64,256]{1,0:T(8,128)(2,1)S(1)} %get-tuple-element.51), channel_id=1, source_target_pairs={{0,8},{4,12},{8,0},{12,4},{1,9},{5,13},{9,1},{13,5},{2,10},{6,14},... | collective-permute-start | bytes 98312 | tf_op jit(solution)/shard_map/ppermute | solution.py:478
  20.6 1.3 %collective-permute-start.6 = (bf16[64,256]{1,0:T(8,128)(2,1)S(1)}, bf16[64,256]{1,0:T(8,128)(2,1)S(1)}, u32[]{:S(2)}, u32[]{:S(2)}) collective-permute-start(bf16[64,256]{1,0:T(8,128)(2,1)S(1)} %get-tuple-element.52), channel_id=1, source_target_pairs={{0,12},{4,8},{8,4},{12,0},{1,13},{5,9},{9,5},{13,1},{2,14},{6,10},... | collective-permute-start | bytes 98312 | tf_op jit(solution)/shard_map/ppermute | solution.py:478
  21.9 2.4 %collective-permute-done.5.refs_2_ = bf16[64,256]{1,0:T(8,128)(2,1)S(1)} collective-permute-done((bf16[64,256]{1,0:T(8,128)(2,1)S(1)}, bf16[64,256]{1,0:T(8,128)(2,1)S(1)}, u32[]{:S(2)}, u32[]{:S(2)}) %collective-permute-start.5) | collective-permute-done | bytes 32800 | tf_op jit(solution)/shard_map/ppermute | solution.py:478
  24.3 0.3 lefts.1
  24.7 0.2 collective-permute-start.8
  24.9 1.1 %collective-permute-start.9 = (bf16[768,256]{1,0:T(8,128)(2,1)S(1)}, bf16[768,256]{1,0:T(8,128)(2,1)S(1)}, u32[]{:S(2)}, u32[]{:S(2)}) collective-permute-start(bf16[768,256]{1,0:T(8,128)(2,1)S(1)} %get-tuple-element.57), channel_id=1, source_target_pairs={{0,12},{4,8},{8,4},{12,0},{1,13},{5,9},{9,5},{13,1},{2,14},{6,10},... | collective-permute-start | bytes 1179656 | tf_op jit(solution)/shard_map/ppermute | solution.py:478
  26.0 1.9 %collective-permute-start.12 = (bf16[16,16,128]{2,1,0:T(8,128)(2,1)S(1)}, bf16[16,16,128]{2,1,0:T(8,128)(2,1)S(1)}, u32[]{:S(2)}, u32[]{:S(2)}) collective-permute-start(bf16[16,16,128]{2,1,0:T(8,128)(2,1)S(1)} %get-tuple-element.59), channel_id=1, source_target_pairs={{0,2},{1,3},{2,0},{3,1},{4,6},{5,7},{6,4},{7,5},{8,10},{9,11},{10,... | collective-permute-start | bytes 196616 | tf_op jit(solution)/shard_map/ppermute | solution.py:478
  27.9 0.4 %collective-permute-start.14 = (bf16[32,16,128]{2,1,0:T(8,128)(2,1)S(1)}, bf16[32,16,128]{2,1,0:T(8,128)(2,1)S(1)}, u32[]{:S(2)}, u32[]{:S(2)}) collective-permute-start(bf16[32,16,128]{2,1,0:T(8,128)(2,1)S(1)} %get-tuple-element.60.refs_4_), channel_id=1, source_target_pairs={{0,1},{1,0},{2,3},{3,2},{4,5},{5,4},{6,7},{7,6},{8,9},{9,8},{10,11... | collective-permute-start | bytes 393224 | tf_op jit(solution)/shard_map/ppermute | solution.py:478
  28.3 2.6 %collective-permute-start.10 = (bf16[16,16,128]{2,1,0:T(8,128)(2,1)S(1)}, bf16[16,16,128]{2,1,0:T(8,128)(2,1)S(1)}, u32[]{:S(2)}, u32[]{:S(2)}) collective-permute-start(bf16[16,16,128]{2,1,0:T(8,128)(2,1)S(1)} %get-tuple-element.58), channel_id=1, source_target_pairs={{0,2},{1,3},{2,0},{3,1},{4,6},{5,7},{6,4},{7,5},{8,10},{9,11},{10,... | collective-permute-start | bytes 196616 | tf_op jit(solution)/shard_map/ppermute | solution.py:478
  31.0 0.5 %turn.4.refs_0_ = bf16[128,16,256]{2,1,0:T(8,128)(2,1)S(1)} custom-call(bf16[768,256]{1,0:T(8,128)(2,1)S(1)} %get-tuple-element.43.refs_0_), custom_call_target="tpu_custom_call" | custom-call | flops 134217728 | bytes 2097152 | tf_op jit(solution)/shard_map/turn/pallas_call | solution.py:271
  31.5 0.5 %turn.6.refs_2_ = bf16[128,16,256]{2,1,0:T(8,128)(2,1)S(1)} custom-call(bf16[768,256]{1,0:T(8,128)(2,1)S(1)} %collective-permute-done.7.refs_4_.refs_0_), custom_call_target="tpu_custom_call" | custom-call | flops 134217728 | bytes 2097152 | tf_op jit(solution)/shard_map/turn/pallas_call | solution.py:271
  32.1 1.8 %collective-permute-start.13 = (bf16[16,16,128]{2,1,0:T(8,128)(2,1)S(1)}, bf16[16,16,128]{2,1,0:T(8,128)(2,1)S(1)}, u32[]{:S(2)}, u32[]{:S(2)}) collective-permute-start(bf16[16,16,128]{2,1,0:T(8,128)(2,1)S(1)} %collective-permute-done.12.refs_7_), channel_id=1, source_target_pairs={{0,1},{1,0},{2,3},{3,2},{4,5},{5,4},{6,7},{7,6},{8,9},{9,8},{10,11... | collective-permute-start | bytes 196616 | tf_op jit(solution)/shard_map/ppermute | solution.py:478
  33.9 0.5 %turn.5.refs_1_ = bf16[128,16,256]{2,1,0:T(8,128)(2,1)S(1)} custom-call(bf16[768,256]{1,0:T(8,128)(2,1)S(1)} %collective-permute-done.8.refs_0_), custom_call_target="tpu_custom_call" | custom-call | flops 134217728 | bytes 2097152 | tf_op jit(solution)/shard_map/turn/pallas_call | solution.py:271
  34.4 0.1 collective-permute-done.10.refs_3_
  34.5 3.5 %collective-permute-start.11 = (bf16[16,16,128]{2,1,0:T(8,128)(2,1)S(1)}, bf16[16,16,128]{2,1,0:T(8,128)(2,1)S(1)}, u32[]{:S(2)}, u32[]{:S(2)}) collective-permute-start(bf16[16,16,128]{2,1,0:T(8,128)(2,1)S(1)} %gate.1.refs_6_), channel_id=1, source_target_pairs={{0,1},{1,0},{2,3},{3,2},{4,5},{5,4},{6,7},{7,6},{8,9},{9,8},{10,11... | collective-permute-start | bytes 196616 | tf_op jit(solution)/shard_map/ppermute | solution.py:478
  38.0 0.5 %turn.7.refs_3_ = bf16[128,16,256]{2,1,0:T(8,128)(2,1)S(1)} custom-call(bf16[768,256]{1,0:T(8,128)(2,1)S(1)} %collective-permute-done.9.refs_0_), custom_call_target="tpu_custom_call" | custom-call | flops 134217728 | bytes 2097152 | tf_op jit(solution)/shard_map/turn/pallas_call | solution.py:271
  38.6 2.4 %stacks.2.refs_6_ = f32[32,192,128]{2,1,0:T(8,128)} custom-call(s32[8,128]{1,0:T(8,128)S(1)} %get-tuple-element.42.plan_hbm, bf16[128,16,256]{2,1,0:T(8,128)(2,1)S(1)} %turn.4.refs_0_, bf16[128,16,256]{2,1,0:T(8,128)(2,1)S(1)} %turn.5.refs_1_, bf16[128,16,256]{2,1,0:T(8,128)(2,1)S(1)} %turn.6.refs_2_, bf16[128,16,256]{2,1,0:T(8,128)(2,1)S(1)} %turn.7.refs_3_, ...), custom_call_target="tpu_custom_call" | custom-call | flops 75497472 | bytes 6291456 | tf_op jit(solution)/shard_map/stacks/pallas_call | solution.py:455
  41.0 1.7 %stacks.3 = f32[32,192,128]{2,1,0:T(8,128)} custom-call(s32[8,128]{1,0:T(8,128)S(1)} %get-tuple-element.42.plan_hbm, bf16[128,16,256]{2,1,0:T(8,128)(2,1)S(1)} %turn.4.refs_0_, bf16[128,16,256]{2,1,0:T(8,128)(2,1)S(1)} %turn.5.refs_1_, bf16[128,16,256]{2,1,0:T(8,128)(2,1)S(1)} %turn.6.refs_2_, ...), custom_call_target="tpu_custom_call", output_to_operand_aliasing={{}: (7, {})} | custom-call | flops 25165824 | bytes 6291456 | tf_op jit(solution)/shard_map/stacks/pallas_call | solution.py:455
  (14 shorter events, 0.2 us)
Async XLA Ops:
  8.6 15.7 %collective-permute-start.7 = (bf16[768,256]{1,0:T(8,128)(2,1)S(1)}, bf16[768,256]{1,0:T(8,128)(2,1)S(1)}, u32[]{:S(2)}, u32[]{:S(2)}) collective-permute-start(bf16[768,256]{1,0:T(8,128)(2,1)S(1)} %get-tuple-element.53), channel_id=1, source_target_pairs={{0,8},{4,12},{8,0},{12,4},{1,9},{5,13},{9,1},{13,5},{2,10},{6,14},... | collective-permute-start | bytes 1179656 | tf_op jit(solution)/shard_map/ppermute | solution.py:478
  11.7 5.8 %collective-permute-start.2 = (bf16[4,64,256]{2,1,0:T(8,128)(2,1)S(1)}, bf16[4,64,256]{2,1,0:T(8,128)(2,1)S(1)}, u32[]{:S(2)}, u32[]{:S(2)}) collective-permute-start(bf16[4,64,256]{2,1,0:T(8,128)(2,1)S(1)} %get-tuple-element.46), channel_id=1, source_target_pairs={{1,2},{2,1},{5,6},{6,5},{9,10},{10,9},{13,14},{14,13},{17,18},{18,... | collective-permute-start | bytes 393224 | tf_op jit(solution)/shard_map/ppermute | solution.py:513
  12.3 7.4 %collective-permute-start.3 = (bf16[4,64,256]{2,1,0:T(8,128)(2,1)S(1)}, bf16[4,64,256]{2,1,0:T(8,128)(2,1)S(1)}, u32[]{:S(2)}, u32[]{:S(2)}) collective-permute-start(bf16[4,64,256]{2,1,0:T(8,128)(2,1)S(1)} %get-tuple-element.47), channel_id=1, source_target_pairs={{0,1},{1,0},{2,3},{3,2},{4,5},{5,4},{6,7},{7,6},{8,9},{9,8},{10,11... | collective-permute-start | bytes 393224 | tf_op jit(solution)/shard_map/ppermute | solution.py:513
  20.0 1.9 %collective-permute-start.4 = (bf16[64,256]{1,0:T(8,128)(2,1)S(1)}, bf16[64,256]{1,0:T(8,128)(2,1)S(1)}, u32[]{:S(2)}, u32[]{:S(2)}) collective-permute-start(bf16[64,256]{1,0:T(8,128)(2,1)S(1)} %get-tuple-element.50), channel_id=1, source_target_pairs={{0,4},{4,0},{8,12},{12,8},{1,5},{5,1},{9,13},{13,9},{2,6},{6,2},{1... | collective-permute-start | bytes 98312 | tf_op jit(solution)/shard_map/ppermute | solution.py:478
  20.0 4.3 %collective-permute-start.5 = (bf16[64,256]{1,0:T(8,128)(2,1)S(1)}, bf16[64,256]{1,0:T(8,128)(2,1)S(1)}, u32[]{:S(2)}, u32[]{:S(2)}) collective-permute-start(bf16[64,256]{1,0:T(8,128)(2,1)S(1)} %get-tuple-element.51), channel_id=1, source_target_pairs={{0,8},{4,12},{8,0},{12,4},{1,9},{5,13},{9,1},{13,5},{2,10},{6,14},... | collective-permute-start | bytes 98312 | tf_op jit(solution)/shard_map/ppermute | solution.py:478
  20.6 3.7 %collective-permute-start.6 = (bf16[64,256]{1,0:T(8,128)(2,1)S(1)}, bf16[64,256]{1,0:T(8,128)(2,1)S(1)}, u32[]{:S(2)}, u32[]{:S(2)}) collective-permute-start(bf16[64,256]{1,0:T(8,128)(2,1)S(1)} %get-tuple-element.52), channel_id=1, source_target_pairs={{0,12},{4,8},{8,4},{12,0},{1,13},{5,9},{9,5},{13,1},{2,14},{6,10},... | collective-permute-start | bytes 98312 | tf_op jit(solution)/shard_map/ppermute | solution.py:478
  24.7 9.2 %collective-permute-start.8 = (bf16[768,256]{1,0:T(8,128)(2,1)S(1)}, bf16[768,256]{1,0:T(8,128)(2,1)S(1)}, u32[]{:S(2)}, u32[]{:S(2)}) collective-permute-start(bf16[768,256]{1,0:T(8,128)(2,1)S(1)} %get-tuple-element.56), channel_id=1, source_target_pairs={{0,4},{4,0},{8,12},{12,8},{1,5},{5,1},{9,13},{13,9},{2,6},{6,2},{1... | collective-permute-start | bytes 1179656 | tf_op jit(solution)/shard_map/ppermute | solution.py:478
  24.9 13.1 %collective-permute-start.9 = (bf16[768,256]{1,0:T(8,128)(2,1)S(1)}, bf16[768,256]{1,0:T(8,128)(2,1)S(1)}, u32[]{:S(2)}, u32[]{:S(2)}) collective-permute-start(bf16[768,256]{1,0:T(8,128)(2,1)S(1)} %get-tuple-element.57), channel_id=1, source_target_pairs={{0,12},{4,8},{8,4},{12,0},{1,13},{5,9},{9,5},{13,1},{2,14},{6,10},... | collective-permute-start | bytes 1179656 | tf_op jit(solution)/shard_map/ppermute | solution.py:478
  26.0 6.0 %collective-permute-start.12 = (bf16[16,16,128]{2,1,0:T(8,128)(2,1)S(1)}, bf16[16,16,128]{2,1,0:T(8,128)(2,1)S(1)}, u32[]{:S(2)}, u32[]{:S(2)}) collective-permute-start(bf16[16,16,128]{2,1,0:T(8,128)(2,1)S(1)} %get-tuple-element.59), channel_id=1, source_target_pairs={{0,2},{1,3},{2,0},{3,1},{4,6},{5,7},{6,4},{7,5},{8,10},{9,11},{10,... | collective-permute-start | bytes 196616 | tf_op jit(solution)/shard_map/ppermute | solution.py:478
  27.9 10.6 %collective-permute-start.14 = (bf16[32,16,128]{2,1,0:T(8,128)(2,1)S(1)}, bf16[32,16,128]{2,1,0:T(8,128)(2,1)S(1)}, u32[]{:S(2)}, u32[]{:S(2)}) collective-permute-start(bf16[32,16,128]{2,1,0:T(8,128)(2,1)S(1)} %get-tuple-element.60.refs_4_), channel_id=1, source_target_pairs={{0,1},{1,0},{2,3},{3,2},{4,5},{5,4},{6,7},{7,6},{8,9},{9,8},{10,11... | collective-permute-start | bytes 393224 | tf_op jit(solution)/shard_map/ppermute | solution.py:478
  28.3 6.2 %collective-permute-start.10 = (bf16[16,16,128]{2,1,0:T(8,128)(2,1)S(1)}, bf16[16,16,128]{2,1,0:T(8,128)(2,1)S(1)}, u32[]{:S(2)}, u32[]{:S(2)}) collective-permute-start(bf16[16,16,128]{2,1,0:T(8,128)(2,1)S(1)} %get-tuple-element.58), channel_id=1, source_target_pairs={{0,2},{1,3},{2,0},{3,1},{4,6},{5,7},{6,4},{7,5},{8,10},{9,11},{10,... | collective-permute-start | bytes 196616 | tf_op jit(solution)/shard_map/ppermute | solution.py:478
  32.1 9.0 %collective-permute-start.13 = (bf16[16,16,128]{2,1,0:T(8,128)(2,1)S(1)}, bf16[16,16,128]{2,1,0:T(8,128)(2,1)S(1)}, u32[]{:S(2)}, u32[]{:S(2)}) collective-permute-start(bf16[16,16,128]{2,1,0:T(8,128)(2,1)S(1)} %collective-permute-done.12.refs_7_), channel_id=1, source_target_pairs={{0,1},{1,0},{2,3},{3,2},{4,5},{5,4},{6,7},{7,6},{8,9},{9,8},{10,11... | collective-permute-start | bytes 196616 | tf_op jit(solution)/shard_map/ppermute | solution.py:478
  34.5 6.5 %collective-permute-start.11 = (bf16[16,16,128]{2,1,0:T(8,128)(2,1)S(1)}, bf16[16,16,128]{2,1,0:T(8,128)(2,1)S(1)}, u32[]{:S(2)}, u32[]{:S(2)}) collective-permute-start(bf16[16,16,128]{2,1,0:T(8,128)(2,1)S(1)} %gate.1.refs_6_), channel_id=1, source_target_pairs={{0,1},{1,0},{2,3},{3,2},{4,5},{5,4},{6,7},{7,6},{8,9},{9,8},{10,11... | collective-permute-start | bytes 196616 | tf_op jit(solution)/shard_map/ppermute | solution.py:478

commit v13 on v9

--- a/solution.py
+++ b/solution.py
@@ -86,16 +86,15 @@
 
 
 def spectra_kernel(
-    n_win, n_rcv, r_dev, valid_hbm, src_hbm, x_hbm, seed_hbm, twice_hbm, *refs
+    n_win, n_rcv, r_dev, cuts, valid_hbm, src_hbm, x_hbm, seed_hbm, twice_hbm, *refs
 ):
     r_refs = refs[:n_win]
     q_refs = refs[n_win:n_win + n_rcv]
     (plan_ref, flag_ref, x_ref, even_ref, odd_ref, white_ref, sel_ref, order_ref, table_ref,
      seed_ref, twice_ref, valid_ref, src_ref, sems, x_sems) = refs[n_win + n_rcv:]
-    chunks, rows, samples = x_ref.shape
-    w_step = rows // r_dev
+    bounds = [(a * r_dev, b * r_dev) for a, b in zip(cuts, cuts[1:])]
     n_own = src_ref.shape[0] // n_rcv
-    quarter = samples // 4
+    quarter = x_ref.shape[1] // 4
     win = lax.axis_index("win")
     rcv = lax.axis_index("rcv")
 
@@ -105,11 +104,12 @@
         return pltpu.make_async_copy(source, target, sems.at[k])
 
     def chunk(k):
-        return pltpu.make_async_copy(x_hbm.at[pl.ds(k * rows, rows)], x_ref.at[k], x_sems.at[k])
+        rows = pl.ds(bounds[k][0], bounds[k][1] - bounds[k][0])
+        return pltpu.make_async_copy(x_hbm.at[rows], x_ref.at[rows], x_sems.at[k])
 
     for k in range(4):
         small(k).start()
-    for k in range(chunks):
+    for k in range(len(bounds)):
         chunk(k).start()
     small(0).wait()
     small(1).wait()
@@ -119,13 +119,14 @@
     stations = []
     for d in range(n_rcv):
         share = pl.multiple_of((rcv ^ d) * n_own, n_own)
-        stations += [order_ref[pl.ds(share, n_own), 0:1]] * w_step
-    wanted = jnp.concatenate(stations, axis=0).astype(jnp.int32) - rcv * r_dev
-    shape = (n_rcv * w_step * n_own, rows)
-    out_row = lax.broadcasted_iota(jnp.int32, shape, 0)
-    column = lax.broadcasted_iota(jnp.int32, shape, 1)
+        stations.append(order_ref[pl.ds(share, n_own), 0:1])
+    per_window = n_rcv * n_own
+    wanted = jnp.concatenate(stations * (sel_ref.shape[0] // per_window), axis=0)
+    wanted = wanted.astype(jnp.int32) - rcv * r_dev
+    out_row = lax.broadcasted_iota(jnp.int32, sel_ref.shape, 0)
+    column = lax.broadcasted_iota(jnp.int32, sel_ref.shape, 1)
     inside = (wanted >= 0) & (wanted < r_dev)
-    hit = inside & (column == wanted + (out_row // n_own) % w_step * r_dev)
+    hit = inside & (column == wanted + out_row // per_window * r_dev)
     sel_ref[...] = hit.astype(jnp.float32).astype(jnp.bfloat16)
     small(3).wait()
 
@@ -133,33 +134,34 @@
         return jnp.dot(lhs, table, preferred_element_type=jnp.float32)
 
     def add_quarters(k, first, last):
-        part = slice(first, last)
-        b0, b1, b2, b3 = (x_ref[k, part, q * quarter:(q + 1) * quarter] for q in range(4))
+        start, stop = bounds[k]
+        part = slice(start + first, start + last)
+        b0, b1, b2, b3 = (x_ref[part, q * quarter:(q + 1) * quarter] for q in range(4))
         x0, x1, x2, x3 = (b.astype(jnp.float32) for b in (b0, b1, b2, b3))
-        even_ref[k, 0, part] = ((x0 + x2) + (x1 + x3)).astype(jnp.bfloat16)
-        even_ref[k, 1, part] = ((x0 + x2) - (x1 + x3)).astype(jnp.bfloat16)
-        odd_ref[k, part] = b0 - b2
-        odd_ref[k, rows + first:rows + last] = b1 - b3
+        even_ref[0, part] = ((x0 + x2) + (x1 + x3)).astype(jnp.bfloat16)
+        even_ref[1, part] = ((x0 + x2) - (x1 + x3)).astype(jnp.bfloat16)
+        odd_ref[2 * start + first:2 * start + last] = b0 - b2
+        odd_ref[start + stop + first:start + stop + last] = b1 - b3
 
     lanes = table_ref.shape[2]
-    lane = lax.broadcasted_iota(jnp.int32, (rows, lanes), 1)
     piece = lanes // n_win
-    real = lane % piece < piece // 2
 
     def odd_spectra(k, m):
-        both = product(odd_ref[k], table_ref[m])
+        start, stop = bounds[k]
+        rows = stop - start
+        both = product(odd_ref[2 * start:2 * stop], table_ref[m])
         second = both[rows:]
         back, forth = pltpu.roll(second, lanes - piece // 2, 1), pltpu.roll(second, piece // 2, 1)
+        real = lax.broadcasted_iota(jnp.int32, (rows, lanes), 1) % piece < piece // 2
         turned = jnp.where(real, back, -forth)
         return both[:rows] + turned if m == 1 else both[:rows] - turned
 
-    parts = 4
-    size = rows // parts
     chunk(0).wait()
-    add_quarters(0, 0, rows)
-    row = lax.broadcasted_iota(jnp.int32, (rows, 1), 0)
-    for k in range(chunks):
-        more = k + 1 < chunks
+    add_quarters(0, 0, bounds[0][1])
+    for k, (start, stop) in enumerate(bounds):
+        rows = stop - start
+        windows = cuts[k + 1] - cuts[k]
+        more = k + 1 < len(bounds)
         if more:
             chunk(k + 1).wait()
         spectra = []
@@ -167,37 +169,41 @@
             if m % 2:
                 spectra.append(odd_spectra(k, m))
             else:
-                spectra.append(product(even_ref[k, m // 2], table_ref[m]))
-            if more:
-                add_quarters(k + 1, m * size, (m + 1) * size)
+                spectra.append(product(even_ref[m // 2, start:stop], table_ref[m]))
+            if more and m < cuts[k + 2] - cuts[k + 1]:
+                add_quarters(k + 1, m * r_dev, (m + 1) * r_dev)
         squares = sum(jnp.sum(s * s, axis=1, keepdims=True) for s in spectra)
         gain = lax.rsqrt(squares / F + 1e-06)
+        row = lax.broadcasted_iota(jnp.int32, (rows, 1), 0)
         keep = jnp.zeros((rows, 1), jnp.float32)
-        for t in range(w_step):
+        for t in range(windows):
             own = (row >= t * r_dev) & (row < (t + 1) * r_dev)
-            keep = jnp.where(own, valid_ref[k * w_step + t].astype(jnp.float32), keep)
+            keep = jnp.where(own, valid_ref[cuts[k] + t].astype(jnp.float32), keep)
         gain = gain * keep
         white = [s * gain for s in spectra]
         for d in range(n_win):
             columns = slice(d * piece, (d + 1) * piece)
             block = jnp.concatenate([part[:, columns] for part in white], axis=1)
-            white_ref[k, d] = block.astype(jnp.bfloat16)
-        count = w_step * n_own
+            white_ref[d, start:stop] = block.astype(jnp.bfloat16)
+        select = sel_ref[:windows * per_window, :rows]
         for j in range(n_win):
-            block = white_ref[k, win ^ j]
-            r_refs[j][k * rows:(k + 1) * rows, :] = block
-            picked = product(sel_ref[...], block).astype(jnp.bfloat16)
-            for d in range(n_rcv):
-                q_refs[d][j, k * count:(k + 1) * count, :] = picked[d * count:(d + 1) * count]
+            block = white_ref[win ^ j, start:stop]
+            r_refs[j][start:stop, :] = block
+            picked = product(select, block).astype(jnp.bfloat16)
+            for t in range(windows):
+                place = (cuts[k] + t) * n_own
+                for d in range(n_rcv):
+                    first = t * per_window + d * n_own
+                    q_refs[d][j, place:place + n_own, :] = picked[first:first + n_own]
 
 
 def spectra_call(traces, valid, src_station, n_win, n_rcv):
     w_dev, r_dev, samples = traces.shape
     n_src = src_station.shape[0]
     n_own = n_src // n_rcv
-    chunks = 2
+    cuts = (0, w_dev // 4, w_dev * 5 // 8, w_dev)
+    largest = max(b - a for a, b in zip(cuts, cuts[1:]))
     every = w_dev * r_dev
-    rows = every // chunks
     lanes = 2 * F // n_win
     seed, twice = (jnp.asarray(t) for t in table_seeds(samples, F, samples // 16, n_win))
     shapes = [jax.ShapeDtypeStruct((every, lanes), jnp.bfloat16)] * n_win
@@ -205,16 +211,16 @@
     shapes += [jax.ShapeDtypeStruct((8, 128), jnp.int32), jax.ShapeDtypeStruct((1,), jnp.int32)]
     vmem = pl.BlockSpec(memory_space=VMEM)
     out = pl.pallas_call(
-        functools.partial(spectra_kernel, n_win, n_rcv, r_dev),
+        functools.partial(spectra_kernel, n_win, n_rcv, r_dev, cuts),
         in_specs=[pl.BlockSpec(memory_space=pltpu.HBM)] * 5,
         out_specs=[vmem] * (len(shapes) - 1) + [pl.BlockSpec(memory_space=SMEM)],
         out_shape=shapes,
         scratch_shapes=[
-            pltpu.VMEM((chunks, rows, samples), jnp.bfloat16),
-            pltpu.VMEM((chunks, 2, rows, samples // 4), jnp.bfloat16),
-            pltpu.VMEM((chunks, 2 * rows, samples // 4), jnp.bfloat16),
-            pltpu.VMEM((chunks, n_win, rows, lanes), jnp.bfloat16),
-            pltpu.VMEM((n_src * (w_dev // chunks), rows), jnp.bfloat16),
+            pltpu.VMEM((every, samples), jnp.bfloat16),
+            pltpu.VMEM((2, every, samples // 4), jnp.bfloat16),
+            pltpu.VMEM((2 * every, samples // 4), jnp.bfloat16),
+            pltpu.VMEM((n_win, every, lanes), jnp.bfloat16),
+            pltpu.VMEM((n_src * largest, r_dev * largest), jnp.bfloat16),
             pltpu.VMEM((n_src, 128), jnp.float32),
             pltpu.VMEM((4, samples // 4, F // 2), jnp.bfloat16),
             pltpu.VMEM(seed.shape, jnp.float32),
@@ -222,7 +228,7 @@
             pltpu.SMEM(valid.shape, jnp.int32),
             pltpu.SMEM(src_station.shape, jnp.int32),
             pltpu.SemaphoreType.DMA((4,)),
-            pltpu.SemaphoreType.DMA((chunks,)),
+            pltpu.SemaphoreType.DMA((len(cuts) - 1,)),
         ],
         compiler_params=pltpu.CompilerParams(vmem_limit_bytes=36 * 2**20),
         cost_estimate=pl.CostEstimate(

time: 42.3 us -> 42.7 us (level)
  Pallas kernels: 15.3 us -> 15.8 us
    pallas_call x1, Pallas kernels: 8.63 us -> 9.07 us  [spectra_call(): pl.pallas_call(functools.partial(spectra_kernel, n_win, n_rcv, r_dev, cut...]
where the time goes in v13:
time: 42.7 us; the launch traced here: 42.6 us
  Pallas kernels  15.8 us (37%)
  starting transfers between devices  13.8 us (32%)
  waiting for transfers between devices  11.9 us (28%)
  between operations  0.93 us (2%)
    ppermute x9, waiting for transfers between devices, swap(): return lax.ppermute(value, axis, [(i, i ^ by) for i in range(size)])  9.61 us
    pallas_call x1, Pallas kernels, spectra_call(): pl.pallas_call(functools.partial(spectra_kernel, n_win, n_rcv, r_dev, cut...  9.07 us
    ppermute x9, starting transfers between devices, swap(): return lax.ppermute(value, axis, [(i, i ^ by) for i in range(size)])  8.7 us
    ppermute x2, starting transfers between devices, body(): near[i] = lax.ppermute(picked[i], 'rcv', pairs)  5.11 us
    pallas_call x2, Pallas kernels, stacks_call(): pl.pallas_call(functools.partial(stacks_kernel, shares, n_win, w_dev, r_d...  4.16 us
    ppermute x2, waiting for transfers between devices, body(): near[i] = lax.ppermute(picked[i], 'rcv', pairs)  2.25 us
    pallas_call x4, Pallas kernels, turn_call(): pl.pallas_call(functools.partial(turn_kernel, r_dev), in_specs=[vmem] * l...  2.15 us
  transfers between devices with their start and end apart: 11, of which 5 were waited for; matrix products, arithmetic and copies ran while one was open for 0% of the time, Pallas kernels for 11%

profile of v13, /device:TPU:0, one launch (start us, length us, event | category | flops | bytes accessed | tf_op | source)
XLA Modules:
  0.0 42.6 jit_solution(1323364421774952780)
XLA Ops:
  0.0 9.1 %spectra.1 = (bf16[768,256]{1,0:T(8,128)(2,1)S(1)}, bf16[768,256]{1,0:T(8,128)(2,1)S(1)}, bf16[768,256]{1,0:T(8,128)(2,1)S(1)}, bf16[768,256]{1,0:T(8,128)(2,1)S...) custom-call(s32[8]{0:T(128)} %valid_hbm.1, ...), custom_call_target="tpu_custom_call" | custom-call | flops 2415919104 | bytes 6291456 | tf_op jit(solution)/shard_map/spectra/pallas_call | solution.py:213
  9.1 3.0 %collective-permute-start.7 = (bf16[768,256]{1,0:T(8,128)(2,1)S(1)}, bf16[768,256]{1,0:T(8,128)(2,1)S(1)}, u32[]{:S(2)}, u32[]{:S(2)}) collective-permute-start(bf16[768,256]{1,0:T(8,128)(2,1)S(1)} %get-tuple-element.51), channel_id=1, source_target_pairs={{0,8},{4,12},{8,0},{12,4},{1,9},{5,13},{9,1},{13,5},{2,10},{6,14},... | collective-permute-start | bytes 1179656 | tf_op jit(solution)/shard_map/ppermute | solution.py:472
  12.1 0.7 %collective-permute-start.2 = (bf16[4,64,256]{2,1,0:T(8,128)(2,1)S(1)}, bf16[4,64,256]{2,1,0:T(8,128)(2,1)S(1)}, u32[]{:S(2)}, u32[]{:S(2)}) collective-permute-start(bf16[4,64,256]{2,1,0:T(8,128)(2,1)S(1)} %get-tuple-element.44), channel_id=1, source_target_pairs={{1,2},{2,1},{5,6},{6,5},{9,10},{10,9},{13,14},{14,13},{17,18},{18,... | collective-permute-start | bytes 393224 | tf_op jit(solution)/shard_map/ppermute | solution.py:507
  12.8 4.5 %collective-permute-start.3 = (bf16[4,64,256]{2,1,0:T(8,128)(2,1)S(1)}, bf16[4,64,256]{2,1,0:T(8,128)(2,1)S(1)}, u32[]{:S(2)}, u32[]{:S(2)}) collective-permute-start(bf16[4,64,256]{2,1,0:T(8,128)(2,1)S(1)} %get-tuple-element.45), channel_id=1, source_target_pairs={{0,1},{1,0},{2,3},{3,2},{4,5},{5,4},{6,7},{7,6},{8,9},{9,8},{10,11... | collective-permute-start | bytes 393224 | tf_op jit(solution)/shard_map/ppermute | solution.py:507
  17.9 2.2 %collective-permute-done.3 = bf16[4,64,256]{2,1,0:T(8,128)(2,1)S(1)} collective-permute-done((bf16[4,64,256]{2,1,0:T(8,128)(2,1)S(1)}, bf16[4,64,256]{2,1,0:T(8,128)(2,1)S(1)}, u32[]{:S(2)}, u32[]{:S(2)}) %collective-permute-start.3) | collective-permute-done | bytes 131104 | tf_op jit(solution)/shard_map/ppermute | solution.py:507
  20.2 0.2 conditional.1
  20.4 0.1 collective-permute-start.4
  20.5 0.6 %collective-permute-start.5 = (bf16[64,256]{1,0:T(8,128)(2,1)S(1)}, bf16[64,256]{1,0:T(8,128)(2,1)S(1)}, u32[]{:S(2)}, u32[]{:S(2)}) collective-permute-start(bf16[64,256]{1,0:T(8,128)(2,1)S(1)} %get-tuple-element.49), channel_id=1, source_target_pairs={{0,8},{4,12},{8,0},{12,4},{1,9},{5,13},{9,1},{13,5},{2,10},{6,14},... | collective-permute-start | bytes 98312 | tf_op jit(solution)/shard_map/ppermute | solution.py:472
  21.1 1.3 %collective-permute-start.6 = (bf16[64,256]{1,0:T(8,128)(2,1)S(1)}, bf16[64,256]{1,0:T(8,128)(2,1)S(1)}, u32[]{:S(2)}, u32[]{:S(2)}) collective-permute-start(bf16[64,256]{1,0:T(8,128)(2,1)S(1)} %get-tuple-element.50), channel_id=1, source_target_pairs={{0,12},{4,8},{8,4},{12,0},{1,13},{5,9},{9,5},{13,1},{2,14},{6,10},... | collective-permute-start | bytes 98312 | tf_op jit(solution)/shard_map/ppermute | solution.py:472
  22.4 2.4 %collective-permute-done.5.refs_2_ = bf16[64,256]{1,0:T(8,128)(2,1)S(1)} collective-permute-done((bf16[64,256]{1,0:T(8,128)(2,1)S(1)}, bf16[64,256]{1,0:T(8,128)(2,1)S(1)}, u32[]{:S(2)}, u32[]{:S(2)}) %collective-permute-start.5) | collective-permute-done | bytes 32800 | tf_op jit(solution)/shard_map/ppermute | solution.py:472
  24.8 0.3 lefts.1
  25.1 0.2 collective-permute-start.8
  25.3 1.1 %collective-permute-start.9 = (bf16[768,256]{1,0:T(8,128)(2,1)S(1)}, bf16[768,256]{1,0:T(8,128)(2,1)S(1)}, u32[]{:S(2)}, u32[]{:S(2)}) collective-permute-start(bf16[768,256]{1,0:T(8,128)(2,1)S(1)} %get-tuple-element.55), channel_id=1, source_target_pairs={{0,12},{4,8},{8,4},{12,0},{1,13},{5,9},{9,5},{13,1},{2,14},{6,10},... | collective-permute-start | bytes 1179656 | tf_op jit(solution)/shard_map/ppermute | solution.py:472
  26.5 1.9 %collective-permute-start.10 = (bf16[32,16,128]{2,1,0:T(8,128)(2,1)S(1)}, bf16[32,16,128]{2,1,0:T(8,128)(2,1)S(1)}, u32[]{:S(2)}, u32[]{:S(2)}) collective-permute-start(bf16[32,16,128]{2,1,0:T(8,128)(2,1)S(1)} %get-tuple-element.56.refs_4_), channel_id=1, source_target_pairs={{0,2},{1,3},{2,0},{3,1},{4,6},{5,7},{6,4},{7,5},{8,10},{9,11},{10,... | collective-permute-start | bytes 393224 | tf_op jit(solution)/shard_map/ppermute | solution.py:472
  28.4 0.5 %turn.4.refs_0_ = bf16[128,16,256]{2,1,0:T(8,128)(2,1)S(1)} custom-call(bf16[768,256]{1,0:T(8,128)(2,1)S(1)} %get-tuple-element.41.refs_0_), custom_call_target="tpu_custom_call" | custom-call | flops 134217728 | bytes 2097152 | tf_op jit(solution)/shard_map/turn/pallas_call | solution.py:277
  28.9 0.5 %collective-permute-start.12 = (bf16[32,16,128]{2,1,0:T(8,128)(2,1)S(1)}, bf16[32,16,128]{2,1,0:T(8,128)(2,1)S(1)}, u32[]{:S(2)}, u32[]{:S(2)}) collective-permute-start(bf16[32,16,128]{2,1,0:T(8,128)(2,1)S(1)} %get-tuple-element.56.refs_4_), channel_id=1, source_target_pairs={{0,1},{1,0},{2,3},{3,2},{4,5},{5,4},{6,7},{7,6},{8,9},{9,8},{10,11... | collective-permute-start | bytes 393224 | tf_op jit(solution)/shard_map/ppermute | solution.py:472
  29.4 0.5 %turn.6.refs_2_ = bf16[128,16,256]{2,1,0:T(8,128)(2,1)S(1)} custom-call(bf16[768,256]{1,0:T(8,128)(2,1)S(1)} %collective-permute-done.7.refs_4_.refs_0_), custom_call_target="tpu_custom_call" | custom-call | flops 134217728 | bytes 2097152 | tf_op jit(solution)/shard_map/turn/pallas_call | solution.py:277
  29.9 0.5 %turn.5.refs_1_ = bf16[128,16,256]{2,1,0:T(8,128)(2,1)S(1)} custom-call(bf16[768,256]{1,0:T(8,128)(2,1)S(1)} %collective-permute-done.8.refs_0_), custom_call_target="tpu_custom_call" | custom-call | flops 134217728 | bytes 2097152 | tf_op jit(solution)/shard_map/turn/pallas_call | solution.py:277
  30.5 5.3 %collective-permute-done.10.refs_3_ = bf16[32,16,128]{2,1,0:T(8,128)(2,1)S(1)} collective-permute-done((bf16[32,16,128]{2,1,0:T(8,128)(2,1)S(1)}, bf16[32,16,128]{2,1,0:T(8,128)(2,1)S(1)}, u32[]{:S(2)}, u32[]{:S(2)}) %collective-permute-start.10) | collective-permute-done | bytes 131104 | tf_op jit(solution)/shard_map/ppermute | solution.py:472
  35.8 0.5 %collective-permute-done.9.refs_0_ = bf16[768,256]{1,0:T(8,128)(2,1)S(1)} collective-permute-done((bf16[768,256]{1,0:T(8,128)(2,1)S(1)}, bf16[768,256]{1,0:T(8,128)(2,1)S(1)}, u32[]{:S(2)}, u32[]{:S(2)}) %collective-permute-start.9) | collective-permute-done | bytes 393248 | tf_op jit(solution)/shard_map/ppermute | solution.py:472
  36.3 0.5 %turn.7.refs_3_ = bf16[128,16,256]{2,1,0:T(8,128)(2,1)S(1)} custom-call(bf16[768,256]{1,0:T(8,128)(2,1)S(1)} %collective-permute-done.9.refs_0_), custom_call_target="tpu_custom_call" | custom-call | flops 134217728 | bytes 2097152 | tf_op jit(solution)/shard_map/turn/pallas_call | solution.py:277
  36.9 2.4 %stacks.2.refs_5_ = f32[32,192,128]{2,1,0:T(8,128)} custom-call(s32[8,128]{1,0:T(8,128)S(1)} %get-tuple-element.40.plan_hbm, bf16[128,16,256]{2,1,0:T(8,128)(2,1)S(1)} %turn.4.refs_0_, bf16[128,16,256]{2,1,0:T(8,128)(2,1)S(1)} %turn.5.refs_1_, bf16[128,16,256]{2,1,0:T(8,128)(2,1)S(1)} %turn.6.refs_2_, bf16[128,16,256]{2,1,0:T(8,128)(2,1)S(1)} %turn.7.refs_3_, ...), custom_call_target="tpu_custom_call" | custom-call | flops 75497472 | bytes 6291456 | tf_op jit(solution)/shard_map/stacks/pallas_call | solution.py:449
  39.3 1.4 %collective-permute-done.11.refs_4_ = bf16[32,16,128]{2,1,0:T(8,128)(2,1)S(1)} collective-permute-done((bf16[32,16,128]{2,1,0:T(8,128)(2,1)S(1)}, bf16[32,16,128]{2,1,0:T(8,128)(2,1)S(1)}, u32[]{:S(2)}, u32[]{:S(2)}) %collective-permute-start.11) | collective-permute-done | bytes 131104 | tf_op jit(solution)/shard_map/ppermute | solution.py:472
  40.7 1.7 %stacks.3 = f32[32,192,128]{2,1,0:T(8,128)} custom-call(s32[8,128]{1,0:T(8,128)S(1)} %get-tuple-element.40.plan_hbm, bf16[128,16,256]{2,1,0:T(8,128)(2,1)S(1)} %turn.4.refs_0_, bf16[128,16,256]{2,1,0:T(8,128)(2,1)S(1)} %turn.5.refs_1_, bf16[128,16,256]{2,1,0:T(8,128)(2,1)S(1)} %turn.6.refs_2_, ...), custom_call_target="tpu_custom_call", output_to_operand_aliasing={{}: (6, {})} | custom-call | flops 25165824 | bytes 6291456 | tf_op jit(solution)/shard_map/stacks/pallas_call | solution.py:449
  (10 shorter events, 0.1 us)
Async XLA Ops:
  9.1 15.7 %collective-permute-start.7 = (bf16[768,256]{1,0:T(8,128)(2,1)S(1)}, bf16[768,256]{1,0:T(8,128)(2,1)S(1)}, u32[]{:S(2)}, u32[]{:S(2)}) collective-permute-start(bf16[768,256]{1,0:T(8,128)(2,1)S(1)} %get-tuple-element.51), channel_id=1, source_target_pairs={{0,8},{4,12},{8,0},{12,4},{1,9},{5,13},{9,1},{13,5},{2,10},{6,14},... | collective-permute-start | bytes 1179656 | tf_op jit(solution)/shard_map/ppermute | solution.py:472
  12.1 5.8 %collective-permute-start.2 = (bf16[4,64,256]{2,1,0:T(8,128)(2,1)S(1)}, bf16[4,64,256]{2,1,0:T(8,128)(2,1)S(1)}, u32[]{:S(2)}, u32[]{:S(2)}) collective-permute-start(bf16[4,64,256]{2,1,0:T(8,128)(2,1)S(1)} %get-tuple-element.44), channel_id=1, source_target_pairs={{1,2},{2,1},{5,6},{6,5},{9,10},{10,9},{13,14},{14,13},{17,18},{18,... | collective-permute-start | bytes 393224 | tf_op jit(solution)/shard_map/ppermute | solution.py:507
  12.8 7.4 %collective-permute-start.3 = (bf16[4,64,256]{2,1,0:T(8,128)(2,1)S(1)}, bf16[4,64,256]{2,1,0:T(8,128)(2,1)S(1)}, u32[]{:S(2)}, u32[]{:S(2)}) collective-permute-start(bf16[4,64,256]{2,1,0:T(8,128)(2,1)S(1)} %get-tuple-element.45), channel_id=1, source_target_pairs={{0,1},{1,0},{2,3},{3,2},{4,5},{5,4},{6,7},{7,6},{8,9},{9,8},{10,11... | collective-permute-start | bytes 393224 | tf_op jit(solution)/shard_map/ppermute | solution.py:507
  20.4 1.9 %collective-permute-start.4 = (bf16[64,256]{1,0:T(8,128)(2,1)S(1)}, bf16[64,256]{1,0:T(8,128)(2,1)S(1)}, u32[]{:S(2)}, u32[]{:S(2)}) collective-permute-start(bf16[64,256]{1,0:T(8,128)(2,1)S(1)} %get-tuple-element.48), channel_id=1, source_target_pairs={{0,4},{4,0},{8,12},{12,8},{1,5},{5,1},{9,13},{13,9},{2,6},{6,2},{1... | collective-permute-start | bytes 98312 | tf_op jit(solution)/shard_map/ppermute | solution.py:472
  20.5 4.3 %collective-permute-start.5 = (bf16[64,256]{1,0:T(8,128)(2,1)S(1)}, bf16[64,256]{1,0:T(8,128)(2,1)S(1)}, u32[]{:S(2)}, u32[]{:S(2)}) collective-permute-start(bf16[64,256]{1,0:T(8,128)(2,1)S(1)} %get-tuple-element.49), channel_id=1, source_target_pairs={{0,8},{4,12},{8,0},{12,4},{1,9},{5,13},{9,1},{13,5},{2,10},{6,14},... | collective-permute-start | bytes 98312 | tf_op jit(solution)/shard_map/ppermute | solution.py:472
  21.1 3.7 %collective-permute-start.6 = (bf16[64,256]{1,0:T(8,128)(2,1)S(1)}, bf16[64,256]{1,0:T(8,128)(2,1)S(1)}, u32[]{:S(2)}, u32[]{:S(2)}) collective-permute-start(bf16[64,256]{1,0:T(8,128)(2,1)S(1)} %get-tuple-element.50), channel_id=1, source_target_pairs={{0,12},{4,8},{8,4},{12,0},{1,13},{5,9},{9,5},{13,1},{2,14},{6,10},... | collective-permute-start | bytes 98312 | tf_op jit(solution)/shard_map/ppermute | solution.py:472
  25.1 4.8 %collective-permute-start.8 = (bf16[768,256]{1,0:T(8,128)(2,1)S(1)}, bf16[768,256]{1,0:T(8,128)(2,1)S(1)}, u32[]{:S(2)}, u32[]{:S(2)}) collective-permute-start(bf16[768,256]{1,0:T(8,128)(2,1)S(1)} %get-tuple-element.54), channel_id=1, source_target_pairs={{0,4},{4,0},{8,12},{12,8},{1,5},{5,1},{9,13},{13,9},{2,6},{6,2},{1... | collective-permute-start | bytes 1179656 | tf_op jit(solution)/shard_map/ppermute | solution.py:472
  25.3 10.9 %collective-permute-start.9 = (bf16[768,256]{1,0:T(8,128)(2,1)S(1)}, bf16[768,256]{1,0:T(8,128)(2,1)S(1)}, u32[]{:S(2)}, u32[]{:S(2)}) collective-permute-start(bf16[768,256]{1,0:T(8,128)(2,1)S(1)} %get-tuple-element.55), channel_id=1, source_target_pairs={{0,12},{4,8},{8,4},{12,0},{1,13},{5,9},{9,5},{13,1},{2,14},{6,10},... | collective-permute-start | bytes 1179656 | tf_op jit(solution)/shard_map/ppermute | solution.py:472
  26.5 9.3 %collective-permute-start.10 = (bf16[32,16,128]{2,1,0:T(8,128)(2,1)S(1)}, bf16[32,16,128]{2,1,0:T(8,128)(2,1)S(1)}, u32[]{:S(2)}, u32[]{:S(2)}) collective-permute-start(bf16[32,16,128]{2,1,0:T(8,128)(2,1)S(1)} %get-tuple-element.56.refs_4_), channel_id=1, source_target_pairs={{0,2},{1,3},{2,0},{3,1},{4,6},{5,7},{6,4},{7,5},{8,10},{9,11},{10,... | collective-permute-start | bytes 393224 | tf_op jit(solution)/shard_map/ppermute | solution.py:472
  28.9 7.9 %collective-permute-start.12 = (bf16[32,16,128]{2,1,0:T(8,128)(2,1)S(1)}, bf16[32,16,128]{2,1,0:T(8,128)(2,1)S(1)}, u32[]{:S(2)}, u32[]{:S(2)}) collective-permute-start(bf16[32,16,128]{2,1,0:T(8,128)(2,1)S(1)} %get-tuple-element.56.refs_4_), channel_id=1, source_target_pairs={{0,1},{1,0},{2,3},{3,2},{4,5},{5,4},{6,7},{7,6},{8,9},{9,8},{10,11... | collective-permute-start | bytes 393224 | tf_op jit(solution)/shard_map/ppermute | solution.py:472
  35.7 5.0 %collective-permute-start.11 = (bf16[32,16,128]{2,1,0:T(8,128)(2,1)S(1)}, bf16[32,16,128]{2,1,0:T(8,128)(2,1)S(1)}, u32[]{:S(2)}, u32[]{:S(2)}) collective-permute-start(bf16[32,16,128]{2,1,0:T(8,128)(2,1)S(1)} %gate.1.refs_6_), channel_id=1, source_target_pairs={{0,1},{1,0},{2,3},{3,2},{4,5},{5,4},{6,7},{7,6},{8,9},{9,8},{10,11... | collective-permute-start | bytes 393224 | tf_op jit(solution)/shard_map/ppermute | solution.py:472

commit v14 on v13

--- a/solution.py
+++ b/solution.py
@@ -170,8 +170,11 @@
                 spectra.append(odd_spectra(k, m))
             else:
                 spectra.append(product(even_ref[m // 2, start:stop], table_ref[m]))
-            if more and m < cuts[k + 2] - cuts[k + 1]:
-                add_quarters(k + 1, m * r_dev, (m + 1) * r_dev)
+            if more:
+                ahead = cuts[k + 2] - cuts[k + 1]
+                first, last = ahead * m // 4, ahead * (m + 1) // 4
+                if first < last:
+                    add_quarters(k + 1, first * r_dev, last * r_dev)
         squares = sum(jnp.sum(s * s, axis=1, keepdims=True) for s in spectra)
         gain = lax.rsqrt(squares / F + 1e-06)
         row = lax.broadcasted_iota(jnp.int32, (rows, 1), 0)
@@ -201,7 +204,7 @@
     w_dev, r_dev, samples = traces.shape
     n_src = src_station.shape[0]
     n_own = n_src // n_rcv
-    cuts = (0, w_dev // 4, w_dev * 5 // 8, w_dev)
+    cuts = (0, w_dev * 3 // 8, w_dev)
     largest = max(b - a for a, b in zip(cuts, cuts[1:]))
     every = w_dev * r_dev
     lanes = 2 * F // n_win

time: 42.7 us -> 42.9 us (level)
  no operation moved by 1% of the time
where the time goes in v14:
time: 42.9 us; the launch traced here: 42.7 us
  Pallas kernels  15.9 us (37%)
  starting transfers between devices  13.8 us (32%)
  waiting for transfers between devices  11.9 us (28%)
  between operations  0.93 us (2%)
    ppermute x9, waiting for transfers between devices, swap(): return lax.ppermute(value, axis, [(i, i ^ by) for i in range(size)])  9.6 us
    pallas_call x1, Pallas kernels, spectra_call(): pl.pallas_call(functools.partial(spectra_kernel, n_win, n_rcv, r_dev, cut...  9.18 us
    ppermute x9, starting transfers between devices, swap(): return lax.ppermute(value, axis, [(i, i ^ by) for i in range(size)])  8.71 us
    ppermute x2, starting transfers between devices, body(): near[i] = lax.ppermute(picked[i], 'rcv', pairs)  5.11 us
    pallas_call x2, Pallas kernels, stacks_call(): pl.pallas_call(functools.partial(stacks_kernel, shares, n_win, w_dev, r_d...  4.16 us
    ppermute x2, waiting for transfers between devices, body(): near[i] = lax.ppermute(picked[i], 'rcv', pairs)  2.25 us
    pallas_call x4, Pallas kernels, turn_call(): pl.pallas_call(functools.partial(turn_kernel, r_dev), in_specs=[vmem] * l...  2.16 us
  transfers between devices with their start and end apart: 11, of which 5 were waited for; matrix products, arithmetic and copies ran while one was open for 0% of the time, Pallas kernels for 11%

profile of v14, /device:TPU:0, one launch (start us, length us, event | category | flops | bytes accessed | tf_op | source)
XLA Modules:
  0.0 42.7 jit_solution(2105521576527979067)
XLA Ops:
  0.0 9.2 %spectra.1 = (bf16[768,256]{1,0:T(8,128)(2,1)S(1)}, bf16[768,256]{1,0:T(8,128)(2,1)S(1)}, bf16[768,256]{1,0:T(8,128)(2,1)S(1)}, bf16[768,256]{1,0:T(8,128)(2,1)S...) custom-call(s32[8]{0:T(128)} %valid_hbm.1, ...), custom_call_target="tpu_custom_call" | custom-call | flops 2415919104 | bytes 6291456 | tf_op jit(solution)/shard_map/spectra/pallas_call | solution.py:216
  9.2 3.0 %collective-permute-start.7 = (bf16[768,256]{1,0:T(8,128)(2,1)S(1)}, bf16[768,256]{1,0:T(8,128)(2,1)S(1)}, u32[]{:S(2)}, u32[]{:S(2)}) collective-permute-start(bf16[768,256]{1,0:T(8,128)(2,1)S(1)} %get-tuple-element.51), channel_id=1, source_target_pairs={{0,8},{4,12},{8,0},{12,4},{1,9},{5,13},{9,1},{13,5},{2,10},{6,14},... | collective-permute-start | bytes 1179656 | tf_op jit(solution)/shard_map/ppermute | solution.py:475
  12.2 0.7 %collective-permute-start.2 = (bf16[4,64,256]{2,1,0:T(8,128)(2,1)S(1)}, bf16[4,64,256]{2,1,0:T(8,128)(2,1)S(1)}, u32[]{:S(2)}, u32[]{:S(2)}) collective-permute-start(bf16[4,64,256]{2,1,0:T(8,128)(2,1)S(1)} %get-tuple-element.44), channel_id=1, source_target_pairs={{1,2},{2,1},{5,6},{6,5},{9,10},{10,9},{13,14},{14,13},{17,18},{18,... | collective-permute-start | bytes 393224 | tf_op jit(solution)/shard_map/ppermute | solution.py:510
  12.9 4.5 %collective-permute-start.3 = (bf16[4,64,256]{2,1,0:T(8,128)(2,1)S(1)}, bf16[4,64,256]{2,1,0:T(8,128)(2,1)S(1)}, u32[]{:S(2)}, u32[]{:S(2)}) collective-permute-start(bf16[4,64,256]{2,1,0:T(8,128)(2,1)S(1)} %get-tuple-element.45), channel_id=1, source_target_pairs={{0,1},{1,0},{2,3},{3,2},{4,5},{5,4},{6,7},{7,6},{8,9},{9,8},{10,11... | collective-permute-start | bytes 393224 | tf_op jit(solution)/shard_map/ppermute | solution.py:510
  18.1 2.2 %collective-permute-done.3 = bf16[4,64,256]{2,1,0:T(8,128)(2,1)S(1)} collective-permute-done((bf16[4,64,256]{2,1,0:T(8,128)(2,1)S(1)}, bf16[4,64,256]{2,1,0:T(8,128)(2,1)S(1)}, u32[]{:S(2)}, u32[]{:S(2)}) %collective-permute-start.3) | collective-permute-done | bytes 131104 | tf_op jit(solution)/shard_map/ppermute | solution.py:510
  20.3 0.2 conditional.1
  20.5 0.1 collective-permute-start.4
  20.6 0.6 %collective-permute-start.5 = (bf16[64,256]{1,0:T(8,128)(2,1)S(1)}, bf16[64,256]{1,0:T(8,128)(2,1)S(1)}, u32[]{:S(2)}, u32[]{:S(2)}) collective-permute-start(bf16[64,256]{1,0:T(8,128)(2,1)S(1)} %get-tuple-element.49), channel_id=1, source_target_pairs={{0,8},{4,12},{8,0},{12,4},{1,9},{5,13},{9,1},{13,5},{2,10},{6,14},... | collective-permute-start | bytes 98312 | tf_op jit(solution)/shard_map/ppermute | solution.py:475
  21.2 1.3 %collective-permute-start.6 = (bf16[64,256]{1,0:T(8,128)(2,1)S(1)}, bf16[64,256]{1,0:T(8,128)(2,1)S(1)}, u32[]{:S(2)}, u32[]{:S(2)}) collective-permute-start(bf16[64,256]{1,0:T(8,128)(2,1)S(1)} %get-tuple-element.50), channel_id=1, source_target_pairs={{0,12},{4,8},{8,4},{12,0},{1,13},{5,9},{9,5},{13,1},{2,14},{6,10},... | collective-permute-start | bytes 98312 | tf_op jit(solution)/shard_map/ppermute | solution.py:475
  22.5 2.4 %collective-permute-done.5.refs_2_ = bf16[64,256]{1,0:T(8,128)(2,1)S(1)} collective-permute-done((bf16[64,256]{1,0:T(8,128)(2,1)S(1)}, bf16[64,256]{1,0:T(8,128)(2,1)S(1)}, u32[]{:S(2)}, u32[]{:S(2)}) %collective-permute-start.5) | collective-permute-done | bytes 32800 | tf_op jit(solution)/shard_map/ppermute | solution.py:475
  24.9 0.3 lefts.1
  25.2 0.2 collective-permute-start.8
  25.4 1.1 %collective-permute-start.9 = (bf16[768,256]{1,0:T(8,128)(2,1)S(1)}, bf16[768,256]{1,0:T(8,128)(2,1)S(1)}, u32[]{:S(2)}, u32[]{:S(2)}) collective-permute-start(bf16[768,256]{1,0:T(8,128)(2,1)S(1)} %get-tuple-element.55), channel_id=1, source_target_pairs={{0,12},{4,8},{8,4},{12,0},{1,13},{5,9},{9,5},{13,1},{2,14},{6,10},... | collective-permute-start | bytes 1179656 | tf_op jit(solution)/shard_map/ppermute | solution.py:475
  26.6 1.9 %collective-permute-start.10 = (bf16[32,16,128]{2,1,0:T(8,128)(2,1)S(1)}, bf16[32,16,128]{2,1,0:T(8,128)(2,1)S(1)}, u32[]{:S(2)}, u32[]{:S(2)}) collective-permute-start(bf16[32,16,128]{2,1,0:T(8,128)(2,1)S(1)} %get-tuple-element.56.refs_4_), channel_id=1, source_target_pairs={{0,2},{1,3},{2,0},{3,1},{4,6},{5,7},{6,4},{7,5},{8,10},{9,11},{10,... | collective-permute-start | bytes 393224 | tf_op jit(solution)/shard_map/ppermute | solution.py:475
  28.5 0.5 %turn.4.refs_0_ = bf16[128,16,256]{2,1,0:T(8,128)(2,1)S(1)} custom-call(bf16[768,256]{1,0:T(8,128)(2,1)S(1)} %get-tuple-element.41.refs_0_), custom_call_target="tpu_custom_call" | custom-call | flops 134217728 | bytes 2097152 | tf_op jit(solution)/shard_map/turn/pallas_call | solution.py:280
  29.0 0.5 %collective-permute-start.12 = (bf16[32,16,128]{2,1,0:T(8,128)(2,1)S(1)}, bf16[32,16,128]{2,1,0:T(8,128)(2,1)S(1)}, u32[]{:S(2)}, u32[]{:S(2)}) collective-permute-start(bf16[32,16,128]{2,1,0:T(8,128)(2,1)S(1)} %get-tuple-element.56.refs_4_), channel_id=1, source_target_pairs={{0,1},{1,0},{2,3},{3,2},{4,5},{5,4},{6,7},{7,6},{8,9},{9,8},{10,11... | collective-permute-start | bytes 393224 | tf_op jit(solution)/shard_map/ppermute | solution.py:475
  29.5 0.5 %turn.6.refs_2_ = bf16[128,16,256]{2,1,0:T(8,128)(2,1)S(1)} custom-call(bf16[768,256]{1,0:T(8,128)(2,1)S(1)} %collective-permute-done.7.refs_4_.refs_0_), custom_call_target="tpu_custom_call" | custom-call | flops 134217728 | bytes 2097152 | tf_op jit(solution)/shard_map/turn/pallas_call | solution.py:280
  30.1 0.5 %turn.5.refs_1_ = bf16[128,16,256]{2,1,0:T(8,128)(2,1)S(1)} custom-call(bf16[768,256]{1,0:T(8,128)(2,1)S(1)} %collective-permute-done.8.refs_0_), custom_call_target="tpu_custom_call" | custom-call | flops 134217728 | bytes 2097152 | tf_op jit(solution)/shard_map/turn/pallas_call | solution.py:280
  30.6 5.2 %collective-permute-done.10.refs_3_ = bf16[32,16,128]{2,1,0:T(8,128)(2,1)S(1)} collective-permute-done((bf16[32,16,128]{2,1,0:T(8,128)(2,1)S(1)}, bf16[32,16,128]{2,1,0:T(8,128)(2,1)S(1)}, u32[]{:S(2)}, u32[]{:S(2)}) %collective-permute-start.10) | collective-permute-done | bytes 131104 | tf_op jit(solution)/shard_map/ppermute | solution.py:475
  35.9 0.5 %collective-permute-done.9.refs_0_ = bf16[768,256]{1,0:T(8,128)(2,1)S(1)} collective-permute-done((bf16[768,256]{1,0:T(8,128)(2,1)S(1)}, bf16[768,256]{1,0:T(8,128)(2,1)S(1)}, u32[]{:S(2)}, u32[]{:S(2)}) %collective-permute-start.9) | collective-permute-done | bytes 393248 | tf_op jit(solution)/shard_map/ppermute | solution.py:475
  36.4 0.5 %turn.7.refs_3_ = bf16[128,16,256]{2,1,0:T(8,128)(2,1)S(1)} custom-call(bf16[768,256]{1,0:T(8,128)(2,1)S(1)} %collective-permute-done.9.refs_0_), custom_call_target="tpu_custom_call" | custom-call | flops 134217728 | bytes 2097152 | tf_op jit(solution)/shard_map/turn/pallas_call | solution.py:280
  37.0 2.4 %stacks.2.refs_5_ = f32[32,192,128]{2,1,0:T(8,128)} custom-call(s32[8,128]{1,0:T(8,128)S(1)} %get-tuple-element.40.plan_hbm, bf16[128,16,256]{2,1,0:T(8,128)(2,1)S(1)} %turn.4.refs_0_, bf16[128,16,256]{2,1,0:T(8,128)(2,1)S(1)} %turn.5.refs_1_, bf16[128,16,256]{2,1,0:T(8,128)(2,1)S(1)} %turn.6.refs_2_, bf16[128,16,256]{2,1,0:T(8,128)(2,1)S(1)} %turn.7.refs_3_, ...), custom_call_target="tpu_custom_call" | custom-call | flops 75497472 | bytes 6291456 | tf_op jit(solution)/shard_map/stacks/pallas_call | solution.py:452
  39.4 1.4 %collective-permute-done.11.refs_4_ = bf16[32,16,128]{2,1,0:T(8,128)(2,1)S(1)} collective-permute-done((bf16[32,16,128]{2,1,0:T(8,128)(2,1)S(1)}, bf16[32,16,128]{2,1,0:T(8,128)(2,1)S(1)}, u32[]{:S(2)}, u32[]{:S(2)}) %collective-permute-start.11) | collective-permute-done | bytes 131104 | tf_op jit(solution)/shard_map/ppermute | solution.py:475
  40.8 1.7 %stacks.3 = f32[32,192,128]{2,1,0:T(8,128)} custom-call(s32[8,128]{1,0:T(8,128)S(1)} %get-tuple-element.40.plan_hbm, bf16[128,16,256]{2,1,0:T(8,128)(2,1)S(1)} %turn.4.refs_0_, bf16[128,16,256]{2,1,0:T(8,128)(2,1)S(1)} %turn.5.refs_1_, bf16[128,16,256]{2,1,0:T(8,128)(2,1)S(1)} %turn.6.refs_2_, ...), custom_call_target="tpu_custom_call", output_to_operand_aliasing={{}: (6, {})} | custom-call | flops 25165824 | bytes 6291456 | tf_op jit(solution)/shard_map/stacks/pallas_call | solution.py:452
  (10 shorter events, 0.1 us)
Async XLA Ops:
  9.2 15.7 %collective-permute-start.7 = (bf16[768,256]{1,0:T(8,128)(2,1)S(1)}, bf16[768,256]{1,0:T(8,128)(2,1)S(1)}, u32[]{:S(2)}, u32[]{:S(2)}) collective-permute-start(bf16[768,256]{1,0:T(8,128)(2,1)S(1)} %get-tuple-element.51), channel_id=1, source_target_pairs={{0,8},{4,12},{8,0},{12,4},{1,9},{5,13},{9,1},{13,5},{2,10},{6,14},... | collective-permute-start | bytes 1179656 | tf_op jit(solution)/shard_map/ppermute | solution.py:475
  12.2 5.8 %collective-permute-start.2 = (bf16[4,64,256]{2,1,0:T(8,128)(2,1)S(1)}, bf16[4,64,256]{2,1,0:T(8,128)(2,1)S(1)}, u32[]{:S(2)}, u32[]{:S(2)}) collective-permute-start(bf16[4,64,256]{2,1,0:T(8,128)(2,1)S(1)} %get-tuple-element.44), channel_id=1, source_target_pairs={{1,2},{2,1},{5,6},{6,5},{9,10},{10,9},{13,14},{14,13},{17,18},{18,... | collective-permute-start | bytes 393224 | tf_op jit(solution)/shard_map/ppermute | solution.py:510
  12.9 7.4 %collective-permute-start.3 = (bf16[4,64,256]{2,1,0:T(8,128)(2,1)S(1)}, bf16[4,64,256]{2,1,0:T(8,128)(2,1)S(1)}, u32[]{:S(2)}, u32[]{:S(2)}) collective-permute-start(bf16[4,64,256]{2,1,0:T(8,128)(2,1)S(1)} %get-tuple-element.45), channel_id=1, source_target_pairs={{0,1},{1,0},{2,3},{3,2},{4,5},{5,4},{6,7},{7,6},{8,9},{9,8},{10,11... | collective-permute-start | bytes 393224 | tf_op jit(solution)/shard_map/ppermute | solution.py:510
  20.5 1.9 %collective-permute-start.4 = (bf16[64,256]{1,0:T(8,128)(2,1)S(1)}, bf16[64,256]{1,0:T(8,128)(2,1)S(1)}, u32[]{:S(2)}, u32[]{:S(2)}) collective-permute-start(bf16[64,256]{1,0:T(8,128)(2,1)S(1)} %get-tuple-element.48), channel_id=1, source_target_pairs={{0,4},{4,0},{8,12},{12,8},{1,5},{5,1},{9,13},{13,9},{2,6},{6,2},{1... | collective-permute-start | bytes 98312 | tf_op jit(solution)/shard_map/ppermute | solution.py:475
  20.6 4.3 %collective-permute-start.5 = (bf16[64,256]{1,0:T(8,128)(2,1)S(1)}, bf16[64,256]{1,0:T(8,128)(2,1)S(1)}, u32[]{:S(2)}, u32[]{:S(2)}) collective-permute-start(bf16[64,256]{1,0:T(8,128)(2,1)S(1)} %get-tuple-element.49), channel_id=1, source_target_pairs={{0,8},{4,12},{8,0},{12,4},{1,9},{5,13},{9,1},{13,5},{2,10},{6,14},... | collective-permute-start | bytes 98312 | tf_op jit(solution)/shard_map/ppermute | solution.py:475
  21.2 3.7 %collective-permute-start.6 = (bf16[64,256]{1,0:T(8,128)(2,1)S(1)}, bf16[64,256]{1,0:T(8,128)(2,1)S(1)}, u32[]{:S(2)}, u32[]{:S(2)}) collective-permute-start(bf16[64,256]{1,0:T(8,128)(2,1)S(1)} %get-tuple-element.50), channel_id=1, source_target_pairs={{0,12},{4,8},{8,4},{12,0},{1,13},{5,9},{9,5},{13,1},{2,14},{6,10},... | collective-permute-start | bytes 98312 | tf_op jit(solution)/shard_map/ppermute | solution.py:475
  25.2 4.8 %collective-permute-start.8 = (bf16[768,256]{1,0:T(8,128)(2,1)S(1)}, bf16[768,256]{1,0:T(8,128)(2,1)S(1)}, u32[]{:S(2)}, u32[]{:S(2)}) collective-permute-start(bf16[768,256]{1,0:T(8,128)(2,1)S(1)} %get-tuple-element.54), channel_id=1, source_target_pairs={{0,4},{4,0},{8,12},{12,8},{1,5},{5,1},{9,13},{13,9},{2,6},{6,2},{1... | collective-permute-start | bytes 1179656 | tf_op jit(solution)/shard_map/ppermute | solution.py:475
  25.4 10.9 %collective-permute-start.9 = (bf16[768,256]{1,0:T(8,128)(2,1)S(1)}, bf16[768,256]{1,0:T(8,128)(2,1)S(1)}, u32[]{:S(2)}, u32[]{:S(2)}) collective-permute-start(bf16[768,256]{1,0:T(8,128)(2,1)S(1)} %get-tuple-element.55), channel_id=1, source_target_pairs={{0,12},{4,8},{8,4},{12,0},{1,13},{5,9},{9,5},{13,1},{2,14},{6,10},... | collective-permute-start | bytes 1179656 | tf_op jit(solution)/shard_map/ppermute | solution.py:475
  26.6 9.3 %collective-permute-start.10 = (bf16[32,16,128]{2,1,0:T(8,128)(2,1)S(1)}, bf16[32,16,128]{2,1,0:T(8,128)(2,1)S(1)}, u32[]{:S(2)}, u32[]{:S(2)}) collective-permute-start(bf16[32,16,128]{2,1,0:T(8,128)(2,1)S(1)} %get-tuple-element.56.refs_4_), channel_id=1, source_target_pairs={{0,2},{1,3},{2,0},{3,1},{4,6},{5,7},{6,4},{7,5},{8,10},{9,11},{10,... | collective-permute-start | bytes 393224 | tf_op jit(solution)/shard_map/ppermute | solution.py:475
  29.0 7.9 %collective-permute-start.12 = (bf16[32,16,128]{2,1,0:T(8,128)(2,1)S(1)}, bf16[32,16,128]{2,1,0:T(8,128)(2,1)S(1)}, u32[]{:S(2)}, u32[]{:S(2)}) collective-permute-start(bf16[32,16,128]{2,1,0:T(8,128)(2,1)S(1)} %get-tuple-element.56.refs_4_), channel_id=1, source_target_pairs={{0,1},{1,0},{2,3},{3,2},{4,5},{5,4},{6,7},{7,6},{8,9},{9,8},{10,11... | collective-permute-start | bytes 393224 | tf_op jit(solution)/shard_map/ppermute | solution.py:475
  35.9 5.0 %collective-permute-start.11 = (bf16[32,16,128]{2,1,0:T(8,128)(2,1)S(1)}, bf16[32,16,128]{2,1,0:T(8,128)(2,1)S(1)}, u32[]{:S(2)}, u32[]{:S(2)}) collective-permute-start(bf16[32,16,128]{2,1,0:T(8,128)(2,1)S(1)} %gate.1.refs_6_), channel_id=1, source_target_pairs={{0,1},{1,0},{2,3},{3,2},{4,5},{5,4},{6,7},{7,6},{8,9},{9,8},{10,11... | collective-permute-start | bytes 393224 | tf_op jit(solution)/shard_map/ppermute | solution.py:475

commit v15 on v9

--- a/solution.py
+++ b/solution.py
@@ -38,15 +38,16 @@
         seeds.append(np.cos(angle).reshape(2, BLOCK, -1))
         step = angles(np.full(8, BLOCK), freqs.reshape(-1), count)
         twice.append(2.0 * np.cos(step))
-    return np.stack(seeds).astype(np.float32), np.stack(twice).astype(np.float32)
-
-
-def make_tables(seed_ref, twice_ref, table_ref):
+    blocks = np.stack(seeds).reshape(4, 2 * BLOCK, -1)
+    return np.concatenate([blocks, np.stack(twice)], axis=1).astype(np.float32)
+
+
+def make_tables(seed_ref, table_ref):
     for first in (0, 2):
         state = {}
         for m in (first, first + 1):
-            twice = jnp.concatenate([twice_ref[m]] * (BLOCK // 8), axis=0)
-            state[m] = (seed_ref[m, 0], seed_ref[m, 1], twice)
+            twice = jnp.concatenate([seed_ref[m, 2 * BLOCK:]] * (BLOCK // 8), axis=0)
+            state[m] = (seed_ref[m, :BLOCK], seed_ref[m, BLOCK:2 * BLOCK], twice)
         for a in range(table_ref.shape[1] // BLOCK):
             for m, (here, after, twice) in state.items():
                 table_ref[m, a * BLOCK:(a + 1) * BLOCK, :] = here.astype(jnp.bfloat16)
@@ -86,12 +87,12 @@
 
 
 def spectra_kernel(
-    n_win, n_rcv, r_dev, valid_hbm, src_hbm, x_hbm, seed_hbm, twice_hbm, *refs
+    n_win, n_rcv, r_dev, valid_hbm, src_hbm, x_hbm, seed_hbm, *refs
 ):
     r_refs = refs[:n_win]
     q_refs = refs[n_win:n_win + n_rcv]
     (plan_ref, flag_ref, x_ref, even_ref, odd_ref, white_ref, sel_ref, order_ref, table_ref,
-     seed_ref, twice_ref, valid_ref, src_ref, sems, x_sems) = refs[n_win + n_rcv:]
+     seed_ref, valid_ref, src_ref, sems, x_sems) = refs[n_win + n_rcv:]
     chunks, rows, samples = x_ref.shape
     w_step = rows // r_dev
     n_own = src_ref.shape[0] // n_rcv
@@ -100,21 +101,20 @@
     rcv = lax.axis_index("rcv")
 
     def small(k):
-        source = (seed_hbm, twice_hbm, src_hbm, valid_hbm)[k]
-        target = (seed_ref, twice_ref, src_ref, valid_ref)[k]
+        source = (seed_hbm, src_hbm, valid_hbm)[k]
+        target = (seed_ref, src_ref, valid_ref)[k]
         return pltpu.make_async_copy(source, target, sems.at[k])
 
     def chunk(k):
         return pltpu.make_async_copy(x_hbm.at[pl.ds(k * rows, rows)], x_ref.at[k], x_sems.at[k])
 
-    for k in range(4):
+    for k in range(3):
         small(k).start()
     for k in range(chunks):
         chunk(k).start()
     small(0).wait()
+    make_tables(seed_ref, table_ref)
     small(1).wait()
-    make_tables(seed_ref, twice_ref, table_ref)
-    small(2).wait()
     order_sources(src_ref, r_dev, n_own, order_ref, plan_ref, flag_ref)
     stations = []
     for d in range(n_rcv):
@@ -127,7 +127,7 @@
     inside = (wanted >= 0) & (wanted < r_dev)
     hit = inside & (column == wanted + (out_row // n_own) % w_step * r_dev)
     sel_ref[...] = hit.astype(jnp.float32).astype(jnp.bfloat16)
-    small(3).wait()
+    small(2).wait()
 
     def product(lhs, table):
         return jnp.dot(lhs, table, preferred_element_type=jnp.float32)
@@ -199,14 +199,14 @@
     every = w_dev * r_dev
     rows = every // chunks
     lanes = 2 * F // n_win
-    seed, twice = (jnp.asarray(t) for t in table_seeds(samples, F, samples // 16, n_win))
+    seed = jnp.asarray(table_seeds(samples, F, samples // 16, n_win))
     shapes = [jax.ShapeDtypeStruct((every, lanes), jnp.bfloat16)] * n_win
     shapes += [jax.ShapeDtypeStruct((n_win, w_dev * n_own, lanes), jnp.bfloat16)] * n_rcv
     shapes += [jax.ShapeDtypeStruct((8, 128), jnp.int32), jax.ShapeDtypeStruct((1,), jnp.int32)]
     vmem = pl.BlockSpec(memory_space=VMEM)
     out = pl.pallas_call(
         functools.partial(spectra_kernel, n_win, n_rcv, r_dev),
-        in_specs=[pl.BlockSpec(memory_space=pltpu.HBM)] * 5,
+        in_specs=[pl.BlockSpec(memory_space=pltpu.HBM)] * 4,
         out_specs=[vmem] * (len(shapes) - 1) + [pl.BlockSpec(memory_space=SMEM)],
         out_shape=shapes,
         scratch_shapes=[
@@ -218,10 +218,9 @@
             pltpu.VMEM((n_src, 128), jnp.float32),
             pltpu.VMEM((4, samples // 4, F // 2), jnp.bfloat16),
             pltpu.VMEM(seed.shape, jnp.float32),
-            pltpu.VMEM(twice.shape, jnp.float32),
             pltpu.SMEM(valid.shape, jnp.int32),
             pltpu.SMEM(src_station.shape, jnp.int32),
-            pltpu.SemaphoreType.DMA((4,)),
+            pltpu.SemaphoreType.DMA((3,)),
             pltpu.SemaphoreType.DMA((chunks,)),
         ],
         compiler_params=pltpu.CompilerParams(vmem_limit_bytes=36 * 2**20),
@@ -230,7 +229,7 @@
             transcendentals=0,
         ),
         name="spectra",
-    )(*(in_hbm(x) for x in (valid, src_station, traces.reshape(every, samples), seed, twice)))
+    )(*(in_hbm(x) for x in (valid, src_station, traces.reshape(every, samples), seed)))
     return out[:n_win], out[n_win:n_win + n_rcv], out[-2], out[-1]
 
 
@@ -387,7 +386,7 @@
 def stacks_kernel(shares, n_win, w_dev, r_dev, n_own, bins, plan_hbm, *refs):
     t_refs = refs[:n_win]
     s_refs = refs[n_win:n_win + len(shares)]
-    out_hbm, prod_ref, out_ref, plan_ref, sems, plan_sem = refs[-6:]
+    out_hbm, prod_ref, out_ref, plan_ref, sem, plan_sem = refs[-6:]
     plan_copy = pltpu.make_async_copy(plan_hbm, plan_ref, plan_sem)
     plan_copy.start()
     windows = n_win * w_dev
@@ -415,16 +414,13 @@
 
     scale = 1.0 / math.sqrt(windows)
     plan_copy.wait()
-    copies = []
     for s in range(count):
         for c in range(2):
             turned = prod_ref[c, pl.ds(s, bins, stride=pitch), :].T
             out_ref[s, pl.ds(c, r_dev, stride=2), :] = turned[:r_dev] * scale
         row = plan_ref[0, (rcv ^ shares[s // n_own]) * n_own + s % n_own]
-        copies.append(pltpu.make_async_copy(out_ref.at[s], out_hbm.at[row], sems.at[s]))
-        copies[-1].start()
-    for copy in copies:
-        copy.wait()
+        pltpu.make_async_copy(out_ref.at[s], out_hbm.at[row], sem).start()
+    pltpu.make_async_copy(out_ref, out_hbm.at[pl.ds(0, count)], sem).wait()
 
 
 def stacks_call(out, plan, turned, sources, shares, n_rcv, w_dev, r_dev, bins):
@@ -450,7 +446,7 @@
             pltpu.VMEM((2, (count // 8 | 1) * 8 * bins, 128), jnp.float32),
             pltpu.VMEM((count, 2 * r_dev, bins), jnp.float32),
             pltpu.SMEM(plan.shape, jnp.int32),
-            pltpu.SemaphoreType.DMA((count,)),
+            pltpu.SemaphoreType.DMA,
             pltpu.SemaphoreType.DMA,
         ],
         compiler_params=pltpu.CompilerParams(vmem_limit_bytes=20 * 2**20),

time: 42.3 us -> 42.2 us (level)
  transfers between devices with their start and end apart: 11 -> 11, of which waited for: 5 -> 5; matrix products, arithmetic and copies ran while one was open for 0% -> 0% of each run, Pallas kernels for 11% -> 10%
where the time goes in v15:
time: 42.2 us; the launch traced here: 42.1 us
  Pallas kernels  15 us (36%)
  starting transfers between devices  13.8 us (33%)
  waiting for transfers between devices  12 us (28%)
  between operations  0.93 us (2%)
    ppermute x9, waiting for transfers between devices, swap(): return lax.ppermute(value, axis, [(i, i ^ by) for i in range(size)])  9.78 us
    ppermute x9, starting transfers between devices, swap(): return lax.ppermute(value, axis, [(i, i ^ by) for i in range(size)])  8.73 us
    pallas_call x1, Pallas kernels, spectra_call(): pl.pallas_call(functools.partial(spectra_kernel, n_win, n_rcv, r_dev), in...  8.61 us
    ppermute x2, starting transfers between devices, body(): near[i] = lax.ppermute(picked[i], 'rcv', pairs)  5.11 us
    pallas_call x2, Pallas kernels, stacks_call(): pl.pallas_call(functools.partial(stacks_kernel, shares, n_win, w_dev, r_d...  3.89 us
    ppermute x2, waiting for transfers between devices, body(): near[i] = lax.ppermute(picked[i], 'rcv', pairs)  2.25 us
    pallas_call x4, Pallas kernels, turn_call(): pl.pallas_call(functools.partial(turn_kernel, r_dev), in_specs=[vmem] * l...  2.15 us
  transfers between devices with their start and end apart: 11, of which 5 were waited for; matrix products, arithmetic and copies ran while one was open for 0% of the time, Pallas kernels for 10%

profile of v15, /device:TPU:0, one launch (start us, length us, event | category | flops | bytes accessed | tf_op | source)
XLA Modules:
  0.0 42.1 jit_solution(6446804684705378077)
XLA Ops:
  0.0 8.6 %spectra.1 = (bf16[768,256]{1,0:T(8,128)(2,1)S(1)}, bf16[768,256]{1,0:T(8,128)(2,1)S(1)}, bf16[768,256]{1,0:T(8,128)(2,1)S(1)}, bf16[768,256]{1,0:T(8,128)(2,1)S...) custom-call(s32[8]{0:T(128)} %valid_hbm.1, ...), custom_call_target="tpu_custom_call" | custom-call | flops 2415919104 | bytes 6291456 | tf_op jit(solution)/shard_map/spectra/pallas_call | solution.py:207
  8.6 3.0 %collective-permute-start.7 = (bf16[768,256]{1,0:T(8,128)(2,1)S(1)}, bf16[768,256]{1,0:T(8,128)(2,1)S(1)}, u32[]{:S(2)}, u32[]{:S(2)}) collective-permute-start(bf16[768,256]{1,0:T(8,128)(2,1)S(1)} %get-tuple-element.51), channel_id=1, source_target_pairs={{0,8},{4,12},{8,0},{12,4},{1,9},{5,13},{9,1},{13,5},{2,10},{6,14},... | collective-permute-start | bytes 1179656 | tf_op jit(solution)/shard_map/ppermute | solution.py:462
  11.7 0.7 %collective-permute-start.2 = (bf16[4,64,256]{2,1,0:T(8,128)(2,1)S(1)}, bf16[4,64,256]{2,1,0:T(8,128)(2,1)S(1)}, u32[]{:S(2)}, u32[]{:S(2)}) collective-permute-start(bf16[4,64,256]{2,1,0:T(8,128)(2,1)S(1)} %get-tuple-element.44), channel_id=1, source_target_pairs={{1,2},{2,1},{5,6},{6,5},{9,10},{10,9},{13,14},{14,13},{17,18},{18,... | collective-permute-start | bytes 393224 | tf_op jit(solution)/shard_map/ppermute | solution.py:497
  12.3 4.5 %collective-permute-start.3 = (bf16[4,64,256]{2,1,0:T(8,128)(2,1)S(1)}, bf16[4,64,256]{2,1,0:T(8,128)(2,1)S(1)}, u32[]{:S(2)}, u32[]{:S(2)}) collective-permute-start(bf16[4,64,256]{2,1,0:T(8,128)(2,1)S(1)} %get-tuple-element.45), channel_id=1, source_target_pairs={{0,1},{1,0},{2,3},{3,2},{4,5},{5,4},{6,7},{7,6},{8,9},{9,8},{10,11... | collective-permute-start | bytes 393224 | tf_op jit(solution)/shard_map/ppermute | solution.py:497
  17.5 2.2 %collective-permute-done.3 = bf16[4,64,256]{2,1,0:T(8,128)(2,1)S(1)} collective-permute-done((bf16[4,64,256]{2,1,0:T(8,128)(2,1)S(1)}, bf16[4,64,256]{2,1,0:T(8,128)(2,1)S(1)}, u32[]{:S(2)}, u32[]{:S(2)}) %collective-permute-start.3) | collective-permute-done | bytes 131104 | tf_op jit(solution)/shard_map/ppermute | solution.py:497
  19.7 0.2 conditional.1
  20.0 0.1 collective-permute-start.4
  20.0 0.6 %collective-permute-start.5 = (bf16[64,256]{1,0:T(8,128)(2,1)S(1)}, bf16[64,256]{1,0:T(8,128)(2,1)S(1)}, u32[]{:S(2)}, u32[]{:S(2)}) collective-permute-start(bf16[64,256]{1,0:T(8,128)(2,1)S(1)} %get-tuple-element.49), channel_id=1, source_target_pairs={{0,8},{4,12},{8,0},{12,4},{1,9},{5,13},{9,1},{13,5},{2,10},{6,14},... | collective-permute-start | bytes 98312 | tf_op jit(solution)/shard_map/ppermute | solution.py:462
  20.6 1.3 %collective-permute-start.6 = (bf16[64,256]{1,0:T(8,128)(2,1)S(1)}, bf16[64,256]{1,0:T(8,128)(2,1)S(1)}, u32[]{:S(2)}, u32[]{:S(2)}) collective-permute-start(bf16[64,256]{1,0:T(8,128)(2,1)S(1)} %get-tuple-element.50), channel_id=1, source_target_pairs={{0,12},{4,8},{8,4},{12,0},{1,13},{5,9},{9,5},{13,1},{2,14},{6,10},... | collective-permute-start | bytes 98312 | tf_op jit(solution)/shard_map/ppermute | solution.py:462
  21.9 2.4 %collective-permute-done.5.refs_2_ = bf16[64,256]{1,0:T(8,128)(2,1)S(1)} collective-permute-done((bf16[64,256]{1,0:T(8,128)(2,1)S(1)}, bf16[64,256]{1,0:T(8,128)(2,1)S(1)}, u32[]{:S(2)}, u32[]{:S(2)}) %collective-permute-start.5) | collective-permute-done | bytes 32800 | tf_op jit(solution)/shard_map/ppermute | solution.py:462
  24.3 0.3 lefts.1
  24.6 0.2 collective-permute-start.8
  24.9 1.1 %collective-permute-start.9 = (bf16[768,256]{1,0:T(8,128)(2,1)S(1)}, bf16[768,256]{1,0:T(8,128)(2,1)S(1)}, u32[]{:S(2)}, u32[]{:S(2)}) collective-permute-start(bf16[768,256]{1,0:T(8,128)(2,1)S(1)} %get-tuple-element.55), channel_id=1, source_target_pairs={{0,12},{4,8},{8,4},{12,0},{1,13},{5,9},{9,5},{13,1},{2,14},{6,10},... | collective-permute-start | bytes 1179656 | tf_op jit(solution)/shard_map/ppermute | solution.py:462
  26.0 1.9 %collective-permute-start.10 = (bf16[32,16,128]{2,1,0:T(8,128)(2,1)S(1)}, bf16[32,16,128]{2,1,0:T(8,128)(2,1)S(1)}, u32[]{:S(2)}, u32[]{:S(2)}) collective-permute-start(bf16[32,16,128]{2,1,0:T(8,128)(2,1)S(1)} %get-tuple-element.56.refs_4_), channel_id=1, source_target_pairs={{0,2},{1,3},{2,0},{3,1},{4,6},{5,7},{6,4},{7,5},{8,10},{9,11},{10,... | collective-permute-start | bytes 393224 | tf_op jit(solution)/shard_map/ppermute | solution.py:462
  27.9 0.5 %turn.4.refs_0_ = bf16[128,16,256]{2,1,0:T(8,128)(2,1)S(1)} custom-call(bf16[768,256]{1,0:T(8,128)(2,1)S(1)} %get-tuple-element.41.refs_0_), custom_call_target="tpu_custom_call" | custom-call | flops 134217728 | bytes 2097152 | tf_op jit(solution)/shard_map/turn/pallas_call | solution.py:270
  28.4 0.5 %collective-permute-start.12 = (bf16[32,16,128]{2,1,0:T(8,128)(2,1)S(1)}, bf16[32,16,128]{2,1,0:T(8,128)(2,1)S(1)}, u32[]{:S(2)}, u32[]{:S(2)}) collective-permute-start(bf16[32,16,128]{2,1,0:T(8,128)(2,1)S(1)} %get-tuple-element.56.refs_4_), channel_id=1, source_target_pairs={{0,1},{1,0},{2,3},{3,2},{4,5},{5,4},{6,7},{7,6},{8,9},{9,8},{10,11... | collective-permute-start | bytes 393224 | tf_op jit(solution)/shard_map/ppermute | solution.py:462
  28.9 0.5 %turn.6.refs_2_ = bf16[128,16,256]{2,1,0:T(8,128)(2,1)S(1)} custom-call(bf16[768,256]{1,0:T(8,128)(2,1)S(1)} %collective-permute-done.7.refs_4_.refs_0_), custom_call_target="tpu_custom_call" | custom-call | flops 134217728 | bytes 2097152 | tf_op jit(solution)/shard_map/turn/pallas_call | solution.py:270
  29.5 0.5 %turn.5.refs_1_ = bf16[128,16,256]{2,1,0:T(8,128)(2,1)S(1)} custom-call(bf16[768,256]{1,0:T(8,128)(2,1)S(1)} %collective-permute-done.8.refs_0_), custom_call_target="tpu_custom_call" | custom-call | flops 134217728 | bytes 2097152 | tf_op jit(solution)/shard_map/turn/pallas_call | solution.py:270
  30.0 5.2 %collective-permute-done.10.refs_3_ = bf16[32,16,128]{2,1,0:T(8,128)(2,1)S(1)} collective-permute-done((bf16[32,16,128]{2,1,0:T(8,128)(2,1)S(1)}, bf16[32,16,128]{2,1,0:T(8,128)(2,1)S(1)}, u32[]{:S(2)}, u32[]{:S(2)}) %collective-permute-start.10) | collective-permute-done | bytes 131104 | tf_op jit(solution)/shard_map/ppermute | solution.py:462
  35.3 0.5 %collective-permute-done.9.refs_0_ = bf16[768,256]{1,0:T(8,128)(2,1)S(1)} collective-permute-done((bf16[768,256]{1,0:T(8,128)(2,1)S(1)}, bf16[768,256]{1,0:T(8,128)(2,1)S(1)}, u32[]{:S(2)}, u32[]{:S(2)}) %collective-permute-start.9) | collective-permute-done | bytes 393248 | tf_op jit(solution)/shard_map/ppermute | solution.py:462
  35.8 0.5 %turn.7.refs_3_ = bf16[128,16,256]{2,1,0:T(8,128)(2,1)S(1)} custom-call(bf16[768,256]{1,0:T(8,128)(2,1)S(1)} %collective-permute-done.9.refs_0_), custom_call_target="tpu_custom_call" | custom-call | flops 134217728 | bytes 2097152 | tf_op jit(solution)/shard_map/turn/pallas_call | solution.py:270
  36.4 2.2 %stacks.2.refs_5_ = f32[32,192,128]{2,1,0:T(8,128)} custom-call(s32[8,128]{1,0:T(8,128)S(1)} %get-tuple-element.40.plan_hbm, bf16[128,16,256]{2,1,0:T(8,128)(2,1)S(1)} %turn.4.refs_0_, bf16[128,16,256]{2,1,0:T(8,128)(2,1)S(1)} %turn.5.refs_1_, bf16[128,16,256]{2,1,0:T(8,128)(2,1)S(1)} %turn.6.refs_2_, bf16[128,16,256]{2,1,0:T(8,128)(2,1)S(1)} %turn.7.refs_3_, ...), custom_call_target="tpu_custom_call" | custom-call | flops 75497472 | bytes 6291456 | tf_op jit(solution)/shard_map/stacks/pallas_call | solution.py:439
  38.6 1.6 %collective-permute-done.11.refs_4_ = bf16[32,16,128]{2,1,0:T(8,128)(2,1)S(1)} collective-permute-done((bf16[32,16,128]{2,1,0:T(8,128)(2,1)S(1)}, bf16[32,16,128]{2,1,0:T(8,128)(2,1)S(1)}, u32[]{:S(2)}, u32[]{:S(2)}) %collective-permute-start.11) | collective-permute-done | bytes 131104 | tf_op jit(solution)/shard_map/ppermute | solution.py:462
  40.2 1.7 %stacks.3 = f32[32,192,128]{2,1,0:T(8,128)} custom-call(s32[8,128]{1,0:T(8,128)S(1)} %get-tuple-element.40.plan_hbm, bf16[128,16,256]{2,1,0:T(8,128)(2,1)S(1)} %turn.4.refs_0_, bf16[128,16,256]{2,1,0:T(8,128)(2,1)S(1)} %turn.5.refs_1_, bf16[128,16,256]{2,1,0:T(8,128)(2,1)S(1)} %turn.6.refs_2_, ...), custom_call_target="tpu_custom_call", output_to_operand_aliasing={{}: (6, {})} | custom-call | flops 25165824 | bytes 6291456 | tf_op jit(solution)/shard_map/stacks/pallas_call | solution.py:439
  (10 shorter events, 0.1 us)
Async XLA Ops:
  8.6 15.7 %collective-permute-start.7 = (bf16[768,256]{1,0:T(8,128)(2,1)S(1)}, bf16[768,256]{1,0:T(8,128)(2,1)S(1)}, u32[]{:S(2)}, u32[]{:S(2)}) collective-permute-start(bf16[768,256]{1,0:T(8,128)(2,1)S(1)} %get-tuple-element.51), channel_id=1, source_target_pairs={{0,8},{4,12},{8,0},{12,4},{1,9},{5,13},{9,1},{13,5},{2,10},{6,14},... | collective-permute-start | bytes 1179656 | tf_op jit(solution)/shard_map/ppermute | solution.py:462
  11.7 5.8 %collective-permute-start.2 = (bf16[4,64,256]{2,1,0:T(8,128)(2,1)S(1)}, bf16[4,64,256]{2,1,0:T(8,128)(2,1)S(1)}, u32[]{:S(2)}, u32[]{:S(2)}) collective-permute-start(bf16[4,64,256]{2,1,0:T(8,128)(2,1)S(1)} %get-tuple-element.44), channel_id=1, source_target_pairs={{1,2},{2,1},{5,6},{6,5},{9,10},{10,9},{13,14},{14,13},{17,18},{18,... | collective-permute-start | bytes 393224 | tf_op jit(solution)/shard_map/ppermute | solution.py:497
  12.3 7.4 %collective-permute-start.3 = (bf16[4,64,256]{2,1,0:T(8,128)(2,1)S(1)}, bf16[4,64,256]{2,1,0:T(8,128)(2,1)S(1)}, u32[]{:S(2)}, u32[]{:S(2)}) collective-permute-start(bf16[4,64,256]{2,1,0:T(8,128)(2,1)S(1)} %get-tuple-element.45), channel_id=1, source_target_pairs={{0,1},{1,0},{2,3},{3,2},{4,5},{5,4},{6,7},{7,6},{8,9},{9,8},{10,11... | collective-permute-start | bytes 393224 | tf_op jit(solution)/shard_map/ppermute | solution.py:497
  20.0 1.9 %collective-permute-start.4 = (bf16[64,256]{1,0:T(8,128)(2,1)S(1)}, bf16[64,256]{1,0:T(8,128)(2,1)S(1)}, u32[]{:S(2)}, u32[]{:S(2)}) collective-permute-start(bf16[64,256]{1,0:T(8,128)(2,1)S(1)} %get-tuple-element.48), channel_id=1, source_target_pairs={{0,4},{4,0},{8,12},{12,8},{1,5},{5,1},{9,13},{13,9},{2,6},{6,2},{1... | collective-permute-start | bytes 98312 | tf_op jit(solution)/shard_map/ppermute | solution.py:462
  20.0 4.3 %collective-permute-start.5 = (bf16[64,256]{1,0:T(8,128)(2,1)S(1)}, bf16[64,256]{1,0:T(8,128)(2,1)S(1)}, u32[]{:S(2)}, u32[]{:S(2)}) collective-permute-start(bf16[64,256]{1,0:T(8,128)(2,1)S(1)} %get-tuple-element.49), channel_id=1, source_target_pairs={{0,8},{4,12},{8,0},{12,4},{1,9},{5,13},{9,1},{13,5},{2,10},{6,14},... | collective-permute-start | bytes 98312 | tf_op jit(solution)/shard_map/ppermute | solution.py:462
  20.6 3.7 %collective-permute-start.6 = (bf16[64,256]{1,0:T(8,128)(2,1)S(1)}, bf16[64,256]{1,0:T(8,128)(2,1)S(1)}, u32[]{:S(2)}, u32[]{:S(2)}) collective-permute-start(bf16[64,256]{1,0:T(8,128)(2,1)S(1)} %get-tuple-element.50), channel_id=1, source_target_pairs={{0,12},{4,8},{8,4},{12,0},{1,13},{5,9},{9,5},{13,1},{2,14},{6,10},... | collective-permute-start | bytes 98312 | tf_op jit(solution)/shard_map/ppermute | solution.py:462
  24.6 4.8 %collective-permute-start.8 = (bf16[768,256]{1,0:T(8,128)(2,1)S(1)}, bf16[768,256]{1,0:T(8,128)(2,1)S(1)}, u32[]{:S(2)}, u32[]{:S(2)}) collective-permute-start(bf16[768,256]{1,0:T(8,128)(2,1)S(1)} %get-tuple-element.54), channel_id=1, source_target_pairs={{0,4},{4,0},{8,12},{12,8},{1,5},{5,1},{9,13},{13,9},{2,6},{6,2},{1... | collective-permute-start | bytes 1179656 | tf_op jit(solution)/shard_map/ppermute | solution.py:462
  24.9 10.9 %collective-permute-start.9 = (bf16[768,256]{1,0:T(8,128)(2,1)S(1)}, bf16[768,256]{1,0:T(8,128)(2,1)S(1)}, u32[]{:S(2)}, u32[]{:S(2)}) collective-permute-start(bf16[768,256]{1,0:T(8,128)(2,1)S(1)} %get-tuple-element.55), channel_id=1, source_target_pairs={{0,12},{4,8},{8,4},{12,0},{1,13},{5,9},{9,5},{13,1},{2,14},{6,10},... | collective-permute-start | bytes 1179656 | tf_op jit(solution)/shard_map/ppermute | solution.py:462
  26.0 9.3 %collective-permute-start.10 = (bf16[32,16,128]{2,1,0:T(8,128)(2,1)S(1)}, bf16[32,16,128]{2,1,0:T(8,128)(2,1)S(1)}, u32[]{:S(2)}, u32[]{:S(2)}) collective-permute-start(bf16[32,16,128]{2,1,0:T(8,128)(2,1)S(1)} %get-tuple-element.56.refs_4_), channel_id=1, source_target_pairs={{0,2},{1,3},{2,0},{3,1},{4,6},{5,7},{6,4},{7,5},{8,10},{9,11},{10,... | collective-permute-start | bytes 393224 | tf_op jit(solution)/shard_map/ppermute | solution.py:462
  28.4 7.9 %collective-permute-start.12 = (bf16[32,16,128]{2,1,0:T(8,128)(2,1)S(1)}, bf16[32,16,128]{2,1,0:T(8,128)(2,1)S(1)}, u32[]{:S(2)}, u32[]{:S(2)}) collective-permute-start(bf16[32,16,128]{2,1,0:T(8,128)(2,1)S(1)} %get-tuple-element.56.refs_4_), channel_id=1, source_target_pairs={{0,1},{1,0},{2,3},{3,2},{4,5},{5,4},{6,7},{7,6},{8,9},{9,8},{10,11... | collective-permute-start | bytes 393224 | tf_op jit(solution)/shard_map/ppermute | solution.py:462
  35.3 5.0 %collective-permute-start.11 = (bf16[32,16,128]{2,1,0:T(8,128)(2,1)S(1)}, bf16[32,16,128]{2,1,0:T(8,128)(2,1)S(1)}, u32[]{:S(2)}, u32[]{:S(2)}) collective-permute-start(bf16[32,16,128]{2,1,0:T(8,128)(2,1)S(1)} %gate.1.refs_6_), channel_id=1, source_target_pairs={{0,1},{1,0},{2,3},{3,2},{4,5},{5,4},{6,7},{7,6},{8,9},{9,8},{10,11... | collective-permute-start | bytes 393224 | tf_op jit(solution)/shard_map/ppermute | solution.py:462
